TPU v7x, 128 devices: a whole 4x4x4 slice. The times are simulated.
128 devices in a mesh: row: 16 (over x, z), col: 8 (over y, core).
Axes of the slice: x: 4, y: 4, z: 4, core: 2. Of those that a mesh axis runs over, the one named last changes fastest.
Arguments:
- amplitudes: float32 [48, 6, 8, 1296], P('row', None, 'col'), may hold values from -6 to 6
- vvvv: float32 [8, 1296, 10368], P('col', 'row'), may hold values from -0.0625 to 0.0625
- ovov: float32 [1728, 8, 216], P('row', 'col'), may hold values from -0.4375 to 0.4375
- eps_occ: float32 [8, 6], replicated, may hold values from -1 to -0.25
- eps_vir: float32 [8, 36], replicated, may hold values from 0.25 to 1.5
- occ_count: int32 [8], replicated, may hold values from 4 to 6, as said below
- vir_count: int32 [8], replicated, may hold values from 1 to 36, 256 in all
Outputs:
- updated: float32 [48, 6, 8, 1296], P('row', None, 'col')
Inputs may be any that keep to these rules, and one draw needn't show every extreme that they name: `occ_count`: every irrep has more than half of its 6 occupied slots live; one irrep has exactly 6. `vir_count`: the entries sum to 256; one of them is exactly 36.
All inputs are finite; a program needn't handle non-finite values.
Results may differ from a plain program's by a relative error of at most 0.00005.
Values sent between devices are 32-bit elements; how exact they have to be, the bound alone decides.
No kernel may reach another device: no remote copies, remote signals or barrier semaphores. Data moves between devices by JAX's collectives and lax.ppermute only.
A program may use at most 128 MiB of HBM per device.

v0:
```python
import jax
import jax.numpy as jnp
from jax import lax
from jax.sharding import PartitionSpec as P


def partner_2(value, axis, stride):
    mask = 2**stride
    pairs = [(source, source ^ mask) for source in range(lax.axis_size(axis))]
    return lax.ppermute(value, axis, pairs)


def on_device(amplitudes, vvvv, ovov, eps_occ, eps_vir, occ_count, vir_count):
    row_devices = lax.axis_size("row")
    row_place = lax.axis_index("row")
    col_place = lax.axis_index("col")
    local_rows = amplitudes.shape[0]
    occ_slots = amplitudes.shape[1]
    irrep_local = amplitudes.shape[2]
    pair_slots = amplitudes.shape[3]
    irreps = eps_occ.shape[0]
    vir_slots = eps_vir.shape[1]
    pair_slice = vvvv.shape[1]
    all_rows = local_rows * row_devices
    occ_live = (jnp.arange(occ_slots)[None, :] < occ_count[:, None]).astype(jnp.float32)
    vir_live = (jnp.arange(vir_slots)[None, :] < vir_count[:, None]).astype(jnp.float32)
    row_first = row_place * local_rows
    shell_index = row_first // occ_slots
    occ_rows = lax.dynamic_slice_in_dim(occ_live.reshape(-1), row_first, local_rows)
    energy_rows = lax.dynamic_slice_in_dim(eps_occ.reshape(-1), row_first, local_rows)
    occ_cols = lax.dynamic_slice_in_dim(occ_live, shell_index, 1, 0)[0]
    energy_cols = lax.dynamic_slice_in_dim(eps_occ, shell_index, 1, 0)[0]
    vir_here = lax.dynamic_slice_in_dim(vir_live, col_place * irrep_local, irrep_local, 0)
    vir_energy = lax.dynamic_slice_in_dim(eps_vir, col_place * irrep_local, irrep_local, 0)
    live_mask = (
        occ_rows[:, None, None, None, None]
        * occ_cols[None, :, None, None, None]
        * vir_here[None, None, :, :, None]
        * vir_here[None, None, :, None, :]
    )
    amplitude_live = (
        amplitudes.reshape(local_rows, occ_slots, irrep_local, vir_slots, vir_slots) * live_mask
    )
    amps_flat = amplitude_live.reshape(local_rows, occ_slots, irrep_local, pair_slots)
    integrals = vvvv.reshape(irrep_local * pair_slice, irreps * pair_slots)
    full_irreps = lax.all_gather(amps_flat, "col", axis=2, tiled=True)
    piece = lax.all_gather(full_irreps, "row", axis=0, tiled=True)
    flat_piece = piece.reshape(piece.shape[0], occ_slots, irreps * pair_slots)
    ladder_slices = jnp.einsum(
        "nkq,pq->nkp", flat_piece, integrals, precision=lax.Precision.HIGHEST
    )
    ladder_slices = ladder_slices.reshape(all_rows, occ_slots, irrep_local, pair_slice)
    ladder = lax.all_to_all(ladder_slices, "row", split_axis=0, concat_axis=3, tiled=True)
    ladder = ladder.reshape(local_rows, occ_slots, irrep_local, vir_slots, vir_slots)
    cycle_panel = ovov
    partner = partner_2(cycle_panel, "row", 0)
    upper_half = row_place // (1 << 0) % 2
    cycle_panel = jnp.where(
        upper_half == 0,
        jnp.concatenate([cycle_panel, partner], 0),
        jnp.concatenate([partner, cycle_panel], 0),
    )
    cycle_block = cycle_panel.reshape(occ_slots, vir_slots, irrep_local, occ_slots, vir_slots)
    cycle_term = jnp.einsum(
        "ikpac,kcpjb->ijpab", amplitude_live, cycle_block, precision=lax.Precision.HIGHEST
    )
    energy_gap = (
        energy_rows[:, None, None, None, None]
        + energy_cols[None, :, None, None, None]
        - vir_energy[None, None, :, :, None]
        - vir_energy[None, None, :, None, :]
    )
    result = live_mask * (ladder + cycle_term) / energy_gap
    return result.reshape(local_rows, occ_slots, irrep_local, pair_slots)


def solution(mesh):
    placed = (
        P("row", None, "col", None),
        P("col", "row", None),
        P("row", "col", None),
        P(),
        P(),
        P(),
        P(),
    )
    return jax.shard_map(
        on_device,
        mesh=mesh,
        in_specs=placed,
        out_specs=P("row", None, "col", None),
        check_vma=False,
    )
```

profile of v0, /device:TPU:1, one launch (start us, length us, event | category | flops | bytes accessed | tf_op | source)
XLA Modules:
  0.0 183.9 jit_solution(15003200837288455028)
XLA Ops:
  6.5 0.7 fusion.16
  7.3 0.7 fusion.17
  8.1 0.7 fusion.18
  8.9 0.7 fusion.19
  10.1 0.9 copy_multiply_fusion
  11.1 15.6 %all_gather.6 = f32[3,6,8,1296]{3,1,0,2:T(8,128)S(1)} all-gather(f32[3,6,1,1296]{3,1,0,2:T(8,128)S(1)} %copy_multiply_fusion), channel_id=1, replica_groups=mesh['row'=16,'col'=8] {'col'}, dimensions={2}, use_global_device_ids=true | all-gather | bytes 839808 | tf_op jit(solution)/shard_map/all_gather | solution.py:46
  26.6 1.1 copy.38
  27.8 1.7 collective-permute-start
  29.5 0.8 reshape.178
  30.3 1.1 reduce.1
  31.5 1.0 reshape.177
  32.6 88.9 %all-gather.2.cloned.1.call-done = f32[48,6,8,1296]{3,2,1,0:T(8,128)} async-done(((f32[3,6,8,1296]{3,2,1,0:T(8,128)}), f32[48,6,8,1296]{3,2,1,0:T(8,128)}) %all-gather.2.cloned.1.call-update) | async-done | bytes 11943952 | tf_op jit(solution)/shard_map/all_gather | solution.py:47
  121.4 10.2 %copy.39 = f32[48,6,8,1296]{3,2,0,1:T(8,128)} copy(f32[48,6,8,1296]{3,2,1,0:T(8,128)} %all-gather.2.cloned.1.call-done) | data formatting | bytes 23887872 | tf_op jit(solution)/shard_map/all_gather | solution.py:47
  131.6 14.0 %reshape.173 = f32[48,6,10368]{2,0,1:T(8,128)} reshape(f32[48,6,8,1296]{3,2,0,1:T(8,128)} %copy.39) | data formatting | bytes 23887872 | tf_op jit(solution)/shard_map/reshape | solution.py:48
  145.7 13.5 %fusion.6 = f32[48,6,1,81]{3,0,1,2:T(8,128)S(1)} fusion(f32[48,6,10368]{2,0,1:T(8,128)} %reshape.173, f32[1,81,10368]{2,0,1:T(1,128)S(1)} %copy-done), kind=kOutput, calls=%fused_computation.7 | convolution fusion | flops 2902376448 | bytes 15396480 | tf_op jit(solution)/shard_map/nkq,pq->nkp/dot_general | solution.py:49
  159.2 0.8 copy.40
  160.0 5.0 %all-to-all-start = ((f32[48,6,1,81]{3,2,1,0:T(1,128)}), f32[48,6,1,81]{3,2,1,0:T(1,128)S(1)}, u32[]{:S(2)}, u32[]{:S(2)}) async-start(f32[48,6,1,81]{3,2,1,0:T(1,128)} %copy.40), calls=%async_computation | async-start | bytes 294912 | tf_op jit(solution)/shard_map/all_to_all | solution.py:53
  165.0 1.8 fusion.13
  166.7 0.2 select_n.46
  167.0 4.9 %all-to-all-done = f32[48,6,1,81]{3,2,1,0:T(1,128)S(1)} async-done(((f32[48,6,1,81]{3,2,1,0:T(1,128)}), f32[48,6,1,81]{3,2,1,0:T(1,128)S(1)}, u32[]{:S(2)}, u32[]{:S(2)}) %all-to-all-start) | async-done | bytes 93344 | tf_op jit(solution)/shard_map/all_to_all | solution.py:53
  172.1 0.2 copy.43
  172.3 3.6 %fusion.5 = f32[3,6,1,36,36]{3,4,0,1,2:T(8,128)S(1)} fusion(f32[3,6,1,36,36]{3,4,0,1,2:T(8,128)S(1)} %copy.43, f32[6,36,6,36,1]{3,2,1,0,4:T(8,128)S(1)} %bitcast.43, f32[3,6,36,36]{3,2,1,0:T(8,128)} %reshape.177, f32[36]{0:T(128)S(1)} %get-tuple-element.6, f32[3,6,36]{2,0,1:T(4,128)S(1)} %broadcast_subtract_fusion, f32[36]{0:T(128)S(1)} %get-tuple-element.5, ...), kind=kOutput, calls=%fused_computation.6 | convolution fusion | flops 60629472 | bytes 474624 | tf_op jit(solution)/shard_map/ikpac,kcpjb->ijpab/dot_general | solution.py:64
  175.9 0.2 copy.44
  176.1 0.9 reshape.179
  (21 shorter events, 1.2 us)
Async XLA Ops:
  6.5 114.9 %all-gather.2.cloned.1.call-start = ((), (), s32[]{:S(2)}) async-start(), calls=%async_computation.1 | async-start | bytes 13787136 | tf_op jit(solution)/shard_map/all_gather | solution.py:47
  27.8 137.2 %collective-permute-start = (f32[108,1,216]{2,1,0:T(1,128)}, f32[108,1,216]{2,1,0:T(1,128)}, u32[]{:S(2)}, u32[]{:S(2)}) collective-permute-start(f32[108,1,216]{2,1,0:T(1,128)} %param.9), channel_id=1, source_target_pairs={{0,8},{8,0},{16,24},{24,16},{32,40},{40,32},{48,56},{56,48},{64,72... | collective-permute-start | bytes 279944 | tf_op jit(solution)/shard_map/ppermute | solution.py:10
  131.6 14.0 %copy-start = (f32[1,81,10368]{2,0,1:T(1,128)S(1)}, f32[1,81,10368]{2,0,1:T(1,128)}, u32[]{:S(2)}) copy-start(f32[1,81,10368]{2,0,1:T(1,128)} %param.8) | copy-start | bytes 10077700
  145.7 19.3 %copy-start.1 = (f32[108,1,216]{2,1,0:T(1,128)S(1)}, f32[108,1,216]{2,1,0:T(1,128)}, u32[]{:S(2)}) copy-start(f32[108,1,216]{2,1,0:T(1,128)} %param.9) | copy-start | bytes 279940
  160.0 11.9 %all-to-all-start = ((f32[48,6,1,81]{3,2,1,0:T(1,128)}), f32[48,6,1,81]{3,2,1,0:T(1,128)S(1)}, u32[]{:S(2)}, u32[]{:S(2)}) async-start(f32[48,6,1,81]{3,2,1,0:T(1,128)} %copy.40), calls=%async_computation | async-start | bytes 294912 | tf_op jit(solution)/shard_map/all_to_all | solution.py:53
Sparse Core Ops, SparseCore 0:
  27.9 93.4 all-gather.1
where the time goes:
time: 185 us; the launch traced here: 184 us
  waiting for transfers between devices  93.8 us (51%)
  local copies, waits for them, and re-layouts  31.8 us (17%)
  matrix products  17.1 us (9%)
  blocking collectives  15.6 us (8%)
  between operations  13.5 us (7%)
  starting transfers between devices  6.7 us (4%)
  other arithmetic  5.57 us (3%)
    all_gather x1, waiting for transfers between devices, on_device(): piece = lax.all_gather(full_irreps, 'row', axis=0, tiled=True)  88.9 us
    all_gather x1, blocking collectives, on_device(): full_irreps = lax.all_gather(amps_flat, 'col', axis=2, tiled=True)  15.6 us
    reshape x1, local copies, waits for them, and re-layouts, on_device(): flat_piece = piece.reshape(piece.shape[0], occ_slots, irreps * pair_slots)  14 us
    dot_general x1, matrix products, on_device(): jnp.einsum('nkq,pq->nkp', flat_piece, integrals, precision=lax.Precision....  13.5 us
    all_gather x1, local copies, waits for them, and re-layouts, on_device(): piece = lax.all_gather(full_irreps, 'row', axis=0, tiled=True)  10.2 us
    all_to_all x1, starting transfers between devices, on_device(): lax.all_to_all(ladder_slices, 'row', split_axis=0, concat_axis=3, tiled=T...  4.98 us
    all_to_all x1, waiting for transfers between devices, on_device(): lax.all_to_all(ladder_slices, 'row', split_axis=0, concat_axis=3, tiled=T...  4.88 us
  transfers between devices with their start and end apart: 3, of which 2 were waited for; matrix products, arithmetic and copies ran while one was open for 24% of the time, Pallas kernels for 0%

commit v1 on v0

v1 whole, which is shorter than its diff:
```python
import jax
import jax.numpy as jnp
from jax import lax
from jax.experimental import pallas as pl
from jax.experimental.pallas import tpu as pltpu
from jax.sharding import Mesh, PartitionSpec as P

AXES = ("x", "z", "y", "core")
SHIFTS = (1, -1, 2)
STEPS = (0, 1, -1, 2)
LANES = 128
TILES = 11
WINDOW = TILES * LANES
PAIR_WINDOW = 21 * LANES
MAIN = 8 * TILES
SHARD = 104
PAIR = 200
QUAD = 2 * PAIR
F32 = jnp.float32
BF16 = jnp.bfloat16
ANY = pl.BlockSpec(memory_space=pl.ANY)
SMEM = pl.BlockSpec(memory_space=pltpu.SMEM)
VMEM = pl.BlockSpec(memory_space=pltpu.VMEM)
PARAMS = pltpu.CompilerParams(vmem_limit_bytes=50 * 1024 * 1024)


def shift(value, axis_of_core0, axis_of_core1, step):
    pairs = []
    for x in range(4):
        for z in range(4):
            for y in range(4):
                for core in range(2):
                    here = {"x": x, "z": z, "y": y, "core": core}
                    there = dict(here)
                    axis = axis_of_core1 if core else axis_of_core0
                    there[axis] = (there[axis] + step) % 4
                    place = [((p["x"] * 4 + p["z"]) * 4 + p["y"]) * 2 + p["core"] for p in (here, there)]
                    pairs.append(tuple(place))
    return lax.ppermute(value, AXES, pairs)


def swap_core(value):
    return lax.ppermute(value, "core", [(0, 1), (1, 0)])


def pack_shard(place, occ, vir, amp, keep, send, wide):
    x, z, y, core = place[0], place[1], place[2], place[3]
    row_place = x * 4 + z
    occ_here = occ[row_place >> 1]
    first = 3 * (row_place & 1)
    irrep = 2 * y + core
    vir_here = vir[irrep]
    wide[...] = jnp.zeros_like(wide)
    for row in range(18):
        wide[row : row + 1, 0:1296] = amp[row // 6, row % 6]
    lane = lax.broadcasted_iota(jnp.int32, wide.shape, 1)
    row = lax.broadcasted_iota(jnp.int32, wide.shape, 0)
    a = jnp.floor((lane.astype(F32) + 0.5) * (1.0 / 36.0)).astype(jnp.int32)
    b = lane - 36 * a
    i_low = (row * 43) >> 8
    j = row - 6 * i_low
    i = i_low + first
    live = (a < vir_here) & (b < vir_here) & (i < occ_here) & (j < occ_here)
    moved = pltpu.roll(jnp.where(live, wide[...], 0.0), 16 * irrep, 1)

    def write(ref, half):
        for t in range(TILES):
            columns = slice(t * LANES, (t + 1) * LANES)
            ref[8 * t : 8 * t + 8, :] = moved[8 * half : 8 * half + 8, columns]
            ref[MAIN + t : MAIN + t + 1, :] = moved[16 + half : 17 + half, columns]
        ref[MAIN + TILES : SHARD, :] = jnp.zeros((SHARD - MAIN - TILES, LANES), F32)

    @pl.when(core == 0)
    def _():
        write(keep, 0)
        write(send, 1)

    @pl.when(core == 1)
    def _():
        write(keep, 1)
        write(send, 0)


def pack_pair(own, other, out):
    out[0:MAIN, :] = own[0:MAIN, :]
    out[MAIN : 2 * MAIN, :] = other[0:MAIN, :]
    out[2 * MAIN : 2 * MAIN + TILES, :] = own[MAIN : MAIN + TILES, :]
    out[2 * MAIN + TILES : 2 * MAIN + 2 * TILES, :] = other[MAIN : MAIN + TILES, :]
    out[2 * MAIN + 2 * TILES : PAIR, :] = jnp.zeros((2, LANES), F32)


def join(*refs):
    out = refs[-1]
    at = 0
    for ref in refs[:-1]:
        rows = ref.shape[0]
        out[at : at + rows, :] = ref[...]
        at += rows


def join_call(*arrays):
    rows = sum(array.shape[0] for array in arrays)
    return pl.pallas_call(
        join,
        out_shape=jax.ShapeDtypeStruct((rows, LANES), F32),
        in_specs=[VMEM] * len(arrays),
        out_specs=VMEM,
        compiler_params=PARAMS,
    )(*arrays)


def cut_windows(place, integrals, gate, up, down, sems):
    y = place[2]
    copies = []
    for at, (ref, step) in enumerate(((up, 1), (down, 3))):
        start = pl.multiple_of(((y + step) & 3) * 2560, LANES)
        copies.append(
            pltpu.make_async_copy(integrals.at[:, :, pl.ds(start, PAIR_WINDOW)], ref, sems.at[at])
        )
    for copy in copies:
        copy.start()
    for copy in copies:
        copy.wait()


def split_turned(block, wide, high, low, first, column):
    wide[0:81, :] = block
    turned = wide[...].T
    upper = turned.astype(BF16)
    high[first : first + WINDOW, column : column + LANES] = upper
    low[first : first + WINDOW, column : column + LANES] = (turned - upper.astype(F32)).astype(BF16)


def turn_local(place, own, other, high, low, wide):
    y, core = place[2], place[3]
    wide[...] = jnp.zeros_like(wide)
    for pair in range(2):
        chip = (y + 2 * pair) & 3
        for side in range(2):
            irrep = 2 * chip + (core if side == 0 else 1 - core)
            start = pl.multiple_of(irrep * 1280, LANES)
            for column, ref in enumerate((own, other)):
                split_turned(
                    ref[:, pl.ds(start, WINDOW)], wide, high, low,
                    (2 * pair + side) * WINDOW, column * LANES,
                )


def turn_moved(place, own, other, high, low, wide):
    core = place[3]
    wide[...] = jnp.zeros_like(wide)
    for side in range(2):
        start = pl.multiple_of((core if side == 0 else 1 - core) * 1280, LANES)
        for column, ref in enumerate((own, other)):
            split_turned(
                ref[:, pl.ds(start, WINDOW)], wide, high, low, side * WINDOW, column * LANES
            )


def turn_call(kernel, place, own, other, depth):
    return pl.pallas_call(
        kernel,
        out_shape=[jax.ShapeDtypeStruct((depth, 2 * LANES), BF16)] * 2,
        in_specs=[SMEM, VMEM, VMEM],
        out_specs=[VMEM, VMEM],
        scratch_shapes=[pltpu.VMEM((LANES, WINDOW), F32)],
        compiler_params=PARAMS,
    )(place, own, other)


def multiply(b0, b1, b2, b3, local_high, local_low, up_high, up_low, down_high, down_low,
             local_sum, up_sum, down_sum, extra):
    blocks = (b0, b1, b2, b3)
    depth = 2 * WINDOW
    for pair in range(2):
        for t in range(2 * TILES):
            row = PAIR * pair + 2 * MAIN + t
            at = (pair * 2 * TILES + t) * LANES
            for d, block in enumerate(blocks):
                extra[4 * d : 4 * d + 4, at : at + LANES] = block[pl.ds(row, 4, stride=QUAD), :]
    total = None
    for pair in range(2):
        rows = []
        for block in blocks:
            for e in range(4):
                base = e * QUAD + pair * PAIR
                rows.append(
                    jnp.concatenate(
                        [block[base + 8 * t : base + 8 * t + 8, :] for t in range(2 * TILES)], axis=1
                    )
                )
        rows.append(extra[:, pair * depth : (pair + 1) * depth])
        left = jnp.concatenate(rows, axis=0)
        high = left.astype(BF16)
        low = (left - high.astype(F32)).astype(BF16)

        def product(right_high, right_low):
            dot = lambda p, q: jnp.dot(p, q, preferred_element_type=F32)
            return dot(high, right_high) + (dot(low, right_high) + dot(high, right_low))

        here = product(
            local_high[pair * depth : (pair + 1) * depth, :],
            local_low[pair * depth : (pair + 1) * depth, :],
        )
        total = here if total is None else total + here
        if pair == 0:
            up_sum[...] = product(up_high[...], up_low[...])
            down_sum[...] = product(down_high[...], down_low[...])
    local_sum[...] = total


def address(place, local_sum, up_sum, down_sum, out):
    x, z, core = place[0], place[1], place[3]
    total = local_sum[...] + up_sum[...] + down_sum[...]
    lane = lax.broadcasted_iota(jnp.int32, (8, LANES), 1)
    row = lax.broadcasted_iota(jnp.int32, (8, LANES), 0)
    for side in range(2):
        columns = slice(side * LANES, (side + 1) * LANES)
        last = total[128:144, columns]
        last_a = pltpu.roll(last, 81, 1)
        last_b = pltpu.roll(last, 34, 1)
        core_there = core if side == 0 else 1 - core
        for d in range(4):
            for e in range(4):
                s = 4 * d + e
                x_step = jnp.where(core == 0, STEPS[e], STEPS[d])
                z_step = jnp.where(core == 0, STEPS[d], STEPS[e])
                there = ((x - x_step) & 3) * 4 + ((z - z_step) & 3)
                main = total[8 * s : 8 * s + 8, columns]
                tail = jnp.where(row == 0, last_a[s : s + 1, :], last_b[s : s + 1, :])
                out[there * 2 + core_there] = jnp.where(lane < 81, main, tail)


def finish(sums, scale, offset, out, wide):
    wide[...] = jnp.zeros_like(wide)
    lane8 = lax.broadcasted_iota(jnp.int32, (1, LANES), 1)
    lane = lax.broadcasted_iota(jnp.int32, (24, LANES), 1)
    for r in range(16):
        mains, lasts = [], []
        for core in range(2):
            block = sums[2 * r + core]
            mains.append(block)
            lasts.append(
                jnp.where(lane8 < 47, pltpu.roll(block, 47, 1)[0:1, :], pltpu.roll(block, 94, 1)[1:2, :])
            )
        stack = jnp.concatenate(mains + lasts + [jnp.zeros((6, LANES), F32)], axis=0)
        tile, start = divmod(81 * r, LANES)
        turned = pltpu.roll(stack, start, 1) if start else stack
        here = slice(tile * LANES, (tile + 1) * LANES)
        wide[:, here] = jnp.where((lane >= start) & (lane < start + 81), turned, wide[:, here])
        if start + 81 > LANES:
            after = slice((tile + 1) * LANES, (tile + 2) * LANES)
            wide[:, after] = jnp.where(lane < start + 81 - LANES, turned, wide[:, after])
    out[...] = wide[0:18, 0:1296] * scale[...] + offset[...]


def local_terms(amplitudes, ovov, eps_occ, eps_vir, occ_count, vir_count, x, z, y, core):
    row_place = x * 4 + z
    col_place = y * 2 + core
    occ_slots, vir_slots = eps_occ.shape[1], eps_vir.shape[1]
    occ_live = (jnp.arange(occ_slots)[None, :] < occ_count[:, None]).astype(F32)
    vir_live = (jnp.arange(vir_slots)[None, :] < vir_count[:, None]).astype(F32)
    shell = row_place // 2
    first = row_place * 3
    occ_rows = lax.dynamic_slice_in_dim(occ_live.reshape(-1), first, 3)
    energy_rows = lax.dynamic_slice_in_dim(eps_occ.reshape(-1), first, 3)
    occ_cols = lax.dynamic_slice_in_dim(occ_live, shell, 1, 0)[0]
    energy_cols = lax.dynamic_slice_in_dim(eps_occ, shell, 1, 0)[0]
    vir_here = lax.dynamic_slice_in_dim(vir_live, col_place, 1, 0)[0]
    vir_energy = lax.dynamic_slice_in_dim(eps_vir, col_place, 1, 0)[0]
    mask = (
        occ_rows[:, None, None, None]
        * occ_cols[None, :, None, None]
        * vir_here[None, None, :, None]
        * vir_here[None, None, None, :]
    )
    live = amplitudes.reshape(3, occ_slots, vir_slots, vir_slots) * mask
    partner = lax.ppermute(ovov, "z", [(0, 1), (1, 0), (2, 3), (3, 2)])
    panel = jnp.where(
        row_place % 2 == 0,
        jnp.concatenate([ovov, partner], 0),
        jnp.concatenate([partner, ovov], 0),
    )
    panel = panel.reshape(occ_slots, vir_slots, occ_slots, vir_slots)
    cycle = jnp.einsum("ikac,kcjb->ijab", live, panel, precision=lax.Precision.HIGHEST)
    gap = (
        energy_rows[:, None, None, None]
        + energy_cols[None, :, None, None]
        - vir_energy[None, None, :, None]
        - vir_energy[None, None, None, :]
    )
    scale = mask / gap
    return scale.reshape(18, 1296), (scale * cycle).reshape(18, 1296)


def on_device(amplitudes, vvvv, ovov, eps_occ, eps_vir, occ_count, vir_count):
    x, z, y, core = (lax.axis_index(name) for name in AXES)
    place = jnp.stack([x, z, y, core]).astype(jnp.int32)
    integrals = vvvv.reshape(81, 1, 10368)
    flat = vvvv.reshape(81, 10368)

    keep, send = pl.pallas_call(
        pack_shard,
        out_shape=[jax.ShapeDtypeStruct((SHARD, LANES), F32)] * 2,
        in_specs=[SMEM, SMEM, SMEM, VMEM],
        out_specs=[VMEM, VMEM],
        scratch_shapes=[pltpu.VMEM((24, WINDOW), F32)],
        compiler_params=PARAMS,
    )(place, occ_count, vir_count, amplitudes)
    got = swap_core(send)
    pair = pl.pallas_call(
        pack_pair,
        out_shape=jax.ShapeDtypeStruct((PAIR, LANES), F32),
        in_specs=[VMEM, VMEM],
        out_specs=VMEM,
        compiler_params=PARAMS,
    )(keep, got)
    far = shift(pair, "y", "y", 2)
    quad = join_call(pair, far)

    up, down = pl.pallas_call(
        cut_windows,
        out_shape=[jax.ShapeDtypeStruct((81, 1, PAIR_WINDOW), F32)] * 2,
        in_specs=[SMEM, ANY, ANY],
        out_specs=[ANY, ANY],
        scratch_shapes=[pltpu.SemaphoreType.DMA((2,))],
        compiler_params=PARAMS,
    )(place, integrals, far)
    from_below = shift(up, "y", "y", 1)
    from_above = shift(down, "y", "y", -1)

    near = join_call(quad, *[shift(quad, "x", "z", step) for step in SHIFTS])
    blocks = [near] + [shift(near, "z", "x", step) for step in SHIFTS]

    other = swap_core(integrals).reshape(81, 10368)
    below_other = swap_core(from_below)
    above_other = swap_core(from_above)
    local_high, local_low = turn_call(turn_local, place, flat, other, 4 * WINDOW)
    moved = lambda a, b: turn_call(
        turn_moved, place, a.reshape(81, PAIR_WINDOW), b.reshape(81, PAIR_WINDOW), 2 * WINDOW
    )
    below_high, below_low = moved(from_below, below_other)
    above_high, above_low = moved(from_above, above_other)

    local_sum, below_sum, above_sum = pl.pallas_call(
        multiply,
        out_shape=[jax.ShapeDtypeStruct((144, 2 * LANES), F32)] * 3,
        in_specs=[VMEM] * 10,
        out_specs=[VMEM] * 3,
        scratch_shapes=[pltpu.VMEM((16, 4 * WINDOW), F32)],
        compiler_params=PARAMS,
    )(*blocks, local_high, local_low, below_high, below_low, above_high, above_low)
    up_back = shift(below_sum, "y", "y", -1)
    down_back = shift(above_sum, "y", "y", 1)
    packed = pl.pallas_call(
        address,
        out_shape=jax.ShapeDtypeStruct((32, 8, LANES), F32),
        in_specs=[SMEM, VMEM, VMEM, VMEM],
        out_specs=VMEM,
        compiler_params=PARAMS,
    )(place, local_sum, up_back, down_back)
    ladder = lax.all_to_all(packed, ("x", "z", "core"), 0, 0, tiled=True)

    scale, offset = local_terms(
        amplitudes, ovov, eps_occ, eps_vir, occ_count, vir_count, x, z, y, core
    )
    result = pl.pallas_call(
        finish,
        out_shape=jax.ShapeDtypeStruct((18, 1296), F32),
        in_specs=[VMEM, VMEM, VMEM],
        out_specs=VMEM,
        scratch_shapes=[pltpu.VMEM((24, WINDOW), F32)],
        compiler_params=PARAMS,
    )(ladder, scale, offset)
    return result.reshape(3, 6, 1, 1296)


def solution(mesh):
    fine = Mesh(mesh.devices.reshape(4, 4, 4, 2), AXES)
    rows, cols = ("x", "z"), ("y", "core")
    return jax.shard_map(
        on_device,
        mesh=fine,
        in_specs=(P(rows, None, cols, None), P(cols, rows, None), P(rows, cols, None), P(), P(), P(), P()),
        out_specs=P(rows, None, cols, None),
        check_vma=False,
    )
```

time: 185 us -> 126 us (0.68)
  waiting for transfers between devices: 93.8 us -> 40.4 us
  Pallas kernels: 0 us -> 23.7 us
  starting transfers between devices: 6.7 us -> 29.7 us
  blocking collectives: 15.6 us -> 0 us
  matrix products: 17.1 us -> 1.52 us
  between operations: 13.5 us -> 0.28 us
  local copies, waits for them, and re-layouts: 31.8 us -> 26.8 us
  other arithmetic: 5.57 us -> 2.6 us
    all_gather x1 -> x0, waiting for transfers between devices: 88.9 us -> none  [on_device(): piece = lax.all_gather(full_irreps, 'row', axis=0, tiled=True)]
    ppermute x1 -> x16, waiting for transfers between devices: 0.01 us -> 34.7 us  [the longest x11 32.1 us: shift(): return lax.ppermute(value, AXES, pairs)]
    pallas_call x0 -> x11, Pallas kernels: none -> 23.7 us  [the longest x3 11.4 us: turn_call(): pl.pallas_call(kernel, out_shape=[jax.ShapeDtypeStruct((depth, 2 * LANES)...]
    ppermute x1 -> x16, starting transfers between devices: 1.72 us -> 24.3 us  [the longest x11 17 us: shift(): return lax.ppermute(value, AXES, pairs)]
    unnamed x4 -> x48, local copies, waits for them, and re-layouts: 0.01 us -> 18.4 us
    reshape x7 -> x5, local copies, waits for them, and re-layouts: 17.9 us -> 1.43 us  [the longest x1 0.75 us: on_device(): return result.reshape(3, 6, 1, 1296)]
    dot_general x2 -> x1, matrix products: 17.1 us -> 1.52 us  [local_terms(): jnp.einsum('ikac,kcjb->ijab', live, panel, precision=lax.Precision.HIGHEST)]
    all_gather x1 -> x0, blocking collectives: 15.6 us -> none  [on_device(): full_irreps = lax.all_gather(amps_flat, 'col', axis=2, tiled=True)]
  transfers between devices with their start and end apart: 3 -> 17, of which waited for: 2 -> 8; matrix products, arithmetic and copies ran while one was open for 24% -> 20% of each run, Pallas kernels for 0% -> 18%
where the time goes in v1:
time: 126 us; the launch traced here: 125 us
  waiting for transfers between devices  40.4 us (32%)
  starting transfers between devices  29.7 us (24%)
  local copies, waits for them, and re-layouts  26.8 us (21%)
  Pallas kernels  23.7 us (19%)
  other arithmetic  2.6 us (2%)
  matrix products  1.52 us (1%)
    ppermute x11, waiting for transfers between devices, shift(): return lax.ppermute(value, AXES, pairs)  32.1 us
    unnamed x48, local copies, waits for them, and re-layouts  18.4 us
    ppermute x11, starting transfers between devices, shift(): return lax.ppermute(value, AXES, pairs)  17 us
    pallas_call x3, Pallas kernels, turn_call(): pl.pallas_call(kernel, out_shape=[jax.ShapeDtypeStruct((depth, 2 * LANES)...  11.4 us
    pallas_call x1, Pallas kernels, on_device(): pl.pallas_call(multiply, out_shape=[jax.ShapeDtypeStruct((144, 2 * LANES)...  8.02 us
    ppermute x4, starting transfers between devices, swap_core(): return lax.ppermute(value, 'core', [(0, 1), (1, 0)])  6.52 us
    all_to_all x1, waiting for transfers between devices, on_device(): ladder = lax.all_to_all(packed, ('x', 'z', 'core'), 0, 0, tiled=True)  5.73 us
    all_to_all x1, starting transfers between devices, on_device(): ladder = lax.all_to_all(packed, ('x', 'z', 'core'), 0, 0, tiled=True)  5.43 us
  transfers between devices with their start and end apart: 17, of which 8 were waited for; matrix products, arithmetic and copies ran while one was open for 20% of the time, Pallas kernels for 18%

profile of v1, /device:TPU:1, one launch (start us, length us, event | category | flops | bytes accessed | tf_op | source)
XLA Modules:
  0.0 125.1 jit_solution(11665751169297446449)
XLA Ops:
  4.6 2.6 %collective-permute-done.other = f32[104,128]{1,0:T(8,128)S(1)} collective-permute-done((f32[104,128]{1,0:T(8,128)S(1)}, f32[104,128]{1,0:T(8,128)S(1)}, u32[]{:S(2)}, u32[]{:S(2)}) %collective-permute-start) | collective-permute-done | bytes 53280 | tf_op jit(solution)/shard_map/ppermute | solution.py:43
  7.2 3.1 %collective-permute-start.1 = (f32[200,128]{1,0:T(8,128)S(1)}, f32[200,128]{1,0:T(8,128)S(1)}, u32[]{:S(2)}, u32[]{:S(2)}) collective-permute-start(f32[200,128]{1,0:T(8,128)S(1)} %shard_map.74.refs_0_), channel_id=1, source_target_pairs={{0,4},{1,5},{2,6},{3,7},{4,0},{5,1},{6,2},{7,3},{8,12},{9,13},{10,... | collective-permute-start | bytes 307208 | tf_op jit(solution)/shard_map/ppermute | solution.py:39
  10.3 2.7 %collective-permute-done.1.refs_1_.gate = f32[200,128]{1,0:T(8,128)S(1)} collective-permute-done((f32[200,128]{1,0:T(8,128)S(1)}, f32[200,128]{1,0:T(8,128)S(1)}, u32[]{:S(2)}, u32[]{:S(2)}) %collective-permute-start.1) | collective-permute-done | bytes 102432 | tf_op jit(solution)/shard_map/ppermute | solution.py:39
  13.0 2.0 %shard_map.78 = (f32[81,1,2688]{2,1,0:T(1,128)S(1)}, f32[81,1,2688]{2,1,0:T(1,128)S(1)}) custom-call(s32[4]{0:T(128)S(1)} %pad_add_fusion.place, f32[81,1,10368]{2,1,0:T(1,128)} %bitcast.50, f32[200,128]{1,0:T(8,128)S(1)} %collective-permute-done.1.refs_1_.gate), custom_call_target="tpu_custom_call" | custom-call | tf_op jit(solution)/shard_map/pallas_call | solution.py:321
  17.9 18.3 %collective-permute-done.9 = f32[81,1,2688]{2,1,0:T(1,128)} collective-permute-done((f32[81,1,2688]{2,1,0:T(1,128)S(1)}, f32[81,1,2688]{2,1,0:T(1,128)}, u32[]{:S(2)}, u32[]{:S(2)}) %collective-permute-start.9) | collective-permute-done | bytes 870944 | tf_op jit(solution)/shard_map/ppermute | solution.py:39
  36.2 2.0 %collective-permute-start.10 = (f32[81,1,2688]{2,1,0:T(1,128)}, f32[81,1,2688]{2,1,0:T(1,128)}, u32[]{:S(2)}, u32[]{:S(2)}) collective-permute-start(f32[81,1,2688]{2,1,0:T(1,128)} %collective-permute-done.9), channel_id=1, source_target_pairs={{0,1},{1,0},{2,3},{3,2},{4,5},{5,4},{6,7},{7,6},{8,9},{9,8},{10,11... | collective-permute-start | bytes 2612744 | tf_op jit(solution)/shard_map/ppermute | solution.py:43
  38.3 1.7 %collective-permute-start.2 = (f32[400,128]{1,0:T(8,128)S(1)}, f32[400,128]{1,0:T(8,128)S(1)}, u32[]{:S(2)}, u32[]{:S(2)}) collective-permute-start(f32[400,128]{1,0:T(8,128)S(1)} %shard_map.75.refs_0_), channel_id=1, source_target_pairs={{0,32},{1,9},{2,34},{3,11},{4,36},{5,13},{6,38},{7,15},{8,40},{9,1... | collective-permute-start | bytes 614408 | tf_op jit(solution)/shard_map/ppermute | solution.py:39
  40.0 2.2 %collective-permute-start.3 = (f32[400,128]{1,0:T(8,128)S(1)}, f32[400,128]{1,0:T(8,128)S(1)}, u32[]{:S(2)}, u32[]{:S(2)}) collective-permute-start(f32[400,128]{1,0:T(8,128)S(1)} %shard_map.75.refs_0_), channel_id=1, source_target_pairs={{0,96},{1,25},{2,98},{3,27},{4,100},{5,29},{6,102},{7,31},{8,104},... | collective-permute-start | bytes 614408 | tf_op jit(solution)/shard_map/ppermute | solution.py:39
  42.2 3.0 %collective-permute-done.2.refs_1_ = f32[400,128]{1,0:T(8,128)S(1)} collective-permute-done((f32[400,128]{1,0:T(8,128)S(1)}, f32[400,128]{1,0:T(8,128)S(1)}, u32[]{:S(2)}, u32[]{:S(2)}) %collective-permute-start.2) | collective-permute-done | bytes 204832 | tf_op jit(solution)/shard_map/ppermute | solution.py:39
  46.9 4.7 %collective-permute-done.4.refs_3_ = f32[400,128]{1,0:T(8,128)S(1)} collective-permute-done((f32[400,128]{1,0:T(8,128)S(1)}, f32[400,128]{1,0:T(8,128)S(1)}, u32[]{:S(2)}, u32[]{:S(2)}) %collective-permute-start.4) | collective-permute-done | bytes 204832 | tf_op jit(solution)/shard_map/ppermute | solution.py:39
  52.7 1.8 %collective-permute-start.6 = (f32[1600,128]{1,0:T(8,128)S(1)}, f32[1600,128]{1,0:T(8,128)S(1)}, u32[]{:S(2)}, u32[]{:S(2)}) collective-permute-start(f32[1600,128]{1,0:T(8,128)S(1)} %shard_map.76.b0), channel_id=1, source_target_pairs={{0,24},{1,97},{2,26},{3,99},{4,28},{5,101},{6,30},{7,103},{8,0},{9... | collective-permute-start | bytes 2457608 | tf_op jit(solution)/shard_map/ppermute | solution.py:39
  55.7 2.9 %collective-permute-start.12 = (f32[81,1,2688]{2,1,0:T(1,128)}, f32[81,1,2688]{2,1,0:T(1,128)}, u32[]{:S(2)}, u32[]{:S(2)}) collective-permute-start(f32[81,1,2688]{2,1,0:T(1,128)} %collective-permute-done.11), channel_id=1, source_target_pairs={{0,1},{1,0},{2,3},{3,2},{4,5},{5,4},{6,7},{7,6},{8,9},{9,8},{10,11... | collective-permute-start | bytes 2612744 | tf_op jit(solution)/shard_map/ppermute | solution.py:43
  58.6 4.0 %copy.58 = f32[1,81,10368]{2,1,0:T(8,128)} copy(f32[1,81,10368]{2,0,1:T(1,128)} %param.8) | data formatting | bytes 6718464
  64.1 1.8 %sub.54 = f32[18,1296]{1,0:T(8,128)} reshape(f32[3,6,36,36]{3,2,1,0:T(8,128)} %sub.53.clone) | data formatting | bytes 186624 | tf_op jit(solution)/shard_map/sub | solution.py:287
  66.8 1.8 %mul.91 = f32[18,1296]{1,0:T(8,128)} reshape(f32[3,6,36,36]{3,2,1,0:T(8,128)} %mul.90.clone) | data formatting | bytes 186624 | tf_op jit(solution)/shard_map/mul | solution.py:272
  73.1 2.5 %shard_map.79 = (bf16[2816,256]{1,0:T(8,128)(2,1)S(1)}, bf16[2816,256]{1,0:T(8,128)(2,1)}) custom-call(s32[4]{0:T(128)S(1)} %pad_add_fusion.place, f32[81,2688]{1,0:T(8,128)S(1)} %bitcast.44, f32[81,2688]{1,0:T(8,128)S(1)} %bitcast.45), custom_call_target="tpu_custom_call" | custom-call | tf_op jit(solution)/shard_map/pallas_call | solution.py:161
  78.8 2.5 %shard_map.80 = (bf16[2816,256]{1,0:T(8,128)(2,1)S(1)}, bf16[2816,256]{1,0:T(8,128)(2,1)}) custom-call(s32[4]{0:T(128)S(1)} %pad_add_fusion.place, f32[81,2688]{1,0:T(8,128)S(1)} %bitcast.43, f32[81,2688]{1,0:T(8,128)S(1)} %bitcast.46), custom_call_target="tpu_custom_call" | custom-call | tf_op jit(solution)/shard_map/pallas_call | solution.py:161
  81.3 4.5 %copy.57 = f32[81,1,10368]{2,0,1:T(8,128)} copy(f32[81,1,10368]{2,1,0:T(1,128)} %collective-permute-done.8) | data formatting | bytes 6718464
  85.8 6.5 %shard_map.77 = (bf16[5632,256]{1,0:T(8,128)(2,1)S(1)}, bf16[5632,256]{1,0:T(8,128)(2,1)}) custom-call(s32[4]{0:T(128)S(1)} %pad_add_fusion.place, f32[81,10368]{1,0:T(8,128)} %bitcast.47, f32[81,10368]{1,0:T(8,128)} %bitcast.48), custom_call_target="tpu_custom_call" | custom-call | tf_op jit(solution)/shard_map/pallas_call | solution.py:161
  93.9 8.0 %shard_map.81 = (f32[144,256]{1,0:T(8,128)S(1)}, f32[144,256]{1,0:T(8,128)}, f32[144,256]{1,0:T(8,128)}) custom-call(f32[1600,128]{1,0:T(8,128)S(1)} %shard_map.76.b0, f32[1600,128]{1,0:T(8,128)S(1)} %collective-permute-done.5.b1, f32[1600,128]{1,0:T(8,128)S(1)} %collective-permute-done.6.b2, f32[1600,128]{1,0:T(8,128)S(1)} %collective-permute-done.7.b3, ...), custom_call_target="tpu_custom_call" | custom-call | tf_op jit(solution)/shard_map/pallas_call | solution.py:345
  104.2 1.9 %fusion.4 = f32[216,216]{1,0:T(8,128)S(1)} fusion(pred[]{:T(512)S(6)} %eq.5, f32[108,1,216]{2,1,0:T(1,128)} %collective-permute-done.15, f32[108,1,216]{2,1,0:T(1,128)} %param.9), kind=kLoop, calls=%fused_computation.14 | loop fusion | flops 139968 | bytes 373249 | tf_op jit(solution)/shard_map/jit(_where)/select_n | solution.py:279
  107.3 2.3 %collective-permute-done.14.down_sum = f32[144,256]{1,0:T(8,128)S(1)} collective-permute-done((f32[144,256]{1,0:T(8,128)}, f32[144,256]{1,0:T(8,128)S(1)}, u32[]{:S(2)}, u32[]{:S(2)}) %collective-permute-start.14) | collective-permute-done | bytes 147488 | tf_op jit(solution)/shard_map/ppermute | solution.py:39
  110.9 5.4 %all-to-all-start = ((f32[32,8,128]{2,1,0:T(8,128)}), f32[32,8,128]{2,1,0:T(8,128)S(1)}, u32[]{:S(2)}, u32[]{:S(2)}) async-start(f32[32,8,128]{2,1,0:T(8,128)} %shard_map.82), calls=%async_computation | async-start | bytes 262144 | tf_op jit(solution)/shard_map/all_to_all | solution.py:362
  118.4 5.7 %all-to-all-done.sums = f32[32,8,128]{2,1,0:T(8,128)S(1)} async-done(((f32[32,8,128]{2,1,0:T(8,128)}), f32[32,8,128]{2,1,0:T(8,128)S(1)}, u32[]{:S(2)}, u32[]{:S(2)}) %all-to-all-start) | async-done | bytes 131104 | tf_op jit(solution)/shard_map/all_to_all | solution.py:362
  (101 shorter events, 30.8 us)
Async XLA Ops:
  0.0 58.6 %copy-start = (f32[8,36]{1,0:T(8,128)S(1)}, f32[8,36]{1,0:T(8,128)}, u32[]{:S(2)}) copy-start(f32[8,36]{1,0:T(8,128)} %param.11) | copy-start | bytes 3460
  0.0 38.2 %copy-start.7 = (s32[8]{0:T(128)S(1)}, s32[8]{0:T(128)}, u32[]{:S(2)}) copy-start(s32[8]{0:T(128)} %occ.1) | copy-start | bytes 100
  0.0 46.8 %copy-start.9 = (s32[8]{0:T(128)S(1)}, s32[8]{0:T(128)}, u32[]{:S(2)}) copy-start(s32[8]{0:T(128)} %vir.1) | copy-start | bytes 100
  0.0 40.0 %copy-start.15 = (f32[8,6]{1,0:T(8,128)S(1)}, f32[8,6]{1,0:T(8,128)}, u32[]{:S(2)}) copy-start(f32[8,6]{1,0:T(8,128)} %param.10) | copy-start | bytes 580
  0.0 81.3 %collective-permute-start.8 = (f32[81,1,10368]{2,1,0:T(1,128)}, f32[81,1,10368]{2,1,0:T(1,128)}, u32[]{:S(2)}, u32[]{:S(2)}) collective-permute-start(f32[81,1,10368]{2,1,0:T(1,128)} %bitcast.49), channel_id=1, source_target_pairs={{0,1},{1,0},{2,3},{3,2},{4,5},{5,4},{6,7},{7,6},{8,9},{9,8},{10,11... | collective-permute-start | bytes 10077704 | tf_op jit(solution)/shard_map/ppermute | solution.py:43
  4.5 2.7 %collective-permute-start = (f32[104,128]{1,0:T(8,128)S(1)}, f32[104,128]{1,0:T(8,128)S(1)}, u32[]{:S(2)}, u32[]{:S(2)}) collective-permute-start(f32[104,128]{1,0:T(8,128)S(1)} %get-tuple-element.19), channel_id=1, source_target_pairs={{0,1},{1,0},{2,3},{3,2},{4,5},{5,4},{6,7},{7,6},{8,9},{9,8},{10,11... | collective-permute-start | bytes 159752 | tf_op jit(solution)/shard_map/ppermute | solution.py:43
  7.2 5.8 %collective-permute-start.1 = (f32[200,128]{1,0:T(8,128)S(1)}, f32[200,128]{1,0:T(8,128)S(1)}, u32[]{:S(2)}, u32[]{:S(2)}) collective-permute-start(f32[200,128]{1,0:T(8,128)S(1)} %shard_map.74.refs_0_), channel_id=1, source_target_pairs={{0,4},{1,5},{2,6},{3,7},{4,0},{5,1},{6,2},{7,3},{8,12},{9,13},{10,... | collective-permute-start | bytes 307208 | tf_op jit(solution)/shard_map/ppermute | solution.py:39
  15.0 21.2 %collective-permute-start.9 = (f32[81,1,2688]{2,1,0:T(1,128)S(1)}, f32[81,1,2688]{2,1,0:T(1,128)}, u32[]{:S(2)}, u32[]{:S(2)}) collective-permute-start(f32[81,1,2688]{2,1,0:T(1,128)S(1)} %get-tuple-element.22), channel_id=1, source_target_pairs={{0,2},{1,3},{2,4},{3,5},{4,6},{5,7},{6,0},{7,1},{8,10},{9,11},{10,... | collective-permute-start | bytes 2612744 | tf_op jit(solution)/shard_map/ppermute | solution.py:39
  16.3 38.1 %collective-permute-start.11 = (f32[81,1,2688]{2,1,0:T(1,128)S(1)}, f32[81,1,2688]{2,1,0:T(1,128)}, u32[]{:S(2)}, u32[]{:S(2)}) collective-permute-start(f32[81,1,2688]{2,1,0:T(1,128)S(1)} %get-tuple-element.25), channel_id=1, source_target_pairs={{0,6},{1,7},{2,0},{3,1},{4,2},{5,3},{6,4},{7,5},{8,14},{9,15},{10,... | collective-permute-start | bytes 2612744 | tf_op jit(solution)/shard_map/ppermute | solution.py:39
  36.2 19.5 %collective-permute-start.10 = (f32[81,1,2688]{2,1,0:T(1,128)}, f32[81,1,2688]{2,1,0:T(1,128)}, u32[]{:S(2)}, u32[]{:S(2)}) collective-permute-start(f32[81,1,2688]{2,1,0:T(1,128)} %collective-permute-done.9), channel_id=1, source_target_pairs={{0,1},{1,0},{2,3},{3,2},{4,5},{5,4},{6,7},{7,6},{8,9},{9,8},{10,11... | collective-permute-start | bytes 2612744 | tf_op jit(solution)/shard_map/ppermute | solution.py:43
  38.3 7.0 %collective-permute-start.2 = (f32[400,128]{1,0:T(8,128)S(1)}, f32[400,128]{1,0:T(8,128)S(1)}, u32[]{:S(2)}, u32[]{:S(2)}) collective-permute-start(f32[400,128]{1,0:T(8,128)S(1)} %shard_map.75.refs_0_), channel_id=1, source_target_pairs={{0,32},{1,9},{2,34},{3,11},{4,36},{5,13},{6,38},{7,15},{8,40},{9,1... | collective-permute-start | bytes 614408 | tf_op jit(solution)/shard_map/ppermute | solution.py:39
  40.0 6.9 %collective-permute-start.3 = (f32[400,128]{1,0:T(8,128)S(1)}, f32[400,128]{1,0:T(8,128)S(1)}, u32[]{:S(2)}, u32[]{:S(2)}) collective-permute-start(f32[400,128]{1,0:T(8,128)S(1)} %shard_map.75.refs_0_), channel_id=1, source_target_pairs={{0,96},{1,25},{2,98},{3,27},{4,100},{5,29},{6,102},{7,31},{8,104},... | collective-permute-start | bytes 614408 | tf_op jit(solution)/shard_map/ppermute | solution.py:39
  45.3 6.4 %collective-permute-start.4 = (f32[400,128]{1,0:T(8,128)S(1)}, f32[400,128]{1,0:T(8,128)S(1)}, u32[]{:S(2)}, u32[]{:S(2)}) collective-permute-start(f32[400,128]{1,0:T(8,128)S(1)} %shard_map.75.refs_0_), channel_id=1, source_target_pairs={{0,64},{1,17},{2,66},{3,19},{4,68},{5,21},{6,70},{7,23},{8,72},{9,... | collective-permute-start | bytes 614408 | tf_op jit(solution)/shard_map/ppermute | solution.py:39
  51.7 42.1 %collective-permute-start.5 = (f32[1600,128]{1,0:T(8,128)S(1)}, f32[1600,128]{1,0:T(8,128)S(1)}, u32[]{:S(2)}, u32[]{:S(2)}) collective-permute-start(f32[1600,128]{1,0:T(8,128)S(1)} %shard_map.76.b0), channel_id=1, source_target_pairs={{0,8},{1,33},{2,10},{3,35},{4,12},{5,37},{6,14},{7,39},{8,16},{9,4... | collective-permute-start | bytes 2457608 | tf_op jit(solution)/shard_map/ppermute | solution.py:39
  52.7 41.1 %collective-permute-start.6 = (f32[1600,128]{1,0:T(8,128)S(1)}, f32[1600,128]{1,0:T(8,128)S(1)}, u32[]{:S(2)}, u32[]{:S(2)}) collective-permute-start(f32[1600,128]{1,0:T(8,128)S(1)} %shard_map.76.b0), channel_id=1, source_target_pairs={{0,24},{1,97},{2,26},{3,99},{4,28},{5,101},{6,30},{7,103},{8,0},{9... | collective-permute-start | bytes 2457608 | tf_op jit(solution)/shard_map/ppermute | solution.py:39
  54.5 39.4 %collective-permute-start.7 = (f32[1600,128]{1,0:T(8,128)S(1)}, f32[1600,128]{1,0:T(8,128)S(1)}, u32[]{:S(2)}, u32[]{:S(2)}) collective-permute-start(f32[1600,128]{1,0:T(8,128)S(1)} %shard_map.76.b0), channel_id=1, source_target_pairs={{0,16},{1,65},{2,18},{3,67},{4,20},{5,69},{6,22},{7,71},{8,24},{9,... | collective-permute-start | bytes 2457608 | tf_op jit(solution)/shard_map/ppermute | solution.py:39
  55.7 21.1 %collective-permute-start.12 = (f32[81,1,2688]{2,1,0:T(1,128)}, f32[81,1,2688]{2,1,0:T(1,128)}, u32[]{:S(2)}, u32[]{:S(2)}) collective-permute-start(f32[81,1,2688]{2,1,0:T(1,128)} %collective-permute-done.11), channel_id=1, source_target_pairs={{0,1},{1,0},{2,3},{3,2},{4,5},{5,4},{6,7},{7,6},{8,9},{9,8},{10,11... | collective-permute-start | bytes 2612744 | tf_op jit(solution)/shard_map/ppermute | solution.py:43
  76.8 27.4 %collective-permute-start.15 = (f32[108,1,216]{2,1,0:T(1,128)}, f32[108,1,216]{2,1,0:T(1,128)}, u32[]{:S(2)}, u32[]{:S(2)}) collective-permute-start(f32[108,1,216]{2,1,0:T(1,128)} %param.9), channel_id=1, source_target_pairs={{0,8},{8,0},{16,24},{24,16},{1,9},{9,1},{17,25},{25,17},{2,10},{10... | collective-permute-start | bytes 279944 | tf_op jit(solution)/shard_map/ppermute | solution.py:278
  101.9 14.5 %copy-start.13 = (f32[3,6,36]{2,0,1:T(4,128)S(1)}, f32[3,6,36]{2,0,1:T(4,128)}, u32[]{:S(2)}) copy-start(f32[3,6,36]{2,0,1:T(4,128)} %copy-done.12) | copy-start | bytes 7780
  101.9 14.5 %copy-start.17 = (f32[36]{0:T(128)S(1)}, f32[36]{0:T(128)}, u32[]{:S(2)}) copy-start(f32[36]{0:T(128)} %copy-done.16) | copy-start | bytes 436
  101.9 14.5 %copy-start.19 = (f32[36]{0:T(128)S(1)}, f32[36]{0:T(128)}, u32[]{:S(2)}) copy-start(f32[36]{0:T(128)} %copy-done.18) | copy-start | bytes 436
  101.9 5.4 %collective-permute-start.13 = (f32[144,256]{1,0:T(8,128)}, f32[144,256]{1,0:T(8,128)S(1)}, u32[]{:S(2)}, u32[]{:S(2)}) collective-permute-start(f32[144,256]{1,0:T(8,128)} %get-tuple-element.29), channel_id=1, source_target_pairs={{0,6},{1,7},{2,0},{3,1},{4,2},{5,3},{6,4},{7,5},{8,14},{9,15},{10,... | collective-permute-start | bytes 442376 | tf_op jit(solution)/shard_map/ppermute | solution.py:39
  103.4 6.2 %collective-permute-start.14 = (f32[144,256]{1,0:T(8,128)}, f32[144,256]{1,0:T(8,128)S(1)}, u32[]{:S(2)}, u32[]{:S(2)}) collective-permute-start(f32[144,256]{1,0:T(8,128)} %get-tuple-element.30), channel_id=1, source_target_pairs={{0,2},{1,3},{2,4},{3,5},{4,6},{5,7},{6,0},{7,1},{8,10},{9,11},{10,... | collective-permute-start | bytes 442376 | tf_op jit(solution)/shard_map/ppermute | solution.py:39
  110.9 13.1 %all-to-all-start = ((f32[32,8,128]{2,1,0:T(8,128)}), f32[32,8,128]{2,1,0:T(8,128)S(1)}, u32[]{:S(2)}, u32[]{:S(2)}) async-start(f32[32,8,128]{2,1,0:T(8,128)} %shard_map.82), calls=%async_computation | async-start | bytes 262144 | tf_op jit(solution)/shard_map/all_to_all | solution.py:362
  (13 other events, 71.7 us)

commit v2 on v0

v2 whole, which is shorter than its diff:
```python
import jax
import jax.numpy as jnp
from jax import lax
from jax.experimental import pallas as pl
from jax.experimental.pallas import tpu as pltpu
from jax.sharding import Mesh, PartitionSpec as P

AXES = ("x", "z", "y", "core")
SHIFTS = (1, -1, 2)
STEPS = (0, 1, -1, 2)
LANES = 128
TILES = 11
WINDOW = TILES * LANES
SPAN = 21
DEPTH = SPAN * LANES
MAIN = 8 * TILES
SHARD = 104
PMAIN = 8 * SPAN
PAIR = 192
QUAD = 2 * PAIR
PSLOT = 88
PROWS = SPAN * PSLOT
F32 = jnp.float32
BF16 = jnp.bfloat16
ANY = pl.BlockSpec(memory_space=pl.ANY)
HBM = pl.BlockSpec(memory_space=pltpu.HBM)
VMEM = pl.BlockSpec(memory_space=pltpu.VMEM)
SMALL = pltpu.CompilerParams(vmem_limit_bytes=8 * 1024 * 1024)
LARGE = pltpu.CompilerParams(vmem_limit_bytes=28 * 1024 * 1024)


def ring(value, axes, step, cross=False):
    pairs = []
    for x in range(4):
        for z in range(4):
            for y in range(4):
                for core in range(2):
                    here = {"x": x, "z": z, "y": y, "core": core}
                    there = dict(here)
                    there[axes[core]] = (there[axes[core]] + step) % 4
                    if cross:
                        there["core"] = 1 - core
                    pairs.append(
                        tuple(((p["x"] * 4 + p["z"]) * 4 + p["y"]) * 2 + p["core"] for p in (here, there))
                    )
    return lax.ppermute(value, AXES, pairs)


def swap_core(value):
    return lax.ppermute(value, "core", [(0, 1), (1, 0)])


def places():
    return tuple(lax.axis_index(name) for name in AXES)


def lane_orbitals(shape):
    lane = lax.broadcasted_iota(jnp.int32, shape, 1)
    a = jnp.floor((lane.astype(F32) + 0.5) * (1.0 / 36.0)).astype(jnp.int32)
    return a, lane - 36 * a


def cut_step(integrals, witness, up, down, home, sems):
    y = lax.axis_index("y")
    cuts = []
    for at, (ref, first, step) in enumerate(((up, 0, 1), (down, 0, 3), (home, 0, 0), (home, SPAN, 2))):
        base = ((y + step) & 3) * 20
        for t in range(SPAN):
            start = pl.multiple_of((base + t) * LANES, LANES)
            cuts.append(
                pltpu.make_async_copy(
                    integrals.at[:, :, pl.ds(start, LANES)], ref.at[first + t, 0:81], sems.at[at, t]
                )
            )
    for copy in cuts:
        copy.start()
    for ref, tiles in ((up, SPAN), (down, SPAN), (home, 2 * SPAN)):
        ref[:, 81:PSLOT] = jnp.zeros((tiles, PSLOT - 81, 1, LANES), F32)
    for copy in cuts:
        copy.wait()


def open_step(occ_ref, vir_ref, amp_ref, keep, send, wide, amp, occ, vir, sems):
    x, z, y, core = places()
    copies = [
        pltpu.make_async_copy(source, target, sems.at[at])
        for at, (source, target) in enumerate(((occ_ref, occ), (vir_ref, vir), (amp_ref, amp)))
    ]
    for copy in copies:
        copy.start()
    wide[...] = jnp.zeros_like(wide)
    for copy in copies:
        copy.wait()
    for row in range(18):
        wide[row : row + 1, 0:1296] = amp[row // 6, row % 6]
    row_place = x * 4 + z
    occ_here = occ[row_place >> 1]
    first = 3 * (row_place & 1)
    irrep = 2 * y + core
    vir_here = vir[irrep]
    a, b = lane_orbitals(wide.shape)
    row = lax.broadcasted_iota(jnp.int32, wide.shape, 0)
    i_low = (row * 43) >> 8
    j = row - 6 * i_low
    live = (a < vir_here) & (b < vir_here) & (i_low + first < occ_here) & (j < occ_here)
    moved = pltpu.roll(jnp.where(live, wide[...], 0.0), 16 * irrep, 1)

    def write(ref, half):
        for t in range(TILES):
            columns = slice(t * LANES, (t + 1) * LANES)
            ref[8 * t : 8 * t + 8, :] = moved[8 * half : 8 * half + 8, columns]
            ref[MAIN + t : MAIN + t + 1, :] = moved[16 + half : 17 + half, columns]
        ref[MAIN + TILES : SHARD, :] = jnp.zeros((SHARD - MAIN - TILES, LANES), F32)

    @pl.when(core == 0)
    def _():
        write(keep, 0)
        write(send, 1)

    @pl.when(core == 1)
    def _():
        write(keep, 1)
        write(send, 0)


def merge_irreps(even, odd, out, at):
    gap = SPAN - TILES
    out[at : at + 8 * gap, :] = even[0 : 8 * gap, :]
    out[at + 8 * gap : at + MAIN, :] = even[8 * gap : MAIN, :] + odd[0:8, :]
    out[at + MAIN : at + PMAIN, :] = odd[8:MAIN, :]
    extra = at + PMAIN
    out[extra : extra + gap, :] = even[MAIN : MAIN + gap, :]
    out[extra + gap : extra + TILES, :] = even[MAIN + gap : MAIN + TILES, :] + odd[MAIN : MAIN + 1, :]
    out[extra + TILES : extra + SPAN, :] = odd[MAIN + 1 : MAIN + TILES, :]
    out[extra + SPAN : at + PAIR, :] = jnp.zeros((PAIR - PMAIN - SPAN, LANES), F32)


def merge_quad(keep, got, far_keep, far_got, out):
    core = lax.axis_index("core")

    @pl.when(core == 0)
    def _():
        merge_irreps(keep, got, out, 0)
        merge_irreps(far_keep, far_got, out, PAIR)

    @pl.when(core == 1)
    def _():
        merge_irreps(got, keep, out, 0)
        merge_irreps(far_got, far_keep, out, PAIR)


def gather_four(b0, b1, b2, b3, near, far):
    for at, block in enumerate((b0, b1, b2, b3)):
        near[at * PAIR : (at + 1) * PAIR, :] = block[0:PAIR, :]
        far[at * PAIR : (at + 1) * PAIR, :] = block[PAIR:QUAD, :]


def nothing(*refs):
    pass


def hold(a, b, *witnesses):
    return pl.pallas_call(
        nothing,
        out_shape=[jax.ShapeDtypeStruct(v.shape, v.dtype) for v in (a, b)],
        in_specs=[ANY] * (2 + len(witnesses)),
        out_specs=[ANY] * 2,
        input_output_aliases={0: 0, 1: 1},
        compiler_params=SMALL,
    )(a, b, *witnesses)


def left_side(blocks, extra):
    for t in range(SPAN):
        for d, block in enumerate(blocks):
            extra[4 * d : 4 * d + 4, t * LANES : (t + 1) * LANES] = block[pl.ds(PMAIN + t, 4, stride=PAIR), :]
    rows = []
    for block in blocks:
        for e in range(4):
            rows.append(
                jnp.concatenate(
                    [block[e * PAIR + 8 * t : e * PAIR + 8 * t + 8, :] for t in range(SPAN)], axis=1
                )
            )
    return split(jnp.concatenate(rows + [extra[...]], axis=0))


def split(value):
    high = value.astype(BF16)
    return high, (value - high.astype(F32)).astype(BF16)


def tiles_side(ref, first):
    return jnp.concatenate(
        [ref[(first + t) * PSLOT : (first + t + 1) * PSLOT, :] for t in range(SPAN)], axis=1
    )


def last_by_last(p, q):
    return lax.dot_general(p, q, (((1,), (1,)), ((), ())), preferred_element_type=F32)


def multiply_near(b0, b1, b2, b3, home, home_other, below, below_other, above, above_other,
                  here_sum, below_sum, above_sum, extra, turned):
    high, low = left_side((b0, b1, b2, b3), extra)
    sides = [tiles_side(ref, 0) for ref in (home, home_other, below, below_other, above, above_other)]
    v_high, v_low = split(jnp.concatenate(sides, axis=0))
    total = last_by_last(v_high, high) + (last_by_last(v_low, high) + last_by_last(v_high, low))
    turned[...] = jnp.zeros_like(turned)
    for at, ref in enumerate((here_sum, below_sum, above_sum)):
        for side in range(2):
            rows = slice((2 * at + side) * PSLOT, (2 * at + side + 1) * PSLOT)
            turned[0:PSLOT, 0:144] = total[rows, :]
            ref[:, side * LANES : (side + 1) * LANES] = turned[...].T[0:144, :]


def multiply_far(b0, b1, b2, b3, home, home_other, here_sum, back_a, back_b, out, extra):
    x, z, y, core = places()
    high, low = left_side((b0, b1, b2, b3), extra)
    partial = here_sum[...] + back_a[...] + back_b[...]
    row = lax.broadcasted_iota(jnp.int32, (8, LANES), 0)
    lane = lax.broadcasted_iota(jnp.int32, (8, LANES), 1)
    pad = jnp.zeros((LANES - PSLOT, DEPTH), BF16)
    sides = [split(tiles_side(ref, SPAN)) for ref in (home, home_other)]
    v_high = jnp.concatenate([sides[0][0], pad, sides[1][0], pad], axis=0)
    v_low = jnp.concatenate([sides[0][1], pad, sides[1][1], pad], axis=0)
    total = partial + (
        last_by_last(high, v_high) + (last_by_last(low, v_high) + last_by_last(high, v_low))
    )
    for side in range(2):
        columns = slice(side * LANES, (side + 1) * LANES)
        last = total[128:144, columns]
        last_a = pltpu.roll(last, 81, 1)
        last_b = pltpu.roll(last, 34, 1)
        core_there = core if side == 0 else 1 - core
        for d in range(4):
            for e in range(4):
                s = 4 * d + e
                x_step = jnp.where(core == 0, STEPS[e], STEPS[d])
                z_step = jnp.where(core == 0, STEPS[d], STEPS[e])
                there = ((x - x_step) & 3) * 4 + ((z - z_step) & 3)
                main = total[8 * s : 8 * s + 8, columns]
                tail = jnp.where(row == 0, last_a[s : s + 1, :], last_b[s : s + 1, :])
                out[there * 2 + core_there] = jnp.where(lane < 81, main, tail)


def local_step(occ_ref, vir_ref, eps_occ_ref, eps_vir_ref, amp_ref, witness,
               scale, live, amp, occ, vir, eps_occ, eps_vir, sems):
    x, z, y, core = places()
    copies = [
        pltpu.make_async_copy(source, target, sems.at[at])
        for at, (source, target) in enumerate(
            ((occ_ref, occ), (vir_ref, vir), (eps_occ_ref, eps_occ), (eps_vir_ref, eps_vir), (amp_ref, amp))
        )
    ]
    for copy in copies:
        copy.start()
    for copy in copies:
        copy.wait()
    row_place = x * 4 + z
    shell = row_place >> 1
    first = 3 * (row_place & 1)
    irrep = 2 * y + core
    a, b = lane_orbitals((1, 1296))
    energy_a = jnp.zeros((1, 1296), F32)
    energy_b = jnp.zeros((1, 1296), F32)
    for slot in range(36):
        value = eps_vir[irrep, slot]
        energy_a = jnp.where(a == slot, value, energy_a)
        energy_b = jnp.where(b == slot, value, energy_b)
    lane_live = (a < vir[irrep]) & (b < vir[irrep])
    occ_here = occ[shell]
    for r in range(18):
        i, j = first + r // 6, r % 6
        here = lane_live & (i < occ_here) & (j < occ_here)
        gap = eps_occ[shell, i] + eps_occ[shell, j] - energy_a - energy_b
        scale[r : r + 1, :] = jnp.where(here, 1.0, 0.0) / gap
        live[r : r + 1, :] = jnp.where(here, amp[r // 6, r % 6], 0.0)


def finish(sums, scale, cycle, out, wide):
    wide[...] = jnp.zeros_like(wide)
    lane8 = lax.broadcasted_iota(jnp.int32, (1, LANES), 1)
    lane = lax.broadcasted_iota(jnp.int32, (24, LANES), 1)
    for r in range(16):
        mains, lasts = [], []
        for core in range(2):
            block = sums[2 * r + core]
            mains.append(block)
            lasts.append(
                jnp.where(lane8 < 47, pltpu.roll(block, 47, 1)[0:1, :], pltpu.roll(block, 94, 1)[1:2, :])
            )
        stack = jnp.concatenate(mains + lasts + [jnp.zeros((6, LANES), F32)], axis=0)
        tile, start = divmod(81 * r, LANES)
        turned = pltpu.roll(stack, start, 1) if start else stack
        here = slice(tile * LANES, (tile + 1) * LANES)
        wide[:, here] = jnp.where((lane >= start) & (lane < start + 81), turned, wide[:, here])
        if start + 81 > LANES:
            after = slice((tile + 1) * LANES, (tile + 2) * LANES)
            wide[:, after] = jnp.where(lane < start + 81 - LANES, turned, wide[:, after])
    out[...] = (wide[0:18, 0:1296] + cycle[...]) * scale[...]


def cycle_term(live, ovov, row_place):
    partner = lax.ppermute(ovov, "z", [(0, 1), (1, 0), (2, 3), (3, 2)])
    panel = jnp.where(
        row_place % 2 == 0,
        jnp.concatenate([ovov, partner], 0),
        jnp.concatenate([partner, ovov], 0),
    )
    panel = panel.reshape(6, 36, 6, 36)
    cycle = jnp.einsum(
        "ikac,kcjb->ijab", live.reshape(3, 6, 36, 36), panel, precision=lax.Precision.HIGHEST
    )
    return cycle.reshape(18, 1296)


def on_device(amplitudes, vvvv, ovov, eps_occ, eps_vir, occ_count, vir_count):
    x, z, y, core = places()
    shape = jax.ShapeDtypeStruct
    keep, send = pl.pallas_call(
        open_step,
        out_shape=[shape((SHARD, LANES), F32)] * 2,
        in_specs=[HBM] * 3,
        out_specs=[VMEM] * 2,
        scratch_shapes=[
            pltpu.VMEM((24, WINDOW), F32),
            pltpu.VMEM((3, 6, 1, 1296), F32),
            pltpu.SMEM((8,), jnp.int32),
            pltpu.SMEM((8,), jnp.int32),
            pltpu.SemaphoreType.DMA((3,)),
        ],
        compiler_params=SMALL,
    )(occ_count, vir_count, amplitudes)
    got = swap_core(send)
    far_keep = ring(keep, "yy", 2)
    far_got = ring(send, "yy", 2, cross=True)
    up, down, home = pl.pallas_call(
        cut_step,
        out_shape=[shape((SPAN, PSLOT, 1, LANES), F32)] * 2 + [shape((2 * SPAN, PSLOT, 1, LANES), F32)],
        in_specs=[HBM, ANY],
        out_specs=[VMEM] * 3,
        scratch_shapes=[pltpu.SemaphoreType.DMA((4, SPAN))],
        compiler_params=SMALL,
        cost_estimate=pl.CostEstimate(flops=0, bytes_accessed=7000000, transcendentals=0),
    )(vvvv.reshape(81, 1, 10368), send)
    home = home.reshape(2 * PROWS, LANES)
    home_other = swap_core(home)
    up, down = hold(up.reshape(PROWS, LANES), down.reshape(PROWS, LANES), far_keep, far_got)
    quad = pl.pallas_call(
        merge_quad,
        out_shape=shape((QUAD, LANES), F32),
        in_specs=[VMEM] * 4,
        out_specs=VMEM,
        compiler_params=SMALL,
    )(keep, got, far_keep, far_got)
    below = ring(up, "yy", 1)
    above = ring(down, "yy", -1)

    near, far = pl.pallas_call(
        gather_four,
        out_shape=[shape((4 * PAIR, LANES), F32)] * 2,
        in_specs=[VMEM] * 4,
        out_specs=[VMEM] * 2,
        compiler_params=SMALL,
    )(quad, *[ring(quad, "xz", step) for step in SHIFTS])
    near_blocks = [near] + [ring(near, "zx", step) for step in SHIFTS]
    far_blocks = [far] + [ring(far, "zx", step) for step in SHIFTS]

    below, above = hold(below, above, *near_blocks[1:])
    below_other, above_other = swap_core(below), swap_core(above)

    scale, live = pl.pallas_call(
        local_step,
        out_shape=[shape((18, 1296), F32)] * 2,
        in_specs=[HBM] * 5 + [ANY],
        out_specs=[VMEM] * 2,
        scratch_shapes=[
            pltpu.VMEM((3, 6, 1, 1296), F32),
            pltpu.SMEM((8,), jnp.int32),
            pltpu.SMEM((8,), jnp.int32),
            pltpu.SMEM((8, 6), F32),
            pltpu.SMEM((8, 36), F32),
            pltpu.SemaphoreType.DMA((5,)),
        ],
        compiler_params=SMALL,
    )(occ_count, vir_count, eps_occ, eps_vir, amplitudes, near)
    cycle = cycle_term(live, ovov, x * 4 + z)

    sums = [shape((144, 2 * LANES), F32)] * 3
    here_sum, below_sum, above_sum = pl.pallas_call(
        multiply_near,
        out_shape=sums,
        in_specs=[VMEM] * 10,
        out_specs=[VMEM] * 3,
        scratch_shapes=[pltpu.VMEM((16, DEPTH), F32), pltpu.VMEM((LANES, 2 * LANES), F32)],
        compiler_params=LARGE,
    )(*near_blocks, home, home_other, below, below_other, above, above_other)
    back_a = ring(below_sum, "yy", -1)
    back_b = ring(above_sum, "yy", 1)
    packed = pl.pallas_call(
        multiply_far,
        out_shape=shape((32, 8, LANES), F32),
        in_specs=[VMEM] * 9,
        out_specs=VMEM,
        scratch_shapes=[pltpu.VMEM((16, DEPTH), F32)],
        compiler_params=LARGE,
    )(*far_blocks, home, home_other, here_sum, back_a, back_b)
    ladder = lax.all_to_all(packed, ("x", "z", "core"), 0, 0, tiled=True)
    result = pl.pallas_call(
        finish,
        out_shape=shape((18, 1296), F32),
        in_specs=[VMEM] * 3,
        out_specs=VMEM,
        scratch_shapes=[pltpu.VMEM((24, WINDOW), F32)],
        compiler_params=SMALL,
    )(ladder, scale, cycle)
    return result.reshape(3, 6, 1, 1296)


def solution(mesh):
    fine = Mesh(mesh.devices.reshape(4, 4, 4, 2), AXES)
    rows, cols = ("x", "z"), ("y", "core")
    return jax.shard_map(
        on_device,
        mesh=fine,
        in_specs=(P(rows, None, cols, None), P(cols, rows, None), P(rows, cols, None), P(), P(), P(), P()),
        out_specs=P(rows, None, cols, None),
        check_vma=False,
    )
```

time: 185 us -> 95.2 us (0.51)
  waiting for transfers between devices: 93.8 us -> 25 us
  starting transfers between devices: 6.7 us -> 37.5 us
  local copies, waits for them, and re-layouts: 31.8 us -> 12.7 us
  blocking collectives: 15.6 us -> 0 us
  matrix products: 17.1 us -> 3.75 us
  between operations: 13.5 us -> 0.15 us
  Pallas kernels: 0 us -> 12.7 us
  other arithmetic: 5.57 us -> 2.53 us
    all_gather x1 -> x0, waiting for transfers between devices: 88.9 us -> none  [on_device(): piece = lax.all_gather(full_irreps, 'row', axis=0, tiled=True)]
    ppermute x1 -> x20, starting transfers between devices: 1.72 us -> 26.4 us  [the longest x15 22.4 us: ring(): return lax.ppermute(value, AXES, pairs)]
    ppermute x1 -> x20, waiting for transfers between devices: 0.01 us -> 21.4 us  [the longest x15 21.4 us: ring(): return lax.ppermute(value, AXES, pairs)]
    all_gather x1 -> x0, blocking collectives: 15.6 us -> none  [on_device(): full_irreps = lax.all_gather(amps_flat, 'col', axis=2, tiled=True)]
    reshape x7 -> x3, local copies, waits for them, and re-layouts: 17.9 us -> 2.77 us  [the longest x1 1.84 us: cycle_term(): live.reshape(3, 6, 36, 36)]
    dot_general x2 -> x1, matrix products: 17.1 us -> 3.75 us  [cycle_term(): jnp.einsum('ikac,kcjb->ijab', live.reshape(3, 6, 36, 36), panel, precisio...]
    pallas_call x0 -> x10, Pallas kernels: none -> 12.7 us  [the longest x1 3.59 us: on_device(): pl.pallas_call(cut_step, out_shape=[shape((SPAN, PSLOT, 1, LANES), F32)]...]
    all_gather x2 -> x0, local copies, waits for them, and re-layouts: 11.3 us -> none  [the longest x1 10.2 us: on_device(): piece = lax.all_gather(full_irreps, 'row', axis=0, tiled=True)]
  transfers between devices with their start and end apart: 3 -> 21, of which waited for: 2 -> 8; matrix products, arithmetic and copies ran while one was open for 24% -> 11% of each run, Pallas kernels for 0% -> 9%
where the time goes in v2:
time: 95.2 us; the launch traced here: 94.3 us
  starting transfers between devices  37.5 us (39%)
  waiting for transfers between devices  25 us (26%)
  local copies, waits for them, and re-layouts  12.7 us (13%)
  Pallas kernels  12.7 us (13%)
  matrix products  3.75 us (4%)
  other arithmetic  2.53 us (3%)
    ppermute x15, starting transfers between devices, ring(): return lax.ppermute(value, AXES, pairs)  22.4 us
    ppermute x15, waiting for transfers between devices, ring(): return lax.ppermute(value, AXES, pairs)  21.4 us
    all_to_all x1, starting transfers between devices, on_device(): ladder = lax.all_to_all(packed, ('x', 'z', 'core'), 0, 0, tiled=True)  11.1 us
    unnamed x32, local copies, waits for them, and re-layouts  7.63 us
    dot_general x1, matrix products, cycle_term(): jnp.einsum('ikac,kcjb->ijab', live.reshape(3, 6, 36, 36), panel, precisio...  3.75 us
    pallas_call x1, Pallas kernels, on_device(): pl.pallas_call(cut_step, out_shape=[shape((SPAN, PSLOT, 1, LANES), F32)]...  3.59 us
    all_to_all x1, waiting for transfers between devices, on_device(): ladder = lax.all_to_all(packed, ('x', 'z', 'core'), 0, 0, tiled=True)  3.53 us
    pallas_call x1, Pallas kernels, on_device(): pl.pallas_call(multiply_near, out_shape=sums, in_specs=[VMEM] * 10, out_s...  3.41 us
  transfers between devices with their start and end apart: 21, of which 8 were waited for; matrix products, arithmetic and copies ran while one was open for 11% of the time, Pallas kernels for 9%

profile of v2, /device:TPU:1, one launch (start us, length us, event | category | flops | bytes accessed | tf_op | source)
XLA Modules:
  0.0 94.3 jit_solution(17300990631700098289)
XLA Ops:
  2.9 4.4 %collective-permute-start.2 = (f32[104,128]{1,0:T(8,128)S(1)}, f32[104,128]{1,0:T(8,128)S(1)}, u32[]{:S(2)}, u32[]{:S(2)}) collective-permute-start(f32[104,128]{1,0:T(8,128)S(1)} %get-tuple-element.22.witness), channel_id=1, source_target_pairs={{0,5},{1,4},{2,7},{3,6},{4,1},{5,0},{6,3},{7,2},{8,13},{9,12},{10,... | collective-permute-start | bytes 159752 | tf_op jit(solution)/shard_map/ppermute | solution.py:46
  7.5 1.9 %collective-permute-done.2.far_got.refs_3_ = f32[104,128]{1,0:T(8,128)S(1)} collective-permute-done((f32[104,128]{1,0:T(8,128)S(1)}, f32[104,128]{1,0:T(8,128)S(1)}, u32[]{:S(2)}, u32[]{:S(2)}) %collective-permute-start.2) | collective-permute-done | bytes 53280 | tf_op jit(solution)/shard_map/ppermute | solution.py:46
  9.4 2.4 %collective-permute-done.1.far_keep.refs_2_ = f32[104,128]{1,0:T(8,128)S(1)} collective-permute-done((f32[104,128]{1,0:T(8,128)S(1)}, f32[104,128]{1,0:T(8,128)S(1)}, u32[]{:S(2)}, u32[]{:S(2)}) %collective-permute-start.1) | collective-permute-done | bytes 53280 | tf_op jit(solution)/shard_map/ppermute | solution.py:46
  11.8 1.7 %collective-permute-start.3 = (f32[384,128]{1,0:T(8,128)S(1)}, f32[384,128]{1,0:T(8,128)S(1)}, u32[]{:S(2)}, u32[]{:S(2)}) collective-permute-start(f32[384,128]{1,0:T(8,128)S(1)} %shard_map.74.b0), channel_id=1, source_target_pairs={{0,32},{1,9},{2,34},{3,11},{4,36},{5,13},{6,38},{7,15},{8,40},{9,1... | collective-permute-start | bytes 589832 | tf_op jit(solution)/shard_map/ppermute | solution.py:46
  13.5 1.9 %copy-done.2 = f32[1,81,10368]{2,0,1:T(1,128)S(1)} copy-done((f32[1,81,10368]{2,0,1:T(1,128)S(1)}, f32[1,81,10368]{2,0,1:T(1,128)}, u32[]{:S(2)}) %copy-start.2) | copy-done | bytes 3359256
  15.5 3.6 %shard_map.76 = (f32[21,88,1,128]{3,2,1,0:T(1,128)S(1)}, f32[21,88,1,128]{3,2,1,0:T(1,128)S(1)}, f32[42,88,1,128]{3,2,1,0:T(1,128)S(1)}) custom-call(f32[81,1,10368]{2,1,0:T(1,128)S(1)} %bitcast.14, f32[104,128]{1,0:T(8,128)S(1)} %get-tuple-element.22.witness), custom_call_target="tpu_custom_call" | custom-call | bytes 7000000 | tf_op jit(solution)/shard_map/pallas_call | solution.py:338
  19.1 1.6 %collective-permute-start.9 = (f32[3696,128]{1,0:T(8,128)S(1)}, f32[3696,128]{1,0:T(8,128)S(1)}, u32[]{:S(2)}, u32[]{:S(2)}) collective-permute-start(f32[3696,128]{1,0:T(8,128)S(1)} %bitcast.11), channel_id=1, source_target_pairs={{0,1},{1,0},{2,3},{3,2},{4,5},{5,4},{6,7},{7,6},{8,9},{9,8},{10,11... | collective-permute-start | bytes 5677064 | tf_op jit(solution)/shard_map/ppermute | solution.py:50
  20.7 3.8 %collective-permute-start.4 = (f32[384,128]{1,0:T(8,128)S(1)}, f32[384,128]{1,0:T(8,128)S(1)}, u32[]{:S(2)}, u32[]{:S(2)}) collective-permute-start(f32[384,128]{1,0:T(8,128)S(1)} %shard_map.74.b0), channel_id=1, source_target_pairs={{0,96},{1,25},{2,98},{3,27},{4,100},{5,29},{6,102},{7,31},{8,104},... | collective-permute-start | bytes 589832 | tf_op jit(solution)/shard_map/ppermute | solution.py:46
  24.8 2.3 %collective-permute-start.14 = (f32[1848,128]{1,0:T(8,128)S(1)}, f32[1848,128]{1,0:T(8,128)S(1)}, u32[]{:S(2)}, u32[]{:S(2)}) collective-permute-start(f32[1848,128]{1,0:T(8,128)S(1)} %get-tuple-element.29), channel_id=1, source_target_pairs={{0,6},{1,7},{2,0},{3,1},{4,2},{5,3},{6,4},{7,5},{8,14},{9,15},{10,... | collective-permute-start | bytes 2838536 | tf_op jit(solution)/shard_map/ppermute | solution.py:46
  27.1 2.0 %collective-permute-done.4.b2 = f32[384,128]{1,0:T(8,128)S(1)} collective-permute-done((f32[384,128]{1,0:T(8,128)S(1)}, f32[384,128]{1,0:T(8,128)S(1)}, u32[]{:S(2)}, u32[]{:S(2)}) %collective-permute-start.4) | collective-permute-done | bytes 196640 | tf_op jit(solution)/shard_map/ppermute | solution.py:46
  33.3 5.5 %collective-permute-done.10.refs_2_.b1 = f32[768,128]{1,0:T(8,128)S(1)} collective-permute-done((f32[768,128]{1,0:T(8,128)S(1)}, f32[768,128]{1,0:T(8,128)S(1)}, u32[]{:S(2)}, u32[]{:S(2)}) %collective-permute-start.10) | collective-permute-done | bytes 393248 | tf_op jit(solution)/shard_map/ppermute | solution.py:46
  40.0 7.2 %collective-permute-done.12.refs_4_.b3 = f32[768,128]{1,0:T(8,128)S(1)} collective-permute-done((f32[768,128]{1,0:T(8,128)S(1)}, f32[768,128]{1,0:T(8,128)S(1)}, u32[]{:S(2)}, u32[]{:S(2)}) %collective-permute-start.12) | collective-permute-done | bytes 393248 | tf_op jit(solution)/shard_map/ppermute | solution.py:46
  49.9 2.0 %collective-permute-start.7 = (f32[768,128]{1,0:T(8,128)S(1)}, f32[768,128]{1,0:T(8,128)}, u32[]{:S(2)}, u32[]{:S(2)}) collective-permute-start(f32[768,128]{1,0:T(8,128)S(1)} %get-tuple-element.23.b0), channel_id=1, source_target_pairs={{0,24},{1,97},{2,26},{3,99},{4,28},{5,101},{6,30},{7,103},{8,0},{9... | collective-permute-start | bytes 1179656 | tf_op jit(solution)/shard_map/ppermute | solution.py:46
  52.2 1.6 %collective-permute-start.19 = (f32[108,1,216]{2,1,0:T(1,128)S(1)}, f32[108,1,216]{2,1,0:T(1,128)S(1)}, u32[]{:S(2)}, u32[]{:S(2)}) collective-permute-start(f32[108,1,216]{2,1,0:T(1,128)S(1)} %copy-done.14), channel_id=1, source_target_pairs={{0,8},{8,0},{16,24},{24,16},{1,9},{9,1},{17,25},{25,17},{2,10},{10... | collective-permute-start | bytes 279944 | tf_op jit(solution)/shard_map/ppermute | solution.py:305
  53.8 3.4 %shard_map.79 = (f32[144,256]{1,0:T(8,128)S(1)}, f32[144,256]{1,0:T(8,128)}, f32[144,256]{1,0:T(8,128)}) custom-call(f32[768,128]{1,0:T(8,128)S(1)} %get-tuple-element.25.b0.witness, f32[768,128]{1,0:T(8,128)S(1)} %collective-permute-done.10.refs_2_.b1, f32[768,128]{1,0:T(8,128)S(1)} %collective-permute-done.11.refs_3_.b2, ...), custom_call_target="tpu_custom_call" | custom-call | tf_op jit(solution)/shard_map/pallas_call | solution.py:391
  57.3 2.6 %collective-permute-start.17 = (f32[144,256]{1,0:T(8,128)}, f32[144,256]{1,0:T(8,128)S(1)}, u32[]{:S(2)}, u32[]{:S(2)}) collective-permute-start(f32[144,256]{1,0:T(8,128)} %get-tuple-element.33), channel_id=1, source_target_pairs={{0,6},{1,7},{2,0},{3,1},{4,2},{5,3},{6,4},{7,5},{8,14},{9,15},{10,... | collective-permute-start | bytes 442376 | tf_op jit(solution)/shard_map/ppermute | solution.py:46
  60.5 2.5 %fusion.1 = f32[216,216]{1,0:T(8,128)} fusion(pred[]{:T(512)S(6)} %eq.5, f32[108,1,216]{2,1,0:T(1,128)} %copy-done.15, f32[108,1,216]{2,1,0:T(1,128)} %param.9), kind=kLoop, calls=%fused_computation.3 | loop fusion | flops 139968 | bytes 373249 | tf_op jit(solution)/shard_map/jit(_where)/select_n | solution.py:306
  63.1 2.1 %select_n.24 = f32[6,36,6,36]{3,2,1,0:T(8,128)} reshape(f32[216,216]{1,0:T(8,128)} %fusion.1) | data formatting | bytes 373248 | tf_op jit(solution)/shard_map/jit(_where)/select_n | solution.py:306
  67.8 1.8 %reshape.47 = f32[3,6,36,36,1]{3,2,1,0,4:T(8,128)} reshape(f32[18,1296]{1,0:T(8,128)} %copy-done.7) | data formatting | bytes 186624 | tf_op jit(solution)/shard_map/reshape | solution.py:313
  69.6 1.5 %copy-done.1 = f32[3696,128]{1,0:T(8,128)S(1)} copy-done((f32[3696,128]{1,0:T(8,128)S(1)}, f32[3696,128]{1,0:T(8,128)}, u32[]{:S(2)}) %copy-start.1) | copy-done | bytes 1892376
  71.2 3.4 %shard_map.80 = f32[32,8,128]{2,1,0:T(8,128)} custom-call(f32[768,128]{1,0:T(8,128)S(1)} %get-tuple-element.23.b0, f32[768,128]{1,0:T(8,128)S(1)} %collective-permute-done.6.b1, f32[768,128]{1,0:T(8,128)} %collective-permute-done.7.b2, f32[768,128]{1,0:T(8,128)} %collective-permute-done.8.b3, f32[3696,128]{1,0:T(8,128)S(1)} %bitcast.13, ...), custom_call_target="tpu_custom_call" | custom-call | tf_op jit(solution)/shard_map/pallas_call | solution.py:401
  74.5 11.1 %all-to-all-start = ((f32[32,8,128]{2,1,0:T(8,128)}), f32[32,8,128]{2,1,0:T(8,128)S(1)}, u32[]{:S(2)}, u32[]{:S(2)}) async-start(f32[32,8,128]{2,1,0:T(8,128)} %shard_map.80), calls=%async_computation | async-start | bytes 262144 | tf_op jit(solution)/shard_map/all_to_all | solution.py:409
  85.6 3.7 %convolution_bitcast_fusion = f32[3,6,36,36]{2,3,0,1:T(8,128)S(1)} fusion(f32[3,6,36,36,1]{3,2,1,0,4:T(8,128)} %reshape.47, f32[6,36,6,36,1]{3,2,1,0,4:T(8,128)} %bitcast.17), kind=kOutput, calls=%fused_computation | convolution fusion | flops 60466176 | bytes 373248 | tf_op jit(solution)/shard_map/ikac,kcjb->ijab/dot_general | solution.py:312
  89.8 3.5 %all-to-all-done.sums = f32[32,8,128]{2,1,0:T(8,128)S(1)} async-done(((f32[32,8,128]{2,1,0:T(8,128)}), f32[32,8,128]{2,1,0:T(8,128)S(1)}, u32[]{:S(2)}, u32[]{:S(2)}) %all-to-all-start) | async-done | bytes 131104 | tf_op jit(solution)/shard_map/all_to_all | solution.py:409
  (67 shorter events, 16.5 us)
Async XLA Ops:
  2.9 6.4 %collective-permute-start.2 = (f32[104,128]{1,0:T(8,128)S(1)}, f32[104,128]{1,0:T(8,128)S(1)}, u32[]{:S(2)}, u32[]{:S(2)}) collective-permute-start(f32[104,128]{1,0:T(8,128)S(1)} %get-tuple-element.22.witness), channel_id=1, source_target_pairs={{0,5},{1,4},{2,7},{3,6},{4,1},{5,0},{6,3},{7,2},{8,13},{9,12},{10,... | collective-permute-start | bytes 159752 | tf_op jit(solution)/shard_map/ppermute | solution.py:46
  7.3 2.1 %collective-permute-start = (f32[104,128]{1,0:T(8,128)S(1)}, f32[104,128]{1,0:T(8,128)S(1)}, u32[]{:S(2)}, u32[]{:S(2)}) collective-permute-start(f32[104,128]{1,0:T(8,128)S(1)} %get-tuple-element.22.witness), channel_id=1, source_target_pairs={{0,1},{1,0},{2,3},{3,2},{4,5},{5,4},{6,7},{7,6},{8,9},{9,8},{10,11... | collective-permute-start | bytes 159752 | tf_op jit(solution)/shard_map/ppermute | solution.py:50
  7.3 4.5 %collective-permute-start.1 = (f32[104,128]{1,0:T(8,128)S(1)}, f32[104,128]{1,0:T(8,128)S(1)}, u32[]{:S(2)}, u32[]{:S(2)}) collective-permute-start(f32[104,128]{1,0:T(8,128)S(1)} %get-tuple-element.21.keep), channel_id=1, source_target_pairs={{0,4},{1,5},{2,6},{3,7},{4,0},{5,1},{6,2},{7,3},{8,12},{9,13},{10,... | collective-permute-start | bytes 159752 | tf_op jit(solution)/shard_map/ppermute | solution.py:46
  11.8 13.0 %collective-permute-start.3 = (f32[384,128]{1,0:T(8,128)S(1)}, f32[384,128]{1,0:T(8,128)S(1)}, u32[]{:S(2)}, u32[]{:S(2)}) collective-permute-start(f32[384,128]{1,0:T(8,128)S(1)} %shard_map.74.b0), channel_id=1, source_target_pairs={{0,32},{1,9},{2,34},{3,11},{4,36},{5,13},{6,38},{7,15},{8,40},{9,1... | collective-permute-start | bytes 589832 | tf_op jit(solution)/shard_map/ppermute | solution.py:46
  19.1 32.8 %collective-permute-start.9 = (f32[3696,128]{1,0:T(8,128)S(1)}, f32[3696,128]{1,0:T(8,128)S(1)}, u32[]{:S(2)}, u32[]{:S(2)}) collective-permute-start(f32[3696,128]{1,0:T(8,128)S(1)} %bitcast.11), channel_id=1, source_target_pairs={{0,1},{1,0},{2,3},{3,2},{4,5},{5,4},{6,7},{7,6},{8,9},{9,8},{10,11... | collective-permute-start | bytes 5677064 | tf_op jit(solution)/shard_map/ppermute | solution.py:50
  20.7 8.5 %collective-permute-start.4 = (f32[384,128]{1,0:T(8,128)S(1)}, f32[384,128]{1,0:T(8,128)S(1)}, u32[]{:S(2)}, u32[]{:S(2)}) collective-permute-start(f32[384,128]{1,0:T(8,128)S(1)} %shard_map.74.b0), channel_id=1, source_target_pairs={{0,96},{1,25},{2,98},{3,27},{4,100},{5,29},{6,102},{7,31},{8,104},... | collective-permute-start | bytes 589832 | tf_op jit(solution)/shard_map/ppermute | solution.py:46
  24.4 6.0 %collective-permute-start.5 = (f32[384,128]{1,0:T(8,128)S(1)}, f32[384,128]{1,0:T(8,128)S(1)}, u32[]{:S(2)}, u32[]{:S(2)}) collective-permute-start(f32[384,128]{1,0:T(8,128)S(1)} %shard_map.74.b0), channel_id=1, source_target_pairs={{0,64},{1,17},{2,66},{3,19},{4,68},{5,21},{6,70},{7,23},{8,72},{9,... | collective-permute-start | bytes 589832 | tf_op jit(solution)/shard_map/ppermute | solution.py:46
  24.4 23.9 %collective-permute-start.13 = (f32[1848,128]{1,0:T(8,128)S(1)}, f32[1848,128]{1,0:T(8,128)S(1)}, u32[]{:S(2)}, u32[]{:S(2)}) collective-permute-start(f32[1848,128]{1,0:T(8,128)S(1)} %get-tuple-element.28), channel_id=1, source_target_pairs={{0,2},{1,3},{2,4},{3,5},{4,6},{5,7},{6,0},{7,1},{8,10},{9,11},{10,... | collective-permute-start | bytes 2838536 | tf_op jit(solution)/shard_map/ppermute | solution.py:46
  24.8 27.4 %copy-start.14 = (f32[108,1,216]{2,1,0:T(1,128)S(1)}, f32[108,1,216]{2,1,0:T(1,128)}, u32[]{:S(2)}) copy-start(f32[108,1,216]{2,1,0:T(1,128)} %param.9) | copy-start | bytes 279940
  24.8 23.4 %collective-permute-start.14 = (f32[1848,128]{1,0:T(8,128)S(1)}, f32[1848,128]{1,0:T(8,128)S(1)}, u32[]{:S(2)}, u32[]{:S(2)}) collective-permute-start(f32[1848,128]{1,0:T(8,128)S(1)} %get-tuple-element.29), channel_id=1, source_target_pairs={{0,6},{1,7},{2,0},{3,1},{4,2},{5,3},{6,4},{7,5},{8,14},{9,15},{10,... | collective-permute-start | bytes 2838536 | tf_op jit(solution)/shard_map/ppermute | solution.py:46
  30.5 8.2 %collective-permute-start.10 = (f32[768,128]{1,0:T(8,128)S(1)}, f32[768,128]{1,0:T(8,128)S(1)}, u32[]{:S(2)}, u32[]{:S(2)}) collective-permute-start(f32[768,128]{1,0:T(8,128)S(1)} %get-tuple-element.25.b0.witness), channel_id=1, source_target_pairs={{0,8},{1,33},{2,10},{3,35},{4,12},{5,37},{6,14},{7,39},{8,16},{9,4... | collective-permute-start | bytes 1179656 | tf_op jit(solution)/shard_map/ppermute | solution.py:46
  31.8 8.2 %collective-permute-start.11 = (f32[768,128]{1,0:T(8,128)S(1)}, f32[768,128]{1,0:T(8,128)S(1)}, u32[]{:S(2)}, u32[]{:S(2)}) collective-permute-start(f32[768,128]{1,0:T(8,128)S(1)} %get-tuple-element.25.b0.witness), channel_id=1, source_target_pairs={{0,24},{1,97},{2,26},{3,99},{4,28},{5,101},{6,30},{7,103},{8,0},{9... | collective-permute-start | bytes 1179656 | tf_op jit(solution)/shard_map/ppermute | solution.py:46
  38.7 8.4 %collective-permute-start.12 = (f32[768,128]{1,0:T(8,128)S(1)}, f32[768,128]{1,0:T(8,128)S(1)}, u32[]{:S(2)}, u32[]{:S(2)}) collective-permute-start(f32[768,128]{1,0:T(8,128)S(1)} %get-tuple-element.25.b0.witness), channel_id=1, source_target_pairs={{0,16},{1,65},{2,18},{3,67},{4,20},{5,69},{6,22},{7,71},{8,24},{9,... | collective-permute-start | bytes 1179656 | tf_op jit(solution)/shard_map/ppermute | solution.py:46
  48.3 3.9 %collective-permute-start.15 = (f32[1848,128]{1,0:T(8,128)S(1)}, f32[1848,128]{1,0:T(8,128)S(1)}, u32[]{:S(2)}, u32[]{:S(2)}) collective-permute-start(f32[1848,128]{1,0:T(8,128)S(1)} %get-tuple-element.30.below), channel_id=1, source_target_pairs={{0,1},{1,0},{2,3},{3,2},{4,5},{5,4},{6,7},{7,6},{8,9},{9,8},{10,11... | collective-permute-start | bytes 2838536 | tf_op jit(solution)/shard_map/ppermute | solution.py:50
  49.0 4.8 %collective-permute-start.16 = (f32[1848,128]{1,0:T(8,128)S(1)}, f32[1848,128]{1,0:T(8,128)S(1)}, u32[]{:S(2)}, u32[]{:S(2)}) collective-permute-start(f32[1848,128]{1,0:T(8,128)S(1)} %get-tuple-element.31.above), channel_id=1, source_target_pairs={{0,1},{1,0},{2,3},{3,2},{4,5},{5,4},{6,7},{7,6},{8,9},{9,8},{10,11... | collective-permute-start | bytes 2838536 | tf_op jit(solution)/shard_map/ppermute | solution.py:50
  49.1 16.1 %copy-start.13 = (s32[8]{0:T(128)S(1)}, s32[8]{0:T(128)}, u32[]{:S(2)}) copy-start(s32[8]{0:T(128)} %vir_ref.3) | copy-start | bytes 100
  49.1 20.5 %collective-permute-start.6 = (f32[768,128]{1,0:T(8,128)S(1)}, f32[768,128]{1,0:T(8,128)S(1)}, u32[]{:S(2)}, u32[]{:S(2)}) collective-permute-start(f32[768,128]{1,0:T(8,128)S(1)} %get-tuple-element.23.b0), channel_id=1, source_target_pairs={{0,8},{1,33},{2,10},{3,35},{4,12},{5,37},{6,14},{7,39},{8,16},{9,4... | collective-permute-start | bytes 1179656 | tf_op jit(solution)/shard_map/ppermute | solution.py:46
  49.9 19.8 %collective-permute-start.7 = (f32[768,128]{1,0:T(8,128)S(1)}, f32[768,128]{1,0:T(8,128)}, u32[]{:S(2)}, u32[]{:S(2)}) collective-permute-start(f32[768,128]{1,0:T(8,128)S(1)} %get-tuple-element.23.b0), channel_id=1, source_target_pairs={{0,24},{1,97},{2,26},{3,99},{4,28},{5,101},{6,30},{7,103},{8,0},{9... | collective-permute-start | bytes 1179656 | tf_op jit(solution)/shard_map/ppermute | solution.py:46
  51.9 17.7 %collective-permute-start.8 = (f32[768,128]{1,0:T(8,128)S(1)}, f32[768,128]{1,0:T(8,128)}, u32[]{:S(2)}, u32[]{:S(2)}) collective-permute-start(f32[768,128]{1,0:T(8,128)S(1)} %get-tuple-element.23.b0), channel_id=1, source_target_pairs={{0,16},{1,65},{2,18},{3,67},{4,20},{5,69},{6,22},{7,71},{8,24},{9,... | collective-permute-start | bytes 1179656 | tf_op jit(solution)/shard_map/ppermute | solution.py:46
  52.2 7.7 %collective-permute-start.19 = (f32[108,1,216]{2,1,0:T(1,128)S(1)}, f32[108,1,216]{2,1,0:T(1,128)S(1)}, u32[]{:S(2)}, u32[]{:S(2)}) collective-permute-start(f32[108,1,216]{2,1,0:T(1,128)S(1)} %copy-done.14), channel_id=1, source_target_pairs={{0,8},{8,0},{16,24},{24,16},{1,9},{9,1},{17,25},{25,17},{2,10},{10... | collective-permute-start | bytes 279944 | tf_op jit(solution)/shard_map/ppermute | solution.py:305
  57.3 12.4 %collective-permute-start.17 = (f32[144,256]{1,0:T(8,128)}, f32[144,256]{1,0:T(8,128)S(1)}, u32[]{:S(2)}, u32[]{:S(2)}) collective-permute-start(f32[144,256]{1,0:T(8,128)} %get-tuple-element.33), channel_id=1, source_target_pairs={{0,6},{1,7},{2,0},{3,1},{4,2},{5,3},{6,4},{7,5},{8,14},{9,15},{10,... | collective-permute-start | bytes 442376 | tf_op jit(solution)/shard_map/ppermute | solution.py:46
  60.5 9.1 %collective-permute-start.18 = (f32[144,256]{1,0:T(8,128)}, f32[144,256]{1,0:T(8,128)}, u32[]{:S(2)}, u32[]{:S(2)}) collective-permute-start(f32[144,256]{1,0:T(8,128)} %get-tuple-element.34), channel_id=1, source_target_pairs={{0,2},{1,3},{2,4},{3,5},{4,6},{5,7},{6,0},{7,1},{8,10},{9,11},{10,... | collective-permute-start | bytes 442376 | tf_op jit(solution)/shard_map/ppermute | solution.py:46
  74.5 18.8 %copy-start.6 = (f32[18,1296]{1,0:T(8,128)S(1)}, f32[18,1296]{1,0:T(8,128)}, u32[]{:S(2)}) copy-start(f32[18,1296]{1,0:T(8,128)} %copy-done.5) | copy-start | bytes 279940
  74.5 18.8 %all-to-all-start = ((f32[32,8,128]{2,1,0:T(8,128)}), f32[32,8,128]{2,1,0:T(8,128)S(1)}, u32[]{:S(2)}, u32[]{:S(2)}) async-start(f32[32,8,128]{2,1,0:T(8,128)} %shard_map.80), calls=%async_computation | async-start | bytes 262144 | tf_op jit(solution)/shard_map/all_to_all | solution.py:409
  (13 other events, 77.2 us)

commit v3 on v2

--- a/solution.py
+++ b/solution.py
@@ -6,7 +6,7 @@
 from jax.sharding import Mesh, PartitionSpec as P
 
 AXES = ("x", "z", "y", "core")
-SHIFTS = (1, -1, 2)
+SHIFTS = ((1, 1), (-1, -1), (2, 2))
 STEPS = (0, 1, -1, 2)
 LANES = 128
 TILES = 11
@@ -25,11 +25,12 @@
 ANY = pl.BlockSpec(memory_space=pl.ANY)
 HBM = pl.BlockSpec(memory_space=pltpu.HBM)
 VMEM = pl.BlockSpec(memory_space=pltpu.VMEM)
+HUGE = pltpu.CompilerParams(vmem_limit_bytes=56 * 1024 * 1024)
 SMALL = pltpu.CompilerParams(vmem_limit_bytes=8 * 1024 * 1024)
 LARGE = pltpu.CompilerParams(vmem_limit_bytes=28 * 1024 * 1024)
 
 
-def ring(value, axes, step, cross=False):
+def ring(value, axes, steps):
     pairs = []
     for x in range(4):
         for z in range(4):
@@ -37,9 +38,7 @@
                 for core in range(2):
                     here = {"x": x, "z": z, "y": y, "core": core}
                     there = dict(here)
-                    there[axes[core]] = (there[axes[core]] + step) % 4
-                    if cross:
-                        there["core"] = 1 - core
+                    there[axes[core]] = (there[axes[core]] + steps[core]) % 4
                     pairs.append(
                         tuple(((p["x"] * 4 + p["z"]) * 4 + p["y"]) * 2 + p["core"] for p in (here, there))
                     )
@@ -60,33 +59,38 @@
     return a, lane - 36 * a
 
 
-def cut_step(integrals, witness, up, down, home, sems):
+def window_copies(integrals, ref, sems, base):
+    copies = []
+    for t in range(SPAN):
+        start = pl.multiple_of((base + t) * LANES, LANES)
+        copies.append(
+            pltpu.make_async_copy(integrals.at[:, :, pl.ds(start, LANES)], ref.at[t, 0:81], sems.at[t])
+        )
+    return copies
+
+
+def cut_home(integrals, integrals_other, witness, near, near_other, far, far_other, sems):
     y = lax.axis_index("y")
-    cuts = []
-    for at, (ref, first, step) in enumerate(((up, 0, 1), (down, 0, 3), (home, 0, 0), (home, SPAN, 2))):
-        base = ((y + step) & 3) * 20
-        for t in range(SPAN):
-            start = pl.multiple_of((base + t) * LANES, LANES)
-            cuts.append(
-                pltpu.make_async_copy(
-                    integrals.at[:, :, pl.ds(start, LANES)], ref.at[first + t, 0:81], sems.at[at, t]
-                )
-            )
-    for copy in cuts:
+    copies = []
+    plan = ((integrals, near, 0), (integrals_other, near_other, 0), (integrals, far, 2), (integrals_other, far_other, 2))
+    for at, (source, ref, step) in enumerate(plan):
+        copies += window_copies(source, ref, sems.at[at], ((y + step) & 3) * 20)
+    for copy in copies:
         copy.start()
-    for ref, tiles in ((up, SPAN), (down, SPAN), (home, 2 * SPAN)):
-        ref[:, 81:PSLOT] = jnp.zeros((tiles, PSLOT - 81, 1, LANES), F32)
-    for copy in cuts:
+    for copy in copies:
         copy.wait()
 
 
-def open_step(occ_ref, vir_ref, amp_ref, keep, send, wide, amp, occ, vir, sems):
+def open_step(occ_ref, vir_ref, amp_ref, integrals, keep, send, first_v, second_v,
+              wide, amp, occ, vir, sems, cut_sems):
     x, z, y, core = places()
     copies = [
         pltpu.make_async_copy(source, target, sems.at[at])
         for at, (source, target) in enumerate(((occ_ref, occ), (vir_ref, vir), (amp_ref, amp)))
     ]
-    for copy in copies:
+    cuts = window_copies(integrals, first_v, cut_sems.at[0], ((y + 1 + 2 * core) & 3) * 20)
+    cuts += window_copies(integrals, second_v, cut_sems.at[1], ((y + 3 - 2 * core) & 3) * 20)
+    for copy in copies + cuts:
         copy.start()
     wide[...] = jnp.zeros_like(wide)
     for copy in copies:
@@ -122,6 +126,9 @@
         write(keep, 1)
         write(send, 0)
 
+    for copy in cuts:
+        copy.wait()
+
 
 def merge_irreps(even, odd, out, at):
     gap = SPAN - TILES
@@ -135,21 +142,24 @@
     out[extra + SPAN : at + PAIR, :] = jnp.zeros((PAIR - PMAIN - SPAN, LANES), F32)
 
 
-def merge_quad(keep, got, far_keep, far_got, out):
+def merge_pair(keep, got, witness, out):
     core = lax.axis_index("core")
 
     @pl.when(core == 0)
     def _():
         merge_irreps(keep, got, out, 0)
-        merge_irreps(far_keep, far_got, out, PAIR)
 
     @pl.when(core == 1)
     def _():
         merge_irreps(got, keep, out, 0)
-        merge_irreps(far_got, far_keep, out, PAIR)
-
-
-def gather_four(b0, b1, b2, b3, near, far):
+
+
+def join_pairs(near, far, out):
+    out[0:PAIR, :] = near[...]
+    out[PAIR:QUAD, :] = far[...]
+
+
+def gather_four(b0, b1, b2, b3, witness, near, far):
     for at, block in enumerate((b0, b1, b2, b3)):
         near[at * PAIR : (at + 1) * PAIR, :] = block[0:PAIR, :]
         far[at * PAIR : (at + 1) * PAIR, :] = block[PAIR:QUAD, :]
@@ -190,10 +200,8 @@
     return high, (value - high.astype(F32)).astype(BF16)
 
 
-def tiles_side(ref, first):
-    return jnp.concatenate(
-        [ref[(first + t) * PSLOT : (first + t + 1) * PSLOT, :] for t in range(SPAN)], axis=1
-    )
+def tiles_side(ref):
+    return jnp.concatenate([ref[t * PSLOT : (t + 1) * PSLOT, :] for t in range(SPAN)], axis=1)
 
 
 def last_by_last(p, q):
@@ -203,7 +211,7 @@
 def multiply_near(b0, b1, b2, b3, home, home_other, below, below_other, above, above_other,
                   here_sum, below_sum, above_sum, extra, turned):
     high, low = left_side((b0, b1, b2, b3), extra)
-    sides = [tiles_side(ref, 0) for ref in (home, home_other, below, below_other, above, above_other)]
+    sides = [tiles_side(ref) for ref in (home, home_other, below, below_other, above, above_other)]
     v_high, v_low = split(jnp.concatenate(sides, axis=0))
     total = last_by_last(v_high, high) + (last_by_last(v_low, high) + last_by_last(v_high, low))
     turned[...] = jnp.zeros_like(turned)
@@ -221,7 +229,7 @@
     row = lax.broadcasted_iota(jnp.int32, (8, LANES), 0)
     lane = lax.broadcasted_iota(jnp.int32, (8, LANES), 1)
     pad = jnp.zeros((LANES - PSLOT, DEPTH), BF16)
-    sides = [split(tiles_side(ref, SPAN)) for ref in (home, home_other)]
+    sides = [split(tiles_side(ref)) for ref in (home, home_other)]
     v_high = jnp.concatenate([sides[0][0], pad, sides[1][0], pad], axis=0)
     v_low = jnp.concatenate([sides[0][1], pad, sides[1][1], pad], axis=0)
     total = partial + (
@@ -244,8 +252,8 @@
                 out[there * 2 + core_there] = jnp.where(lane < 81, main, tail)
 
 
-def local_step(occ_ref, vir_ref, eps_occ_ref, eps_vir_ref, amp_ref, witness,
-               scale, live, amp, occ, vir, eps_occ, eps_vir, sems):
+def local_step(occ_ref, vir_ref, eps_occ_ref, eps_vir_ref, amp_ref, ovov, partner,
+               scale, cycle, amp, occ, vir, eps_occ, eps_vir, left_a, left_b, panel_a, panel_b, sems):
     x, z, y, core = places()
     copies = [
         pltpu.make_async_copy(source, target, sems.at[at])
@@ -255,6 +263,15 @@
     ]
     for copy in copies:
         copy.start()
+    panel_a[...] = jnp.zeros_like(panel_a)
+    panel_b[...] = jnp.zeros_like(panel_b)
+    left_a[...] = jnp.zeros_like(left_a)
+    left_b[...] = jnp.zeros_like(left_b)
+    lower = (z & 1) == 0
+    for r in range(108):
+        own, other = ovov[r], partner[r]
+        panel_a[r : r + 1, 0:216] = jnp.where(lower, own, other)
+        panel_b[r : r + 1, 0:216] = jnp.where(lower, other, own)
     for copy in copies:
         copy.wait()
     row_place = x * 4 + z
@@ -271,11 +288,31 @@
     lane_live = (a < vir[irrep]) & (b < vir[irrep])
     occ_here = occ[shell]
     for r in range(18):
-        i, j = first + r // 6, r % 6
-        here = lane_live & (i < occ_here) & (j < occ_here)
-        gap = eps_occ[shell, i] + eps_occ[shell, j] - energy_a - energy_b
+        low, k = r // 6, r % 6
+        i = first + low
+        here = lane_live & (i < occ_here) & (k < occ_here)
+        gap = eps_occ[shell, i] + eps_occ[shell, k] - energy_a - energy_b
         scale[r : r + 1, :] = jnp.where(here, 1.0, 0.0) / gap
-        live[r : r + 1, :] = jnp.where(here, amp[r // 6, r % 6], 0.0)
+        live = jnp.where(here, amp[low, k], 0.0)
+        left, column = (left_a, 36 * k) if k < 3 else (left_b, 36 * (k - 3))
+        for slot in range(36):
+            left[36 * low + slot : 36 * low + slot + 1, column : column + 36] = live[
+                :, 36 * slot : 36 * slot + 36
+            ]
+    dot = lambda p, q: jnp.dot(p, q, preferred_element_type=F32)
+    total = None
+    for left, panel in ((left_a, panel_a), (left_b, panel_b)):
+        p_high, p_low = split(left[:, 0:112])
+        q_high, q_low = split(panel[...])
+        part = dot(p_high, q_high) + (dot(p_low, q_high) + dot(p_high, q_low))
+        total = part if total is None else total + part
+    for low in range(3):
+        for j in range(6):
+            r = 6 * low + j
+            for slot in range(36):
+                cycle[r : r + 1, 36 * slot : 36 * slot + 36] = total[
+                    36 * low + slot : 36 * low + slot + 1, 36 * j : 36 * j + 36
+                ]
 
 
 def finish(sums, scale, cycle, out, wide):
@@ -301,79 +338,78 @@
     out[...] = (wide[0:18, 0:1296] + cycle[...]) * scale[...]
 
 
-def cycle_term(live, ovov, row_place):
-    partner = lax.ppermute(ovov, "z", [(0, 1), (1, 0), (2, 3), (3, 2)])
-    panel = jnp.where(
-        row_place % 2 == 0,
-        jnp.concatenate([ovov, partner], 0),
-        jnp.concatenate([partner, ovov], 0),
-    )
-    panel = panel.reshape(6, 36, 6, 36)
-    cycle = jnp.einsum(
-        "ikac,kcjb->ijab", live.reshape(3, 6, 36, 36), panel, precision=lax.Precision.HIGHEST
-    )
-    return cycle.reshape(18, 1296)
-
-
 def on_device(amplitudes, vvvv, ovov, eps_occ, eps_vir, occ_count, vir_count):
     x, z, y, core = places()
     shape = jax.ShapeDtypeStruct
-    keep, send = pl.pallas_call(
+    integrals = vvvv.reshape(81, 1, 10368)
+    window = shape((SPAN, PSLOT, 1, LANES), F32)
+    flat = lambda value: value.reshape(PROWS, LANES)
+    keep, send, first_v, second_v = pl.pallas_call(
         open_step,
-        out_shape=[shape((SHARD, LANES), F32)] * 2,
-        in_specs=[HBM] * 3,
-        out_specs=[VMEM] * 2,
+        out_shape=[shape((SHARD, LANES), F32)] * 2 + [window] * 2,
+        in_specs=[HBM] * 4,
+        out_specs=[VMEM] * 2 + [ANY] * 2,
         scratch_shapes=[
             pltpu.VMEM((24, WINDOW), F32),
             pltpu.VMEM((3, 6, 1, 1296), F32),
             pltpu.SMEM((8,), jnp.int32),
             pltpu.SMEM((8,), jnp.int32),
             pltpu.SemaphoreType.DMA((3,)),
+            pltpu.SemaphoreType.DMA((2, SPAN)),
         ],
-        compiler_params=SMALL,
-    )(occ_count, vir_count, amplitudes)
+        compiler_params=HUGE,
+    )(occ_count, vir_count, amplitudes, integrals)
     got = swap_core(send)
-    far_keep = ring(keep, "yy", 2)
-    far_got = ring(send, "yy", 2, cross=True)
-    up, down, home = pl.pallas_call(
-        cut_step,
-        out_shape=[shape((SPAN, PSLOT, 1, LANES), F32)] * 2 + [shape((2 * SPAN, PSLOT, 1, LANES), F32)],
-        in_specs=[HBM, ANY],
-        out_specs=[VMEM] * 3,
-        scratch_shapes=[pltpu.SemaphoreType.DMA((4, SPAN))],
-        compiler_params=SMALL,
-        cost_estimate=pl.CostEstimate(flops=0, bytes_accessed=7000000, transcendentals=0),
-    )(vvvv.reshape(81, 1, 10368), send)
-    home = home.reshape(2 * PROWS, LANES)
-    home_other = swap_core(home)
-    up, down = hold(up.reshape(PROWS, LANES), down.reshape(PROWS, LANES), far_keep, far_got)
+    integrals_other = swap_core(integrals)
+    partner = lax.ppermute(ovov, "z", [(0, 1), (1, 0), (2, 3), (3, 2)])
+    pair = pl.pallas_call(
+        merge_pair,
+        out_shape=shape((PAIR, LANES), F32),
+        in_specs=[VMEM] * 2 + [ANY],
+        out_specs=VMEM,
+        compiler_params=SMALL,
+    )(keep, got, partner)
+    far_pair = ring(pair, "yy", (2, 2))
     quad = pl.pallas_call(
-        merge_quad,
+        join_pairs,
         out_shape=shape((QUAD, LANES), F32),
-        in_specs=[VMEM] * 4,
+        in_specs=[VMEM] * 2,
         out_specs=VMEM,
         compiler_params=SMALL,
-    )(keep, got, far_keep, far_got)
-    below = ring(up, "yy", 1)
-    above = ring(down, "yy", -1)
+    )(pair, far_pair)
+    first_v, second_v = hold(
+        flat(first_v), flat(second_v), far_pair
+    )
+    moved_a = ring(first_v, "yy", (1, -1))
+    moved_b = ring(second_v, "yy", (-1, 1))
 
     near, far = pl.pallas_call(
         gather_four,
         out_shape=[shape((4 * PAIR, LANES), F32)] * 2,
-        in_specs=[VMEM] * 4,
+        in_specs=[VMEM] * 4 + [ANY],
         out_specs=[VMEM] * 2,
         compiler_params=SMALL,
-    )(quad, *[ring(quad, "xz", step) for step in SHIFTS])
+    )(quad, *[ring(quad, "xz", step) for step in SHIFTS], integrals_other)
     near_blocks = [near] + [ring(near, "zx", step) for step in SHIFTS]
     far_blocks = [far] + [ring(far, "zx", step) for step in SHIFTS]
 
-    below, above = hold(below, above, *near_blocks[1:])
-    below_other, above_other = swap_core(below), swap_core(above)
-
-    scale, live = pl.pallas_call(
+    moved_a, moved_b = hold(moved_a, moved_b, *near_blocks[1:])
+    swapped_a, swapped_b = swap_core(moved_a), swap_core(moved_b)
+    homes = pl.pallas_call(
+        cut_home,
+        out_shape=[window] * 4,
+        in_specs=[HBM, HBM, ANY],
+        out_specs=[VMEM] * 4,
+        scratch_shapes=[pltpu.SemaphoreType.DMA((4, SPAN))],
+        compiler_params=SMALL,
+        cost_estimate=pl.CostEstimate(flops=0, bytes_accessed=7000000, transcendentals=0),
+    )(integrals, integrals_other, near_blocks[1])
+    near_v, near_v_other, far_v, far_v_other = (flat(value) for value in homes)
+
+    scale, cycle = pl.pallas_call(
         local_step,
         out_shape=[shape((18, 1296), F32)] * 2,
-        in_specs=[HBM] * 5 + [ANY],
+        in_specs=[HBM] * 5 + [VMEM] * 2,
         out_specs=[VMEM] * 2,
         scratch_shapes=[
             pltpu.VMEM((3, 6, 1, 1296), F32),
@@ -381,11 +417,15 @@
             pltpu.SMEM((8,), jnp.int32),
             pltpu.SMEM((8, 6), F32),
             pltpu.SMEM((8, 36), F32),
+            pltpu.VMEM((112, 256), F32),
+            pltpu.VMEM((112, 256), F32),
+            pltpu.VMEM((112, 256), F32),
+            pltpu.VMEM((112, 256), F32),
             pltpu.SemaphoreType.DMA((5,)),
         ],
         compiler_params=SMALL,
-    )(occ_count, vir_count, eps_occ, eps_vir, amplitudes, near)
-    cycle = cycle_term(live, ovov, x * 4 + z)
+        cost_estimate=pl.CostEstimate(flops=100000000, bytes_accessed=1000000, transcendentals=0),
+    )(occ_count, vir_count, eps_occ, eps_vir, amplitudes, ovov, partner)
 
     sums = [shape((144, 2 * LANES), F32)] * 3
     here_sum, below_sum, above_sum = pl.pallas_call(
@@ -395,9 +435,9 @@
         out_specs=[VMEM] * 3,
         scratch_shapes=[pltpu.VMEM((16, DEPTH), F32), pltpu.VMEM((LANES, 2 * LANES), F32)],
         compiler_params=LARGE,
-    )(*near_blocks, home, home_other, below, below_other, above, above_other)
-    back_a = ring(below_sum, "yy", -1)
-    back_b = ring(above_sum, "yy", 1)
+    )(*near_blocks, near_v, near_v_other, moved_a, swapped_b, moved_b, swapped_a)
+    back_a = ring(below_sum, "yy", (-1, 1))
+    back_b = ring(above_sum, "yy", (1, -1))
     packed = pl.pallas_call(
         multiply_far,
         out_shape=shape((32, 8, LANES), F32),
@@ -405,7 +445,7 @@
         out_specs=VMEM,
         scratch_shapes=[pltpu.VMEM((16, DEPTH), F32)],
         compiler_params=LARGE,
-    )(*far_blocks, home, home_other, here_sum, back_a, back_b)
+    )(*far_blocks, far_v, far_v_other, here_sum, back_a, back_b)
     ladder = lax.all_to_all(packed, ("x", "z", "core"), 0, 0, tiled=True)
     result = pl.pallas_call(
         finish,

time: 95.2 us -> 136 us (1.43)
  Pallas kernels: 12.7 us -> 66.4 us
  local copies, waits for them, and re-layouts: 12.7 us -> 2.8 us
  matrix products: 3.75 us -> 0 us
  waiting for transfers between devices: 25 us -> 28.7 us
  other arithmetic: 2.53 us -> 0 us
    pallas_call x3 -> x4, Pallas kernels: 4.33 us -> 58.3 us  [the longest x1 54.9 us: on_device(): pl.pallas_call(open_step, out_shape=[shape((SHARD, LANES), F32)] * 2 + [w...]
    unnamed x32 -> x18, local copies, waits for them, and re-layouts: 7.63 us -> 2.04 us
    dot_general x1 -> x0, matrix products: 3.75 us -> none  [cycle_term(): jnp.einsum('ikac,kcjb->ijab', live.reshape(3, 6, 36, 36), panel, precisio...]
    ppermute x4, starting transfers between devices: 2.42 us -> 5.76 us  [swap_core(): return lax.ppermute(value, 'core', [(0, 1), (1, 0)])]
    select_n x1 -> x0, other arithmetic: 2.53 us -> none  [cycle_term(): jnp.where(row_place % 2 == 0, jnp.concatenate([ovov, partner], 0), jnp.co...]
    all_to_all x1, starting transfers between devices: 11.1 us -> 8.78 us  [on_device(): ladder = lax.all_to_all(packed, ('x', 'z', 'core'), 0, 0, tiled=True)]
    select_n x1 -> x0, local copies, waits for them, and re-layouts: 2.1 us -> none  [cycle_term(): jnp.where(row_place % 2 == 0, jnp.concatenate([ovov, partner], 0), jnp.co...]
    reshape x2 -> x0, local copies, waits for them, and re-layouts: 2.02 us -> none  [the longest x1 1.84 us: cycle_term(): live.reshape(3, 6, 36, 36)]
  transfers between devices with their start and end apart: 21 -> 20, of which waited for: 8 -> 11; matrix products, arithmetic and copies ran while one was open for 11% -> 0% of each run, Pallas kernels for 9% -> 47%
where the time goes in v3:
time: 136 us; the launch traced here: 135 us
  Pallas kernels  66.4 us (49%)
  starting transfers between devices  37.2 us (27%)
  waiting for transfers between devices  28.7 us (21%)
  local copies, waits for them, and re-layouts  2.8 us (2%)
    pallas_call x1, Pallas kernels, on_device(): pl.pallas_call(open_step, out_shape=[shape((SHARD, LANES), F32)] * 2 + [w...  54.9 us
    ppermute x14, waiting for transfers between devices, ring(): return lax.ppermute(value, AXES, pairs)  22.7 us
    ppermute x14, starting transfers between devices, ring(): return lax.ppermute(value, AXES, pairs)  20.9 us
    all_to_all x1, starting transfers between devices, on_device(): ladder = lax.all_to_all(packed, ('x', 'z', 'core'), 0, 0, tiled=True)  8.78 us
    ppermute x4, starting transfers between devices, swap_core(): return lax.ppermute(value, 'core', [(0, 1), (1, 0)])  5.76 us
    all_to_all x1, waiting for transfers between devices, on_device(): ladder = lax.all_to_all(packed, ('x', 'z', 'core'), 0, 0, tiled=True)  4.81 us
    pallas_call x1, Pallas kernels, on_device(): pl.pallas_call(cut_home, out_shape=[window] * 4, in_specs=[HBM, HBM, ANY]...  3.42 us
    pallas_call x1, Pallas kernels, on_device(): pl.pallas_call(local_step, out_shape=[shape((18, 1296), F32)] * 2, in_spe...  2.83 us
  transfers between devices with their start and end apart: 20, of which 11 were waited for; matrix products, arithmetic and copies ran while one was open for 0% of the time, Pallas kernels for 47%

profile of v3, /device:TPU:1, one launch (start us, length us, event | category | flops | bytes accessed | tf_op | source)
XLA Modules:
  0.0 135.3 jit_solution(14334641912502206454)
XLA Ops:
  0.0 1.4 %collective-permute-start.6 = (f32[81,1,10368]{2,1,0:T(1,128)}, f32[81,1,10368]{2,1,0:T(1,128)S(1)}, u32[]{:S(2)}, u32[]{:S(2)}) collective-permute-start(f32[81,1,10368]{2,1,0:T(1,128)} %bitcast.7), channel_id=1, source_target_pairs={{0,1},{1,0},{2,3},{3,2},{4,5},{5,4},{6,7},{7,6},{8,9},{9,8},{10,11... | collective-permute-start | bytes 10077704 | tf_op jit(solution)/shard_map/ppermute | solution.py:49
  1.4 1.7 %collective-permute-start.1 = (f32[108,1,216]{2,1,0:T(1,128)}, f32[108,1,216]{2,1,0:T(1,128)S(1)}, u32[]{:S(2)}, u32[]{:S(2)}) collective-permute-start(f32[108,1,216]{2,1,0:T(1,128)} %ovov.1), channel_id=1, source_target_pairs={{0,8},{8,0},{16,24},{24,16},{1,9},{9,1},{17,25},{25,17},{2,10},{10... | collective-permute-start | bytes 279944 | tf_op jit(solution)/shard_map/ppermute | solution.py:364
  3.1 54.9 %shard_map.73 = (f32[104,128]{1,0:T(8,128)}, f32[104,128]{1,0:T(8,128)}, f32[21,88,1,128]{3,2,1,0:T(1,128)}, f32[21,88,1,128]{3,2,1,0:T(1,128)}) custom-call(s32[8]{0:T(128)} %occ_ref.3, s32[8]{0:T(128)} %vir_ref.3, f32[3,6,1,1296]{3,2,1,0:T(1,128)} %amp_ref.3, f32[81,1,10368]{2,1,0:T(1,128)} %bitcast.8), custom_call_target="tpu_custom_call" | custom-call | tf_op jit(solution)/shard_map/pallas_call | solution.py:347
  60.4 3.0 %collective-permute-start.2 = (f32[192,128]{1,0:T(8,128)S(1)}, f32[192,128]{1,0:T(8,128)S(1)}, u32[]{:S(2)}, u32[]{:S(2)}) collective-permute-start(f32[192,128]{1,0:T(8,128)S(1)} %shard_map.74.near), channel_id=1, source_target_pairs={{0,4},{1,5},{2,6},{3,7},{4,0},{5,1},{6,2},{7,3},{8,12},{9,13},{10,... | collective-permute-start | bytes 294920 | tf_op jit(solution)/shard_map/ppermute | solution.py:45
  63.4 2.7 %collective-permute-done.2.far.refs_2_ = f32[192,128]{1,0:T(8,128)S(1)} collective-permute-done((f32[192,128]{1,0:T(8,128)S(1)}, f32[192,128]{1,0:T(8,128)S(1)}, u32[]{:S(2)}, u32[]{:S(2)}) %collective-permute-start.2) | collective-permute-done | bytes 98336 | tf_op jit(solution)/shard_map/ppermute | solution.py:45
  67.3 2.7 %collective-permute-start.13 = (f32[1848,128]{1,0:T(8,128)}, f32[1848,128]{1,0:T(8,128)S(1)}, u32[]{:S(2)}, u32[]{:S(2)}) collective-permute-start(f32[1848,128]{1,0:T(8,128)} %get-tuple-element.34), channel_id=1, source_target_pairs={{0,2},{1,7},{2,4},{3,1},{4,6},{5,3},{6,0},{7,5},{8,10},{9,15},{10,... | collective-permute-start | bytes 2838536 | tf_op jit(solution)/shard_map/ppermute | solution.py:45
  70.3 2.5 %collective-permute-start.4 = (f32[384,128]{1,0:T(8,128)S(1)}, f32[384,128]{1,0:T(8,128)S(1)}, u32[]{:S(2)}, u32[]{:S(2)}) collective-permute-start(f32[384,128]{1,0:T(8,128)S(1)} %shard_map.75.b0), channel_id=1, source_target_pairs={{0,96},{1,25},{2,98},{3,27},{4,100},{5,29},{6,102},{7,31},{8,104},... | collective-permute-start | bytes 589832 | tf_op jit(solution)/shard_map/ppermute | solution.py:45
  72.8 3.3 %collective-permute-done.3.b1 = f32[384,128]{1,0:T(8,128)S(1)} collective-permute-done((f32[384,128]{1,0:T(8,128)S(1)}, f32[384,128]{1,0:T(8,128)S(1)}, u32[]{:S(2)}, u32[]{:S(2)}) %collective-permute-start.3) | collective-permute-done | bytes 196640 | tf_op jit(solution)/shard_map/ppermute | solution.py:45
  76.1 2.1 %collective-permute-start.5 = (f32[384,128]{1,0:T(8,128)S(1)}, f32[384,128]{1,0:T(8,128)S(1)}, u32[]{:S(2)}, u32[]{:S(2)}) collective-permute-start(f32[384,128]{1,0:T(8,128)S(1)} %shard_map.75.b0), channel_id=1, source_target_pairs={{0,64},{1,17},{2,66},{3,19},{4,68},{5,21},{6,70},{7,23},{8,72},{9,... | collective-permute-start | bytes 589832 | tf_op jit(solution)/shard_map/ppermute | solution.py:45
  78.2 3.9 %collective-permute-done.5.b3 = f32[384,128]{1,0:T(8,128)S(1)} collective-permute-done((f32[384,128]{1,0:T(8,128)S(1)}, f32[384,128]{1,0:T(8,128)S(1)}, u32[]{:S(2)}, u32[]{:S(2)}) %collective-permute-start.5) | collective-permute-done | bytes 196640 | tf_op jit(solution)/shard_map/ppermute | solution.py:45
  83.5 1.6 %collective-permute-start.11 = (f32[768,128]{1,0:T(8,128)S(1)}, f32[768,128]{1,0:T(8,128)S(1)}, u32[]{:S(2)}, u32[]{:S(2)}) collective-permute-start(f32[768,128]{1,0:T(8,128)S(1)} %get-tuple-element.27.b0), channel_id=1, source_target_pairs={{0,24},{1,97},{2,26},{3,99},{4,28},{5,101},{6,30},{7,103},{8,0},{9... | collective-permute-start | bytes 1179656 | tf_op jit(solution)/shard_map/ppermute | solution.py:45
  86.5 3.0 %collective-permute-done.13.refs_0_ = f32[1848,128]{1,0:T(8,128)S(1)} collective-permute-done((f32[1848,128]{1,0:T(8,128)}, f32[1848,128]{1,0:T(8,128)S(1)}, u32[]{:S(2)}, u32[]{:S(2)}) %collective-permute-start.13) | collective-permute-done | bytes 946208 | tf_op jit(solution)/shard_map/ppermute | solution.py:45
  89.5 3.8 %collective-permute-done.14.refs_1_ = f32[1848,128]{1,0:T(8,128)S(1)} collective-permute-done((f32[1848,128]{1,0:T(8,128)S(1)}, f32[1848,128]{1,0:T(8,128)S(1)}, u32[]{:S(2)}, u32[]{:S(2)}) %collective-permute-start.14) | collective-permute-done | bytes 946208 | tf_op jit(solution)/shard_map/ppermute | solution.py:45
  94.1 1.8 %collective-permute-done.12.refs_4_.b3 = f32[768,128]{1,0:T(8,128)S(1)} collective-permute-done((f32[768,128]{1,0:T(8,128)S(1)}, f32[768,128]{1,0:T(8,128)S(1)}, u32[]{:S(2)}, u32[]{:S(2)}) %collective-permute-start.12) | collective-permute-done | bytes 393248 | tf_op jit(solution)/shard_map/ppermute | solution.py:45
  95.9 4.0 %collective-permute-start.15 = (f32[1848,128]{1,0:T(8,128)S(1)}, f32[1848,128]{1,0:T(8,128)S(1)}, u32[]{:S(2)}, u32[]{:S(2)}) collective-permute-start(f32[1848,128]{1,0:T(8,128)S(1)} %get-tuple-element.37.above), channel_id=1, source_target_pairs={{0,1},{1,0},{2,3},{3,2},{4,5},{5,4},{6,7},{7,6},{8,9},{9,8},{10,11... | collective-permute-start | bytes 2838536 | tf_op jit(solution)/shard_map/ppermute | solution.py:49
  99.9 2.7 %collective-permute-start.8 = (f32[768,128]{1,0:T(8,128)S(1)}, f32[768,128]{1,0:T(8,128)S(1)}, u32[]{:S(2)}, u32[]{:S(2)}) collective-permute-start(f32[768,128]{1,0:T(8,128)S(1)} %get-tuple-element.26.b0), channel_id=1, source_target_pairs={{0,24},{1,97},{2,26},{3,99},{4,28},{5,101},{6,30},{7,103},{8,0},{9... | collective-permute-start | bytes 1179656 | tf_op jit(solution)/shard_map/ppermute | solution.py:45
  103.2 3.4 %shard_map.77 = (f32[21,88,1,128]{3,2,1,0:T(1,128)S(1)}, f32[21,88,1,128]{3,2,1,0:T(1,128)S(1)}, f32[21,88,1,128]{3,2,1,0:T(1,128)S(1)}, f32[21,88,1,128]{3,2,1,0:T(1,128)S(1)}) custom-call(f32[81,1,10368]{2,1,0:T(1,128)S(1)} %bitcast.9, f32[81,1,10368]{2,1,0:T(1,128)S(1)} %collective-permute-done.6.witness.integrals_other, ...), custom_call_target="tpu_custom_call" | custom-call | bytes 7000000 | tf_op jit(solution)/shard_map/pallas_call | solution.py:398
  106.7 2.8 %shard_map.80 = (f32[144,256]{1,0:T(8,128)S(1)}, f32[144,256]{1,0:T(8,128)S(1)}, f32[144,256]{1,0:T(8,128)S(1)}) custom-call(f32[768,128]{1,0:T(8,128)S(1)} %get-tuple-element.27.b0, f32[768,128]{1,0:T(8,128)S(1)} %collective-permute-done.10.witness.refs_2_.b1, f32[768,128]{1,0:T(8,128)S(1)} %collective-permute-done.11.refs_3_.b2, ...), custom_call_target="tpu_custom_call" | custom-call | tf_op jit(solution)/shard_map/pallas_call | solution.py:431
  109.7 2.5 %collective-permute-start.18 = (f32[144,256]{1,0:T(8,128)S(1)}, f32[144,256]{1,0:T(8,128)S(1)}, u32[]{:S(2)}, u32[]{:S(2)}) collective-permute-start(f32[144,256]{1,0:T(8,128)S(1)} %get-tuple-element.40), channel_id=1, source_target_pairs={{0,2},{1,7},{2,4},{3,1},{4,6},{5,3},{6,0},{7,5},{8,10},{9,15},{10,... | collective-permute-start | bytes 442376 | tf_op jit(solution)/shard_map/ppermute | solution.py:45
  112.3 2.5 %collective-permute-done.17.back_a = f32[144,256]{1,0:T(8,128)S(1)} collective-permute-done((f32[144,256]{1,0:T(8,128)S(1)}, f32[144,256]{1,0:T(8,128)S(1)}, u32[]{:S(2)}, u32[]{:S(2)}) %collective-permute-start.17) | collective-permute-done | bytes 147488 | tf_op jit(solution)/shard_map/ppermute | solution.py:45
  115.5 2.2 %shard_map.81 = f32[32,8,128]{2,1,0:T(8,128)} custom-call(f32[768,128]{1,0:T(8,128)S(1)} %get-tuple-element.26.b0, f32[768,128]{1,0:T(8,128)S(1)} %collective-permute-done.7.b1, f32[768,128]{1,0:T(8,128)S(1)} %collective-permute-done.8.b2, f32[768,128]{1,0:T(8,128)S(1)} %collective-permute-done.9.b3, f32[1848,128]{1,0:T(8,128)S(1)} %bitcast.11, ...), custom_call_target="tpu_custom_call" | custom-call | tf_op jit(solution)/shard_map/pallas_call | solution.py:441
  117.8 8.8 %all-to-all-start = ((f32[32,8,128]{2,1,0:T(8,128)}), f32[32,8,128]{2,1,0:T(8,128)S(1)}, u32[]{:S(2)}, u32[]{:S(2)}) async-start(f32[32,8,128]{2,1,0:T(8,128)} %shard_map.81), calls=%async_computation | async-start | bytes 262144 | tf_op jit(solution)/shard_map/all_to_all | solution.py:449
  126.6 2.8 %shard_map.82 = (f32[18,1296]{1,0:T(8,128)S(1)}, f32[18,1296]{1,0:T(8,128)S(1)}) custom-call(s32[8]{0:T(128)S(1)} %copy-done.4, s32[8]{0:T(128)S(1)} %copy-done.5, f32[8,6]{1,0:T(8,128)S(1)} %copy-done.7, f32[8,36]{1,0:T(8,128)S(1)} %copy-done.8, f32[3,6,1,1296]{3,2,1,0:T(1,128)S(1)} %copy-done.2, f32[108,1,216]{2,1,0:T(1,128)S(1)} %copy-done.6, ...), custom_call_target="tpu_custom_call" | custom-call | flops 100000000 | bytes 1000000 | tf_op jit(solution)/shard_map/pallas_call | solution.py:409
  129.5 4.8 %all-to-all-done.sums = f32[32,8,128]{2,1,0:T(8,128)S(1)} async-done(((f32[32,8,128]{2,1,0:T(8,128)}), f32[32,8,128]{2,1,0:T(8,128)S(1)}, u32[]{:S(2)}, u32[]{:S(2)}) %all-to-all-start) | async-done | bytes 131104 | tf_op jit(solution)/shard_map/all_to_all | solution.py:449
  (46 shorter events, 10.0 us)
Async XLA Ops:
  0.0 82.2 %collective-permute-start.6 = (f32[81,1,10368]{2,1,0:T(1,128)}, f32[81,1,10368]{2,1,0:T(1,128)S(1)}, u32[]{:S(2)}, u32[]{:S(2)}) collective-permute-start(f32[81,1,10368]{2,1,0:T(1,128)} %bitcast.7), channel_id=1, source_target_pairs={{0,1},{1,0},{2,3},{3,2},{4,5},{5,4},{6,7},{7,6},{8,9},{9,8},{10,11... | collective-permute-start | bytes 10077704 | tf_op jit(solution)/shard_map/ppermute | solution.py:49
  1.4 58.2 %collective-permute-start.1 = (f32[108,1,216]{2,1,0:T(1,128)}, f32[108,1,216]{2,1,0:T(1,128)S(1)}, u32[]{:S(2)}, u32[]{:S(2)}) collective-permute-start(f32[108,1,216]{2,1,0:T(1,128)} %ovov.1), channel_id=1, source_target_pairs={{0,8},{8,0},{16,24},{24,16},{1,9},{9,1},{17,25},{25,17},{2,10},{10... | collective-permute-start | bytes 279944 | tf_op jit(solution)/shard_map/ppermute | solution.py:364
  58.0 1.5 %collective-permute-start = (f32[104,128]{1,0:T(8,128)}, f32[104,128]{1,0:T(8,128)S(1)}, u32[]{:S(2)}, u32[]{:S(2)}) collective-permute-start(f32[104,128]{1,0:T(8,128)} %get-tuple-element.25), channel_id=1, source_target_pairs={{0,1},{1,0},{2,3},{3,2},{4,5},{5,4},{6,7},{7,6},{8,9},{9,8},{10,11... | collective-permute-start | bytes 159752 | tf_op jit(solution)/shard_map/ppermute | solution.py:49
  60.4 5.7 %collective-permute-start.2 = (f32[192,128]{1,0:T(8,128)S(1)}, f32[192,128]{1,0:T(8,128)S(1)}, u32[]{:S(2)}, u32[]{:S(2)}) collective-permute-start(f32[192,128]{1,0:T(8,128)S(1)} %shard_map.74.near), channel_id=1, source_target_pairs={{0,4},{1,5},{2,6},{3,7},{4,0},{5,1},{6,2},{7,3},{8,12},{9,13},{10,... | collective-permute-start | bytes 294920 | tf_op jit(solution)/shard_map/ppermute | solution.py:45
  67.3 22.2 %collective-permute-start.13 = (f32[1848,128]{1,0:T(8,128)}, f32[1848,128]{1,0:T(8,128)S(1)}, u32[]{:S(2)}, u32[]{:S(2)}) collective-permute-start(f32[1848,128]{1,0:T(8,128)} %get-tuple-element.34), channel_id=1, source_target_pairs={{0,2},{1,7},{2,4},{3,1},{4,6},{5,3},{6,0},{7,5},{8,10},{9,15},{10,... | collective-permute-start | bytes 2838536 | tf_op jit(solution)/shard_map/ppermute | solution.py:45
  70.0 23.2 %collective-permute-start.14 = (f32[1848,128]{1,0:T(8,128)S(1)}, f32[1848,128]{1,0:T(8,128)S(1)}, u32[]{:S(2)}, u32[]{:S(2)}) collective-permute-start(f32[1848,128]{1,0:T(8,128)S(1)} %get-tuple-element.35), channel_id=1, source_target_pairs={{0,6},{1,3},{2,0},{3,5},{4,2},{5,7},{6,4},{7,1},{8,14},{9,11},{10,... | collective-permute-start | bytes 2838536 | tf_op jit(solution)/shard_map/ppermute | solution.py:45
  70.0 33.2 %copy-start = (f32[1,81,10368]{2,0,1:T(1,128)S(1)}, f32[1,81,10368]{2,0,1:T(1,128)}, u32[]{:S(2)}) copy-start(f32[1,81,10368]{2,0,1:T(1,128)} %param.8) | copy-start | bytes 10077700
  70.0 6.1 %collective-permute-start.3 = (f32[384,128]{1,0:T(8,128)S(1)}, f32[384,128]{1,0:T(8,128)S(1)}, u32[]{:S(2)}, u32[]{:S(2)}) collective-permute-start(f32[384,128]{1,0:T(8,128)S(1)} %shard_map.75.b0), channel_id=1, source_target_pairs={{0,32},{1,9},{2,34},{3,11},{4,36},{5,13},{6,38},{7,15},{8,40},{9,1... | collective-permute-start | bytes 589832 | tf_op jit(solution)/shard_map/ppermute | solution.py:45
  70.3 8.0 %collective-permute-start.4 = (f32[384,128]{1,0:T(8,128)S(1)}, f32[384,128]{1,0:T(8,128)S(1)}, u32[]{:S(2)}, u32[]{:S(2)}) collective-permute-start(f32[384,128]{1,0:T(8,128)S(1)} %shard_map.75.b0), channel_id=1, source_target_pairs={{0,96},{1,25},{2,98},{3,27},{4,100},{5,29},{6,102},{7,31},{8,104},... | collective-permute-start | bytes 589832 | tf_op jit(solution)/shard_map/ppermute | solution.py:45
  76.1 6.0 %collective-permute-start.5 = (f32[384,128]{1,0:T(8,128)S(1)}, f32[384,128]{1,0:T(8,128)S(1)}, u32[]{:S(2)}, u32[]{:S(2)}) collective-permute-start(f32[384,128]{1,0:T(8,128)S(1)} %shard_map.75.b0), channel_id=1, source_target_pairs={{0,64},{1,17},{2,66},{3,19},{4,68},{5,21},{6,70},{7,23},{8,72},{9,... | collective-permute-start | bytes 589832 | tf_op jit(solution)/shard_map/ppermute | solution.py:45
  82.2 11.0 %collective-permute-start.10 = (f32[768,128]{1,0:T(8,128)S(1)}, f32[768,128]{1,0:T(8,128)S(1)}, u32[]{:S(2)}, u32[]{:S(2)}) collective-permute-start(f32[768,128]{1,0:T(8,128)S(1)} %get-tuple-element.27.b0), channel_id=1, source_target_pairs={{0,8},{1,33},{2,10},{3,35},{4,12},{5,37},{6,14},{7,39},{8,16},{9,4... | collective-permute-start | bytes 1179656 | tf_op jit(solution)/shard_map/ppermute | solution.py:45
  83.5 10.6 %collective-permute-start.11 = (f32[768,128]{1,0:T(8,128)S(1)}, f32[768,128]{1,0:T(8,128)S(1)}, u32[]{:S(2)}, u32[]{:S(2)}) collective-permute-start(f32[768,128]{1,0:T(8,128)S(1)} %get-tuple-element.27.b0), channel_id=1, source_target_pairs={{0,24},{1,97},{2,26},{3,99},{4,28},{5,101},{6,30},{7,103},{8,0},{9... | collective-permute-start | bytes 1179656 | tf_op jit(solution)/shard_map/ppermute | solution.py:45
  85.2 10.8 %collective-permute-start.12 = (f32[768,128]{1,0:T(8,128)S(1)}, f32[768,128]{1,0:T(8,128)S(1)}, u32[]{:S(2)}, u32[]{:S(2)}) collective-permute-start(f32[768,128]{1,0:T(8,128)S(1)} %get-tuple-element.27.b0), channel_id=1, source_target_pairs={{0,16},{1,65},{2,18},{3,67},{4,20},{5,69},{6,22},{7,71},{8,24},{9,... | collective-permute-start | bytes 1179656 | tf_op jit(solution)/shard_map/ppermute | solution.py:45
  95.9 10.7 %collective-permute-start.15 = (f32[1848,128]{1,0:T(8,128)S(1)}, f32[1848,128]{1,0:T(8,128)S(1)}, u32[]{:S(2)}, u32[]{:S(2)}) collective-permute-start(f32[1848,128]{1,0:T(8,128)S(1)} %get-tuple-element.37.above), channel_id=1, source_target_pairs={{0,1},{1,0},{2,3},{3,2},{4,5},{5,4},{6,7},{7,6},{8,9},{9,8},{10,11... | collective-permute-start | bytes 2838536 | tf_op jit(solution)/shard_map/ppermute | solution.py:49
  99.9 6.8 %collective-permute-start.16 = (f32[1848,128]{1,0:T(8,128)S(1)}, f32[1848,128]{1,0:T(8,128)S(1)}, u32[]{:S(2)}, u32[]{:S(2)}) collective-permute-start(f32[1848,128]{1,0:T(8,128)S(1)} %get-tuple-element.36.below), channel_id=1, source_target_pairs={{0,1},{1,0},{2,3},{3,2},{4,5},{5,4},{6,7},{7,6},{8,9},{9,8},{10,11... | collective-permute-start | bytes 2838536 | tf_op jit(solution)/shard_map/ppermute | solution.py:49
  99.9 12.3 %collective-permute-start.7 = (f32[768,128]{1,0:T(8,128)S(1)}, f32[768,128]{1,0:T(8,128)S(1)}, u32[]{:S(2)}, u32[]{:S(2)}) collective-permute-start(f32[768,128]{1,0:T(8,128)S(1)} %get-tuple-element.26.b0), channel_id=1, source_target_pairs={{0,8},{1,33},{2,10},{3,35},{4,12},{5,37},{6,14},{7,39},{8,16},{9,4... | collective-permute-start | bytes 1179656 | tf_op jit(solution)/shard_map/ppermute | solution.py:45
  99.9 12.3 %collective-permute-start.8 = (f32[768,128]{1,0:T(8,128)S(1)}, f32[768,128]{1,0:T(8,128)S(1)}, u32[]{:S(2)}, u32[]{:S(2)}) collective-permute-start(f32[768,128]{1,0:T(8,128)S(1)} %get-tuple-element.26.b0), channel_id=1, source_target_pairs={{0,24},{1,97},{2,26},{3,99},{4,28},{5,101},{6,30},{7,103},{8,0},{9... | collective-permute-start | bytes 1179656 | tf_op jit(solution)/shard_map/ppermute | solution.py:45
  102.6 9.7 %collective-permute-start.9 = (f32[768,128]{1,0:T(8,128)S(1)}, f32[768,128]{1,0:T(8,128)S(1)}, u32[]{:S(2)}, u32[]{:S(2)}) collective-permute-start(f32[768,128]{1,0:T(8,128)S(1)} %get-tuple-element.26.b0), channel_id=1, source_target_pairs={{0,16},{1,65},{2,18},{3,67},{4,20},{5,69},{6,22},{7,71},{8,24},{9,... | collective-permute-start | bytes 1179656 | tf_op jit(solution)/shard_map/ppermute | solution.py:45
  109.4 17.2 %copy-start.2 = (f32[3,6,1,1296]{3,2,1,0:T(1,128)S(1)}, f32[3,6,1,1296]{3,2,1,0:T(1,128)}, u32[]{:S(2)}) copy-start(f32[3,6,1,1296]{3,2,1,0:T(1,128)} %amp_ref.3) | copy-start | bytes 279940
  109.4 17.2 %copy-start.4 = (s32[8]{0:T(128)S(1)}, s32[8]{0:T(128)}, u32[]{:S(2)}) copy-start(s32[8]{0:T(128)} %occ_ref.3) | copy-start | bytes 100
  109.4 17.2 %copy-start.5 = (s32[8]{0:T(128)S(1)}, s32[8]{0:T(128)}, u32[]{:S(2)}) copy-start(s32[8]{0:T(128)} %vir_ref.3) | copy-start | bytes 100
  109.5 5.3 %collective-permute-start.17 = (f32[144,256]{1,0:T(8,128)S(1)}, f32[144,256]{1,0:T(8,128)S(1)}, u32[]{:S(2)}, u32[]{:S(2)}) collective-permute-start(f32[144,256]{1,0:T(8,128)S(1)} %get-tuple-element.39), channel_id=1, source_target_pairs={{0,6},{1,3},{2,0},{3,5},{4,2},{5,7},{6,4},{7,1},{8,14},{9,11},{10,... | collective-permute-start | bytes 442376 | tf_op jit(solution)/shard_map/ppermute | solution.py:45
  109.7 5.8 %collective-permute-start.18 = (f32[144,256]{1,0:T(8,128)S(1)}, f32[144,256]{1,0:T(8,128)S(1)}, u32[]{:S(2)}, u32[]{:S(2)}) collective-permute-start(f32[144,256]{1,0:T(8,128)S(1)} %get-tuple-element.40), channel_id=1, source_target_pairs={{0,2},{1,7},{2,4},{3,1},{4,6},{5,3},{6,0},{7,5},{8,10},{9,15},{10,... | collective-permute-start | bytes 442376 | tf_op jit(solution)/shard_map/ppermute | solution.py:45
  117.8 16.5 %all-to-all-start = ((f32[32,8,128]{2,1,0:T(8,128)}), f32[32,8,128]{2,1,0:T(8,128)S(1)}, u32[]{:S(2)}, u32[]{:S(2)}) async-start(f32[32,8,128]{2,1,0:T(8,128)} %shard_map.81), calls=%async_computation | async-start | bytes 262144 | tf_op jit(solution)/shard_map/all_to_all | solution.py:449
  (5 other events, 53.5 us)

commit v4 on v3

--- a/solution.py
+++ b/solution.py
@@ -59,37 +59,27 @@
     return a, lane - 36 * a
 
 
-def window_copies(integrals, ref, sems, base):
+def window_copies(integrals, ref, first, sems, base):
     copies = []
     for t in range(SPAN):
         start = pl.multiple_of((base + t) * LANES, LANES)
         copies.append(
-            pltpu.make_async_copy(integrals.at[:, :, pl.ds(start, LANES)], ref.at[t, 0:81], sems.at[t])
+            pltpu.make_async_copy(integrals.at[:, :, pl.ds(start, LANES)], ref.at[first + t, 0:81], sems.at[t])
         )
     return copies
 
 
-def cut_home(integrals, integrals_other, witness, near, near_other, far, far_other, sems):
-    y = lax.axis_index("y")
-    copies = []
-    plan = ((integrals, near, 0), (integrals_other, near_other, 0), (integrals, far, 2), (integrals_other, far_other, 2))
-    for at, (source, ref, step) in enumerate(plan):
-        copies += window_copies(source, ref, sems.at[at], ((y + step) & 3) * 20)
-    for copy in copies:
-        copy.start()
-    for copy in copies:
-        copy.wait()
-
-
-def open_step(occ_ref, vir_ref, amp_ref, integrals, keep, send, first_v, second_v,
+def open_step(occ_ref, vir_ref, amp_ref, integrals, keep, send, first_v, second_v, home,
               wide, amp, occ, vir, sems, cut_sems):
     x, z, y, core = places()
     copies = [
         pltpu.make_async_copy(source, target, sems.at[at])
         for at, (source, target) in enumerate(((occ_ref, occ), (vir_ref, vir), (amp_ref, amp)))
     ]
-    cuts = window_copies(integrals, first_v, cut_sems.at[0], ((y + 1 + 2 * core) & 3) * 20)
-    cuts += window_copies(integrals, second_v, cut_sems.at[1], ((y + 3 - 2 * core) & 3) * 20)
+    cuts = window_copies(integrals, first_v, 0, cut_sems.at[0], ((y + 1 + 2 * core) & 3) * 20)
+    cuts += window_copies(integrals, second_v, 0, cut_sems.at[1], ((y + 3 - 2 * core) & 3) * 20)
+    cuts += window_copies(integrals, home, 0, cut_sems.at[2], y * 20)
+    cuts += window_copies(integrals, home, SPAN, cut_sems.at[3], ((y + 2) & 3) * 20)
     for copy in copies + cuts:
         copy.start()
     wide[...] = jnp.zeros_like(wide)
@@ -154,12 +144,12 @@
         merge_irreps(got, keep, out, 0)
 
 
-def join_pairs(near, far, out):
+def join_pairs(near, far, witness, out):
     out[0:PAIR, :] = near[...]
     out[PAIR:QUAD, :] = far[...]
 
 
-def gather_four(b0, b1, b2, b3, witness, near, far):
+def gather_four(b0, b1, b2, b3, near, far):
     for at, block in enumerate((b0, b1, b2, b3)):
         near[at * PAIR : (at + 1) * PAIR, :] = block[0:PAIR, :]
         far[at * PAIR : (at + 1) * PAIR, :] = block[PAIR:QUAD, :]
@@ -200,8 +190,10 @@
     return high, (value - high.astype(F32)).astype(BF16)
 
 
-def tiles_side(ref):
-    return jnp.concatenate([ref[t * PSLOT : (t + 1) * PSLOT, :] for t in range(SPAN)], axis=1)
+def tiles_side(ref, first):
+    return jnp.concatenate(
+        [ref[(first + t) * PSLOT : (first + t + 1) * PSLOT, :] for t in range(SPAN)], axis=1
+    )
 
 
 def last_by_last(p, q):
@@ -211,7 +203,7 @@
 def multiply_near(b0, b1, b2, b3, home, home_other, below, below_other, above, above_other,
                   here_sum, below_sum, above_sum, extra, turned):
     high, low = left_side((b0, b1, b2, b3), extra)
-    sides = [tiles_side(ref) for ref in (home, home_other, below, below_other, above, above_other)]
+    sides = [tiles_side(ref, 0) for ref in (home, home_other, below, below_other, above, above_other)]
     v_high, v_low = split(jnp.concatenate(sides, axis=0))
     total = last_by_last(v_high, high) + (last_by_last(v_low, high) + last_by_last(v_high, low))
     turned[...] = jnp.zeros_like(turned)
@@ -229,7 +221,7 @@
     row = lax.broadcasted_iota(jnp.int32, (8, LANES), 0)
     lane = lax.broadcasted_iota(jnp.int32, (8, LANES), 1)
     pad = jnp.zeros((LANES - PSLOT, DEPTH), BF16)
-    sides = [split(tiles_side(ref)) for ref in (home, home_other)]
+    sides = [split(tiles_side(ref, SPAN)) for ref in (home, home_other)]
     v_high = jnp.concatenate([sides[0][0], pad, sides[1][0], pad], axis=0)
     v_low = jnp.concatenate([sides[0][1], pad, sides[1][1], pad], axis=0)
     total = partial + (
@@ -335,7 +327,9 @@
         if start + 81 > LANES:
             after = slice((tile + 1) * LANES, (tile + 2) * LANES)
             wide[:, after] = jnp.where(lane < start + 81 - LANES, turned, wide[:, after])
-    out[...] = (wide[0:18, 0:1296] + cycle[...]) * scale[...]
+    total = (wide[0:18, 0:1296] + cycle[...]) * scale[...]
+    for r in range(18):
+        out[r // 6, r % 6] = total[r : r + 1, :]
 
 
 def on_device(amplitudes, vvvv, ovov, eps_occ, eps_vir, occ_count, vir_count):
@@ -344,23 +338,25 @@
     integrals = vvvv.reshape(81, 1, 10368)
     window = shape((SPAN, PSLOT, 1, LANES), F32)
     flat = lambda value: value.reshape(PROWS, LANES)
-    keep, send, first_v, second_v = pl.pallas_call(
+    keep, send, first_v, second_v, home = pl.pallas_call(
         open_step,
-        out_shape=[shape((SHARD, LANES), F32)] * 2 + [window] * 2,
+        out_shape=[shape((SHARD, LANES), F32)] * 2 + [window] * 2
+        + [shape((2 * SPAN, PSLOT, 1, LANES), F32)],
         in_specs=[HBM] * 4,
-        out_specs=[VMEM] * 2 + [ANY] * 2,
+        out_specs=[VMEM] * 2 + [ANY] * 3,
         scratch_shapes=[
             pltpu.VMEM((24, WINDOW), F32),
             pltpu.VMEM((3, 6, 1, 1296), F32),
             pltpu.SMEM((8,), jnp.int32),
             pltpu.SMEM((8,), jnp.int32),
             pltpu.SemaphoreType.DMA((3,)),
-            pltpu.SemaphoreType.DMA((2, SPAN)),
+            pltpu.SemaphoreType.DMA((4, SPAN)),
         ],
         compiler_params=HUGE,
     )(occ_count, vir_count, amplitudes, integrals)
     got = swap_core(send)
-    integrals_other = swap_core(integrals)
+    home = home.reshape(2 * PROWS, LANES)
+    home_other = swap_core(home)
     partner = lax.ppermute(ovov, "z", [(0, 1), (1, 0), (2, 3), (3, 2)])
     pair = pl.pallas_call(
         merge_pair,
@@ -373,10 +369,10 @@
     quad = pl.pallas_call(
         join_pairs,
         out_shape=shape((QUAD, LANES), F32),
-        in_specs=[VMEM] * 2,
+        in_specs=[VMEM] * 2 + [ANY],
         out_specs=VMEM,
         compiler_params=SMALL,
-    )(pair, far_pair)
+    )(pair, far_pair, home_other)
     first_v, second_v = hold(
         flat(first_v), flat(second_v), far_pair
     )
@@ -386,25 +382,15 @@
     near, far = pl.pallas_call(
         gather_four,
         out_shape=[shape((4 * PAIR, LANES), F32)] * 2,
-        in_specs=[VMEM] * 4 + [ANY],
+        in_specs=[VMEM] * 4,
         out_specs=[VMEM] * 2,
         compiler_params=SMALL,
-    )(quad, *[ring(quad, "xz", step) for step in SHIFTS], integrals_other)
+    )(quad, *[ring(quad, "xz", step) for step in SHIFTS])
     near_blocks = [near] + [ring(near, "zx", step) for step in SHIFTS]
     far_blocks = [far] + [ring(far, "zx", step) for step in SHIFTS]
 
     moved_a, moved_b = hold(moved_a, moved_b, *near_blocks[1:])
     swapped_a, swapped_b = swap_core(moved_a), swap_core(moved_b)
-    homes = pl.pallas_call(
-        cut_home,
-        out_shape=[window] * 4,
-        in_specs=[HBM, HBM, ANY],
-        out_specs=[VMEM] * 4,
-        scratch_shapes=[pltpu.SemaphoreType.DMA((4, SPAN))],
-        compiler_params=SMALL,
-        cost_estimate=pl.CostEstimate(flops=0, bytes_accessed=7000000, transcendentals=0),
-    )(integrals, integrals_other, near_blocks[1])
-    near_v, near_v_other, far_v, far_v_other = (flat(value) for value in homes)
 
     scale, cycle = pl.pallas_call(
         local_step,
@@ -435,7 +421,7 @@
         out_specs=[VMEM] * 3,
         scratch_shapes=[pltpu.VMEM((16, DEPTH), F32), pltpu.VMEM((LANES, 2 * LANES), F32)],
         compiler_params=LARGE,
-    )(*near_blocks, near_v, near_v_other, moved_a, swapped_b, moved_b, swapped_a)
+    )(*near_blocks, home, home_other, moved_a, swapped_b, moved_b, swapped_a)
     back_a = ring(below_sum, "yy", (-1, 1))
     back_b = ring(above_sum, "yy", (1, -1))
     packed = pl.pallas_call(
@@ -445,17 +431,16 @@
         out_specs=VMEM,
         scratch_shapes=[pltpu.VMEM((16, DEPTH), F32)],
         compiler_params=LARGE,
-    )(*far_blocks, far_v, far_v_other, here_sum, back_a, back_b)
+    )(*far_blocks, home, home_other, here_sum, back_a, back_b)
     ladder = lax.all_to_all(packed, ("x", "z", "core"), 0, 0, tiled=True)
-    result = pl.pallas_call(
+    return pl.pallas_call(
         finish,
-        out_shape=shape((18, 1296), F32),
+        out_shape=shape((3, 6, 1, 1296), F32),
         in_specs=[VMEM] * 3,
         out_specs=VMEM,
         scratch_shapes=[pltpu.VMEM((24, WINDOW), F32)],
         compiler_params=SMALL,
     )(ladder, scale, cycle)
-    return result.reshape(3, 6, 1, 1296)
 
 
 def solution(mesh):

time: 136 us -> 184 us (1.35)
  Pallas kernels: 66.4 us -> 117 us
  local copies, waits for them, and re-layouts: 2.8 us -> 0.84 us
    pallas_call x1, Pallas kernels: 54.9 us -> 108 us  [on_device(): pl.pallas_call(open_step, out_shape=[shape((SHARD, LANES), F32)] * 2 + [w...]
    pallas_call x2 -> x1, Pallas kernels: 3.66 us -> 0.88 us  [on_device(): pl.pallas_call(finish, out_shape=shape((3, 6, 1, 1296), F32), in_specs=[V...]
    ppermute x14, waiting for transfers between devices: 22.7 us -> 20.3 us  [ring(): return lax.ppermute(value, AXES, pairs)]
  transfers between devices with their start and end apart: 20 -> 20, of which waited for: 11 -> 13; matrix products, arithmetic and copies ran while one was open for 0% -> 0% of each run, Pallas kernels for 47% -> 3%
where the time goes in v4:
time: 184 us; the launch traced here: 183 us
  Pallas kernels  117 us (64%)
  starting transfers between devices  37.2 us (20%)
  waiting for transfers between devices  28.4 us (15%)
    pallas_call x1, Pallas kernels, on_device(): pl.pallas_call(open_step, out_shape=[shape((SHARD, LANES), F32)] * 2 + [w...  108 us
    ppermute x14, starting transfers between devices, ring(): return lax.ppermute(value, AXES, pairs)  20.8 us
    ppermute x14, waiting for transfers between devices, ring(): return lax.ppermute(value, AXES, pairs)  20.3 us
    all_to_all x1, starting transfers between devices, on_device(): ladder = lax.all_to_all(packed, ('x', 'z', 'core'), 0, 0, tiled=True)  8.47 us
    ppermute x4, starting transfers between devices, swap_core(): return lax.ppermute(value, 'core', [(0, 1), (1, 0)])  6.18 us
    all_to_all x1, waiting for transfers between devices, on_device(): ladder = lax.all_to_all(packed, ('x', 'z', 'core'), 0, 0, tiled=True)  4.82 us
  transfers between devices with their start and end apart: 20, of which 13 were waited for; matrix products, arithmetic and copies ran while one was open for 0% of the time, Pallas kernels for 3%

profile of v4, /device:TPU:1, one launch (start us, length us, event | category | flops | bytes accessed | tf_op | source)
XLA Modules:
  0.0 183.3 jit_solution(7700137749201649130)
XLA Ops:
  0.0 108.0 %shard_map.73 = (f32[104,128]{1,0:T(8,128)}, f32[104,128]{1,0:T(8,128)}, f32[21,88,1,128]{3,2,1,0:T(1,128)}, f32[21,88,1,128]{3,2,1,0:T(1,128)}, f32[42,88,1,128]{3,2,1,0:T(1,128)}) custom-call(s32[8]{0:T(128)} %occ_ref.3, s32[8]{0:T(128)} %vir_ref.3, f32[3,6,1,1296]{3,2,1,0:T(1,128)} %amp_ref.3, f32[81,1,10368]{2,1,0:T(1,128)} %bitcast.7), custom_call_target="tpu_custom_call" | custom-call | tf_op jit(solution)/shard_map/pallas_call | solution.py:341
  108.0 1.5 collective-permute-start.3
  109.6 1.7 collective-permute-start.1
  111.7 1.7 collective-permute-done.got
  115.4 3.0 %collective-permute-start.2 = (f32[192,128]{1,0:T(8,128)S(1)}, f32[192,128]{1,0:T(8,128)S(1)}, u32[]{:S(2)}, u32[]{:S(2)}) collective-permute-start(f32[192,128]{1,0:T(8,128)S(1)} %shard_map.74.near), channel_id=1, source_target_pairs={{0,4},{1,5},{2,6},{3,7},{4,0},{5,1},{6,2},{7,3},{8,12},{9,13},{10,... | collective-permute-start | bytes 294920 | tf_op jit(solution)/shard_map/ppermute | solution.py:45
  118.4 2.1 %collective-permute-done.2.far.refs_2_ = f32[192,128]{1,0:T(8,128)S(1)} collective-permute-done((f32[192,128]{1,0:T(8,128)S(1)}, f32[192,128]{1,0:T(8,128)S(1)}, u32[]{:S(2)}, u32[]{:S(2)}) %collective-permute-start.2) | collective-permute-done | bytes 98336 | tf_op jit(solution)/shard_map/ppermute | solution.py:45
  120.5 2.7 %collective-permute-start.13 = (f32[1848,128]{1,0:T(8,128)}, f32[1848,128]{1,0:T(8,128)S(1)}, u32[]{:S(2)}, u32[]{:S(2)}) collective-permute-start(f32[1848,128]{1,0:T(8,128)} %get-tuple-element.28), channel_id=1, source_target_pairs={{0,2},{1,7},{2,4},{3,1},{4,6},{5,3},{6,0},{7,5},{8,10},{9,15},{10,... | collective-permute-start | bytes 2838536 | tf_op jit(solution)/shard_map/ppermute | solution.py:45
  123.2 1.4 collective-permute-start.4
  124.6 2.2 %collective-permute-start.5 = (f32[384,128]{1,0:T(8,128)S(1)}, f32[384,128]{1,0:T(8,128)S(1)}, u32[]{:S(2)}, u32[]{:S(2)}) collective-permute-start(f32[384,128]{1,0:T(8,128)S(1)} %shard_map.75.b0), channel_id=1, source_target_pairs={{0,96},{1,25},{2,98},{3,27},{4,100},{5,29},{6,102},{7,31},{8,104},... | collective-permute-start | bytes 589832 | tf_op jit(solution)/shard_map/ppermute | solution.py:45
  128.0 2.0 %collective-permute-done.4.b1 = f32[384,128]{1,0:T(8,128)S(1)} collective-permute-done((f32[384,128]{1,0:T(8,128)S(1)}, f32[384,128]{1,0:T(8,128)S(1)}, u32[]{:S(2)}, u32[]{:S(2)}) %collective-permute-start.4) | collective-permute-done | bytes 196640 | tf_op jit(solution)/shard_map/ppermute | solution.py:45
  130.1 1.4 collective-permute-done.5.b2
  131.5 1.5 collective-permute-done.6.b3
  134.4 1.6 collective-permute-start.11
  137.4 4.3 %collective-permute-done.13.refs_0_ = f32[1848,128]{1,0:T(8,128)S(1)} collective-permute-done((f32[1848,128]{1,0:T(8,128)}, f32[1848,128]{1,0:T(8,128)S(1)}, u32[]{:S(2)}, u32[]{:S(2)}) %collective-permute-start.13) | collective-permute-done | bytes 946208 | tf_op jit(solution)/shard_map/ppermute | solution.py:45
  141.7 5.5 %collective-permute-done.14.refs_1_ = f32[1848,128]{1,0:T(8,128)S(1)} collective-permute-done((f32[1848,128]{1,0:T(8,128)}, f32[1848,128]{1,0:T(8,128)S(1)}, u32[]{:S(2)}, u32[]{:S(2)}) %collective-permute-start.14) | collective-permute-done | bytes 946208 | tf_op jit(solution)/shard_map/ppermute | solution.py:45
  147.2 4.3 %collective-permute-start.15 = (f32[1848,128]{1,0:T(8,128)S(1)}, f32[1848,128]{1,0:T(8,128)S(1)}, u32[]{:S(2)}, u32[]{:S(2)}) collective-permute-start(f32[1848,128]{1,0:T(8,128)S(1)} %get-tuple-element.31.above), channel_id=1, source_target_pairs={{0,1},{1,0},{2,3},{3,2},{4,5},{5,4},{6,7},{7,6},{8,9},{9,8},{10,11... | collective-permute-start | bytes 2838536 | tf_op jit(solution)/shard_map/ppermute | solution.py:49
  152.2 2.0 %collective-permute-start.8 = (f32[768,128]{1,0:T(8,128)S(1)}, f32[768,128]{1,0:T(8,128)S(1)}, u32[]{:S(2)}, u32[]{:S(2)}) collective-permute-start(f32[768,128]{1,0:T(8,128)S(1)} %get-tuple-element.24.b0), channel_id=1, source_target_pairs={{0,24},{1,97},{2,26},{3,99},{4,28},{5,101},{6,30},{7,103},{8,0},{9... | collective-permute-start | bytes 1179656 | tf_op jit(solution)/shard_map/ppermute | solution.py:45
  155.0 2.7 %shard_map.79 = (f32[144,256]{1,0:T(8,128)S(1)}, f32[144,256]{1,0:T(8,128)S(1)}, f32[144,256]{1,0:T(8,128)S(1)}) custom-call(f32[768,128]{1,0:T(8,128)S(1)} %get-tuple-element.25.b0, f32[768,128]{1,0:T(8,128)S(1)} %collective-permute-done.10.refs_2_.b1, f32[768,128]{1,0:T(8,128)S(1)} %collective-permute-done.11.refs_3_.b2, ...), custom_call_target="tpu_custom_call" | custom-call | tf_op jit(solution)/shard_map/pallas_call | solution.py:417
  158.0 2.5 %collective-permute-start.18 = (f32[144,256]{1,0:T(8,128)S(1)}, f32[144,256]{1,0:T(8,128)S(1)}, u32[]{:S(2)}, u32[]{:S(2)}) collective-permute-start(f32[144,256]{1,0:T(8,128)S(1)} %get-tuple-element.34), channel_id=1, source_target_pairs={{0,2},{1,7},{2,4},{3,1},{4,6},{5,3},{6,0},{7,5},{8,10},{9,15},{10,... | collective-permute-start | bytes 442376 | tf_op jit(solution)/shard_map/ppermute | solution.py:45
  160.5 2.6 %collective-permute-done.8.b2 = f32[768,128]{1,0:T(8,128)S(1)} collective-permute-done((f32[768,128]{1,0:T(8,128)S(1)}, f32[768,128]{1,0:T(8,128)S(1)}, u32[]{:S(2)}, u32[]{:S(2)}) %collective-permute-start.8) | collective-permute-done | bytes 393248 | tf_op jit(solution)/shard_map/ppermute | solution.py:45
  164.0 2.2 %shard_map.80 = f32[32,8,128]{2,1,0:T(8,128)} custom-call(f32[768,128]{1,0:T(8,128)S(1)} %get-tuple-element.24.b0, f32[768,128]{1,0:T(8,128)S(1)} %collective-permute-done.7.b1, f32[768,128]{1,0:T(8,128)S(1)} %collective-permute-done.8.b2, f32[768,128]{1,0:T(8,128)S(1)} %collective-permute-done.9.b3, f32[3696,128]{1,0:T(8,128)S(1)} %bitcast.6, ...), custom_call_target="tpu_custom_call" | custom-call | tf_op jit(solution)/shard_map/pallas_call | solution.py:427
  166.2 8.5 %all-to-all-start = ((f32[32,8,128]{2,1,0:T(8,128)}), f32[32,8,128]{2,1,0:T(8,128)S(1)}, u32[]{:S(2)}, u32[]{:S(2)}) async-start(f32[32,8,128]{2,1,0:T(8,128)} %shard_map.80), calls=%async_computation | async-start | bytes 262144 | tf_op jit(solution)/shard_map/all_to_all | solution.py:435
  174.7 2.8 %shard_map.81 = (f32[18,1296]{1,0:T(8,128)S(1)}, f32[18,1296]{1,0:T(8,128)S(1)}) custom-call(s32[8]{0:T(128)S(1)} %copy-done.3, s32[8]{0:T(128)S(1)} %copy-done.4, f32[8,6]{1,0:T(8,128)S(1)} %copy-done.6, f32[8,36]{1,0:T(8,128)S(1)} %copy-done.7, f32[3,6,1,1296]{3,2,1,0:T(1,128)S(1)} %copy-done.1, f32[108,1,216]{2,1,0:T(1,128)S(1)} %copy-done.5, ...), custom_call_target="tpu_custom_call" | custom-call | flops 100000000 | bytes 1000000 | tf_op jit(solution)/shard_map/pallas_call | solution.py:395
  177.6 4.8 %all-to-all-done.sums = f32[32,8,128]{2,1,0:T(8,128)S(1)} async-done(((f32[32,8,128]{2,1,0:T(8,128)}), f32[32,8,128]{2,1,0:T(8,128)S(1)}, u32[]{:S(2)}, u32[]{:S(2)}) %all-to-all-start) | async-done | bytes 131104 | tf_op jit(solution)/shard_map/all_to_all | solution.py:435
  (42 shorter events, 9.8 us)
Async XLA Ops:
  0.0 109.5 %copy-start.5 = (f32[108,1,216]{2,1,0:T(1,128)S(1)}, f32[108,1,216]{2,1,0:T(1,128)}, u32[]{:S(2)}) copy-start(f32[108,1,216]{2,1,0:T(1,128)} %ovov.1) | copy-start | bytes 279940
  108.0 15.2 %collective-permute-start.3 = (f32[3696,128]{1,0:T(8,128)}, f32[3696,128]{1,0:T(8,128)S(1)}, u32[]{:S(2)}, u32[]{:S(2)}) collective-permute-start(f32[3696,128]{1,0:T(8,128)} %bitcast.4), channel_id=1, source_target_pairs={{0,1},{1,0},{2,3},{3,2},{4,5},{5,4},{6,7},{7,6},{8,9},{9,8},{10,11... | collective-permute-start | bytes 5677064 | tf_op jit(solution)/shard_map/ppermute | solution.py:49
  109.6 5.0 %collective-permute-start.1 = (f32[108,1,216]{2,1,0:T(1,128)S(1)}, f32[108,1,216]{2,1,0:T(1,128)S(1)}, u32[]{:S(2)}, u32[]{:S(2)}) collective-permute-start(f32[108,1,216]{2,1,0:T(1,128)S(1)} %copy-done.5), channel_id=1, source_target_pairs={{0,8},{8,0},{16,24},{24,16},{1,9},{9,1},{17,25},{25,17},{2,10},{10... | collective-permute-start | bytes 279944 | tf_op jit(solution)/shard_map/ppermute | solution.py:360
  111.3 2.0 %collective-permute-start = (f32[104,128]{1,0:T(8,128)}, f32[104,128]{1,0:T(8,128)S(1)}, u32[]{:S(2)}, u32[]{:S(2)}) collective-permute-start(f32[104,128]{1,0:T(8,128)} %get-tuple-element.22), channel_id=1, source_target_pairs={{0,1},{1,0},{2,3},{3,2},{4,5},{5,4},{6,7},{7,6},{8,9},{9,8},{10,11... | collective-permute-start | bytes 159752 | tf_op jit(solution)/shard_map/ppermute | solution.py:49
  115.4 5.1 %collective-permute-start.2 = (f32[192,128]{1,0:T(8,128)S(1)}, f32[192,128]{1,0:T(8,128)S(1)}, u32[]{:S(2)}, u32[]{:S(2)}) collective-permute-start(f32[192,128]{1,0:T(8,128)S(1)} %shard_map.74.near), channel_id=1, source_target_pairs={{0,4},{1,5},{2,6},{3,7},{4,0},{5,1},{6,2},{7,3},{8,12},{9,13},{10,... | collective-permute-start | bytes 294920 | tf_op jit(solution)/shard_map/ppermute | solution.py:45
  120.5 21.2 %collective-permute-start.13 = (f32[1848,128]{1,0:T(8,128)}, f32[1848,128]{1,0:T(8,128)S(1)}, u32[]{:S(2)}, u32[]{:S(2)}) collective-permute-start(f32[1848,128]{1,0:T(8,128)} %get-tuple-element.28), channel_id=1, source_target_pairs={{0,2},{1,7},{2,4},{3,1},{4,6},{5,3},{6,0},{7,5},{8,10},{9,15},{10,... | collective-permute-start | bytes 2838536 | tf_op jit(solution)/shard_map/ppermute | solution.py:45
  123.2 24.0 %collective-permute-start.14 = (f32[1848,128]{1,0:T(8,128)}, f32[1848,128]{1,0:T(8,128)S(1)}, u32[]{:S(2)}, u32[]{:S(2)}) collective-permute-start(f32[1848,128]{1,0:T(8,128)} %get-tuple-element.29), channel_id=1, source_target_pairs={{0,6},{1,3},{2,0},{3,5},{4,2},{5,7},{6,4},{7,1},{8,14},{9,11},{10,... | collective-permute-start | bytes 2838536 | tf_op jit(solution)/shard_map/ppermute | solution.py:45
  123.2 31.8 %copy-start = (f32[42,88,1,128]{3,2,1,0:T(1,128)S(1)}, f32[42,88,1,128]{3,2,1,0:T(1,128)}, u32[]{:S(2)}) copy-start(f32[42,88,1,128]{3,2,1,0:T(1,128)} %get-tuple-element.23) | copy-start | bytes 5677060
  123.2 6.8 %collective-permute-start.4 = (f32[384,128]{1,0:T(8,128)S(1)}, f32[384,128]{1,0:T(8,128)S(1)}, u32[]{:S(2)}, u32[]{:S(2)}) collective-permute-start(f32[384,128]{1,0:T(8,128)S(1)} %shard_map.75.b0), channel_id=1, source_target_pairs={{0,32},{1,9},{2,34},{3,11},{4,36},{5,13},{6,38},{7,15},{8,40},{9,1... | collective-permute-start | bytes 589832 | tf_op jit(solution)/shard_map/ppermute | solution.py:45
  124.6 6.9 %collective-permute-start.5 = (f32[384,128]{1,0:T(8,128)S(1)}, f32[384,128]{1,0:T(8,128)S(1)}, u32[]{:S(2)}, u32[]{:S(2)}) collective-permute-start(f32[384,128]{1,0:T(8,128)S(1)} %shard_map.75.b0), channel_id=1, source_target_pairs={{0,96},{1,25},{2,98},{3,27},{4,100},{5,29},{6,102},{7,31},{8,104},... | collective-permute-start | bytes 589832 | tf_op jit(solution)/shard_map/ppermute | solution.py:45
  126.8 6.3 %collective-permute-start.6 = (f32[384,128]{1,0:T(8,128)S(1)}, f32[384,128]{1,0:T(8,128)S(1)}, u32[]{:S(2)}, u32[]{:S(2)}) collective-permute-start(f32[384,128]{1,0:T(8,128)S(1)} %shard_map.75.b0), channel_id=1, source_target_pairs={{0,64},{1,17},{2,66},{3,19},{4,68},{5,21},{6,70},{7,23},{8,72},{9,... | collective-permute-start | bytes 589832 | tf_op jit(solution)/shard_map/ppermute | solution.py:45
  133.1 14.1 %collective-permute-start.10 = (f32[768,128]{1,0:T(8,128)S(1)}, f32[768,128]{1,0:T(8,128)S(1)}, u32[]{:S(2)}, u32[]{:S(2)}) collective-permute-start(f32[768,128]{1,0:T(8,128)S(1)} %get-tuple-element.25.b0), channel_id=1, source_target_pairs={{0,8},{1,33},{2,10},{3,35},{4,12},{5,37},{6,14},{7,39},{8,16},{9,4... | collective-permute-start | bytes 1179656 | tf_op jit(solution)/shard_map/ppermute | solution.py:45
  134.4 12.8 %collective-permute-start.11 = (f32[768,128]{1,0:T(8,128)S(1)}, f32[768,128]{1,0:T(8,128)S(1)}, u32[]{:S(2)}, u32[]{:S(2)}) collective-permute-start(f32[768,128]{1,0:T(8,128)S(1)} %get-tuple-element.25.b0), channel_id=1, source_target_pairs={{0,24},{1,97},{2,26},{3,99},{4,28},{5,101},{6,30},{7,103},{8,0},{9... | collective-permute-start | bytes 1179656 | tf_op jit(solution)/shard_map/ppermute | solution.py:45
  136.1 11.1 %collective-permute-start.12 = (f32[768,128]{1,0:T(8,128)S(1)}, f32[768,128]{1,0:T(8,128)S(1)}, u32[]{:S(2)}, u32[]{:S(2)}) collective-permute-start(f32[768,128]{1,0:T(8,128)S(1)} %get-tuple-element.25.b0), channel_id=1, source_target_pairs={{0,16},{1,65},{2,18},{3,67},{4,20},{5,69},{6,22},{7,71},{8,24},{9,... | collective-permute-start | bytes 1179656 | tf_op jit(solution)/shard_map/ppermute | solution.py:45
  147.2 7.5 %collective-permute-start.15 = (f32[1848,128]{1,0:T(8,128)S(1)}, f32[1848,128]{1,0:T(8,128)S(1)}, u32[]{:S(2)}, u32[]{:S(2)}) collective-permute-start(f32[1848,128]{1,0:T(8,128)S(1)} %get-tuple-element.31.above), channel_id=1, source_target_pairs={{0,1},{1,0},{2,3},{3,2},{4,5},{5,4},{6,7},{7,6},{8,9},{9,8},{10,11... | collective-permute-start | bytes 2838536 | tf_op jit(solution)/shard_map/ppermute | solution.py:49
  151.5 3.5 %collective-permute-start.16 = (f32[1848,128]{1,0:T(8,128)S(1)}, f32[1848,128]{1,0:T(8,128)S(1)}, u32[]{:S(2)}, u32[]{:S(2)}) collective-permute-start(f32[1848,128]{1,0:T(8,128)S(1)} %get-tuple-element.30.below), channel_id=1, source_target_pairs={{0,1},{1,0},{2,3},{3,2},{4,5},{5,4},{6,7},{7,6},{8,9},{9,8},{10,11... | collective-permute-start | bytes 2838536 | tf_op jit(solution)/shard_map/ppermute | solution.py:49
  151.5 9.0 %collective-permute-start.7 = (f32[768,128]{1,0:T(8,128)S(1)}, f32[768,128]{1,0:T(8,128)S(1)}, u32[]{:S(2)}, u32[]{:S(2)}) collective-permute-start(f32[768,128]{1,0:T(8,128)S(1)} %get-tuple-element.24.b0), channel_id=1, source_target_pairs={{0,8},{1,33},{2,10},{3,35},{4,12},{5,37},{6,14},{7,39},{8,16},{9,4... | collective-permute-start | bytes 1179656 | tf_op jit(solution)/shard_map/ppermute | solution.py:45
  152.2 10.9 %collective-permute-start.8 = (f32[768,128]{1,0:T(8,128)S(1)}, f32[768,128]{1,0:T(8,128)S(1)}, u32[]{:S(2)}, u32[]{:S(2)}) collective-permute-start(f32[768,128]{1,0:T(8,128)S(1)} %get-tuple-element.24.b0), channel_id=1, source_target_pairs={{0,24},{1,97},{2,26},{3,99},{4,28},{5,101},{6,30},{7,103},{8,0},{9... | collective-permute-start | bytes 1179656 | tf_op jit(solution)/shard_map/ppermute | solution.py:45
  154.2 9.7 %collective-permute-start.9 = (f32[768,128]{1,0:T(8,128)S(1)}, f32[768,128]{1,0:T(8,128)S(1)}, u32[]{:S(2)}, u32[]{:S(2)}) collective-permute-start(f32[768,128]{1,0:T(8,128)S(1)} %get-tuple-element.24.b0), channel_id=1, source_target_pairs={{0,16},{1,65},{2,18},{3,67},{4,20},{5,69},{6,22},{7,71},{8,24},{9,... | collective-permute-start | bytes 1179656 | tf_op jit(solution)/shard_map/ppermute | solution.py:45
  157.8 6.1 %collective-permute-start.17 = (f32[144,256]{1,0:T(8,128)S(1)}, f32[144,256]{1,0:T(8,128)S(1)}, u32[]{:S(2)}, u32[]{:S(2)}) collective-permute-start(f32[144,256]{1,0:T(8,128)S(1)} %get-tuple-element.33), channel_id=1, source_target_pairs={{0,6},{1,3},{2,0},{3,5},{4,2},{5,7},{6,4},{7,1},{8,14},{9,11},{10,... | collective-permute-start | bytes 442376 | tf_op jit(solution)/shard_map/ppermute | solution.py:45
  158.0 6.0 %collective-permute-start.18 = (f32[144,256]{1,0:T(8,128)S(1)}, f32[144,256]{1,0:T(8,128)S(1)}, u32[]{:S(2)}, u32[]{:S(2)}) collective-permute-start(f32[144,256]{1,0:T(8,128)S(1)} %get-tuple-element.34), channel_id=1, source_target_pairs={{0,2},{1,7},{2,4},{3,1},{4,6},{5,3},{6,0},{7,5},{8,10},{9,15},{10,... | collective-permute-start | bytes 442376 | tf_op jit(solution)/shard_map/ppermute | solution.py:45
  164.0 10.7 %copy-start.6 = (f32[8,6]{1,0:T(8,128)S(1)}, f32[8,6]{1,0:T(8,128)}, u32[]{:S(2)}) copy-start(f32[8,6]{1,0:T(8,128)} %eps_occ_ref.1) | copy-start | bytes 580
  164.0 10.8 %copy-start.7 = (f32[8,36]{1,0:T(8,128)S(1)}, f32[8,36]{1,0:T(8,128)}, u32[]{:S(2)}) copy-start(f32[8,36]{1,0:T(8,128)} %eps_vir_ref.1) | copy-start | bytes 3460
  166.2 16.2 %all-to-all-start = ((f32[32,8,128]{2,1,0:T(8,128)}), f32[32,8,128]{2,1,0:T(8,128)S(1)}, u32[]{:S(2)}, u32[]{:S(2)}) async-start(f32[32,8,128]{2,1,0:T(8,128)} %shard_map.80), calls=%async_computation | async-start | bytes 262144 | tf_op jit(solution)/shard_map/all_to_all | solution.py:435
  (4 other events, 33.0 us)

commit v5 on v4

--- a/solution.py
+++ b/solution.py
@@ -343,7 +343,7 @@
         out_shape=[shape((SHARD, LANES), F32)] * 2 + [window] * 2
         + [shape((2 * SPAN, PSLOT, 1, LANES), F32)],
         in_specs=[HBM] * 4,
-        out_specs=[VMEM] * 2 + [ANY] * 3,
+        out_specs=[VMEM] * 5,
         scratch_shapes=[
             pltpu.VMEM((24, WINDOW), F32),
             pltpu.VMEM((3, 6, 1, 1296), F32),

time: 184 us -> 81 us (0.44)
  Pallas kernels: 117 us -> 14.2 us
    pallas_call x1, Pallas kernels: 108 us -> 5.5 us  [on_device(): pl.pallas_call(open_step, out_shape=[shape((SHARD, LANES), F32)] * 2 + [w...]
  transfers between devices with their start and end apart: 20 -> 20, of which waited for: 13 -> 13; matrix products, arithmetic and copies ran while one was open for 0% -> 0% of each run, Pallas kernels for 3% -> 7%
where the time goes in v5:
time: 81 us; the launch traced here: 80.7 us
  starting transfers between devices  37.2 us (46%)
  waiting for transfers between devices  28.4 us (35%)
  Pallas kernels  14.2 us (18%)
  local copies, waits for them, and re-layouts  0.84 us (1%)
    ppermute x14, starting transfers between devices, ring(): return lax.ppermute(value, AXES, pairs)  20.8 us
    ppermute x14, waiting for transfers between devices, ring(): return lax.ppermute(value, AXES, pairs)  20.3 us
    all_to_all x1, starting transfers between devices, on_device(): ladder = lax.all_to_all(packed, ('x', 'z', 'core'), 0, 0, tiled=True)  8.47 us
    ppermute x4, starting transfers between devices, swap_core(): return lax.ppermute(value, 'core', [(0, 1), (1, 0)])  6.18 us
    pallas_call x1, Pallas kernels, on_device(): pl.pallas_call(open_step, out_shape=[shape((SHARD, LANES), F32)] * 2 + [w...  5.5 us
    all_to_all x1, waiting for transfers between devices, on_device(): ladder = lax.all_to_all(packed, ('x', 'z', 'core'), 0, 0, tiled=True)  4.82 us
    pallas_call x1, Pallas kernels, on_device(): pl.pallas_call(local_step, out_shape=[shape((18, 1296), F32)] * 2, in_spe...  2.83 us
    pallas_call x1, Pallas kernels, on_device(): pl.pallas_call(multiply_near, out_shape=sums, in_specs=[VMEM] * 10, out_s...  2.73 us
  transfers between devices with their start and end apart: 20, of which 13 were waited for; matrix products, arithmetic and copies ran while one was open for 0% of the time, Pallas kernels for 7%

profile of v5, /device:TPU:1, one launch (start us, length us, event | category | flops | bytes accessed | tf_op | source)
XLA Modules:
  0.0 80.7 jit_solution(7851344703077516552)
XLA Ops:
  0.0 5.5 %shard_map.73 = (f32[104,128]{1,0:T(8,128)}, f32[104,128]{1,0:T(8,128)}, f32[21,88,1,128]{3,2,1,0:T(1,128)}, f32[21,88,1,128]{3,2,1,0:T(1,128)}, f32[42,88,1,128]{3,2,1,0:T(1,128)}) custom-call(s32[8]{0:T(128)} %occ_ref.3, s32[8]{0:T(128)} %vir_ref.3, f32[3,6,1,1296]{3,2,1,0:T(1,128)} %amp_ref.3, f32[81,1,10368]{2,1,0:T(1,128)} %bitcast.7), custom_call_target="tpu_custom_call" | custom-call | tf_op jit(solution)/shard_map/pallas_call | solution.py:341
  5.5 1.5 %collective-permute-start.3 = (f32[3696,128]{1,0:T(8,128)}, f32[3696,128]{1,0:T(8,128)S(1)}, u32[]{:S(2)}, u32[]{:S(2)}) collective-permute-start(f32[3696,128]{1,0:T(8,128)} %bitcast.4), channel_id=1, source_target_pairs={{0,1},{1,0},{2,3},{3,2},{4,5},{5,4},{6,7},{7,6},{8,9},{9,8},{10,11... | collective-permute-start | bytes 5677064 | tf_op jit(solution)/shard_map/ppermute | solution.py:49
  7.0 1.7 %collective-permute-start.1 = (f32[108,1,216]{2,1,0:T(1,128)S(1)}, f32[108,1,216]{2,1,0:T(1,128)S(1)}, u32[]{:S(2)}, u32[]{:S(2)}) collective-permute-start(f32[108,1,216]{2,1,0:T(1,128)S(1)} %copy-done.5), channel_id=1, source_target_pairs={{0,8},{8,0},{16,24},{24,16},{1,9},{9,1},{17,25},{25,17},{2,10},{10... | collective-permute-start | bytes 279944 | tf_op jit(solution)/shard_map/ppermute | solution.py:360
  9.1 1.7 %collective-permute-done.got = f32[104,128]{1,0:T(8,128)S(1)} collective-permute-done((f32[104,128]{1,0:T(8,128)}, f32[104,128]{1,0:T(8,128)S(1)}, u32[]{:S(2)}, u32[]{:S(2)}) %collective-permute-start) | collective-permute-done | bytes 53280 | tf_op jit(solution)/shard_map/ppermute | solution.py:49
  12.9 3.0 %collective-permute-start.2 = (f32[192,128]{1,0:T(8,128)S(1)}, f32[192,128]{1,0:T(8,128)S(1)}, u32[]{:S(2)}, u32[]{:S(2)}) collective-permute-start(f32[192,128]{1,0:T(8,128)S(1)} %shard_map.74.near), channel_id=1, source_target_pairs={{0,4},{1,5},{2,6},{3,7},{4,0},{5,1},{6,2},{7,3},{8,12},{9,13},{10,... | collective-permute-start | bytes 294920 | tf_op jit(solution)/shard_map/ppermute | solution.py:45
  15.9 2.1 %collective-permute-done.2.far.refs_2_ = f32[192,128]{1,0:T(8,128)S(1)} collective-permute-done((f32[192,128]{1,0:T(8,128)S(1)}, f32[192,128]{1,0:T(8,128)S(1)}, u32[]{:S(2)}, u32[]{:S(2)}) %collective-permute-start.2) | collective-permute-done | bytes 98336 | tf_op jit(solution)/shard_map/ppermute | solution.py:45
  17.9 2.7 %collective-permute-start.13 = (f32[1848,128]{1,0:T(8,128)}, f32[1848,128]{1,0:T(8,128)S(1)}, u32[]{:S(2)}, u32[]{:S(2)}) collective-permute-start(f32[1848,128]{1,0:T(8,128)} %get-tuple-element.28), channel_id=1, source_target_pairs={{0,2},{1,7},{2,4},{3,1},{4,6},{5,3},{6,0},{7,5},{8,10},{9,15},{10,... | collective-permute-start | bytes 2838536 | tf_op jit(solution)/shard_map/ppermute | solution.py:45
  20.7 1.4 %collective-permute-start.4 = (f32[384,128]{1,0:T(8,128)S(1)}, f32[384,128]{1,0:T(8,128)S(1)}, u32[]{:S(2)}, u32[]{:S(2)}) collective-permute-start(f32[384,128]{1,0:T(8,128)S(1)} %shard_map.75.b0), channel_id=1, source_target_pairs={{0,32},{1,9},{2,34},{3,11},{4,36},{5,13},{6,38},{7,15},{8,40},{9,1... | collective-permute-start | bytes 589832 | tf_op jit(solution)/shard_map/ppermute | solution.py:45
  22.1 2.2 %collective-permute-start.5 = (f32[384,128]{1,0:T(8,128)S(1)}, f32[384,128]{1,0:T(8,128)S(1)}, u32[]{:S(2)}, u32[]{:S(2)}) collective-permute-start(f32[384,128]{1,0:T(8,128)S(1)} %shard_map.75.b0), channel_id=1, source_target_pairs={{0,96},{1,25},{2,98},{3,27},{4,100},{5,29},{6,102},{7,31},{8,104},... | collective-permute-start | bytes 589832 | tf_op jit(solution)/shard_map/ppermute | solution.py:45
  25.5 2.0 %collective-permute-done.4.b1 = f32[384,128]{1,0:T(8,128)S(1)} collective-permute-done((f32[384,128]{1,0:T(8,128)S(1)}, f32[384,128]{1,0:T(8,128)S(1)}, u32[]{:S(2)}, u32[]{:S(2)}) %collective-permute-start.4) | collective-permute-done | bytes 196640 | tf_op jit(solution)/shard_map/ppermute | solution.py:45
  27.5 1.4 %collective-permute-done.5.b2 = f32[384,128]{1,0:T(8,128)S(1)} collective-permute-done((f32[384,128]{1,0:T(8,128)S(1)}, f32[384,128]{1,0:T(8,128)S(1)}, u32[]{:S(2)}, u32[]{:S(2)}) %collective-permute-start.5) | collective-permute-done | bytes 196640 | tf_op jit(solution)/shard_map/ppermute | solution.py:45
  29.0 1.5 %collective-permute-done.6.b3 = f32[384,128]{1,0:T(8,128)S(1)} collective-permute-done((f32[384,128]{1,0:T(8,128)S(1)}, f32[384,128]{1,0:T(8,128)S(1)}, u32[]{:S(2)}, u32[]{:S(2)}) %collective-permute-start.6) | collective-permute-done | bytes 196640 | tf_op jit(solution)/shard_map/ppermute | solution.py:45
  31.9 1.6 %collective-permute-start.11 = (f32[768,128]{1,0:T(8,128)S(1)}, f32[768,128]{1,0:T(8,128)S(1)}, u32[]{:S(2)}, u32[]{:S(2)}) collective-permute-start(f32[768,128]{1,0:T(8,128)S(1)} %get-tuple-element.25.b0), channel_id=1, source_target_pairs={{0,24},{1,97},{2,26},{3,99},{4,28},{5,101},{6,30},{7,103},{8,0},{9... | collective-permute-start | bytes 1179656 | tf_op jit(solution)/shard_map/ppermute | solution.py:45
  34.9 4.3 %collective-permute-done.13.refs_0_ = f32[1848,128]{1,0:T(8,128)S(1)} collective-permute-done((f32[1848,128]{1,0:T(8,128)}, f32[1848,128]{1,0:T(8,128)S(1)}, u32[]{:S(2)}, u32[]{:S(2)}) %collective-permute-start.13) | collective-permute-done | bytes 946208 | tf_op jit(solution)/shard_map/ppermute | solution.py:45
  39.2 5.5 %collective-permute-done.14.refs_1_ = f32[1848,128]{1,0:T(8,128)S(1)} collective-permute-done((f32[1848,128]{1,0:T(8,128)}, f32[1848,128]{1,0:T(8,128)S(1)}, u32[]{:S(2)}, u32[]{:S(2)}) %collective-permute-start.14) | collective-permute-done | bytes 946208 | tf_op jit(solution)/shard_map/ppermute | solution.py:45
  44.7 4.3 %collective-permute-start.15 = (f32[1848,128]{1,0:T(8,128)S(1)}, f32[1848,128]{1,0:T(8,128)S(1)}, u32[]{:S(2)}, u32[]{:S(2)}) collective-permute-start(f32[1848,128]{1,0:T(8,128)S(1)} %get-tuple-element.31.above), channel_id=1, source_target_pairs={{0,1},{1,0},{2,3},{3,2},{4,5},{5,4},{6,7},{7,6},{8,9},{9,8},{10,11... | collective-permute-start | bytes 2838536 | tf_op jit(solution)/shard_map/ppermute | solution.py:49
  49.7 2.0 %collective-permute-start.8 = (f32[768,128]{1,0:T(8,128)S(1)}, f32[768,128]{1,0:T(8,128)S(1)}, u32[]{:S(2)}, u32[]{:S(2)}) collective-permute-start(f32[768,128]{1,0:T(8,128)S(1)} %get-tuple-element.24.b0), channel_id=1, source_target_pairs={{0,24},{1,97},{2,26},{3,99},{4,28},{5,101},{6,30},{7,103},{8,0},{9... | collective-permute-start | bytes 1179656 | tf_op jit(solution)/shard_map/ppermute | solution.py:45
  52.5 2.7 %shard_map.79 = (f32[144,256]{1,0:T(8,128)S(1)}, f32[144,256]{1,0:T(8,128)S(1)}, f32[144,256]{1,0:T(8,128)S(1)}) custom-call(f32[768,128]{1,0:T(8,128)S(1)} %get-tuple-element.25.b0, f32[768,128]{1,0:T(8,128)S(1)} %collective-permute-done.10.refs_2_.b1, f32[768,128]{1,0:T(8,128)S(1)} %collective-permute-done.11.refs_3_.b2, ...), custom_call_target="tpu_custom_call" | custom-call | tf_op jit(solution)/shard_map/pallas_call | solution.py:417
  55.5 2.5 %collective-permute-start.18 = (f32[144,256]{1,0:T(8,128)S(1)}, f32[144,256]{1,0:T(8,128)S(1)}, u32[]{:S(2)}, u32[]{:S(2)}) collective-permute-start(f32[144,256]{1,0:T(8,128)S(1)} %get-tuple-element.34), channel_id=1, source_target_pairs={{0,2},{1,7},{2,4},{3,1},{4,6},{5,3},{6,0},{7,5},{8,10},{9,15},{10,... | collective-permute-start | bytes 442376 | tf_op jit(solution)/shard_map/ppermute | solution.py:45
  58.0 2.6 %collective-permute-done.8.b2 = f32[768,128]{1,0:T(8,128)S(1)} collective-permute-done((f32[768,128]{1,0:T(8,128)S(1)}, f32[768,128]{1,0:T(8,128)S(1)}, u32[]{:S(2)}, u32[]{:S(2)}) %collective-permute-start.8) | collective-permute-done | bytes 393248 | tf_op jit(solution)/shard_map/ppermute | solution.py:45
  61.4 2.2 %shard_map.80 = f32[32,8,128]{2,1,0:T(8,128)} custom-call(f32[768,128]{1,0:T(8,128)S(1)} %get-tuple-element.24.b0, f32[768,128]{1,0:T(8,128)S(1)} %collective-permute-done.7.b1, f32[768,128]{1,0:T(8,128)S(1)} %collective-permute-done.8.b2, f32[768,128]{1,0:T(8,128)S(1)} %collective-permute-done.9.b3, f32[3696,128]{1,0:T(8,128)S(1)} %bitcast.6, ...), custom_call_target="tpu_custom_call" | custom-call | tf_op jit(solution)/shard_map/pallas_call | solution.py:427
  63.7 8.5 %all-to-all-start = ((f32[32,8,128]{2,1,0:T(8,128)}), f32[32,8,128]{2,1,0:T(8,128)S(1)}, u32[]{:S(2)}, u32[]{:S(2)}) async-start(f32[32,8,128]{2,1,0:T(8,128)} %shard_map.80), calls=%async_computation | async-start | bytes 262144 | tf_op jit(solution)/shard_map/all_to_all | solution.py:435
  72.2 2.8 %shard_map.81 = (f32[18,1296]{1,0:T(8,128)S(1)}, f32[18,1296]{1,0:T(8,128)S(1)}) custom-call(s32[8]{0:T(128)S(1)} %copy-done.3, s32[8]{0:T(128)S(1)} %copy-done.4, f32[8,6]{1,0:T(8,128)S(1)} %copy-done.6, f32[8,36]{1,0:T(8,128)S(1)} %copy-done.7, f32[3,6,1,1296]{3,2,1,0:T(1,128)S(1)} %copy-done.1, f32[108,1,216]{2,1,0:T(1,128)S(1)} %copy-done.5, ...), custom_call_target="tpu_custom_call" | custom-call | flops 100000000 | bytes 1000000 | tf_op jit(solution)/shard_map/pallas_call | solution.py:395
  75.0 4.8 %all-to-all-done.sums = f32[32,8,128]{2,1,0:T(8,128)S(1)} async-done(((f32[32,8,128]{2,1,0:T(8,128)}), f32[32,8,128]{2,1,0:T(8,128)S(1)}, u32[]{:S(2)}, u32[]{:S(2)}) %all-to-all-start) | async-done | bytes 131104 | tf_op jit(solution)/shard_map/all_to_all | solution.py:435
  (42 shorter events, 9.8 us)
Async XLA Ops:
  5.5 15.2 %collective-permute-start.3 = (f32[3696,128]{1,0:T(8,128)}, f32[3696,128]{1,0:T(8,128)S(1)}, u32[]{:S(2)}, u32[]{:S(2)}) collective-permute-start(f32[3696,128]{1,0:T(8,128)} %bitcast.4), channel_id=1, source_target_pairs={{0,1},{1,0},{2,3},{3,2},{4,5},{5,4},{6,7},{7,6},{8,9},{9,8},{10,11... | collective-permute-start | bytes 5677064 | tf_op jit(solution)/shard_map/ppermute | solution.py:49
  7.0 5.0 %collective-permute-start.1 = (f32[108,1,216]{2,1,0:T(1,128)S(1)}, f32[108,1,216]{2,1,0:T(1,128)S(1)}, u32[]{:S(2)}, u32[]{:S(2)}) collective-permute-start(f32[108,1,216]{2,1,0:T(1,128)S(1)} %copy-done.5), channel_id=1, source_target_pairs={{0,8},{8,0},{16,24},{24,16},{1,9},{9,1},{17,25},{25,17},{2,10},{10... | collective-permute-start | bytes 279944 | tf_op jit(solution)/shard_map/ppermute | solution.py:360
  8.8 2.0 %collective-permute-start = (f32[104,128]{1,0:T(8,128)}, f32[104,128]{1,0:T(8,128)S(1)}, u32[]{:S(2)}, u32[]{:S(2)}) collective-permute-start(f32[104,128]{1,0:T(8,128)} %get-tuple-element.22), channel_id=1, source_target_pairs={{0,1},{1,0},{2,3},{3,2},{4,5},{5,4},{6,7},{7,6},{8,9},{9,8},{10,11... | collective-permute-start | bytes 159752 | tf_op jit(solution)/shard_map/ppermute | solution.py:49
  12.9 5.1 %collective-permute-start.2 = (f32[192,128]{1,0:T(8,128)S(1)}, f32[192,128]{1,0:T(8,128)S(1)}, u32[]{:S(2)}, u32[]{:S(2)}) collective-permute-start(f32[192,128]{1,0:T(8,128)S(1)} %shard_map.74.near), channel_id=1, source_target_pairs={{0,4},{1,5},{2,6},{3,7},{4,0},{5,1},{6,2},{7,3},{8,12},{9,13},{10,... | collective-permute-start | bytes 294920 | tf_op jit(solution)/shard_map/ppermute | solution.py:45
  17.9 21.2 %collective-permute-start.13 = (f32[1848,128]{1,0:T(8,128)}, f32[1848,128]{1,0:T(8,128)S(1)}, u32[]{:S(2)}, u32[]{:S(2)}) collective-permute-start(f32[1848,128]{1,0:T(8,128)} %get-tuple-element.28), channel_id=1, source_target_pairs={{0,2},{1,7},{2,4},{3,1},{4,6},{5,3},{6,0},{7,5},{8,10},{9,15},{10,... | collective-permute-start | bytes 2838536 | tf_op jit(solution)/shard_map/ppermute | solution.py:45
  20.7 24.0 %collective-permute-start.14 = (f32[1848,128]{1,0:T(8,128)}, f32[1848,128]{1,0:T(8,128)S(1)}, u32[]{:S(2)}, u32[]{:S(2)}) collective-permute-start(f32[1848,128]{1,0:T(8,128)} %get-tuple-element.29), channel_id=1, source_target_pairs={{0,6},{1,3},{2,0},{3,5},{4,2},{5,7},{6,4},{7,1},{8,14},{9,11},{10,... | collective-permute-start | bytes 2838536 | tf_op jit(solution)/shard_map/ppermute | solution.py:45
  20.7 31.8 %copy-start = (f32[42,88,1,128]{3,2,1,0:T(1,128)S(1)}, f32[42,88,1,128]{3,2,1,0:T(1,128)}, u32[]{:S(2)}) copy-start(f32[42,88,1,128]{3,2,1,0:T(1,128)} %get-tuple-element.23) | copy-start | bytes 5677060
  20.7 6.8 %collective-permute-start.4 = (f32[384,128]{1,0:T(8,128)S(1)}, f32[384,128]{1,0:T(8,128)S(1)}, u32[]{:S(2)}, u32[]{:S(2)}) collective-permute-start(f32[384,128]{1,0:T(8,128)S(1)} %shard_map.75.b0), channel_id=1, source_target_pairs={{0,32},{1,9},{2,34},{3,11},{4,36},{5,13},{6,38},{7,15},{8,40},{9,1... | collective-permute-start | bytes 589832 | tf_op jit(solution)/shard_map/ppermute | solution.py:45
  22.1 6.9 %collective-permute-start.5 = (f32[384,128]{1,0:T(8,128)S(1)}, f32[384,128]{1,0:T(8,128)S(1)}, u32[]{:S(2)}, u32[]{:S(2)}) collective-permute-start(f32[384,128]{1,0:T(8,128)S(1)} %shard_map.75.b0), channel_id=1, source_target_pairs={{0,96},{1,25},{2,98},{3,27},{4,100},{5,29},{6,102},{7,31},{8,104},... | collective-permute-start | bytes 589832 | tf_op jit(solution)/shard_map/ppermute | solution.py:45
  24.3 6.3 %collective-permute-start.6 = (f32[384,128]{1,0:T(8,128)S(1)}, f32[384,128]{1,0:T(8,128)S(1)}, u32[]{:S(2)}, u32[]{:S(2)}) collective-permute-start(f32[384,128]{1,0:T(8,128)S(1)} %shard_map.75.b0), channel_id=1, source_target_pairs={{0,64},{1,17},{2,66},{3,19},{4,68},{5,21},{6,70},{7,23},{8,72},{9,... | collective-permute-start | bytes 589832 | tf_op jit(solution)/shard_map/ppermute | solution.py:45
  30.6 14.1 %collective-permute-start.10 = (f32[768,128]{1,0:T(8,128)S(1)}, f32[768,128]{1,0:T(8,128)S(1)}, u32[]{:S(2)}, u32[]{:S(2)}) collective-permute-start(f32[768,128]{1,0:T(8,128)S(1)} %get-tuple-element.25.b0), channel_id=1, source_target_pairs={{0,8},{1,33},{2,10},{3,35},{4,12},{5,37},{6,14},{7,39},{8,16},{9,4... | collective-permute-start | bytes 1179656 | tf_op jit(solution)/shard_map/ppermute | solution.py:45
  31.9 12.8 %collective-permute-start.11 = (f32[768,128]{1,0:T(8,128)S(1)}, f32[768,128]{1,0:T(8,128)S(1)}, u32[]{:S(2)}, u32[]{:S(2)}) collective-permute-start(f32[768,128]{1,0:T(8,128)S(1)} %get-tuple-element.25.b0), channel_id=1, source_target_pairs={{0,24},{1,97},{2,26},{3,99},{4,28},{5,101},{6,30},{7,103},{8,0},{9... | collective-permute-start | bytes 1179656 | tf_op jit(solution)/shard_map/ppermute | solution.py:45
  33.5 11.1 %collective-permute-start.12 = (f32[768,128]{1,0:T(8,128)S(1)}, f32[768,128]{1,0:T(8,128)S(1)}, u32[]{:S(2)}, u32[]{:S(2)}) collective-permute-start(f32[768,128]{1,0:T(8,128)S(1)} %get-tuple-element.25.b0), channel_id=1, source_target_pairs={{0,16},{1,65},{2,18},{3,67},{4,20},{5,69},{6,22},{7,71},{8,24},{9,... | collective-permute-start | bytes 1179656 | tf_op jit(solution)/shard_map/ppermute | solution.py:45
  44.7 7.5 %collective-permute-start.15 = (f32[1848,128]{1,0:T(8,128)S(1)}, f32[1848,128]{1,0:T(8,128)S(1)}, u32[]{:S(2)}, u32[]{:S(2)}) collective-permute-start(f32[1848,128]{1,0:T(8,128)S(1)} %get-tuple-element.31.above), channel_id=1, source_target_pairs={{0,1},{1,0},{2,3},{3,2},{4,5},{5,4},{6,7},{7,6},{8,9},{9,8},{10,11... | collective-permute-start | bytes 2838536 | tf_op jit(solution)/shard_map/ppermute | solution.py:49
  49.0 3.5 %collective-permute-start.16 = (f32[1848,128]{1,0:T(8,128)S(1)}, f32[1848,128]{1,0:T(8,128)S(1)}, u32[]{:S(2)}, u32[]{:S(2)}) collective-permute-start(f32[1848,128]{1,0:T(8,128)S(1)} %get-tuple-element.30.below), channel_id=1, source_target_pairs={{0,1},{1,0},{2,3},{3,2},{4,5},{5,4},{6,7},{7,6},{8,9},{9,8},{10,11... | collective-permute-start | bytes 2838536 | tf_op jit(solution)/shard_map/ppermute | solution.py:49
  49.0 9.0 %collective-permute-start.7 = (f32[768,128]{1,0:T(8,128)S(1)}, f32[768,128]{1,0:T(8,128)S(1)}, u32[]{:S(2)}, u32[]{:S(2)}) collective-permute-start(f32[768,128]{1,0:T(8,128)S(1)} %get-tuple-element.24.b0), channel_id=1, source_target_pairs={{0,8},{1,33},{2,10},{3,35},{4,12},{5,37},{6,14},{7,39},{8,16},{9,4... | collective-permute-start | bytes 1179656 | tf_op jit(solution)/shard_map/ppermute | solution.py:45
  49.7 10.9 %collective-permute-start.8 = (f32[768,128]{1,0:T(8,128)S(1)}, f32[768,128]{1,0:T(8,128)S(1)}, u32[]{:S(2)}, u32[]{:S(2)}) collective-permute-start(f32[768,128]{1,0:T(8,128)S(1)} %get-tuple-element.24.b0), channel_id=1, source_target_pairs={{0,24},{1,97},{2,26},{3,99},{4,28},{5,101},{6,30},{7,103},{8,0},{9... | collective-permute-start | bytes 1179656 | tf_op jit(solution)/shard_map/ppermute | solution.py:45
  51.7 9.7 %collective-permute-start.9 = (f32[768,128]{1,0:T(8,128)S(1)}, f32[768,128]{1,0:T(8,128)S(1)}, u32[]{:S(2)}, u32[]{:S(2)}) collective-permute-start(f32[768,128]{1,0:T(8,128)S(1)} %get-tuple-element.24.b0), channel_id=1, source_target_pairs={{0,16},{1,65},{2,18},{3,67},{4,20},{5,69},{6,22},{7,71},{8,24},{9,... | collective-permute-start | bytes 1179656 | tf_op jit(solution)/shard_map/ppermute | solution.py:45
  55.2 6.1 %collective-permute-start.17 = (f32[144,256]{1,0:T(8,128)S(1)}, f32[144,256]{1,0:T(8,128)S(1)}, u32[]{:S(2)}, u32[]{:S(2)}) collective-permute-start(f32[144,256]{1,0:T(8,128)S(1)} %get-tuple-element.33), channel_id=1, source_target_pairs={{0,6},{1,3},{2,0},{3,5},{4,2},{5,7},{6,4},{7,1},{8,14},{9,11},{10,... | collective-permute-start | bytes 442376 | tf_op jit(solution)/shard_map/ppermute | solution.py:45
  55.5 6.0 %collective-permute-start.18 = (f32[144,256]{1,0:T(8,128)S(1)}, f32[144,256]{1,0:T(8,128)S(1)}, u32[]{:S(2)}, u32[]{:S(2)}) collective-permute-start(f32[144,256]{1,0:T(8,128)S(1)} %get-tuple-element.34), channel_id=1, source_target_pairs={{0,2},{1,7},{2,4},{3,1},{4,6},{5,3},{6,0},{7,5},{8,10},{9,15},{10,... | collective-permute-start | bytes 442376 | tf_op jit(solution)/shard_map/ppermute | solution.py:45
  61.4 10.7 %copy-start.4 = (s32[8]{0:T(128)S(1)}, s32[8]{0:T(128)}, u32[]{:S(2)}) copy-start(s32[8]{0:T(128)} %vir_ref.3) | copy-start | bytes 100
  61.4 10.7 %copy-start.6 = (f32[8,6]{1,0:T(8,128)S(1)}, f32[8,6]{1,0:T(8,128)}, u32[]{:S(2)}) copy-start(f32[8,6]{1,0:T(8,128)} %eps_occ_ref.1) | copy-start | bytes 580
  61.4 10.7 %copy-start.7 = (f32[8,36]{1,0:T(8,128)S(1)}, f32[8,36]{1,0:T(8,128)}, u32[]{:S(2)}) copy-start(f32[8,36]{1,0:T(8,128)} %eps_vir_ref.1) | copy-start | bytes 3460
  63.7 16.2 %all-to-all-start = ((f32[32,8,128]{2,1,0:T(8,128)}), f32[32,8,128]{2,1,0:T(8,128)S(1)}, u32[]{:S(2)}, u32[]{:S(2)}) async-start(f32[32,8,128]{2,1,0:T(8,128)} %shard_map.80), calls=%async_computation | async-start | bytes 262144 | tf_op jit(solution)/shard_map/all_to_all | solution.py:435
  (4 other events, 29.3 us)

commit v6 on v5

--- a/solution.py
+++ b/solution.py
@@ -69,19 +69,37 @@
     return copies
 
 
-def open_step(occ_ref, vir_ref, amp_ref, integrals, keep, send, first_v, second_v, home,
-              wide, amp, occ, vir, sems, cut_sems):
+def open_step(occ_ref, vir_ref, amp_ref, integrals, keep_out, send_out, first_out, second_out, home_out,
+              wide, amp, occ, vir, keep, send, first_v, second_v, home, sems, cut_sems, out_sems):
     x, z, y, core = places()
     copies = [
         pltpu.make_async_copy(source, target, sems.at[at])
         for at, (source, target) in enumerate(((occ_ref, occ), (vir_ref, vir), (amp_ref, amp)))
     ]
-    cuts = window_copies(integrals, first_v, 0, cut_sems.at[0], ((y + 1 + 2 * core) & 3) * 20)
-    cuts += window_copies(integrals, second_v, 0, cut_sems.at[1], ((y + 3 - 2 * core) & 3) * 20)
-    cuts += window_copies(integrals, home, 0, cut_sems.at[2], y * 20)
-    cuts += window_copies(integrals, home, SPAN, cut_sems.at[3], ((y + 2) & 3) * 20)
-    for copy in copies + cuts:
+    groups = [
+        window_copies(integrals, first_v, 0, cut_sems.at[0], ((y + 1 + 2 * core) & 3) * 20),
+        window_copies(integrals, second_v, 0, cut_sems.at[1], ((y + 3 - 2 * core) & 3) * 20),
+        window_copies(integrals, home, 0, cut_sems.at[2], y * 20),
+        window_copies(integrals, home, SPAN, cut_sems.at[3], ((y + 2) & 3) * 20),
+    ]
+    outs = [
+        pltpu.make_async_copy(source, target, out_sems.at[at])
+        for at, (source, target) in enumerate(
+            (
+                (first_v, first_out),
+                (second_v, second_out),
+                (home.at[0:SPAN], home_out.at[0:SPAN]),
+                (home.at[SPAN : 2 * SPAN], home_out.at[SPAN : 2 * SPAN]),
+                (keep, keep_out),
+                (send, send_out),
+            )
+        )
+    ]
+    for copy in copies:
         copy.start()
+    for group in groups:
+        for copy in group:
+            copy.start()
     wide[...] = jnp.zeros_like(wide)
     for copy in copies:
         copy.wait()
@@ -116,7 +134,13 @@
         write(keep, 1)
         write(send, 0)
 
-    for copy in cuts:
+    for copy in outs[4:]:
+        copy.start()
+    for group, out in zip(groups, outs):
+        for copy in group:
+            copy.wait()
+        out.start()
+    for copy in outs:
         copy.wait()
 
 
@@ -132,7 +156,7 @@
     out[extra + SPAN : at + PAIR, :] = jnp.zeros((PAIR - PMAIN - SPAN, LANES), F32)
 
 
-def merge_pair(keep, got, witness, out):
+def merge_pair(keep, got, out):
     core = lax.axis_index("core")
 
     @pl.when(core == 0)
@@ -144,7 +168,7 @@
         merge_irreps(got, keep, out, 0)
 
 
-def join_pairs(near, far, witness, out):
+def join_pairs(near, far, home_other, out):
     out[0:PAIR, :] = near[...]
     out[PAIR:QUAD, :] = far[...]
 
@@ -343,14 +367,20 @@
         out_shape=[shape((SHARD, LANES), F32)] * 2 + [window] * 2
         + [shape((2 * SPAN, PSLOT, 1, LANES), F32)],
         in_specs=[HBM] * 4,
-        out_specs=[VMEM] * 5,
+        out_specs=[ANY] * 5,
         scratch_shapes=[
             pltpu.VMEM((24, WINDOW), F32),
             pltpu.VMEM((3, 6, 1, 1296), F32),
             pltpu.SMEM((8,), jnp.int32),
             pltpu.SMEM((8,), jnp.int32),
+            pltpu.VMEM((SHARD, LANES), F32),
+            pltpu.VMEM((SHARD, LANES), F32),
+            pltpu.VMEM((SPAN, PSLOT, 1, LANES), F32),
+            pltpu.VMEM((SPAN, PSLOT, 1, LANES), F32),
+            pltpu.VMEM((2 * SPAN, PSLOT, 1, LANES), F32),
             pltpu.SemaphoreType.DMA((3,)),
             pltpu.SemaphoreType.DMA((4, SPAN)),
+            pltpu.SemaphoreType.DMA((6,)),
         ],
         compiler_params=HUGE,
     )(occ_count, vir_count, amplitudes, integrals)
@@ -361,10 +391,10 @@
     pair = pl.pallas_call(
         merge_pair,
         out_shape=shape((PAIR, LANES), F32),
-        in_specs=[VMEM] * 2 + [ANY],
+        in_specs=[VMEM] * 2,
         out_specs=VMEM,
         compiler_params=SMALL,
-    )(keep, got, partner)
+    )(keep, got)
     far_pair = ring(pair, "yy", (2, 2))
     quad = pl.pallas_call(
         join_pairs,
@@ -374,7 +404,7 @@
         compiler_params=SMALL,
     )(pair, far_pair, home_other)
     first_v, second_v = hold(
-        flat(first_v), flat(second_v), far_pair
+        flat(first_v), flat(second_v), far_pair, partner
     )
     moved_a = ring(first_v, "yy", (1, -1))
     moved_b = ring(second_v, "yy", (-1, 1))

time: 81 us -> 83.2 us (1.027)
  waiting for transfers between devices: 28.4 us -> 31.9 us
  starting transfers between devices: 37.2 us -> 35.8 us
    ppermute x4, waiting for transfers between devices: 1.96 us -> 3.7 us  [swap_core(): return lax.ppermute(value, 'core', [(0, 1), (1, 0)])]
    ppermute x1, waiting for transfers between devices: 1.25 us -> 2.68 us  [on_device(): partner = lax.ppermute(ovov, 'z', [(0, 1), (1, 0), (2, 3), (3, 2)])]
    ppermute x14, starting transfers between devices: 20.8 us -> 19.6 us  [ring(): return lax.ppermute(value, AXES, pairs)]
    all_to_all x1, starting transfers between devices: 8.47 us -> 7.45 us  [on_device(): ladder = lax.all_to_all(packed, ('x', 'z', 'core'), 0, 0, tiled=True)]
    ppermute x4, starting transfers between devices: 6.18 us -> 7.12 us  [swap_core(): return lax.ppermute(value, 'core', [(0, 1), (1, 0)])]
  transfers between devices with their start and end apart: 20 -> 20, of which waited for: 13 -> 11; matrix products, arithmetic and copies ran while one was open for 0% -> 0% of each run, Pallas kernels for 7% -> 7%
where the time goes in v6:
time: 83.2 us; the launch traced here: 82.9 us
  starting transfers between devices  35.8 us (43%)
  waiting for transfers between devices  31.9 us (38%)
  Pallas kernels  14.2 us (17%)
  local copies, waits for them, and re-layouts  0.84 us (1%)
    ppermute x14, waiting for transfers between devices, ring(): return lax.ppermute(value, AXES, pairs)  20.8 us
    ppermute x14, starting transfers between devices, ring(): return lax.ppermute(value, AXES, pairs)  19.6 us
    all_to_all x1, starting transfers between devices, on_device(): ladder = lax.all_to_all(packed, ('x', 'z', 'core'), 0, 0, tiled=True)  7.45 us
    ppermute x4, starting transfers between devices, swap_core(): return lax.ppermute(value, 'core', [(0, 1), (1, 0)])  7.12 us
    pallas_call x1, Pallas kernels, on_device(): pl.pallas_call(open_step, out_shape=[shape((SHARD, LANES), F32)] * 2 + [w...  5.42 us
    all_to_all x1, waiting for transfers between devices, on_device(): ladder = lax.all_to_all(packed, ('x', 'z', 'core'), 0, 0, tiled=True)  4.82 us
    ppermute x4, waiting for transfers between devices, swap_core(): return lax.ppermute(value, 'core', [(0, 1), (1, 0)])  3.7 us
    pallas_call x1, Pallas kernels, on_device(): pl.pallas_call(local_step, out_shape=[shape((18, 1296), F32)] * 2, in_spe...  2.83 us
  transfers between devices with their start and end apart: 20, of which 11 were waited for; matrix products, arithmetic and copies ran while one was open for 0% of the time, Pallas kernels for 7%

profile of v6, /device:TPU:1, one launch (start us, length us, event | category | flops | bytes accessed | tf_op | source)
XLA Modules:
  0.0 82.9 jit_solution(1155488278765015325)
XLA Ops:
  0.0 5.4 %shard_map.73 = (f32[104,128]{1,0:T(8,128)}, f32[104,128]{1,0:T(8,128)}, f32[21,88,1,128]{3,2,1,0:T(1,128)}, f32[21,88,1,128]{3,2,1,0:T(1,128)}, f32[42,88,1,128]{3,2,1,0:T(1,128)}) custom-call(s32[8]{0:T(128)} %occ_ref.3, s32[8]{0:T(128)} %vir_ref.3, f32[3,6,1,1296]{3,2,1,0:T(1,128)} %amp_ref.3, f32[81,1,10368]{2,1,0:T(1,128)} %bitcast.7), custom_call_target="tpu_custom_call" | custom-call | tf_op jit(solution)/shard_map/pallas_call | solution.py:365
  5.4 1.5 %collective-permute-start.2 = (f32[3696,128]{1,0:T(8,128)}, f32[3696,128]{1,0:T(8,128)S(1)}, u32[]{:S(2)}, u32[]{:S(2)}) collective-permute-start(f32[3696,128]{1,0:T(8,128)} %bitcast.4), channel_id=1, source_target_pairs={{0,1},{1,0},{2,3},{3,2},{4,5},{5,4},{6,7},{7,6},{8,9},{9,8},{10,11... | collective-permute-start | bytes 5677064 | tf_op jit(solution)/shard_map/ppermute | solution.py:49
  7.0 3.7 %collective-permute-done.got = f32[104,128]{1,0:T(8,128)S(1)} collective-permute-done((f32[104,128]{1,0:T(8,128)}, f32[104,128]{1,0:T(8,128)S(1)}, u32[]{:S(2)}, u32[]{:S(2)}) %collective-permute-start) | collective-permute-done | bytes 53280 | tf_op jit(solution)/shard_map/ppermute | solution.py:49
  11.5 3.1 %collective-permute-start.1 = (f32[192,128]{1,0:T(8,128)S(1)}, f32[192,128]{1,0:T(8,128)S(1)}, u32[]{:S(2)}, u32[]{:S(2)}) collective-permute-start(f32[192,128]{1,0:T(8,128)S(1)} %shard_map.74.near), channel_id=1, source_target_pairs={{0,4},{1,5},{2,6},{3,7},{4,0},{5,1},{6,2},{7,3},{8,12},{9,13},{10,... | collective-permute-start | bytes 294920 | tf_op jit(solution)/shard_map/ppermute | solution.py:45
  14.6 1.6 %collective-permute-start.12 = (f32[108,1,216]{2,1,0:T(1,128)S(1)}, f32[108,1,216]{2,1,0:T(1,128)S(1)}, u32[]{:S(2)}, u32[]{:S(2)}) collective-permute-start(f32[108,1,216]{2,1,0:T(1,128)S(1)} %copy-done.5), channel_id=1, source_target_pairs={{0,8},{8,0},{16,24},{24,16},{1,9},{9,1},{17,25},{25,17},{2,10},{10... | collective-permute-start | bytes 279944 | tf_op jit(solution)/shard_map/ppermute | solution.py:390
  16.2 2.7 %collective-permute-done.12.refs_3_.partner = f32[108,1,216]{2,1,0:T(1,128)S(1)} collective-permute-done((f32[108,1,216]{2,1,0:T(1,128)S(1)}, f32[108,1,216]{2,1,0:T(1,128)S(1)}, u32[]{:S(2)}, u32[]{:S(2)}) %collective-permute-start.12) | collective-permute-done | bytes 93344 | tf_op jit(solution)/shard_map/ppermute | solution.py:390
  20.4 1.3 %collective-permute-start.3 = (f32[384,128]{1,0:T(8,128)S(1)}, f32[384,128]{1,0:T(8,128)S(1)}, u32[]{:S(2)}, u32[]{:S(2)}) collective-permute-start(f32[384,128]{1,0:T(8,128)S(1)} %shard_map.75.b0), channel_id=1, source_target_pairs={{0,32},{1,9},{2,34},{3,11},{4,36},{5,13},{6,38},{7,15},{8,40},{9,1... | collective-permute-start | bytes 589832 | tf_op jit(solution)/shard_map/ppermute | solution.py:45
  21.8 2.2 %collective-permute-start.4 = (f32[384,128]{1,0:T(8,128)S(1)}, f32[384,128]{1,0:T(8,128)S(1)}, u32[]{:S(2)}, u32[]{:S(2)}) collective-permute-start(f32[384,128]{1,0:T(8,128)S(1)} %shard_map.75.b0), channel_id=1, source_target_pairs={{0,96},{1,25},{2,98},{3,27},{4,100},{5,29},{6,102},{7,31},{8,104},... | collective-permute-start | bytes 589832 | tf_op jit(solution)/shard_map/ppermute | solution.py:45
  25.2 2.0 %collective-permute-done.3.b1 = f32[384,128]{1,0:T(8,128)S(1)} collective-permute-done((f32[384,128]{1,0:T(8,128)S(1)}, f32[384,128]{1,0:T(8,128)S(1)}, u32[]{:S(2)}, u32[]{:S(2)}) %collective-permute-start.3) | collective-permute-done | bytes 196640 | tf_op jit(solution)/shard_map/ppermute | solution.py:45
  27.2 1.4 %collective-permute-done.4.b2 = f32[384,128]{1,0:T(8,128)S(1)} collective-permute-done((f32[384,128]{1,0:T(8,128)S(1)}, f32[384,128]{1,0:T(8,128)S(1)}, u32[]{:S(2)}, u32[]{:S(2)}) %collective-permute-start.4) | collective-permute-done | bytes 196640 | tf_op jit(solution)/shard_map/ppermute | solution.py:45
  28.7 1.5 %collective-permute-done.5.b3 = f32[384,128]{1,0:T(8,128)S(1)} collective-permute-done((f32[384,128]{1,0:T(8,128)S(1)}, f32[384,128]{1,0:T(8,128)S(1)}, u32[]{:S(2)}, u32[]{:S(2)}) %collective-permute-start.5) | collective-permute-done | bytes 196640 | tf_op jit(solution)/shard_map/ppermute | solution.py:45
  30.3 2.8 %collective-permute-start.10 = (f32[768,128]{1,0:T(8,128)S(1)}, f32[768,128]{1,0:T(8,128)S(1)}, u32[]{:S(2)}, u32[]{:S(2)}) collective-permute-start(f32[768,128]{1,0:T(8,128)S(1)} %get-tuple-element.25.b0), channel_id=1, source_target_pairs={{0,24},{1,97},{2,26},{3,99},{4,28},{5,101},{6,30},{7,103},{8,0},{9... | collective-permute-start | bytes 1179656 | tf_op jit(solution)/shard_map/ppermute | solution.py:45
  34.0 5.6 %collective-permute-done.13.refs_0_ = f32[1848,128]{1,0:T(8,128)S(1)} collective-permute-done((f32[1848,128]{1,0:T(8,128)}, f32[1848,128]{1,0:T(8,128)S(1)}, u32[]{:S(2)}, u32[]{:S(2)}) %collective-permute-start.13) | collective-permute-done | bytes 946208 | tf_op jit(solution)/shard_map/ppermute | solution.py:45
  39.6 4.0 %collective-permute-done.14.refs_1_ = f32[1848,128]{1,0:T(8,128)S(1)} collective-permute-done((f32[1848,128]{1,0:T(8,128)}, f32[1848,128]{1,0:T(8,128)S(1)}, u32[]{:S(2)}, u32[]{:S(2)}) %collective-permute-start.14) | collective-permute-done | bytes 946208 | tf_op jit(solution)/shard_map/ppermute | solution.py:45
  43.6 2.1 %collective-permute-done.9.refs_2_.b1 = f32[768,128]{1,0:T(8,128)S(1)} collective-permute-done((f32[768,128]{1,0:T(8,128)S(1)}, f32[768,128]{1,0:T(8,128)S(1)}, u32[]{:S(2)}, u32[]{:S(2)}) %collective-permute-start.9) | collective-permute-done | bytes 393248 | tf_op jit(solution)/shard_map/ppermute | solution.py:45
  45.7 5.5 %collective-permute-start.15 = (f32[1848,128]{1,0:T(8,128)S(1)}, f32[1848,128]{1,0:T(8,128)S(1)}, u32[]{:S(2)}, u32[]{:S(2)}) collective-permute-start(f32[1848,128]{1,0:T(8,128)S(1)} %get-tuple-element.31.above), channel_id=1, source_target_pairs={{0,1},{1,0},{2,3},{3,2},{4,5},{5,4},{6,7},{7,6},{8,9},{9,8},{10,11... | collective-permute-start | bytes 2838536 | tf_op jit(solution)/shard_map/ppermute | solution.py:49
  51.2 1.8 %collective-permute-start.6 = (f32[768,128]{1,0:T(8,128)S(1)}, f32[768,128]{1,0:T(8,128)S(1)}, u32[]{:S(2)}, u32[]{:S(2)}) collective-permute-start(f32[768,128]{1,0:T(8,128)S(1)} %get-tuple-element.24.b0), channel_id=1, source_target_pairs={{0,8},{1,33},{2,10},{3,35},{4,12},{5,37},{6,14},{7,39},{8,16},{9,4... | collective-permute-start | bytes 1179656 | tf_op jit(solution)/shard_map/ppermute | solution.py:45
  55.2 2.7 %shard_map.79 = (f32[144,256]{1,0:T(8,128)S(1)}, f32[144,256]{1,0:T(8,128)S(1)}, f32[144,256]{1,0:T(8,128)S(1)}) custom-call(f32[768,128]{1,0:T(8,128)S(1)} %get-tuple-element.25.b0, f32[768,128]{1,0:T(8,128)S(1)} %collective-permute-done.9.refs_2_.b1, f32[768,128]{1,0:T(8,128)S(1)} %collective-permute-done.10.refs_3_.b2, ...), custom_call_target="tpu_custom_call" | custom-call | tf_op jit(solution)/shard_map/pallas_call | solution.py:447
  58.0 2.7 %collective-permute-start.18 = (f32[144,256]{1,0:T(8,128)S(1)}, f32[144,256]{1,0:T(8,128)S(1)}, u32[]{:S(2)}, u32[]{:S(2)}) collective-permute-start(f32[144,256]{1,0:T(8,128)S(1)} %get-tuple-element.34), channel_id=1, source_target_pairs={{0,2},{1,7},{2,4},{3,1},{4,6},{5,3},{6,0},{7,5},{8,10},{9,15},{10,... | collective-permute-start | bytes 442376 | tf_op jit(solution)/shard_map/ppermute | solution.py:45
  60.7 3.9 %collective-permute-done.8.b3 = f32[768,128]{1,0:T(8,128)S(1)} collective-permute-done((f32[768,128]{1,0:T(8,128)S(1)}, f32[768,128]{1,0:T(8,128)S(1)}, u32[]{:S(2)}, u32[]{:S(2)}) %collective-permute-start.8) | collective-permute-done | bytes 393248 | tf_op jit(solution)/shard_map/ppermute | solution.py:45
  64.7 2.2 %shard_map.80 = f32[32,8,128]{2,1,0:T(8,128)} custom-call(f32[768,128]{1,0:T(8,128)S(1)} %get-tuple-element.24.b0, f32[768,128]{1,0:T(8,128)S(1)} %collective-permute-done.6.b1, f32[768,128]{1,0:T(8,128)S(1)} %collective-permute-done.7.b2, f32[768,128]{1,0:T(8,128)S(1)} %collective-permute-done.8.b3, f32[3696,128]{1,0:T(8,128)S(1)} %bitcast.6, ...), custom_call_target="tpu_custom_call" | custom-call | tf_op jit(solution)/shard_map/pallas_call | solution.py:457
  66.9 7.5 %all-to-all-start = ((f32[32,8,128]{2,1,0:T(8,128)}), f32[32,8,128]{2,1,0:T(8,128)S(1)}, u32[]{:S(2)}, u32[]{:S(2)}) async-start(f32[32,8,128]{2,1,0:T(8,128)} %shard_map.80), calls=%async_computation | async-start | bytes 262144 | tf_op jit(solution)/shard_map/all_to_all | solution.py:465
  74.4 2.8 %shard_map.81 = (f32[18,1296]{1,0:T(8,128)S(1)}, f32[18,1296]{1,0:T(8,128)S(1)}) custom-call(s32[8]{0:T(128)S(1)} %copy-done.3, s32[8]{0:T(128)S(1)} %copy-done.4, f32[8,6]{1,0:T(8,128)S(1)} %copy-done.6, f32[8,36]{1,0:T(8,128)S(1)} %copy-done.7, f32[3,6,1,1296]{3,2,1,0:T(1,128)S(1)} %copy-done.1, f32[108,1,216]{2,1,0:T(1,128)S(1)} %copy-done.5, ...), custom_call_target="tpu_custom_call" | custom-call | flops 100000000 | bytes 1000000 | tf_op jit(solution)/shard_map/pallas_call | solution.py:425
  77.2 4.8 %all-to-all-done.sums = f32[32,8,128]{2,1,0:T(8,128)S(1)} async-done(((f32[32,8,128]{2,1,0:T(8,128)}), f32[32,8,128]{2,1,0:T(8,128)S(1)}, u32[]{:S(2)}, u32[]{:S(2)}) %all-to-all-start) | async-done | bytes 131104 | tf_op jit(solution)/shard_map/all_to_all | solution.py:465
  (42 shorter events, 7.8 us)
Async XLA Ops:
  0.0 14.6 %copy-start.5 = (f32[108,1,216]{2,1,0:T(1,128)S(1)}, f32[108,1,216]{2,1,0:T(1,128)}, u32[]{:S(2)}) copy-start(f32[108,1,216]{2,1,0:T(1,128)} %ovov.1) | copy-start | bytes 279940
  5.4 15.0 %collective-permute-start.2 = (f32[3696,128]{1,0:T(8,128)}, f32[3696,128]{1,0:T(8,128)S(1)}, u32[]{:S(2)}, u32[]{:S(2)}) collective-permute-start(f32[3696,128]{1,0:T(8,128)} %bitcast.4), channel_id=1, source_target_pairs={{0,1},{1,0},{2,3},{3,2},{4,5},{5,4},{6,7},{7,6},{8,9},{9,8},{10,11... | collective-permute-start | bytes 5677064 | tf_op jit(solution)/shard_map/ppermute | solution.py:49
  6.9 3.8 %collective-permute-start = (f32[104,128]{1,0:T(8,128)}, f32[104,128]{1,0:T(8,128)S(1)}, u32[]{:S(2)}, u32[]{:S(2)}) collective-permute-start(f32[104,128]{1,0:T(8,128)} %get-tuple-element.22), channel_id=1, source_target_pairs={{0,1},{1,0},{2,3},{3,2},{4,5},{5,4},{6,7},{7,6},{8,9},{9,8},{10,11... | collective-permute-start | bytes 159752 | tf_op jit(solution)/shard_map/ppermute | solution.py:49
  11.5 7.4 %collective-permute-start.1 = (f32[192,128]{1,0:T(8,128)S(1)}, f32[192,128]{1,0:T(8,128)S(1)}, u32[]{:S(2)}, u32[]{:S(2)}) collective-permute-start(f32[192,128]{1,0:T(8,128)S(1)} %shard_map.74.near), channel_id=1, source_target_pairs={{0,4},{1,5},{2,6},{3,7},{4,0},{5,1},{6,2},{7,3},{8,12},{9,13},{10,... | collective-permute-start | bytes 294920 | tf_op jit(solution)/shard_map/ppermute | solution.py:45
  14.6 4.3 %collective-permute-start.12 = (f32[108,1,216]{2,1,0:T(1,128)S(1)}, f32[108,1,216]{2,1,0:T(1,128)S(1)}, u32[]{:S(2)}, u32[]{:S(2)}) collective-permute-start(f32[108,1,216]{2,1,0:T(1,128)S(1)} %copy-done.5), channel_id=1, source_target_pairs={{0,8},{8,0},{16,24},{24,16},{1,9},{9,1},{17,25},{25,17},{2,10},{10... | collective-permute-start | bytes 279944 | tf_op jit(solution)/shard_map/ppermute | solution.py:390
  18.9 20.7 %collective-permute-start.13 = (f32[1848,128]{1,0:T(8,128)}, f32[1848,128]{1,0:T(8,128)S(1)}, u32[]{:S(2)}, u32[]{:S(2)}) collective-permute-start(f32[1848,128]{1,0:T(8,128)} %get-tuple-element.28), channel_id=1, source_target_pairs={{0,2},{1,7},{2,4},{3,1},{4,6},{5,3},{6,0},{7,5},{8,10},{9,15},{10,... | collective-permute-start | bytes 2838536 | tf_op jit(solution)/shard_map/ppermute | solution.py:45
  19.9 23.6 %collective-permute-start.14 = (f32[1848,128]{1,0:T(8,128)}, f32[1848,128]{1,0:T(8,128)S(1)}, u32[]{:S(2)}, u32[]{:S(2)}) collective-permute-start(f32[1848,128]{1,0:T(8,128)} %get-tuple-element.29), channel_id=1, source_target_pairs={{0,6},{1,3},{2,0},{3,5},{4,2},{5,7},{6,4},{7,1},{8,14},{9,11},{10,... | collective-permute-start | bytes 2838536 | tf_op jit(solution)/shard_map/ppermute | solution.py:45
  20.4 34.7 %copy-start = (f32[42,88,1,128]{3,2,1,0:T(1,128)S(1)}, f32[42,88,1,128]{3,2,1,0:T(1,128)}, u32[]{:S(2)}) copy-start(f32[42,88,1,128]{3,2,1,0:T(1,128)} %get-tuple-element.23) | copy-start | bytes 5677060
  20.4 6.8 %collective-permute-start.3 = (f32[384,128]{1,0:T(8,128)S(1)}, f32[384,128]{1,0:T(8,128)S(1)}, u32[]{:S(2)}, u32[]{:S(2)}) collective-permute-start(f32[384,128]{1,0:T(8,128)S(1)} %shard_map.75.b0), channel_id=1, source_target_pairs={{0,32},{1,9},{2,34},{3,11},{4,36},{5,13},{6,38},{7,15},{8,40},{9,1... | collective-permute-start | bytes 589832 | tf_op jit(solution)/shard_map/ppermute | solution.py:45
  21.8 6.9 %collective-permute-start.4 = (f32[384,128]{1,0:T(8,128)S(1)}, f32[384,128]{1,0:T(8,128)S(1)}, u32[]{:S(2)}, u32[]{:S(2)}) collective-permute-start(f32[384,128]{1,0:T(8,128)S(1)} %shard_map.75.b0), channel_id=1, source_target_pairs={{0,96},{1,25},{2,98},{3,27},{4,100},{5,29},{6,102},{7,31},{8,104},... | collective-permute-start | bytes 589832 | tf_op jit(solution)/shard_map/ppermute | solution.py:45
  24.0 6.3 %collective-permute-start.5 = (f32[384,128]{1,0:T(8,128)S(1)}, f32[384,128]{1,0:T(8,128)S(1)}, u32[]{:S(2)}, u32[]{:S(2)}) collective-permute-start(f32[384,128]{1,0:T(8,128)S(1)} %shard_map.75.b0), channel_id=1, source_target_pairs={{0,64},{1,17},{2,66},{3,19},{4,68},{5,21},{6,70},{7,23},{8,72},{9,... | collective-permute-start | bytes 589832 | tf_op jit(solution)/shard_map/ppermute | solution.py:45
  30.3 13.3 %collective-permute-start.10 = (f32[768,128]{1,0:T(8,128)S(1)}, f32[768,128]{1,0:T(8,128)S(1)}, u32[]{:S(2)}, u32[]{:S(2)}) collective-permute-start(f32[768,128]{1,0:T(8,128)S(1)} %get-tuple-element.25.b0), channel_id=1, source_target_pairs={{0,24},{1,97},{2,26},{3,99},{4,28},{5,101},{6,30},{7,103},{8,0},{9... | collective-permute-start | bytes 1179656 | tf_op jit(solution)/shard_map/ppermute | solution.py:45
  33.1 10.5 %collective-permute-start.11 = (f32[768,128]{1,0:T(8,128)S(1)}, f32[768,128]{1,0:T(8,128)S(1)}, u32[]{:S(2)}, u32[]{:S(2)}) collective-permute-start(f32[768,128]{1,0:T(8,128)S(1)} %get-tuple-element.25.b0), channel_id=1, source_target_pairs={{0,16},{1,65},{2,18},{3,67},{4,20},{5,69},{6,22},{7,71},{8,24},{9,... | collective-permute-start | bytes 1179656 | tf_op jit(solution)/shard_map/ppermute | solution.py:45
  33.4 12.3 %collective-permute-start.9 = (f32[768,128]{1,0:T(8,128)S(1)}, f32[768,128]{1,0:T(8,128)S(1)}, u32[]{:S(2)}, u32[]{:S(2)}) collective-permute-start(f32[768,128]{1,0:T(8,128)S(1)} %get-tuple-element.25.b0), channel_id=1, source_target_pairs={{0,8},{1,33},{2,10},{3,35},{4,12},{5,37},{6,14},{7,39},{8,16},{9,4... | collective-permute-start | bytes 1179656 | tf_op jit(solution)/shard_map/ppermute | solution.py:45
  45.7 9.5 %collective-permute-start.15 = (f32[1848,128]{1,0:T(8,128)S(1)}, f32[1848,128]{1,0:T(8,128)S(1)}, u32[]{:S(2)}, u32[]{:S(2)}) collective-permute-start(f32[1848,128]{1,0:T(8,128)S(1)} %get-tuple-element.31.above), channel_id=1, source_target_pairs={{0,1},{1,0},{2,3},{3,2},{4,5},{5,4},{6,7},{7,6},{8,9},{9,8},{10,11... | collective-permute-start | bytes 2838536 | tf_op jit(solution)/shard_map/ppermute | solution.py:49
  51.2 3.9 %collective-permute-start.16 = (f32[1848,128]{1,0:T(8,128)S(1)}, f32[1848,128]{1,0:T(8,128)S(1)}, u32[]{:S(2)}, u32[]{:S(2)}) collective-permute-start(f32[1848,128]{1,0:T(8,128)S(1)} %get-tuple-element.30.below), channel_id=1, source_target_pairs={{0,1},{1,0},{2,3},{3,2},{4,5},{5,4},{6,7},{7,6},{8,9},{9,8},{10,11... | collective-permute-start | bytes 2838536 | tf_op jit(solution)/shard_map/ppermute | solution.py:49
  51.2 9.4 %collective-permute-start.6 = (f32[768,128]{1,0:T(8,128)S(1)}, f32[768,128]{1,0:T(8,128)S(1)}, u32[]{:S(2)}, u32[]{:S(2)}) collective-permute-start(f32[768,128]{1,0:T(8,128)S(1)} %get-tuple-element.24.b0), channel_id=1, source_target_pairs={{0,8},{1,33},{2,10},{3,35},{4,12},{5,37},{6,14},{7,39},{8,16},{9,4... | collective-permute-start | bytes 1179656 | tf_op jit(solution)/shard_map/ppermute | solution.py:45
  53.0 7.7 %collective-permute-start.7 = (f32[768,128]{1,0:T(8,128)S(1)}, f32[768,128]{1,0:T(8,128)S(1)}, u32[]{:S(2)}, u32[]{:S(2)}) collective-permute-start(f32[768,128]{1,0:T(8,128)S(1)} %get-tuple-element.24.b0), channel_id=1, source_target_pairs={{0,24},{1,97},{2,26},{3,99},{4,28},{5,101},{6,30},{7,103},{8,0},{9... | collective-permute-start | bytes 1179656 | tf_op jit(solution)/shard_map/ppermute | solution.py:45
  54.0 10.6 %collective-permute-start.8 = (f32[768,128]{1,0:T(8,128)S(1)}, f32[768,128]{1,0:T(8,128)S(1)}, u32[]{:S(2)}, u32[]{:S(2)}) collective-permute-start(f32[768,128]{1,0:T(8,128)S(1)} %get-tuple-element.24.b0), channel_id=1, source_target_pairs={{0,16},{1,65},{2,18},{3,67},{4,20},{5,69},{6,22},{7,71},{8,24},{9,... | collective-permute-start | bytes 1179656 | tf_op jit(solution)/shard_map/ppermute | solution.py:45
  57.9 6.7 %collective-permute-start.17 = (f32[144,256]{1,0:T(8,128)S(1)}, f32[144,256]{1,0:T(8,128)S(1)}, u32[]{:S(2)}, u32[]{:S(2)}) collective-permute-start(f32[144,256]{1,0:T(8,128)S(1)} %get-tuple-element.33), channel_id=1, source_target_pairs={{0,6},{1,3},{2,0},{3,5},{4,2},{5,7},{6,4},{7,1},{8,14},{9,11},{10,... | collective-permute-start | bytes 442376 | tf_op jit(solution)/shard_map/ppermute | solution.py:45
  58.0 6.6 %collective-permute-start.18 = (f32[144,256]{1,0:T(8,128)S(1)}, f32[144,256]{1,0:T(8,128)S(1)}, u32[]{:S(2)}, u32[]{:S(2)}) collective-permute-start(f32[144,256]{1,0:T(8,128)S(1)} %get-tuple-element.34), channel_id=1, source_target_pairs={{0,2},{1,7},{2,4},{3,1},{4,6},{5,3},{6,0},{7,5},{8,10},{9,15},{10,... | collective-permute-start | bytes 442376 | tf_op jit(solution)/shard_map/ppermute | solution.py:45
  64.7 9.7 %copy-start.6 = (f32[8,6]{1,0:T(8,128)S(1)}, f32[8,6]{1,0:T(8,128)}, u32[]{:S(2)}) copy-start(f32[8,6]{1,0:T(8,128)} %eps_occ_ref.1) | copy-start | bytes 580
  64.7 9.7 %copy-start.7 = (f32[8,36]{1,0:T(8,128)S(1)}, f32[8,36]{1,0:T(8,128)}, u32[]{:S(2)}) copy-start(f32[8,36]{1,0:T(8,128)} %eps_vir_ref.1) | copy-start | bytes 3460
  66.9 15.2 %all-to-all-start = ((f32[32,8,128]{2,1,0:T(8,128)}), f32[32,8,128]{2,1,0:T(8,128)S(1)}, u32[]{:S(2)}, u32[]{:S(2)}) async-start(f32[32,8,128]{2,1,0:T(8,128)} %shard_map.80), calls=%async_computation | async-start | bytes 262144 | tf_op jit(solution)/shard_map/all_to_all | solution.py:465
  (4 other events, 30.0 us)

commit v7 on v6

--- a/solution.py
+++ b/solution.py
@@ -156,7 +156,7 @@
     out[extra + SPAN : at + PAIR, :] = jnp.zeros((PAIR - PMAIN - SPAN, LANES), F32)
 
 
-def merge_pair(keep, got, out):
+def merge_pair(keep, got, home, out, home_out):
     core = lax.axis_index("core")
 
     @pl.when(core == 0)
@@ -183,15 +183,16 @@
     pass
 
 
-def hold(a, b, *witnesses):
+def hold(values, *witnesses):
+    kept = range(len(values))
     return pl.pallas_call(
         nothing,
-        out_shape=[jax.ShapeDtypeStruct(v.shape, v.dtype) for v in (a, b)],
-        in_specs=[ANY] * (2 + len(witnesses)),
-        out_specs=[ANY] * 2,
-        input_output_aliases={0: 0, 1: 1},
-        compiler_params=SMALL,
-    )(a, b, *witnesses)
+        out_shape=[jax.ShapeDtypeStruct(value.shape, value.dtype) for value in values],
+        in_specs=[ANY] * (len(values) + len(witnesses)),
+        out_specs=[ANY] * len(values),
+        input_output_aliases={at: at for at in kept},
+        compiler_params=SMALL,
+    )(*values, *witnesses)
 
 
 def left_side(blocks, extra):
@@ -385,16 +386,18 @@
         compiler_params=HUGE,
     )(occ_count, vir_count, amplitudes, integrals)
     got = swap_core(send)
+    moved_a = ring(flat(first_v), "yy", (1, -1))
+    partner = lax.ppermute(ovov, "z", [(0, 1), (1, 0), (2, 3), (3, 2)])
     home = home.reshape(2 * PROWS, LANES)
+    pair, home = pl.pallas_call(
+        merge_pair,
+        out_shape=[shape((PAIR, LANES), F32), shape(home.shape, F32)],
+        in_specs=[VMEM] * 2 + [ANY],
+        out_specs=[VMEM, ANY],
+        input_output_aliases={2: 1},
+        compiler_params=SMALL,
+    )(keep, got, home)
     home_other = swap_core(home)
-    partner = lax.ppermute(ovov, "z", [(0, 1), (1, 0), (2, 3), (3, 2)])
-    pair = pl.pallas_call(
-        merge_pair,
-        out_shape=shape((PAIR, LANES), F32),
-        in_specs=[VMEM] * 2,
-        out_specs=VMEM,
-        compiler_params=SMALL,
-    )(keep, got)
     far_pair = ring(pair, "yy", (2, 2))
     quad = pl.pallas_call(
         join_pairs,
@@ -403,10 +406,7 @@
         out_specs=VMEM,
         compiler_params=SMALL,
     )(pair, far_pair, home_other)
-    first_v, second_v = hold(
-        flat(first_v), flat(second_v), far_pair, partner
-    )
-    moved_a = ring(first_v, "yy", (1, -1))
+    (second_v,) = hold([flat(second_v)], far_pair, partner)
     moved_b = ring(second_v, "yy", (-1, 1))
 
     near, far = pl.pallas_call(
@@ -419,7 +419,7 @@
     near_blocks = [near] + [ring(near, "zx", step) for step in SHIFTS]
     far_blocks = [far] + [ring(far, "zx", step) for step in SHIFTS]
 
-    moved_a, moved_b = hold(moved_a, moved_b, *near_blocks[1:])
+    moved_a, moved_b = hold([moved_a, moved_b], *near_blocks[1:])
     swapped_a, swapped_b = swap_core(moved_a), swap_core(moved_b)
 
     scale, cycle = pl.pallas_call(

time: 83.2 us -> 81.4 us (0.978)
  Pallas kernels: 14.2 us -> 17.3 us
  waiting for transfers between devices: 31.9 us -> 28.8 us
  starting transfers between devices: 35.8 us -> 34 us
    ppermute x4, waiting for transfers between devices: 3.7 us -> 1.5 us  [swap_core(): return lax.ppermute(value, 'core', [(0, 1), (1, 0)])]
    pallas_call x1, Pallas kernels: 2.22 us -> 3.84 us  [on_device(): pl.pallas_call(multiply_far, out_shape=shape((32, 8, LANES), F32), in_spe...]
    pallas_call x1, Pallas kernels: 2.74 us -> 4.29 us  [on_device(): pl.pallas_call(multiply_near, out_shape=sums, in_specs=[VMEM] * 10, out_s...]
    ppermute x14, starting transfers between devices: 19.6 us -> 18.1 us  [ring(): return lax.ppermute(value, AXES, pairs)]
  transfers between devices with their start and end apart: 20 -> 20, of which waited for: 11 -> 13; matrix products, arithmetic and copies ran while one was open for 0% -> 0% of each run, Pallas kernels for 7% -> 9%
where the time goes in v7:
time: 81.4 us; the launch traced here: 81.1 us
  starting transfers between devices  34 us (42%)
  waiting for transfers between devices  28.8 us (35%)
  Pallas kernels  17.3 us (21%)
  local copies, waits for them, and re-layouts  0.84 us (1%)
    ppermute x14, waiting for transfers between devices, ring(): return lax.ppermute(value, AXES, pairs)  20.3 us
    ppermute x14, starting transfers between devices, ring(): return lax.ppermute(value, AXES, pairs)  18.1 us
    all_to_all x1, starting transfers between devices, on_device(): ladder = lax.all_to_all(packed, ('x', 'z', 'core'), 0, 0, tiled=True)  7.33 us
    ppermute x4, starting transfers between devices, swap_core(): return lax.ppermute(value, 'core', [(0, 1), (1, 0)])  6.92 us
    pallas_call x1, Pallas kernels, on_device(): pl.pallas_call(open_step, out_shape=[shape((SHARD, LANES), F32)] * 2 + [w...  5.41 us
    all_to_all x1, waiting for transfers between devices, on_device(): ladder = lax.all_to_all(packed, ('x', 'z', 'core'), 0, 0, tiled=True)  4.82 us
    pallas_call x1, Pallas kernels, on_device(): pl.pallas_call(multiply_near, out_shape=sums, in_specs=[VMEM] * 10, out_s...  4.29 us
    pallas_call x1, Pallas kernels, on_device(): pl.pallas_call(multiply_far, out_shape=shape((32, 8, LANES), F32), in_spe...  3.84 us
  transfers between devices with their start and end apart: 20, of which 13 were waited for; matrix products, arithmetic and copies ran while one was open for 0% of the time, Pallas kernels for 9%

profile of v7, /device:TPU:1, one launch (start us, length us, event | category | flops | bytes accessed | tf_op | source)
XLA Modules:
  0.0 81.1 jit_solution(7646256473760132751)
XLA Ops:
  0.0 5.4 %shard_map.73 = (f32[104,128]{1,0:T(8,128)}, f32[104,128]{1,0:T(8,128)}, f32[21,88,1,128]{3,2,1,0:T(1,128)}, f32[21,88,1,128]{3,2,1,0:T(1,128)}, f32[42,88,1,128]{3,2,1,0:T(1,128)}) custom-call(s32[8]{0:T(128)} %occ_ref.3, s32[8]{0:T(128)} %vir_ref.3, f32[3,6,1,1296]{3,2,1,0:T(1,128)} %amp_ref.3, f32[81,1,10368]{2,1,0:T(1,128)} %bitcast.5), custom_call_target="tpu_custom_call" | custom-call | tf_op jit(solution)/shard_map/pallas_call | solution.py:366
  5.4 1.5 %collective-permute-start = (f32[104,128]{1,0:T(8,128)}, f32[104,128]{1,0:T(8,128)S(1)}, u32[]{:S(2)}, u32[]{:S(2)}) collective-permute-start(f32[104,128]{1,0:T(8,128)} %get-tuple-element.22), channel_id=1, source_target_pairs={{0,1},{1,0},{2,3},{3,2},{4,5},{5,4},{6,7},{7,6},{8,9},{9,8},{10,11... | collective-permute-start | bytes 159752 | tf_op jit(solution)/shard_map/ppermute | solution.py:49
  9.3 3.0 %collective-permute-start.1 = (f32[192,128]{1,0:T(8,128)S(1)}, f32[192,128]{1,0:T(8,128)S(1)}, u32[]{:S(2)}, u32[]{:S(2)}) collective-permute-start(f32[192,128]{1,0:T(8,128)S(1)} %get-tuple-element.24.near), channel_id=1, source_target_pairs={{0,4},{1,5},{2,6},{3,7},{4,0},{5,1},{6,2},{7,3},{8,12},{9,13},{10,... | collective-permute-start | bytes 294920 | tf_op jit(solution)/shard_map/ppermute | solution.py:45
  12.3 1.6 %collective-permute-start.13 = (f32[108,1,216]{2,1,0:T(1,128)S(1)}, f32[108,1,216]{2,1,0:T(1,128)S(1)}, u32[]{:S(2)}, u32[]{:S(2)}) collective-permute-start(f32[108,1,216]{2,1,0:T(1,128)S(1)} %copy-done.5), channel_id=1, source_target_pairs={{0,8},{8,0},{16,24},{24,16},{1,9},{9,1},{17,25},{25,17},{2,10},{10... | collective-permute-start | bytes 279944 | tf_op jit(solution)/shard_map/ppermute | solution.py:390
  14.7 2.2 %collective-permute-done.13.refs_2_.partner = f32[108,1,216]{2,1,0:T(1,128)S(1)} collective-permute-done((f32[108,1,216]{2,1,0:T(1,128)S(1)}, f32[108,1,216]{2,1,0:T(1,128)S(1)}, u32[]{:S(2)}, u32[]{:S(2)}) %collective-permute-start.13) | collective-permute-done | bytes 93344 | tf_op jit(solution)/shard_map/ppermute | solution.py:390
  17.3 1.3 %collective-permute-start.3 = (f32[384,128]{1,0:T(8,128)S(1)}, f32[384,128]{1,0:T(8,128)S(1)}, u32[]{:S(2)}, u32[]{:S(2)}) collective-permute-start(f32[384,128]{1,0:T(8,128)S(1)} %shard_map.75.b0), channel_id=1, source_target_pairs={{0,32},{1,9},{2,34},{3,11},{4,36},{5,13},{6,38},{7,15},{8,40},{9,1... | collective-permute-start | bytes 589832 | tf_op jit(solution)/shard_map/ppermute | solution.py:45
  18.6 2.2 %collective-permute-start.4 = (f32[384,128]{1,0:T(8,128)S(1)}, f32[384,128]{1,0:T(8,128)S(1)}, u32[]{:S(2)}, u32[]{:S(2)}) collective-permute-start(f32[384,128]{1,0:T(8,128)S(1)} %shard_map.75.b0), channel_id=1, source_target_pairs={{0,96},{1,25},{2,98},{3,27},{4,100},{5,29},{6,102},{7,31},{8,104},... | collective-permute-start | bytes 589832 | tf_op jit(solution)/shard_map/ppermute | solution.py:45
  20.8 1.2 %collective-permute-start.5 = (f32[384,128]{1,0:T(8,128)S(1)}, f32[384,128]{1,0:T(8,128)S(1)}, u32[]{:S(2)}, u32[]{:S(2)}) collective-permute-start(f32[384,128]{1,0:T(8,128)S(1)} %shard_map.75.b0), channel_id=1, source_target_pairs={{0,64},{1,17},{2,66},{3,19},{4,68},{5,21},{6,70},{7,23},{8,72},{9,... | collective-permute-start | bytes 589832 | tf_op jit(solution)/shard_map/ppermute | solution.py:45
  22.0 2.0 %collective-permute-done.3.b1 = f32[384,128]{1,0:T(8,128)S(1)} collective-permute-done((f32[384,128]{1,0:T(8,128)S(1)}, f32[384,128]{1,0:T(8,128)S(1)}, u32[]{:S(2)}, u32[]{:S(2)}) %collective-permute-start.3) | collective-permute-done | bytes 196640 | tf_op jit(solution)/shard_map/ppermute | solution.py:45
  24.1 1.4 %collective-permute-done.4.b2 = f32[384,128]{1,0:T(8,128)S(1)} collective-permute-done((f32[384,128]{1,0:T(8,128)S(1)}, f32[384,128]{1,0:T(8,128)S(1)}, u32[]{:S(2)}, u32[]{:S(2)}) %collective-permute-start.4) | collective-permute-done | bytes 196640 | tf_op jit(solution)/shard_map/ppermute | solution.py:45
  25.5 1.8 %collective-permute-done.5.b3 = f32[384,128]{1,0:T(8,128)S(1)} collective-permute-done((f32[384,128]{1,0:T(8,128)S(1)}, f32[384,128]{1,0:T(8,128)S(1)}, u32[]{:S(2)}, u32[]{:S(2)}) %collective-permute-start.5) | collective-permute-done | bytes 196640 | tf_op jit(solution)/shard_map/ppermute | solution.py:45
  27.4 2.5 %collective-permute-start.10 = (f32[768,128]{1,0:T(8,128)S(1)}, f32[768,128]{1,0:T(8,128)S(1)}, u32[]{:S(2)}, u32[]{:S(2)}) collective-permute-start(f32[768,128]{1,0:T(8,128)S(1)} %get-tuple-element.27.b0), channel_id=1, source_target_pairs={{0,24},{1,97},{2,26},{3,99},{4,28},{5,101},{6,30},{7,103},{8,0},{9... | collective-permute-start | bytes 1179656 | tf_op jit(solution)/shard_map/ppermute | solution.py:45
  30.8 1.6 %collective-permute-done.12.refs_0_ = f32[1848,128]{1,0:T(8,128)S(1)} collective-permute-done((f32[1848,128]{1,0:T(8,128)S(1)}, f32[1848,128]{1,0:T(8,128)S(1)}, u32[]{:S(2)}, u32[]{:S(2)}) %collective-permute-start.12) | collective-permute-done | bytes 946208 | tf_op jit(solution)/shard_map/ppermute | solution.py:45
  32.4 6.9 %collective-permute-done.14.refs_1_ = f32[1848,128]{1,0:T(8,128)S(1)} collective-permute-done((f32[1848,128]{1,0:T(8,128)S(1)}, f32[1848,128]{1,0:T(8,128)S(1)}, u32[]{:S(2)}, u32[]{:S(2)}) %collective-permute-start.14) | collective-permute-done | bytes 946208 | tf_op jit(solution)/shard_map/ppermute | solution.py:45
  39.3 3.2 %collective-permute-done.9.refs_2_.b1 = f32[768,128]{1,0:T(8,128)S(1)} collective-permute-done((f32[768,128]{1,0:T(8,128)S(1)}, f32[768,128]{1,0:T(8,128)S(1)}, u32[]{:S(2)}, u32[]{:S(2)}) %collective-permute-start.9) | collective-permute-done | bytes 393248 | tf_op jit(solution)/shard_map/ppermute | solution.py:45
  42.6 5.0 %collective-permute-start.15 = (f32[1848,128]{1,0:T(8,128)S(1)}, f32[1848,128]{1,0:T(8,128)S(1)}, u32[]{:S(2)}, u32[]{:S(2)}) collective-permute-start(f32[1848,128]{1,0:T(8,128)S(1)} %get-tuple-element.31.above), channel_id=1, source_target_pairs={{0,1},{1,0},{2,3},{3,2},{4,5},{5,4},{6,7},{7,6},{8,9},{9,8},{10,11... | collective-permute-start | bytes 2838536 | tf_op jit(solution)/shard_map/ppermute | solution.py:49
  48.5 1.7 %collective-permute-start.7 = (f32[768,128]{1,0:T(8,128)S(1)}, f32[768,128]{1,0:T(8,128)S(1)}, u32[]{:S(2)}, u32[]{:S(2)}) collective-permute-start(f32[768,128]{1,0:T(8,128)S(1)} %get-tuple-element.26.b0), channel_id=1, source_target_pairs={{0,24},{1,97},{2,26},{3,99},{4,28},{5,101},{6,30},{7,103},{8,0},{9... | collective-permute-start | bytes 1179656 | tf_op jit(solution)/shard_map/ppermute | solution.py:45
  51.0 4.3 %shard_map.79 = (f32[144,256]{1,0:T(8,128)S(1)}, f32[144,256]{1,0:T(8,128)S(1)}, f32[144,256]{1,0:T(8,128)S(1)}) custom-call(f32[768,128]{1,0:T(8,128)S(1)} %get-tuple-element.27.b0, f32[768,128]{1,0:T(8,128)S(1)} %collective-permute-done.9.refs_2_.b1, f32[768,128]{1,0:T(8,128)S(1)} %collective-permute-done.10.refs_3_.b2, ...), custom_call_target="tpu_custom_call" | custom-call | tf_op jit(solution)/shard_map/pallas_call | solution.py:447
  55.4 2.7 %collective-permute-start.18 = (f32[144,256]{1,0:T(8,128)S(1)}, f32[144,256]{1,0:T(8,128)S(1)}, u32[]{:S(2)}, u32[]{:S(2)}) collective-permute-start(f32[144,256]{1,0:T(8,128)S(1)} %get-tuple-element.34), channel_id=1, source_target_pairs={{0,2},{1,7},{2,4},{3,1},{4,6},{5,3},{6,0},{7,5},{8,10},{9,15},{10,... | collective-permute-start | bytes 442376 | tf_op jit(solution)/shard_map/ppermute | solution.py:45
  60.2 1.1 %collective-permute-done.17.back_a = f32[144,256]{1,0:T(8,128)S(1)} collective-permute-done((f32[144,256]{1,0:T(8,128)S(1)}, f32[144,256]{1,0:T(8,128)S(1)}, u32[]{:S(2)}, u32[]{:S(2)}) %collective-permute-start.17) | collective-permute-done | bytes 147488 | tf_op jit(solution)/shard_map/ppermute | solution.py:45
  61.4 3.8 %shard_map.80 = f32[32,8,128]{2,1,0:T(8,128)} custom-call(f32[768,128]{1,0:T(8,128)S(1)} %get-tuple-element.26.b0, f32[768,128]{1,0:T(8,128)S(1)} %collective-permute-done.6.b1, f32[768,128]{1,0:T(8,128)S(1)} %collective-permute-done.7.b2, f32[768,128]{1,0:T(8,128)S(1)} %collective-permute-done.8.b3, f32[3696,128]{1,0:T(8,128)} %get-tuple-element.25.home, ...), custom_call_target="tpu_custom_call" | custom-call | tf_op jit(solution)/shard_map/pallas_call | solution.py:457
  65.2 7.3 %all-to-all-start = ((f32[32,8,128]{2,1,0:T(8,128)}), f32[32,8,128]{2,1,0:T(8,128)S(1)}, u32[]{:S(2)}, u32[]{:S(2)}) async-start(f32[32,8,128]{2,1,0:T(8,128)} %shard_map.80), calls=%async_computation | async-start | bytes 262144 | tf_op jit(solution)/shard_map/all_to_all | solution.py:465
  72.6 2.8 %shard_map.81 = (f32[18,1296]{1,0:T(8,128)S(1)}, f32[18,1296]{1,0:T(8,128)S(1)}) custom-call(s32[8]{0:T(128)S(1)} %copy-done.3, s32[8]{0:T(128)S(1)} %copy-done.4, f32[8,6]{1,0:T(8,128)S(1)} %copy-done.6, f32[8,36]{1,0:T(8,128)S(1)} %copy-done.7, f32[3,6,1,1296]{3,2,1,0:T(1,128)S(1)} %copy-done.1, f32[108,1,216]{2,1,0:T(1,128)S(1)} %copy-done.5, ...), custom_call_target="tpu_custom_call" | custom-call | flops 100000000 | bytes 1000000 | tf_op jit(solution)/shard_map/pallas_call | solution.py:425
  75.4 4.8 %all-to-all-done.sums = f32[32,8,128]{2,1,0:T(8,128)S(1)} async-done(((f32[32,8,128]{2,1,0:T(8,128)}), f32[32,8,128]{2,1,0:T(8,128)S(1)}, u32[]{:S(2)}, u32[]{:S(2)}) %all-to-all-start) | async-done | bytes 131104 | tf_op jit(solution)/shard_map/all_to_all | solution.py:465
  (44 shorter events, 9.3 us)
Async XLA Ops:
  0.0 12.3 %copy-start.5 = (f32[108,1,216]{2,1,0:T(1,128)S(1)}, f32[108,1,216]{2,1,0:T(1,128)}, u32[]{:S(2)}) copy-start(f32[108,1,216]{2,1,0:T(1,128)} %ovov.1) | copy-start | bytes 279940
  5.4 11.4 %copy-start = (f32[21,88,1,128]{3,2,1,0:T(1,128)S(1)}, f32[21,88,1,128]{3,2,1,0:T(1,128)}, u32[]{:S(2)}) copy-start(f32[21,88,1,128]{3,2,1,0:T(1,128)} %get-tuple-element.29) | copy-start | bytes 2838532
  5.4 2.6 %collective-permute-start = (f32[104,128]{1,0:T(8,128)}, f32[104,128]{1,0:T(8,128)S(1)}, u32[]{:S(2)}, u32[]{:S(2)}) collective-permute-start(f32[104,128]{1,0:T(8,128)} %get-tuple-element.22), channel_id=1, source_target_pairs={{0,1},{1,0},{2,3},{3,2},{4,5},{5,4},{6,7},{7,6},{8,9},{9,8},{10,11... | collective-permute-start | bytes 159752 | tf_op jit(solution)/shard_map/ppermute | solution.py:49
  8.9 8.4 %collective-permute-start.2 = (f32[3696,128]{1,0:T(8,128)}, f32[3696,128]{1,0:T(8,128)S(1)}, u32[]{:S(2)}, u32[]{:S(2)}) collective-permute-start(f32[3696,128]{1,0:T(8,128)} %get-tuple-element.25.home), channel_id=1, source_target_pairs={{0,1},{1,0},{2,3},{3,2},{4,5},{5,4},{6,7},{7,6},{8,9},{9,8},{10,11... | collective-permute-start | bytes 5677064 | tf_op jit(solution)/shard_map/ppermute | solution.py:49
  9.3 7.6 %collective-permute-start.1 = (f32[192,128]{1,0:T(8,128)S(1)}, f32[192,128]{1,0:T(8,128)S(1)}, u32[]{:S(2)}, u32[]{:S(2)}) collective-permute-start(f32[192,128]{1,0:T(8,128)S(1)} %get-tuple-element.24.near), channel_id=1, source_target_pairs={{0,4},{1,5},{2,6},{3,7},{4,0},{5,1},{6,2},{7,3},{8,12},{9,13},{10,... | collective-permute-start | bytes 294920 | tf_op jit(solution)/shard_map/ppermute | solution.py:45
  12.3 4.6 %collective-permute-start.13 = (f32[108,1,216]{2,1,0:T(1,128)S(1)}, f32[108,1,216]{2,1,0:T(1,128)S(1)}, u32[]{:S(2)}, u32[]{:S(2)}) collective-permute-start(f32[108,1,216]{2,1,0:T(1,128)S(1)} %copy-done.5), channel_id=1, source_target_pairs={{0,8},{8,0},{16,24},{24,16},{1,9},{9,1},{17,25},{25,17},{2,10},{10... | collective-permute-start | bytes 279944 | tf_op jit(solution)/shard_map/ppermute | solution.py:390
  13.9 18.4 %collective-permute-start.12 = (f32[1848,128]{1,0:T(8,128)S(1)}, f32[1848,128]{1,0:T(8,128)S(1)}, u32[]{:S(2)}, u32[]{:S(2)}) collective-permute-start(f32[1848,128]{1,0:T(8,128)S(1)} %bitcast.6), channel_id=1, source_target_pairs={{0,2},{1,7},{2,4},{3,1},{4,6},{5,3},{6,0},{7,5},{8,10},{9,15},{10,... | collective-permute-start | bytes 2838536 | tf_op jit(solution)/shard_map/ppermute | solution.py:45
  16.9 22.4 %collective-permute-start.14 = (f32[1848,128]{1,0:T(8,128)S(1)}, f32[1848,128]{1,0:T(8,128)S(1)}, u32[]{:S(2)}, u32[]{:S(2)}) collective-permute-start(f32[1848,128]{1,0:T(8,128)S(1)} %shard_map.77), channel_id=1, source_target_pairs={{0,6},{1,3},{2,0},{3,5},{4,2},{5,7},{6,4},{7,1},{8,14},{9,11},{10,... | collective-permute-start | bytes 2838536 | tf_op jit(solution)/shard_map/ppermute | solution.py:45
  17.3 6.8 %collective-permute-start.3 = (f32[384,128]{1,0:T(8,128)S(1)}, f32[384,128]{1,0:T(8,128)S(1)}, u32[]{:S(2)}, u32[]{:S(2)}) collective-permute-start(f32[384,128]{1,0:T(8,128)S(1)} %shard_map.75.b0), channel_id=1, source_target_pairs={{0,32},{1,9},{2,34},{3,11},{4,36},{5,13},{6,38},{7,15},{8,40},{9,1... | collective-permute-start | bytes 589832 | tf_op jit(solution)/shard_map/ppermute | solution.py:45
  18.6 6.9 %collective-permute-start.4 = (f32[384,128]{1,0:T(8,128)S(1)}, f32[384,128]{1,0:T(8,128)S(1)}, u32[]{:S(2)}, u32[]{:S(2)}) collective-permute-start(f32[384,128]{1,0:T(8,128)S(1)} %shard_map.75.b0), channel_id=1, source_target_pairs={{0,96},{1,25},{2,98},{3,27},{4,100},{5,29},{6,102},{7,31},{8,104},... | collective-permute-start | bytes 589832 | tf_op jit(solution)/shard_map/ppermute | solution.py:45
  20.8 6.6 %collective-permute-start.5 = (f32[384,128]{1,0:T(8,128)S(1)}, f32[384,128]{1,0:T(8,128)S(1)}, u32[]{:S(2)}, u32[]{:S(2)}) collective-permute-start(f32[384,128]{1,0:T(8,128)S(1)} %shard_map.75.b0), channel_id=1, source_target_pairs={{0,64},{1,17},{2,66},{3,19},{4,68},{5,21},{6,70},{7,23},{8,72},{9,... | collective-permute-start | bytes 589832 | tf_op jit(solution)/shard_map/ppermute | solution.py:45
  27.4 11.9 %collective-permute-start.10 = (f32[768,128]{1,0:T(8,128)S(1)}, f32[768,128]{1,0:T(8,128)S(1)}, u32[]{:S(2)}, u32[]{:S(2)}) collective-permute-start(f32[768,128]{1,0:T(8,128)S(1)} %get-tuple-element.27.b0), channel_id=1, source_target_pairs={{0,24},{1,97},{2,26},{3,99},{4,28},{5,101},{6,30},{7,103},{8,0},{9... | collective-permute-start | bytes 1179656 | tf_op jit(solution)/shard_map/ppermute | solution.py:45
  30.0 9.3 %collective-permute-start.11 = (f32[768,128]{1,0:T(8,128)S(1)}, f32[768,128]{1,0:T(8,128)S(1)}, u32[]{:S(2)}, u32[]{:S(2)}) collective-permute-start(f32[768,128]{1,0:T(8,128)S(1)} %get-tuple-element.27.b0), channel_id=1, source_target_pairs={{0,16},{1,65},{2,18},{3,67},{4,20},{5,69},{6,22},{7,71},{8,24},{9,... | collective-permute-start | bytes 1179656 | tf_op jit(solution)/shard_map/ppermute | solution.py:45
  30.2 12.3 %collective-permute-start.9 = (f32[768,128]{1,0:T(8,128)S(1)}, f32[768,128]{1,0:T(8,128)S(1)}, u32[]{:S(2)}, u32[]{:S(2)}) collective-permute-start(f32[768,128]{1,0:T(8,128)S(1)} %get-tuple-element.27.b0), channel_id=1, source_target_pairs={{0,8},{1,33},{2,10},{3,35},{4,12},{5,37},{6,14},{7,39},{8,16},{9,4... | collective-permute-start | bytes 1179656 | tf_op jit(solution)/shard_map/ppermute | solution.py:45
  42.6 8.1 %collective-permute-start.15 = (f32[1848,128]{1,0:T(8,128)S(1)}, f32[1848,128]{1,0:T(8,128)S(1)}, u32[]{:S(2)}, u32[]{:S(2)}) collective-permute-start(f32[1848,128]{1,0:T(8,128)S(1)} %get-tuple-element.31.above), channel_id=1, source_target_pairs={{0,1},{1,0},{2,3},{3,2},{4,5},{5,4},{6,7},{7,6},{8,9},{9,8},{10,11... | collective-permute-start | bytes 2838536 | tf_op jit(solution)/shard_map/ppermute | solution.py:49
  47.5 3.5 %collective-permute-start.16 = (f32[1848,128]{1,0:T(8,128)S(1)}, f32[1848,128]{1,0:T(8,128)S(1)}, u32[]{:S(2)}, u32[]{:S(2)}) collective-permute-start(f32[1848,128]{1,0:T(8,128)S(1)} %get-tuple-element.30.below), channel_id=1, source_target_pairs={{0,1},{1,0},{2,3},{3,2},{4,5},{5,4},{6,7},{7,6},{8,9},{9,8},{10,11... | collective-permute-start | bytes 2838536 | tf_op jit(solution)/shard_map/ppermute | solution.py:49
  47.5 10.5 %collective-permute-start.6 = (f32[768,128]{1,0:T(8,128)S(1)}, f32[768,128]{1,0:T(8,128)S(1)}, u32[]{:S(2)}, u32[]{:S(2)}) collective-permute-start(f32[768,128]{1,0:T(8,128)S(1)} %get-tuple-element.26.b0), channel_id=1, source_target_pairs={{0,8},{1,33},{2,10},{3,35},{4,12},{5,37},{6,14},{7,39},{8,16},{9,4... | collective-permute-start | bytes 1179656 | tf_op jit(solution)/shard_map/ppermute | solution.py:45
  48.5 10.7 %collective-permute-start.7 = (f32[768,128]{1,0:T(8,128)S(1)}, f32[768,128]{1,0:T(8,128)S(1)}, u32[]{:S(2)}, u32[]{:S(2)}) collective-permute-start(f32[768,128]{1,0:T(8,128)S(1)} %get-tuple-element.26.b0), channel_id=1, source_target_pairs={{0,24},{1,97},{2,26},{3,99},{4,28},{5,101},{6,30},{7,103},{8,0},{9... | collective-permute-start | bytes 1179656 | tf_op jit(solution)/shard_map/ppermute | solution.py:45
  50.2 10.0 %collective-permute-start.8 = (f32[768,128]{1,0:T(8,128)S(1)}, f32[768,128]{1,0:T(8,128)S(1)}, u32[]{:S(2)}, u32[]{:S(2)}) collective-permute-start(f32[768,128]{1,0:T(8,128)S(1)} %get-tuple-element.26.b0), channel_id=1, source_target_pairs={{0,16},{1,65},{2,18},{3,67},{4,20},{5,69},{6,22},{7,71},{8,24},{9,... | collective-permute-start | bytes 1179656 | tf_op jit(solution)/shard_map/ppermute | solution.py:45
  55.3 6.0 %collective-permute-start.17 = (f32[144,256]{1,0:T(8,128)S(1)}, f32[144,256]{1,0:T(8,128)S(1)}, u32[]{:S(2)}, u32[]{:S(2)}) collective-permute-start(f32[144,256]{1,0:T(8,128)S(1)} %get-tuple-element.33), channel_id=1, source_target_pairs={{0,6},{1,3},{2,0},{3,5},{4,2},{5,7},{6,4},{7,1},{8,14},{9,11},{10,... | collective-permute-start | bytes 442376 | tf_op jit(solution)/shard_map/ppermute | solution.py:45
  55.4 5.9 %collective-permute-start.18 = (f32[144,256]{1,0:T(8,128)S(1)}, f32[144,256]{1,0:T(8,128)S(1)}, u32[]{:S(2)}, u32[]{:S(2)}) collective-permute-start(f32[144,256]{1,0:T(8,128)S(1)} %get-tuple-element.34), channel_id=1, source_target_pairs={{0,2},{1,7},{2,4},{3,1},{4,6},{5,3},{6,0},{7,5},{8,10},{9,15},{10,... | collective-permute-start | bytes 442376 | tf_op jit(solution)/shard_map/ppermute | solution.py:45
  61.3 11.2 %copy-start.6 = (f32[8,6]{1,0:T(8,128)S(1)}, f32[8,6]{1,0:T(8,128)}, u32[]{:S(2)}) copy-start(f32[8,6]{1,0:T(8,128)} %eps_occ_ref.1) | copy-start | bytes 580
  61.4 11.2 %copy-start.7 = (f32[8,36]{1,0:T(8,128)S(1)}, f32[8,36]{1,0:T(8,128)}, u32[]{:S(2)}) copy-start(f32[8,36]{1,0:T(8,128)} %eps_vir_ref.1) | copy-start | bytes 3460
  65.2 15.0 %all-to-all-start = ((f32[32,8,128]{2,1,0:T(8,128)}), f32[32,8,128]{2,1,0:T(8,128)S(1)}, u32[]{:S(2)}, u32[]{:S(2)}) async-start(f32[32,8,128]{2,1,0:T(8,128)} %shard_map.80), calls=%async_computation | async-start | bytes 262144 | tf_op jit(solution)/shard_map/all_to_all | solution.py:465
  (5 other events, 39.6 us)

commit v8 on v7

--- a/solution.py
+++ b/solution.py
@@ -225,11 +225,26 @@
     return lax.dot_general(p, q, (((1,), (1,)), ((), ())), preferred_element_type=F32)
 
 
-def multiply_near(b0, b1, b2, b3, home, home_other, below, below_other, above, above_other,
+def split_home(home, home_other, witness, near_high, near_low, far_high, far_low):
+    for side, ref in enumerate((home, home_other)):
+        high, low = split(tiles_side(ref, 0))
+        rows = slice(side * PSLOT, (side + 1) * PSLOT)
+        near_high[rows, :] = high
+        near_low[rows, :] = low
+        high, low = split(tiles_side(ref, SPAN))
+        pad = jnp.zeros((LANES - PSLOT, DEPTH), BF16)
+        rows = slice(side * LANES, (side + 1) * LANES)
+        far_high[rows, :] = jnp.concatenate([high, pad], axis=0)
+        far_low[rows, :] = jnp.concatenate([low, pad], axis=0)
+
+
+def multiply_near(b0, b1, b2, b3, near_high, near_low, below, below_other, above, above_other,
                   here_sum, below_sum, above_sum, extra, turned):
     high, low = left_side((b0, b1, b2, b3), extra)
-    sides = [tiles_side(ref, 0) for ref in (home, home_other, below, below_other, above, above_other)]
+    sides = [tiles_side(ref, 0) for ref in (below, below_other, above, above_other)]
     v_high, v_low = split(jnp.concatenate(sides, axis=0))
+    v_high = jnp.concatenate([near_high[...], v_high], axis=0)
+    v_low = jnp.concatenate([near_low[...], v_low], axis=0)
     total = last_by_last(v_high, high) + (last_by_last(v_low, high) + last_by_last(v_high, low))
     turned[...] = jnp.zeros_like(turned)
     for at, ref in enumerate((here_sum, below_sum, above_sum)):
@@ -239,18 +254,14 @@
             ref[:, side * LANES : (side + 1) * LANES] = turned[...].T[0:144, :]
 
 
-def multiply_far(b0, b1, b2, b3, home, home_other, here_sum, back_a, back_b, out, extra):
+def multiply_far(b0, b1, b2, b3, v_high, v_low, here_sum, back_a, back_b, out, extra):
     x, z, y, core = places()
     high, low = left_side((b0, b1, b2, b3), extra)
     partial = here_sum[...] + back_a[...] + back_b[...]
     row = lax.broadcasted_iota(jnp.int32, (8, LANES), 0)
     lane = lax.broadcasted_iota(jnp.int32, (8, LANES), 1)
-    pad = jnp.zeros((LANES - PSLOT, DEPTH), BF16)
-    sides = [split(tiles_side(ref, SPAN)) for ref in (home, home_other)]
-    v_high = jnp.concatenate([sides[0][0], pad, sides[1][0], pad], axis=0)
-    v_low = jnp.concatenate([sides[0][1], pad, sides[1][1], pad], axis=0)
     total = partial + (
-        last_by_last(high, v_high) + (last_by_last(low, v_high) + last_by_last(high, v_low))
+        last_by_last(high, v_high[...]) + (last_by_last(low, v_high[...]) + last_by_last(high, v_low[...]))
     )
     for side in range(2):
         columns = slice(side * LANES, (side + 1) * LANES)
@@ -406,7 +417,7 @@
         out_specs=VMEM,
         compiler_params=SMALL,
     )(pair, far_pair, home_other)
-    (second_v,) = hold([flat(second_v)], far_pair, partner)
+    (second_v,) = hold([flat(second_v)], far_pair)
     moved_b = ring(second_v, "yy", (-1, 1))
 
     near, far = pl.pallas_call(
@@ -416,10 +427,18 @@
         out_specs=[VMEM] * 2,
         compiler_params=SMALL,
     )(quad, *[ring(quad, "xz", step) for step in SHIFTS])
+    near_high, near_low, far_high, far_low = pl.pallas_call(
+        split_home,
+        out_shape=[shape((2 * PSLOT, DEPTH), BF16)] * 2 + [shape((2 * LANES, DEPTH), BF16)] * 2,
+        in_specs=[VMEM] * 2 + [ANY],
+        out_specs=[VMEM] * 4,
+        compiler_params=LARGE,
+        cost_estimate=pl.CostEstimate(flops=1, bytes_accessed=1, transcendentals=0),
+    )(home, home_other, near)
     near_blocks = [near] + [ring(near, "zx", step) for step in SHIFTS]
     far_blocks = [far] + [ring(far, "zx", step) for step in SHIFTS]
 
-    moved_a, moved_b = hold([moved_a, moved_b], *near_blocks[1:])
+    moved_a, moved_b = hold([moved_a, moved_b], *near_blocks[1:], near_high, partner)
     swapped_a, swapped_b = swap_core(moved_a), swap_core(moved_b)
 
     scale, cycle = pl.pallas_call(
@@ -451,7 +470,7 @@
         out_specs=[VMEM] * 3,
         scratch_shapes=[pltpu.VMEM((16, DEPTH), F32), pltpu.VMEM((LANES, 2 * LANES), F32)],
         compiler_params=LARGE,
-    )(*near_blocks, home, home_other, moved_a, swapped_b, moved_b, swapped_a)
+    )(*near_blocks, near_high, near_low, moved_a, swapped_b, moved_b, swapped_a)
     back_a = ring(below_sum, "yy", (-1, 1))
     back_b = ring(above_sum, "yy", (1, -1))
     packed = pl.pallas_call(
@@ -461,7 +480,7 @@
         out_specs=VMEM,
         scratch_shapes=[pltpu.VMEM((16, DEPTH), F32)],
         compiler_params=LARGE,
-    )(*far_blocks, home, home_other, here_sum, back_a, back_b)
+    )(*far_blocks, far_high, far_low, here_sum, back_a, back_b)
     ladder = lax.all_to_all(packed, ("x", "z", "core"), 0, 0, tiled=True)
     return pl.pallas_call(
         finish,

time: 81.4 us -> 79.5 us (0.977)
  waiting for transfers between devices: 28.8 us -> 26.5 us
  starting transfers between devices: 34 us -> 35.5 us
  Pallas kernels: 17.3 us -> 16.3 us
    ppermute x14, starting transfers between devices: 18.1 us -> 20.5 us  [ring(): return lax.ppermute(value, AXES, pairs)]
    ppermute x1, waiting for transfers between devices: 2.16 us -> 0.01 us  [on_device(): partner = lax.ppermute(ovov, 'z', [(0, 1), (1, 0), (2, 3), (3, 2)])]
    pallas_call x0 -> x1, Pallas kernels: none -> 2.13 us  [on_device(): pl.pallas_call(split_home, out_shape=[shape((2 * PSLOT, DEPTH), BF16)] *...]
    ppermute x1, starting transfers between devices: 1.64 us -> 0.01 us  [on_device(): partner = lax.ppermute(ovov, 'z', [(0, 1), (1, 0), (2, 3), (3, 2)])]
    pallas_call x1, Pallas kernels: 3.84 us -> 2.24 us  [on_device(): pl.pallas_call(multiply_far, out_shape=shape((32, 8, LANES), F32), in_spe...]
    pallas_call x1, Pallas kernels: 4.29 us -> 2.73 us  [on_device(): pl.pallas_call(multiply_near, out_shape=sums, in_specs=[VMEM] * 10, out_s...]
  transfers between devices with their start and end apart: 20 -> 20, of which waited for: 13 -> 11; matrix products, arithmetic and copies ran while one was open for 0% -> 0% of each run, Pallas kernels for 9% -> 10%
where the time goes in v8:
time: 79.5 us; the launch traced here: 79.2 us
  starting transfers between devices  35.5 us (45%)
  waiting for transfers between devices  26.5 us (33%)
  Pallas kernels  16.3 us (21%)
  local copies, waits for them, and re-layouts  0.85 us (1%)
    ppermute x14, waiting for transfers between devices, ring(): return lax.ppermute(value, AXES, pairs)  20.6 us
    ppermute x14, starting transfers between devices, ring(): return lax.ppermute(value, AXES, pairs)  20.5 us
    all_to_all x1, starting transfers between devices, on_device(): ladder = lax.all_to_all(packed, ('x', 'z', 'core'), 0, 0, tiled=True)  7.54 us
    ppermute x4, starting transfers between devices, swap_core(): return lax.ppermute(value, 'core', [(0, 1), (1, 0)])  7.38 us
    pallas_call x1, Pallas kernels, on_device(): pl.pallas_call(open_step, out_shape=[shape((SHARD, LANES), F32)] * 2 + [w...  5.38 us
    all_to_all x1, waiting for transfers between devices, on_device(): ladder = lax.all_to_all(packed, ('x', 'z', 'core'), 0, 0, tiled=True)  4.82 us
    pallas_call x1, Pallas kernels, on_device(): pl.pallas_call(local_step, out_shape=[shape((18, 1296), F32)] * 2, in_spe...  2.83 us
    pallas_call x1, Pallas kernels, on_device(): pl.pallas_call(multiply_near, out_shape=sums, in_specs=[VMEM] * 10, out_s...  2.73 us
  transfers between devices with their start and end apart: 20, of which 11 were waited for; matrix products, arithmetic and copies ran while one was open for 0% of the time, Pallas kernels for 10%

profile of v8, /device:TPU:1, one launch (start us, length us, event | category | flops | bytes accessed | tf_op | source)
XLA Modules:
  0.0 79.2 jit_solution(11115191217836624510)
XLA Ops:
  0.0 5.4 %shard_map.73 = (f32[104,128]{1,0:T(8,128)}, f32[104,128]{1,0:T(8,128)}, f32[21,88,1,128]{3,2,1,0:T(1,128)}, f32[21,88,1,128]{3,2,1,0:T(1,128)}, f32[42,88,1,128]{3,2,1,0:T(1,128)}) custom-call(s32[8]{0:T(128)} %occ_ref.3, s32[8]{0:T(128)} %vir_ref.3, f32[3,6,1,1296]{3,2,1,0:T(1,128)} %amp_ref.3, f32[81,1,10368]{2,1,0:T(1,128)} %bitcast.5), custom_call_target="tpu_custom_call" | custom-call | tf_op jit(solution)/shard_map/pallas_call | solution.py:377
  5.4 1.5 %collective-permute-start = (f32[104,128]{1,0:T(8,128)}, f32[104,128]{1,0:T(8,128)S(1)}, u32[]{:S(2)}, u32[]{:S(2)}) collective-permute-start(f32[104,128]{1,0:T(8,128)} %get-tuple-element.26), channel_id=1, source_target_pairs={{0,1},{1,0},{2,3},{3,2},{4,5},{5,4},{6,7},{7,6},{8,9},{9,8},{10,11... | collective-permute-start | bytes 159752 | tf_op jit(solution)/shard_map/ppermute | solution.py:49
  9.3 3.0 %collective-permute-start.1 = (f32[192,128]{1,0:T(8,128)S(1)}, f32[192,128]{1,0:T(8,128)S(1)}, u32[]{:S(2)}, u32[]{:S(2)}) collective-permute-start(f32[192,128]{1,0:T(8,128)S(1)} %get-tuple-element.28.near), channel_id=1, source_target_pairs={{0,4},{1,5},{2,6},{3,7},{4,0},{5,1},{6,2},{7,3},{8,12},{9,13},{10,... | collective-permute-start | bytes 294920 | tf_op jit(solution)/shard_map/ppermute | solution.py:45
  13.0 2.0 %collective-permute-done.1.far.refs_1_ = f32[192,128]{1,0:T(8,128)S(1)} collective-permute-done((f32[192,128]{1,0:T(8,128)S(1)}, f32[192,128]{1,0:T(8,128)S(1)}, u32[]{:S(2)}, u32[]{:S(2)}) %collective-permute-start.1) | collective-permute-done | bytes 98336 | tf_op jit(solution)/shard_map/ppermute | solution.py:45
  15.1 1.3 %collective-permute-start.13 = (f32[1848,128]{1,0:T(8,128)S(1)}, f32[1848,128]{1,0:T(8,128)S(1)}, u32[]{:S(2)}, u32[]{:S(2)}) collective-permute-start(f32[1848,128]{1,0:T(8,128)S(1)} %shard_map.78), channel_id=1, source_target_pairs={{0,6},{1,3},{2,0},{3,5},{4,2},{5,7},{6,4},{7,1},{8,14},{9,11},{10,... | collective-permute-start | bytes 2838536 | tf_op jit(solution)/shard_map/ppermute | solution.py:45
  16.4 1.7 %collective-permute-start.3 = (f32[384,128]{1,0:T(8,128)S(1)}, f32[384,128]{1,0:T(8,128)S(1)}, u32[]{:S(2)}, u32[]{:S(2)}) collective-permute-start(f32[384,128]{1,0:T(8,128)S(1)} %shard_map.75.b0), channel_id=1, source_target_pairs={{0,32},{1,9},{2,34},{3,11},{4,36},{5,13},{6,38},{7,15},{8,40},{9,1... | collective-permute-start | bytes 589832 | tf_op jit(solution)/shard_map/ppermute | solution.py:45
  18.1 2.2 %collective-permute-start.4 = (f32[384,128]{1,0:T(8,128)S(1)}, f32[384,128]{1,0:T(8,128)S(1)}, u32[]{:S(2)}, u32[]{:S(2)}) collective-permute-start(f32[384,128]{1,0:T(8,128)S(1)} %shard_map.75.b0), channel_id=1, source_target_pairs={{0,96},{1,25},{2,98},{3,27},{4,100},{5,29},{6,102},{7,31},{8,104},... | collective-permute-start | bytes 589832 | tf_op jit(solution)/shard_map/ppermute | solution.py:45
  21.6 2.0 %collective-permute-done.3.b1 = f32[384,128]{1,0:T(8,128)S(1)} collective-permute-done((f32[384,128]{1,0:T(8,128)S(1)}, f32[384,128]{1,0:T(8,128)S(1)}, u32[]{:S(2)}, u32[]{:S(2)}) %collective-permute-start.3) | collective-permute-done | bytes 196640 | tf_op jit(solution)/shard_map/ppermute | solution.py:45
  23.6 1.4 %collective-permute-done.4.b2 = f32[384,128]{1,0:T(8,128)S(1)} collective-permute-done((f32[384,128]{1,0:T(8,128)S(1)}, f32[384,128]{1,0:T(8,128)S(1)}, u32[]{:S(2)}, u32[]{:S(2)}) %collective-permute-start.4) | collective-permute-done | bytes 196640 | tf_op jit(solution)/shard_map/ppermute | solution.py:45
  25.0 1.5 %collective-permute-done.5.b3 = f32[384,128]{1,0:T(8,128)S(1)} collective-permute-done((f32[384,128]{1,0:T(8,128)S(1)}, f32[384,128]{1,0:T(8,128)S(1)}, u32[]{:S(2)}, u32[]{:S(2)}) %collective-permute-start.5) | collective-permute-done | bytes 196640 | tf_op jit(solution)/shard_map/ppermute | solution.py:45
  26.6 2.8 %collective-permute-start.10 = (f32[768,128]{1,0:T(8,128)S(1)}, f32[768,128]{1,0:T(8,128)S(1)}, u32[]{:S(2)}, u32[]{:S(2)}) collective-permute-start(f32[768,128]{1,0:T(8,128)S(1)} %get-tuple-element.31.witness.b0), channel_id=1, source_target_pairs={{0,24},{1,97},{2,26},{3,99},{4,28},{5,101},{6,30},{7,103},{8,0},{9... | collective-permute-start | bytes 1179656 | tf_op jit(solution)/shard_map/ppermute | solution.py:45
  30.3 2.1 %shard_map.77 = (bf16[176,2688]{1,0:T(8,128)(2,1)S(1)}, bf16[176,2688]{1,0:T(8,128)(2,1)S(1)}, bf16[256,2688]{1,0:T(8,128)(2,1)S(1)}, bf16[256,2688]{1,0:T(8,128)(2,1)S(1)}) custom-call(f32[3696,128]{1,0:T(8,128)} %get-tuple-element.29.home, f32[3696,128]{1,0:T(8,128)S(1)} %collective-permute-done.2.home_other, f32[768,128]{1,0:T(8,128)S(1)} %get-tuple-element.31.witness.b0), custom_call_target="tpu_custom_call" | custom-call | flops 1 | bytes 1 | tf_op jit(solution)/shard_map/pallas_call | solution.py:430
  32.9 4.2 %collective-permute-done.13.refs_1_ = f32[1848,128]{1,0:T(8,128)S(1)} collective-permute-done((f32[1848,128]{1,0:T(8,128)S(1)}, f32[1848,128]{1,0:T(8,128)S(1)}, u32[]{:S(2)}, u32[]{:S(2)}) %collective-permute-start.13) | collective-permute-done | bytes 946208 | tf_op jit(solution)/shard_map/ppermute | solution.py:45
  37.1 1.4 %collective-permute-done.10.refs_3_.b2 = f32[768,128]{1,0:T(8,128)S(1)} collective-permute-done((f32[768,128]{1,0:T(8,128)S(1)}, f32[768,128]{1,0:T(8,128)S(1)}, u32[]{:S(2)}, u32[]{:S(2)}) %collective-permute-start.10) | collective-permute-done | bytes 393248 | tf_op jit(solution)/shard_map/ppermute | solution.py:45
  38.4 3.6 %collective-permute-done.9.refs_2_.b1 = f32[768,128]{1,0:T(8,128)S(1)} collective-permute-done((f32[768,128]{1,0:T(8,128)S(1)}, f32[768,128]{1,0:T(8,128)S(1)}, u32[]{:S(2)}, u32[]{:S(2)}) %collective-permute-start.9) | collective-permute-done | bytes 393248 | tf_op jit(solution)/shard_map/ppermute | solution.py:45
  42.1 5.4 %collective-permute-start.15 = (f32[1848,128]{1,0:T(8,128)S(1)}, f32[1848,128]{1,0:T(8,128)S(1)}, u32[]{:S(2)}, u32[]{:S(2)}) collective-permute-start(f32[1848,128]{1,0:T(8,128)S(1)} %get-tuple-element.39.above), channel_id=1, source_target_pairs={{0,1},{1,0},{2,3},{3,2},{4,5},{5,4},{6,7},{7,6},{8,9},{9,8},{10,11... | collective-permute-start | bytes 2838536 | tf_op jit(solution)/shard_map/ppermute | solution.py:49
  47.5 1.7 %collective-permute-start.6 = (f32[768,128]{1,0:T(8,128)S(1)}, f32[768,128]{1,0:T(8,128)S(1)}, u32[]{:S(2)}, u32[]{:S(2)}) collective-permute-start(f32[768,128]{1,0:T(8,128)S(1)} %get-tuple-element.30.b0), channel_id=1, source_target_pairs={{0,8},{1,33},{2,10},{3,35},{4,12},{5,37},{6,14},{7,39},{8,16},{9,4... | collective-permute-start | bytes 1179656 | tf_op jit(solution)/shard_map/ppermute | solution.py:45
  51.4 2.7 %shard_map.80 = (f32[144,256]{1,0:T(8,128)S(1)}, f32[144,256]{1,0:T(8,128)S(1)}, f32[144,256]{1,0:T(8,128)S(1)}) custom-call(f32[768,128]{1,0:T(8,128)S(1)} %get-tuple-element.31.witness.b0, f32[768,128]{1,0:T(8,128)S(1)} %collective-permute-done.9.refs_2_.b1, f32[768,128]{1,0:T(8,128)S(1)} %collective-permute-done.10.refs_3_.b2, ...), custom_call_target="tpu_custom_call" | custom-call | tf_op jit(solution)/shard_map/pallas_call | solution.py:466
  54.2 2.7 %collective-permute-start.18 = (f32[144,256]{1,0:T(8,128)S(1)}, f32[144,256]{1,0:T(8,128)S(1)}, u32[]{:S(2)}, u32[]{:S(2)}) collective-permute-start(f32[144,256]{1,0:T(8,128)S(1)} %get-tuple-element.42), channel_id=1, source_target_pairs={{0,2},{1,7},{2,4},{3,1},{4,6},{5,3},{6,0},{7,5},{8,10},{9,15},{10,... | collective-permute-start | bytes 442376 | tf_op jit(solution)/shard_map/ppermute | solution.py:45
  56.9 3.9 %collective-permute-done.8.b3 = f32[768,128]{1,0:T(8,128)S(1)} collective-permute-done((f32[768,128]{1,0:T(8,128)S(1)}, f32[768,128]{1,0:T(8,128)S(1)}, u32[]{:S(2)}, u32[]{:S(2)}) %collective-permute-start.8) | collective-permute-done | bytes 393248 | tf_op jit(solution)/shard_map/ppermute | solution.py:45
  60.8 2.2 %shard_map.81 = f32[32,8,128]{2,1,0:T(8,128)} custom-call(f32[768,128]{1,0:T(8,128)S(1)} %get-tuple-element.30.b0, f32[768,128]{1,0:T(8,128)S(1)} %collective-permute-done.6.b1, f32[768,128]{1,0:T(8,128)S(1)} %collective-permute-done.7.b2, f32[768,128]{1,0:T(8,128)S(1)} %collective-permute-done.8.b3, bf16[256,2688]{1,0:T(8,128)(2,1)S(1)} %get-tuple-element.32.v_high, ...), custom_call_target="tpu_custom_call" | custom-call | tf_op jit(solution)/shard_map/pallas_call | solution.py:476
  63.1 7.5 %all-to-all-start = ((f32[32,8,128]{2,1,0:T(8,128)}), f32[32,8,128]{2,1,0:T(8,128)S(1)}, u32[]{:S(2)}, u32[]{:S(2)}) async-start(f32[32,8,128]{2,1,0:T(8,128)} %shard_map.81), calls=%async_computation | async-start | bytes 262144 | tf_op jit(solution)/shard_map/all_to_all | solution.py:484
  70.7 2.8 %shard_map.82 = (f32[18,1296]{1,0:T(8,128)S(1)}, f32[18,1296]{1,0:T(8,128)S(1)}) custom-call(s32[8]{0:T(128)S(1)} %copy-done.3, s32[8]{0:T(128)S(1)} %copy-done.4, f32[8,6]{1,0:T(8,128)S(1)} %copy-done.6, f32[8,36]{1,0:T(8,128)S(1)} %copy-done.7, f32[3,6,1,1296]{3,2,1,0:T(1,128)S(1)} %copy-done.1, f32[108,1,216]{2,1,0:T(1,128)S(1)} %copy-done.5, ...), custom_call_target="tpu_custom_call" | custom-call | flops 100000000 | bytes 1000000 | tf_op jit(solution)/shard_map/pallas_call | solution.py:444
  73.5 4.8 %all-to-all-done.sums = f32[32,8,128]{2,1,0:T(8,128)S(1)} async-done(((f32[32,8,128]{2,1,0:T(8,128)}), f32[32,8,128]{2,1,0:T(8,128)S(1)}, u32[]{:S(2)}, u32[]{:S(2)}) %all-to-all-start) | async-done | bytes 131104 | tf_op jit(solution)/shard_map/all_to_all | solution.py:484
  (45 shorter events, 8.9 us)
Async XLA Ops:
  5.4 2.6 %collective-permute-start = (f32[104,128]{1,0:T(8,128)}, f32[104,128]{1,0:T(8,128)S(1)}, u32[]{:S(2)}, u32[]{:S(2)}) collective-permute-start(f32[104,128]{1,0:T(8,128)} %get-tuple-element.26), channel_id=1, source_target_pairs={{0,1},{1,0},{2,3},{3,2},{4,5},{5,4},{6,7},{7,6},{8,9},{9,8},{10,11... | collective-permute-start | bytes 159752 | tf_op jit(solution)/shard_map/ppermute | solution.py:49
  8.8 7.6 %collective-permute-start.2 = (f32[3696,128]{1,0:T(8,128)}, f32[3696,128]{1,0:T(8,128)S(1)}, u32[]{:S(2)}, u32[]{:S(2)}) collective-permute-start(f32[3696,128]{1,0:T(8,128)} %get-tuple-element.29.home), channel_id=1, source_target_pairs={{0,1},{1,0},{2,3},{3,2},{4,5},{5,4},{6,7},{7,6},{8,9},{9,8},{10,11... | collective-permute-start | bytes 5677064 | tf_op jit(solution)/shard_map/ppermute | solution.py:49
  9.3 5.8 %collective-permute-start.1 = (f32[192,128]{1,0:T(8,128)S(1)}, f32[192,128]{1,0:T(8,128)S(1)}, u32[]{:S(2)}, u32[]{:S(2)}) collective-permute-start(f32[192,128]{1,0:T(8,128)S(1)} %get-tuple-element.28.near), channel_id=1, source_target_pairs={{0,4},{1,5},{2,6},{3,7},{4,0},{5,1},{6,2},{7,3},{8,12},{9,13},{10,... | collective-permute-start | bytes 294920 | tf_op jit(solution)/shard_map/ppermute | solution.py:45
  12.3 20.6 %collective-permute-start.12 = (f32[1848,128]{1,0:T(8,128)S(1)}, f32[1848,128]{1,0:T(8,128)S(1)}, u32[]{:S(2)}, u32[]{:S(2)}) collective-permute-start(f32[1848,128]{1,0:T(8,128)S(1)} %bitcast.6), channel_id=1, source_target_pairs={{0,2},{1,7},{2,4},{3,1},{4,6},{5,3},{6,0},{7,5},{8,10},{9,15},{10,... | collective-permute-start | bytes 2838536 | tf_op jit(solution)/shard_map/ppermute | solution.py:45
  15.1 22.0 %collective-permute-start.13 = (f32[1848,128]{1,0:T(8,128)S(1)}, f32[1848,128]{1,0:T(8,128)S(1)}, u32[]{:S(2)}, u32[]{:S(2)}) collective-permute-start(f32[1848,128]{1,0:T(8,128)S(1)} %shard_map.78), channel_id=1, source_target_pairs={{0,6},{1,3},{2,0},{3,5},{4,2},{5,7},{6,4},{7,1},{8,14},{9,11},{10,... | collective-permute-start | bytes 2838536 | tf_op jit(solution)/shard_map/ppermute | solution.py:45
  16.4 7.2 %collective-permute-start.3 = (f32[384,128]{1,0:T(8,128)S(1)}, f32[384,128]{1,0:T(8,128)S(1)}, u32[]{:S(2)}, u32[]{:S(2)}) collective-permute-start(f32[384,128]{1,0:T(8,128)S(1)} %shard_map.75.b0), channel_id=1, source_target_pairs={{0,32},{1,9},{2,34},{3,11},{4,36},{5,13},{6,38},{7,15},{8,40},{9,1... | collective-permute-start | bytes 589832 | tf_op jit(solution)/shard_map/ppermute | solution.py:45
  18.1 6.9 %collective-permute-start.4 = (f32[384,128]{1,0:T(8,128)S(1)}, f32[384,128]{1,0:T(8,128)S(1)}, u32[]{:S(2)}, u32[]{:S(2)}) collective-permute-start(f32[384,128]{1,0:T(8,128)S(1)} %shard_map.75.b0), channel_id=1, source_target_pairs={{0,96},{1,25},{2,98},{3,27},{4,100},{5,29},{6,102},{7,31},{8,104},... | collective-permute-start | bytes 589832 | tf_op jit(solution)/shard_map/ppermute | solution.py:45
  20.3 6.3 %collective-permute-start.5 = (f32[384,128]{1,0:T(8,128)S(1)}, f32[384,128]{1,0:T(8,128)S(1)}, u32[]{:S(2)}, u32[]{:S(2)}) collective-permute-start(f32[384,128]{1,0:T(8,128)S(1)} %shard_map.75.b0), channel_id=1, source_target_pairs={{0,64},{1,17},{2,66},{3,19},{4,68},{5,21},{6,70},{7,23},{8,72},{9,... | collective-permute-start | bytes 589832 | tf_op jit(solution)/shard_map/ppermute | solution.py:45
  23.6 6.1 %collective-permute-start.14 = (f32[108,1,216]{2,1,0:T(1,128)S(1)}, f32[108,1,216]{2,1,0:T(1,128)S(1)}, u32[]{:S(2)}, u32[]{:S(2)}) collective-permute-start(f32[108,1,216]{2,1,0:T(1,128)S(1)} %copy-done.5), channel_id=1, source_target_pairs={{0,8},{8,0},{16,24},{24,16},{1,9},{9,1},{17,25},{25,17},{2,10},{10... | collective-permute-start | bytes 279944 | tf_op jit(solution)/shard_map/ppermute | solution.py:401
  26.6 11.8 %collective-permute-start.10 = (f32[768,128]{1,0:T(8,128)S(1)}, f32[768,128]{1,0:T(8,128)S(1)}, u32[]{:S(2)}, u32[]{:S(2)}) collective-permute-start(f32[768,128]{1,0:T(8,128)S(1)} %get-tuple-element.31.witness.b0), channel_id=1, source_target_pairs={{0,24},{1,97},{2,26},{3,99},{4,28},{5,101},{6,30},{7,103},{8,0},{9... | collective-permute-start | bytes 1179656 | tf_op jit(solution)/shard_map/ppermute | solution.py:45
  29.5 8.9 %collective-permute-start.11 = (f32[768,128]{1,0:T(8,128)S(1)}, f32[768,128]{1,0:T(8,128)S(1)}, u32[]{:S(2)}, u32[]{:S(2)}) collective-permute-start(f32[768,128]{1,0:T(8,128)S(1)} %get-tuple-element.31.witness.b0), channel_id=1, source_target_pairs={{0,16},{1,65},{2,18},{3,67},{4,20},{5,69},{6,22},{7,71},{8,24},{9,... | collective-permute-start | bytes 1179656 | tf_op jit(solution)/shard_map/ppermute | solution.py:45
  29.7 12.3 %collective-permute-start.9 = (f32[768,128]{1,0:T(8,128)S(1)}, f32[768,128]{1,0:T(8,128)S(1)}, u32[]{:S(2)}, u32[]{:S(2)}) collective-permute-start(f32[768,128]{1,0:T(8,128)S(1)} %get-tuple-element.31.witness.b0), channel_id=1, source_target_pairs={{0,8},{1,33},{2,10},{3,35},{4,12},{5,37},{6,14},{7,39},{8,16},{9,4... | collective-permute-start | bytes 1179656 | tf_op jit(solution)/shard_map/ppermute | solution.py:45
  42.1 9.4 %collective-permute-start.15 = (f32[1848,128]{1,0:T(8,128)S(1)}, f32[1848,128]{1,0:T(8,128)S(1)}, u32[]{:S(2)}, u32[]{:S(2)}) collective-permute-start(f32[1848,128]{1,0:T(8,128)S(1)} %get-tuple-element.39.above), channel_id=1, source_target_pairs={{0,1},{1,0},{2,3},{3,2},{4,5},{5,4},{6,7},{7,6},{8,9},{9,8},{10,11... | collective-permute-start | bytes 2838536 | tf_op jit(solution)/shard_map/ppermute | solution.py:49
  47.5 3.9 %collective-permute-start.16 = (f32[1848,128]{1,0:T(8,128)S(1)}, f32[1848,128]{1,0:T(8,128)S(1)}, u32[]{:S(2)}, u32[]{:S(2)}) collective-permute-start(f32[1848,128]{1,0:T(8,128)S(1)} %get-tuple-element.38.below), channel_id=1, source_target_pairs={{0,1},{1,0},{2,3},{3,2},{4,5},{5,4},{6,7},{7,6},{8,9},{9,8},{10,11... | collective-permute-start | bytes 2838536 | tf_op jit(solution)/shard_map/ppermute | solution.py:49
  47.5 9.4 %collective-permute-start.6 = (f32[768,128]{1,0:T(8,128)S(1)}, f32[768,128]{1,0:T(8,128)S(1)}, u32[]{:S(2)}, u32[]{:S(2)}) collective-permute-start(f32[768,128]{1,0:T(8,128)S(1)} %get-tuple-element.30.b0), channel_id=1, source_target_pairs={{0,8},{1,33},{2,10},{3,35},{4,12},{5,37},{6,14},{7,39},{8,16},{9,4... | collective-permute-start | bytes 1179656 | tf_op jit(solution)/shard_map/ppermute | solution.py:45
  49.2 7.7 %collective-permute-start.7 = (f32[768,128]{1,0:T(8,128)S(1)}, f32[768,128]{1,0:T(8,128)S(1)}, u32[]{:S(2)}, u32[]{:S(2)}) collective-permute-start(f32[768,128]{1,0:T(8,128)S(1)} %get-tuple-element.30.b0), channel_id=1, source_target_pairs={{0,24},{1,97},{2,26},{3,99},{4,28},{5,101},{6,30},{7,103},{8,0},{9... | collective-permute-start | bytes 1179656 | tf_op jit(solution)/shard_map/ppermute | solution.py:45
  50.2 10.6 %collective-permute-start.8 = (f32[768,128]{1,0:T(8,128)S(1)}, f32[768,128]{1,0:T(8,128)S(1)}, u32[]{:S(2)}, u32[]{:S(2)}) collective-permute-start(f32[768,128]{1,0:T(8,128)S(1)} %get-tuple-element.30.b0), channel_id=1, source_target_pairs={{0,16},{1,65},{2,18},{3,67},{4,20},{5,69},{6,22},{7,71},{8,24},{9,... | collective-permute-start | bytes 1179656 | tf_op jit(solution)/shard_map/ppermute | solution.py:45
  54.2 6.6 %collective-permute-start.17 = (f32[144,256]{1,0:T(8,128)S(1)}, f32[144,256]{1,0:T(8,128)S(1)}, u32[]{:S(2)}, u32[]{:S(2)}) collective-permute-start(f32[144,256]{1,0:T(8,128)S(1)} %get-tuple-element.41), channel_id=1, source_target_pairs={{0,6},{1,3},{2,0},{3,5},{4,2},{5,7},{6,4},{7,1},{8,14},{9,11},{10,... | collective-permute-start | bytes 442376 | tf_op jit(solution)/shard_map/ppermute | solution.py:45
  54.2 6.5 %collective-permute-start.18 = (f32[144,256]{1,0:T(8,128)S(1)}, f32[144,256]{1,0:T(8,128)S(1)}, u32[]{:S(2)}, u32[]{:S(2)}) collective-permute-start(f32[144,256]{1,0:T(8,128)S(1)} %get-tuple-element.42), channel_id=1, source_target_pairs={{0,2},{1,7},{2,4},{3,1},{4,6},{5,3},{6,0},{7,5},{8,10},{9,15},{10,... | collective-permute-start | bytes 442376 | tf_op jit(solution)/shard_map/ppermute | solution.py:45
  60.8 9.8 %copy-start.1 = (f32[3,6,1,1296]{3,2,1,0:T(1,128)S(1)}, f32[3,6,1,1296]{3,2,1,0:T(1,128)}, u32[]{:S(2)}) copy-start(f32[3,6,1,1296]{3,2,1,0:T(1,128)} %amp_ref.3) | copy-start | bytes 279940
  60.8 9.8 %copy-start.3 = (s32[8]{0:T(128)S(1)}, s32[8]{0:T(128)}, u32[]{:S(2)}) copy-start(s32[8]{0:T(128)} %occ_ref.3) | copy-start | bytes 100
  60.8 9.8 %copy-start.4 = (s32[8]{0:T(128)S(1)}, s32[8]{0:T(128)}, u32[]{:S(2)}) copy-start(s32[8]{0:T(128)} %vir_ref.3) | copy-start | bytes 100
  60.8 9.8 %copy-start.6 = (f32[8,6]{1,0:T(8,128)S(1)}, f32[8,6]{1,0:T(8,128)}, u32[]{:S(2)}) copy-start(f32[8,6]{1,0:T(8,128)} %eps_occ_ref.1) | copy-start | bytes 580
  63.1 15.3 %all-to-all-start = ((f32[32,8,128]{2,1,0:T(8,128)}), f32[32,8,128]{2,1,0:T(8,128)S(1)}, u32[]{:S(2)}, u32[]{:S(2)}) async-start(f32[32,8,128]{2,1,0:T(8,128)} %shard_map.81), calls=%async_computation | async-start | bytes 262144 | tf_op jit(solution)/shard_map/all_to_all | solution.py:484
  (5 other events, 32.3 us)

commit v9 on v8

--- a/solution.py
+++ b/solution.py
@@ -26,6 +26,7 @@
 HBM = pl.BlockSpec(memory_space=pltpu.HBM)
 VMEM = pl.BlockSpec(memory_space=pltpu.VMEM)
 HUGE = pltpu.CompilerParams(vmem_limit_bytes=56 * 1024 * 1024)
+TIGHT = pltpu.CompilerParams(vmem_limit_bytes=(65536 - 900) * 1024)
 SMALL = pltpu.CompilerParams(vmem_limit_bytes=8 * 1024 * 1024)
 LARGE = pltpu.CompilerParams(vmem_limit_bytes=28 * 1024 * 1024)
 
@@ -59,47 +60,55 @@
     return a, lane - 36 * a
 
 
-def window_copies(integrals, ref, first, sems, base):
+def window_copies(integrals, ref, sems, base):
     copies = []
     for t in range(SPAN):
         start = pl.multiple_of((base + t) * LANES, LANES)
         copies.append(
-            pltpu.make_async_copy(integrals.at[:, :, pl.ds(start, LANES)], ref.at[first + t, 0:81], sems.at[t])
+            pltpu.make_async_copy(integrals.at[:, :, pl.ds(start, LANES)], ref.at[t, 0:81], sems.at[t])
         )
     return copies
 
 
-def open_step(occ_ref, vir_ref, amp_ref, integrals, keep_out, send_out, first_out, second_out, home_out,
-              wide, amp, occ, vir, keep, send, first_v, second_v, home, sems, cut_sems, out_sems):
+def cut_step(integrals, witness, second_out, home_out, second_v, home, cut_sems, home_sems, out_sems):
+    y, core = lax.axis_index("y"), lax.axis_index("core")
+    cuts = window_copies(integrals, second_v, cut_sems, ((y + 3 - 2 * core) & 3) * 20)
+    homes = []
+    for at in range(2):
+        start = pl.multiple_of(((y + 2 * at) & 3) * 2560, LANES)
+        homes.append(
+            pltpu.make_async_copy(
+                integrals.at[:, :, pl.ds(start, DEPTH)], home.at[at, 0:81], home_sems.at[at]
+            )
+        )
+    for copy in cuts + homes:
+        copy.start()
+    outs = [pltpu.make_async_copy(second_v, second_out, out_sems.at[0])]
+    outs += [pltpu.make_async_copy(home.at[at], home_out.at[at], out_sems.at[1 + at]) for at in range(2)]
+    for copy in cuts:
+        copy.wait()
+    outs[0].start()
+    for copy, out in zip(homes, outs[1:]):
+        copy.wait()
+        out.start()
+    for out in outs:
+        out.wait()
+
+
+def open_step(occ_ref, vir_ref, amp_ref, integrals, keep_out, send_out, first_out,
+              wide, amp, occ, vir, keep, send, first_v, sems, cut_sems, out_sems):
     x, z, y, core = places()
     copies = [
         pltpu.make_async_copy(source, target, sems.at[at])
         for at, (source, target) in enumerate(((occ_ref, occ), (vir_ref, vir), (amp_ref, amp)))
     ]
-    groups = [
-        window_copies(integrals, first_v, 0, cut_sems.at[0], ((y + 1 + 2 * core) & 3) * 20),
-        window_copies(integrals, second_v, 0, cut_sems.at[1], ((y + 3 - 2 * core) & 3) * 20),
-        window_copies(integrals, home, 0, cut_sems.at[2], y * 20),
-        window_copies(integrals, home, SPAN, cut_sems.at[3], ((y + 2) & 3) * 20),
-    ]
+    cuts = window_copies(integrals, first_v, cut_sems, ((y + 1 + 2 * core) & 3) * 20)
     outs = [
         pltpu.make_async_copy(source, target, out_sems.at[at])
-        for at, (source, target) in enumerate(
-            (
-                (first_v, first_out),
-                (second_v, second_out),
-                (home.at[0:SPAN], home_out.at[0:SPAN]),
-                (home.at[SPAN : 2 * SPAN], home_out.at[SPAN : 2 * SPAN]),
-                (keep, keep_out),
-                (send, send_out),
-            )
-        )
+        for at, (source, target) in enumerate(((keep, keep_out), (send, send_out), (first_v, first_out)))
     ]
-    for copy in copies:
+    for copy in copies + cuts:
         copy.start()
-    for group in groups:
-        for copy in group:
-            copy.start()
     wide[...] = jnp.zeros_like(wide)
     for copy in copies:
         copy.wait()
@@ -134,12 +143,11 @@
         write(keep, 1)
         write(send, 0)
 
-    for copy in outs[4:]:
+    for copy in outs[:2]:
         copy.start()
-    for group, out in zip(groups, outs):
-        for copy in group:
-            copy.wait()
-        out.start()
+    for copy in cuts:
+        copy.wait()
+    outs[2].start()
     for copy in outs:
         copy.wait()
 
@@ -156,7 +164,7 @@
     out[extra + SPAN : at + PAIR, :] = jnp.zeros((PAIR - PMAIN - SPAN, LANES), F32)
 
 
-def merge_pair(keep, got, home, out, home_out):
+def merge_pair(keep, got, out):
     core = lax.axis_index("core")
 
     @pl.when(core == 0)
@@ -168,12 +176,12 @@
         merge_irreps(got, keep, out, 0)
 
 
-def join_pairs(near, far, home_other, out):
+def join_pairs(near, far, out):
     out[0:PAIR, :] = near[...]
     out[PAIR:QUAD, :] = far[...]
 
 
-def gather_four(b0, b1, b2, b3, near, far):
+def gather_four(b0, b1, b2, b3, witness, near, far):
     for at, block in enumerate((b0, b1, b2, b3)):
         near[at * PAIR : (at + 1) * PAIR, :] = block[0:PAIR, :]
         far[at * PAIR : (at + 1) * PAIR, :] = block[PAIR:QUAD, :]
@@ -183,7 +191,7 @@
     pass
 
 
-def hold(values, *witnesses):
+def hold(values, *witnesses, params=SMALL):
     kept = range(len(values))
     return pl.pallas_call(
         nothing,
@@ -191,7 +199,7 @@
         in_specs=[ANY] * (len(values) + len(witnesses)),
         out_specs=[ANY] * len(values),
         input_output_aliases={at: at for at in kept},
-        compiler_params=SMALL,
+        compiler_params=params,
     )(*values, *witnesses)
 
 
@@ -221,17 +229,21 @@
     )
 
 
+def rows_side(ref, first):
+    return jnp.concatenate([ref[pl.ds(first + t, PSLOT, stride=SPAN), :] for t in range(SPAN)], axis=1)
+
+
 def last_by_last(p, q):
     return lax.dot_general(p, q, (((1,), (1,)), ((), ())), preferred_element_type=F32)
 
 
 def split_home(home, home_other, witness, near_high, near_low, far_high, far_low):
     for side, ref in enumerate((home, home_other)):
-        high, low = split(tiles_side(ref, 0))
+        high, low = split(rows_side(ref, 0))
         rows = slice(side * PSLOT, (side + 1) * PSLOT)
         near_high[rows, :] = high
         near_low[rows, :] = low
-        high, low = split(tiles_side(ref, SPAN))
+        high, low = split(rows_side(ref, PROWS))
         pad = jnp.zeros((LANES - PSLOT, DEPTH), BF16)
         rows = slice(side * LANES, (side + 1) * LANES)
         far_high[rows, :] = jnp.concatenate([high, pad], axis=0)
@@ -374,12 +386,11 @@
     integrals = vvvv.reshape(81, 1, 10368)
     window = shape((SPAN, PSLOT, 1, LANES), F32)
     flat = lambda value: value.reshape(PROWS, LANES)
-    keep, send, first_v, second_v, home = pl.pallas_call(
+    keep, send, first_v = pl.pallas_call(
         open_step,
-        out_shape=[shape((SHARD, LANES), F32)] * 2 + [window] * 2
-        + [shape((2 * SPAN, PSLOT, 1, LANES), F32)],
+        out_shape=[shape((SHARD, LANES), F32)] * 2 + [window],
         in_specs=[HBM] * 4,
-        out_specs=[ANY] * 5,
+        out_specs=[ANY] * 3,
         scratch_shapes=[
             pltpu.VMEM((24, WINDOW), F32),
             pltpu.VMEM((3, 6, 1, 1296), F32),
@@ -388,45 +399,57 @@
             pltpu.VMEM((SHARD, LANES), F32),
             pltpu.VMEM((SHARD, LANES), F32),
             pltpu.VMEM((SPAN, PSLOT, 1, LANES), F32),
-            pltpu.VMEM((SPAN, PSLOT, 1, LANES), F32),
-            pltpu.VMEM((2 * SPAN, PSLOT, 1, LANES), F32),
             pltpu.SemaphoreType.DMA((3,)),
-            pltpu.SemaphoreType.DMA((4, SPAN)),
-            pltpu.SemaphoreType.DMA((6,)),
+            pltpu.SemaphoreType.DMA((SPAN,)),
+            pltpu.SemaphoreType.DMA((3,)),
         ],
         compiler_params=HUGE,
     )(occ_count, vir_count, amplitudes, integrals)
     got = swap_core(send)
     moved_a = ring(flat(first_v), "yy", (1, -1))
     partner = lax.ppermute(ovov, "z", [(0, 1), (1, 0), (2, 3), (3, 2)])
+    pair = pl.pallas_call(
+        merge_pair,
+        out_shape=shape((PAIR, LANES), F32),
+        in_specs=[VMEM] * 2,
+        out_specs=VMEM,
+        compiler_params=SMALL,
+    )(keep, got)
+    second_v, home = pl.pallas_call(
+        cut_step,
+        out_shape=[window, shape((2, PSLOT, 1, DEPTH), F32)],
+        in_specs=[HBM, ANY],
+        out_specs=[ANY] * 2,
+        scratch_shapes=[
+            pltpu.VMEM((SPAN, PSLOT, 1, LANES), F32),
+            pltpu.VMEM((2, PSLOT, 1, DEPTH), F32),
+            pltpu.SemaphoreType.DMA((SPAN,)),
+            pltpu.SemaphoreType.DMA((2,)),
+            pltpu.SemaphoreType.DMA((3,)),
+        ],
+        compiler_params=TIGHT,
+        cost_estimate=pl.CostEstimate(flops=0, bytes_accessed=7000000, transcendentals=0),
+    )(integrals, pair)
     home = home.reshape(2 * PROWS, LANES)
-    pair, home = pl.pallas_call(
-        merge_pair,
-        out_shape=[shape((PAIR, LANES), F32), shape(home.shape, F32)],
-        in_specs=[VMEM] * 2 + [ANY],
-        out_specs=[VMEM, ANY],
-        input_output_aliases={2: 1},
-        compiler_params=SMALL,
-    )(keep, got, home)
-    home_other = swap_core(home)
     far_pair = ring(pair, "yy", (2, 2))
     quad = pl.pallas_call(
         join_pairs,
         out_shape=shape((QUAD, LANES), F32),
-        in_specs=[VMEM] * 2 + [ANY],
+        in_specs=[VMEM] * 2,
         out_specs=VMEM,
         compiler_params=SMALL,
-    )(pair, far_pair, home_other)
-    (second_v,) = hold([flat(second_v)], far_pair)
+    )(pair, far_pair)
+    second_v, home = hold([flat(second_v), home], far_pair, params=TIGHT)
+    home_other = swap_core(home)
     moved_b = ring(second_v, "yy", (-1, 1))
 
     near, far = pl.pallas_call(
         gather_four,
         out_shape=[shape((4 * PAIR, LANES), F32)] * 2,
-        in_specs=[VMEM] * 4,
+        in_specs=[VMEM] * 4 + [ANY],
         out_specs=[VMEM] * 2,
         compiler_params=SMALL,
-    )(quad, *[ring(quad, "xz", step) for step in SHIFTS])
+    )(quad, *[ring(quad, "xz", step) for step in SHIFTS], home_other)
     near_high, near_low, far_high, far_low = pl.pallas_call(
         split_home,
         out_shape=[shape((2 * PSLOT, DEPTH), BF16)] * 2 + [shape((2 * LANES, DEPTH), BF16)] * 2,

time: 79.5 us -> 83.1 us (1.045)
  waiting for transfers between devices: 26.5 us -> 28.2 us
  local copies, waits for them, and re-layouts: 0.85 us -> 2.37 us
    pallas_call x1 -> x2, Pallas kernels: 0.01 us -> 3.94 us  [the longest x1 3.29 us: on_device(): pl.pallas_call(cut_step, out_shape=[window, shape((2, PSLOT, 1, DEPTH), F...]
    pallas_call x1, Pallas kernels: 5.38 us -> 2.75 us  [on_device(): pl.pallas_call(open_step, out_shape=[shape((SHARD, LANES), F32)] * 2 + [w...]
    ppermute x4, starting transfers between devices: 7.38 us -> 5.68 us  [swap_core(): return lax.ppermute(value, 'core', [(0, 1), (1, 0)])]
    unnamed x18 -> x20, local copies, waits for them, and re-layouts: 0.85 us -> 2.37 us
    pallas_call x1, Pallas kernels: 2.13 us -> 0.62 us  [on_device(): pl.pallas_call(split_home, out_shape=[shape((2 * PSLOT, DEPTH), BF16)] *...]
    ppermute x14, waiting for transfers between devices: 20.6 us -> 21.8 us  [ring(): return lax.ppermute(value, AXES, pairs)]
    all_to_all x1, starting transfers between devices: 7.54 us -> 8.54 us  [on_device(): ladder = lax.all_to_all(packed, ('x', 'z', 'core'), 0, 0, tiled=True)]
    pallas_call x1, Pallas kernels: 0.01 us -> 0.91 us  [on_device(): pl.pallas_call(join_pairs, out_shape=shape((QUAD, LANES), F32), in_specs=...]
  transfers between devices with their start and end apart: 20 -> 20, of which waited for: 11 -> 10; matrix products, arithmetic and copies ran while one was open for 0% -> 0% of each run, Pallas kernels for 10% -> 13%
where the time goes in v9:
time: 83.1 us; the launch traced here: 82.8 us
  starting transfers between devices  35.1 us (42%)
  waiting for transfers between devices  28.2 us (34%)
  Pallas kernels  16.9 us (20%)
  local copies, waits for them, and re-layouts  2.37 us (3%)
    ppermute x14, waiting for transfers between devices, ring(): return lax.ppermute(value, AXES, pairs)  21.8 us
    ppermute x14, starting transfers between devices, ring(): return lax.ppermute(value, AXES, pairs)  20.1 us
    all_to_all x1, starting transfers between devices, on_device(): ladder = lax.all_to_all(packed, ('x', 'z', 'core'), 0, 0, tiled=True)  8.54 us
    ppermute x4, starting transfers between devices, swap_core(): return lax.ppermute(value, 'core', [(0, 1), (1, 0)])  5.68 us
    all_to_all x1, waiting for transfers between devices, on_device(): ladder = lax.all_to_all(packed, ('x', 'z', 'core'), 0, 0, tiled=True)  4.82 us
    pallas_call x1, Pallas kernels, on_device(): pl.pallas_call(cut_step, out_shape=[window, shape((2, PSLOT, 1, DEPTH), F...  3.29 us
    pallas_call x1, Pallas kernels, on_device(): pl.pallas_call(local_step, out_shape=[shape((18, 1296), F32)] * 2, in_spe...  2.83 us
    pallas_call x1, Pallas kernels, on_device(): pl.pallas_call(open_step, out_shape=[shape((SHARD, LANES), F32)] * 2 + [w...  2.75 us
  transfers between devices with their start and end apart: 20, of which 10 were waited for; matrix products, arithmetic and copies ran while one was open for 0% of the time, Pallas kernels for 13%

profile of v9, /device:TPU:1, one launch (start us, length us, event | category | flops | bytes accessed | tf_op | source)
XLA Modules:
  0.0 82.8 jit_solution(16062591666413614772)
XLA Ops:
  0.0 2.8 %shard_map.73 = (f32[104,128]{1,0:T(8,128)}, f32[104,128]{1,0:T(8,128)}, f32[21,88,1,128]{3,2,1,0:T(1,128)}) custom-call(s32[8]{0:T(128)} %occ_ref.3, s32[8]{0:T(128)} %vir_ref.3, f32[3,6,1,1296]{3,2,1,0:T(1,128)} %amp_ref.3, f32[81,1,10368]{2,1,0:T(1,128)} %bitcast.5), custom_call_target="tpu_custom_call" | custom-call | tf_op jit(solution)/shard_map/pallas_call | solution.py:389
  2.8 1.5 %collective-permute-start = (f32[104,128]{1,0:T(8,128)}, f32[104,128]{1,0:T(8,128)S(1)}, u32[]{:S(2)}, u32[]{:S(2)}) collective-permute-start(f32[104,128]{1,0:T(8,128)} %get-tuple-element.26), channel_id=1, source_target_pairs={{0,1},{1,0},{2,3},{3,2},{4,5},{5,4},{6,7},{7,6},{8,9},{9,8},{10,11... | collective-permute-start | bytes 159752 | tf_op jit(solution)/shard_map/ppermute | solution.py:50
  6.8 3.0 %collective-permute-start.1 = (f32[192,128]{1,0:T(8,128)}, f32[192,128]{1,0:T(8,128)S(1)}, u32[]{:S(2)}, u32[]{:S(2)}) collective-permute-start(f32[192,128]{1,0:T(8,128)} %shard_map.74.near.witness), channel_id=1, source_target_pairs={{0,4},{1,5},{2,6},{3,7},{4,0},{5,1},{6,2},{7,3},{8,12},{9,13},{10,... | collective-permute-start | bytes 294920 | tf_op jit(solution)/shard_map/ppermute | solution.py:46
  9.8 3.3 %shard_map.76 = (f32[21,88,1,128]{3,2,1,0:T(1,128)}, f32[2,88,1,2688]{3,2,1,0:T(1,128)}) custom-call(f32[81,1,10368]{2,1,0:T(1,128)} %bitcast.6, f32[192,128]{1,0:T(8,128)} %shard_map.74.near.witness), custom_call_target="tpu_custom_call" | custom-call | bytes 7000000 | tf_op jit(solution)/shard_map/pallas_call | solution.py:418
  14.4 2.8 %collective-permute-start.12 = (f32[1848,128]{1,0:T(8,128)}, f32[1848,128]{1,0:T(8,128)S(1)}, u32[]{:S(2)}, u32[]{:S(2)}) collective-permute-start(f32[1848,128]{1,0:T(8,128)} %bitcast.8), channel_id=1, source_target_pairs={{0,2},{1,7},{2,4},{3,1},{4,6},{5,3},{6,0},{7,5},{8,10},{9,15},{10,... | collective-permute-start | bytes 2838536 | tf_op jit(solution)/shard_map/ppermute | solution.py:46
  19.0 1.7 %collective-permute-start.2 = (f32[384,128]{1,0:T(8,128)S(1)}, f32[384,128]{1,0:T(8,128)S(1)}, u32[]{:S(2)}, u32[]{:S(2)}) collective-permute-start(f32[384,128]{1,0:T(8,128)S(1)} %shard_map.75.b0), channel_id=1, source_target_pairs={{0,32},{1,9},{2,34},{3,11},{4,36},{5,13},{6,38},{7,15},{8,40},{9,1... | collective-permute-start | bytes 589832 | tf_op jit(solution)/shard_map/ppermute | solution.py:46
  20.7 2.2 %collective-permute-start.3 = (f32[384,128]{1,0:T(8,128)S(1)}, f32[384,128]{1,0:T(8,128)S(1)}, u32[]{:S(2)}, u32[]{:S(2)}) collective-permute-start(f32[384,128]{1,0:T(8,128)S(1)} %shard_map.75.b0), channel_id=1, source_target_pairs={{0,96},{1,25},{2,98},{3,27},{4,100},{5,29},{6,102},{7,31},{8,104},... | collective-permute-start | bytes 589832 | tf_op jit(solution)/shard_map/ppermute | solution.py:46
  22.9 3.3 %collective-permute-done.2.b1 = f32[384,128]{1,0:T(8,128)S(1)} collective-permute-done((f32[384,128]{1,0:T(8,128)S(1)}, f32[384,128]{1,0:T(8,128)S(1)}, u32[]{:S(2)}, u32[]{:S(2)}) %collective-permute-start.2) | collective-permute-done | bytes 196640 | tf_op jit(solution)/shard_map/ppermute | solution.py:46
  26.2 1.3 %collective-permute-start.4 = (f32[384,128]{1,0:T(8,128)S(1)}, f32[384,128]{1,0:T(8,128)S(1)}, u32[]{:S(2)}, u32[]{:S(2)}) collective-permute-start(f32[384,128]{1,0:T(8,128)S(1)} %shard_map.75.b0), channel_id=1, source_target_pairs={{0,64},{1,17},{2,66},{3,19},{4,68},{5,21},{6,70},{7,23},{8,72},{9,... | collective-permute-start | bytes 589832 | tf_op jit(solution)/shard_map/ppermute | solution.py:46
  28.2 4.3 %collective-permute-done.4.b3 = f32[384,128]{1,0:T(8,128)S(1)} collective-permute-done((f32[384,128]{1,0:T(8,128)S(1)}, f32[384,128]{1,0:T(8,128)S(1)}, u32[]{:S(2)}, u32[]{:S(2)}) %collective-permute-start.4) | collective-permute-done | bytes 196640 | tf_op jit(solution)/shard_map/ppermute | solution.py:46
  32.6 2.3 %collective-permute-start.10 = (f32[768,128]{1,0:T(8,128)S(1)}, f32[768,128]{1,0:T(8,128)S(1)}, u32[]{:S(2)}, u32[]{:S(2)}) collective-permute-start(f32[768,128]{1,0:T(8,128)S(1)} %get-tuple-element.31.witness.b0), channel_id=1, source_target_pairs={{0,24},{1,97},{2,26},{3,99},{4,28},{5,101},{6,30},{7,103},{8,0},{9... | collective-permute-start | bytes 1179656 | tf_op jit(solution)/shard_map/ppermute | solution.py:46
  36.6 1.1 %collective-permute-done.12.refs_0_ = f32[1848,128]{1,0:T(8,128)S(1)} collective-permute-done((f32[1848,128]{1,0:T(8,128)}, f32[1848,128]{1,0:T(8,128)S(1)}, u32[]{:S(2)}, u32[]{:S(2)}) %collective-permute-start.12) | collective-permute-done | bytes 946208 | tf_op jit(solution)/shard_map/ppermute | solution.py:46
  37.7 1.3 %collective-permute-done.13.refs_1_ = f32[1848,128]{1,0:T(8,128)S(1)} collective-permute-done((f32[1848,128]{1,0:T(8,128)}, f32[1848,128]{1,0:T(8,128)S(1)}, u32[]{:S(2)}, u32[]{:S(2)}) %collective-permute-start.13) | collective-permute-done | bytes 946208 | tf_op jit(solution)/shard_map/ppermute | solution.py:46
  39.0 4.8 %collective-permute-done.10.refs_3_.b2 = f32[768,128]{1,0:T(8,128)S(1)} collective-permute-done((f32[768,128]{1,0:T(8,128)S(1)}, f32[768,128]{1,0:T(8,128)S(1)}, u32[]{:S(2)}, u32[]{:S(2)}) %collective-permute-start.10) | collective-permute-done | bytes 393248 | tf_op jit(solution)/shard_map/ppermute | solution.py:46
  43.8 3.7 %collective-permute-done.9.refs_2_.b1 = f32[768,128]{1,0:T(8,128)S(1)} collective-permute-done((f32[768,128]{1,0:T(8,128)S(1)}, f32[768,128]{1,0:T(8,128)S(1)}, u32[]{:S(2)}, u32[]{:S(2)}) %collective-permute-start.9) | collective-permute-done | bytes 393248 | tf_op jit(solution)/shard_map/ppermute | solution.py:46
  47.5 3.5 %collective-permute-start.15 = (f32[1848,128]{1,0:T(8,128)S(1)}, f32[1848,128]{1,0:T(8,128)S(1)}, u32[]{:S(2)}, u32[]{:S(2)}) collective-permute-start(f32[1848,128]{1,0:T(8,128)S(1)} %get-tuple-element.39.above), channel_id=1, source_target_pairs={{0,1},{1,0},{2,3},{3,2},{4,5},{5,4},{6,7},{7,6},{8,9},{9,8},{10,11... | collective-permute-start | bytes 2838536 | tf_op jit(solution)/shard_map/ppermute | solution.py:50
  51.0 2.7 %collective-permute-start.7 = (f32[768,128]{1,0:T(8,128)S(1)}, f32[768,128]{1,0:T(8,128)S(1)}, u32[]{:S(2)}, u32[]{:S(2)}) collective-permute-start(f32[768,128]{1,0:T(8,128)S(1)} %get-tuple-element.30.b0), channel_id=1, source_target_pairs={{0,24},{1,97},{2,26},{3,99},{4,28},{5,101},{6,30},{7,103},{8,0},{9... | collective-permute-start | bytes 1179656 | tf_op jit(solution)/shard_map/ppermute | solution.py:46
  54.5 2.8 %shard_map.81 = (f32[144,256]{1,0:T(8,128)S(1)}, f32[144,256]{1,0:T(8,128)S(1)}, f32[144,256]{1,0:T(8,128)S(1)}) custom-call(f32[768,128]{1,0:T(8,128)S(1)} %get-tuple-element.31.witness.b0, f32[768,128]{1,0:T(8,128)S(1)} %collective-permute-done.9.refs_2_.b1, f32[768,128]{1,0:T(8,128)S(1)} %collective-permute-done.10.refs_3_.b2, ...), custom_call_target="tpu_custom_call" | custom-call | tf_op jit(solution)/shard_map/pallas_call | solution.py:489
  57.4 2.6 %collective-permute-start.18 = (f32[144,256]{1,0:T(8,128)S(1)}, f32[144,256]{1,0:T(8,128)S(1)}, u32[]{:S(2)}, u32[]{:S(2)}) collective-permute-start(f32[144,256]{1,0:T(8,128)S(1)} %get-tuple-element.42), channel_id=1, source_target_pairs={{0,2},{1,7},{2,4},{3,1},{4,6},{5,3},{6,0},{7,5},{8,10},{9,15},{10,... | collective-permute-start | bytes 442376 | tf_op jit(solution)/shard_map/ppermute | solution.py:46
  60.0 3.4 %collective-permute-done.6.b1 = f32[768,128]{1,0:T(8,128)S(1)} collective-permute-done((f32[768,128]{1,0:T(8,128)S(1)}, f32[768,128]{1,0:T(8,128)S(1)}, u32[]{:S(2)}, u32[]{:S(2)}) %collective-permute-start.6) | collective-permute-done | bytes 393248 | tf_op jit(solution)/shard_map/ppermute | solution.py:46
  63.4 2.2 %shard_map.82 = f32[32,8,128]{2,1,0:T(8,128)} custom-call(f32[768,128]{1,0:T(8,128)S(1)} %get-tuple-element.30.b0, f32[768,128]{1,0:T(8,128)S(1)} %collective-permute-done.6.b1, f32[768,128]{1,0:T(8,128)S(1)} %collective-permute-done.7.b2, f32[768,128]{1,0:T(8,128)S(1)} %collective-permute-done.8.b3, bf16[256,2688]{1,0:T(8,128)(2,1)S(1)} %get-tuple-element.32.v_high, ...), custom_call_target="tpu_custom_call" | custom-call | tf_op jit(solution)/shard_map/pallas_call | solution.py:499
  65.6 8.5 %all-to-all-start = ((f32[32,8,128]{2,1,0:T(8,128)}), f32[32,8,128]{2,1,0:T(8,128)S(1)}, u32[]{:S(2)}, u32[]{:S(2)}) async-start(f32[32,8,128]{2,1,0:T(8,128)} %shard_map.82), calls=%async_computation | async-start | bytes 262144 | tf_op jit(solution)/shard_map/all_to_all | solution.py:507
  74.2 2.8 %shard_map.83 = (f32[18,1296]{1,0:T(8,128)S(1)}, f32[18,1296]{1,0:T(8,128)S(1)}) custom-call(s32[8]{0:T(128)S(1)} %copy-done.5, s32[8]{0:T(128)S(1)} %copy-done.6, f32[8,6]{1,0:T(8,128)S(1)} %copy-done.8, f32[8,36]{1,0:T(8,128)S(1)} %copy-done.9, f32[3,6,1,1296]{3,2,1,0:T(1,128)S(1)} %copy-done.3, f32[108,1,216]{2,1,0:T(1,128)S(1)} %copy-done.7, ...), custom_call_target="tpu_custom_call" | custom-call | flops 100000000 | bytes 1000000 | tf_op jit(solution)/shard_map/pallas_call | solution.py:467
  77.1 4.8 %all-to-all-done.sums = f32[32,8,128]{2,1,0:T(8,128)S(1)} async-done(((f32[32,8,128]{2,1,0:T(8,128)}), f32[32,8,128]{2,1,0:T(8,128)S(1)}, u32[]{:S(2)}, u32[]{:S(2)}) %all-to-all-start) | async-done | bytes 131104 | tf_op jit(solution)/shard_map/all_to_all | solution.py:507
  (48 shorter events, 10.1 us)
Async XLA Ops:
  2.8 2.6 %collective-permute-start = (f32[104,128]{1,0:T(8,128)}, f32[104,128]{1,0:T(8,128)S(1)}, u32[]{:S(2)}, u32[]{:S(2)}) collective-permute-start(f32[104,128]{1,0:T(8,128)} %get-tuple-element.26), channel_id=1, source_target_pairs={{0,1},{1,0},{2,3},{3,2},{4,5},{5,4},{6,7},{7,6},{8,9},{9,8},{10,11... | collective-permute-start | bytes 159752 | tf_op jit(solution)/shard_map/ppermute | solution.py:50
  6.8 6.3 %collective-permute-start.1 = (f32[192,128]{1,0:T(8,128)}, f32[192,128]{1,0:T(8,128)S(1)}, u32[]{:S(2)}, u32[]{:S(2)}) collective-permute-start(f32[192,128]{1,0:T(8,128)} %shard_map.74.near.witness), channel_id=1, source_target_pairs={{0,4},{1,5},{2,6},{3,7},{4,0},{5,1},{6,2},{7,3},{8,12},{9,13},{10,... | collective-permute-start | bytes 294920 | tf_op jit(solution)/shard_map/ppermute | solution.py:46
  13.1 14.4 %copy-start.7 = (f32[108,1,216]{2,1,0:T(1,128)S(1)}, f32[108,1,216]{2,1,0:T(1,128)}, u32[]{:S(2)}) copy-start(f32[108,1,216]{2,1,0:T(1,128)} %ovov.1) | copy-start | bytes 279940
  13.8 22.2 %copy-start = (f32[3696,128]{1,0:T(8,128)S(1)}, f32[3696,128]{1,0:T(8,128)}, u32[]{:S(2)}) copy-start(f32[3696,128]{1,0:T(8,128)} %get-tuple-element.29.home) | copy-start | bytes 5677060
  13.8 18.7 %collective-permute-start.5 = (f32[3696,128]{1,0:T(8,128)}, f32[3696,128]{1,0:T(8,128)S(1)}, u32[]{:S(2)}, u32[]{:S(2)}) collective-permute-start(f32[3696,128]{1,0:T(8,128)} %get-tuple-element.29.home), channel_id=1, source_target_pairs={{0,1},{1,0},{2,3},{3,2},{4,5},{5,4},{6,7},{7,6},{8,9},{9,8},{10,11... | collective-permute-start | bytes 5677064 | tf_op jit(solution)/shard_map/ppermute | solution.py:50
  14.4 23.3 %collective-permute-start.12 = (f32[1848,128]{1,0:T(8,128)}, f32[1848,128]{1,0:T(8,128)S(1)}, u32[]{:S(2)}, u32[]{:S(2)}) collective-permute-start(f32[1848,128]{1,0:T(8,128)} %bitcast.8), channel_id=1, source_target_pairs={{0,2},{1,7},{2,4},{3,1},{4,6},{5,3},{6,0},{7,5},{8,10},{9,15},{10,... | collective-permute-start | bytes 2838536 | tf_op jit(solution)/shard_map/ppermute | solution.py:46
  17.2 21.8 %collective-permute-start.13 = (f32[1848,128]{1,0:T(8,128)}, f32[1848,128]{1,0:T(8,128)S(1)}, u32[]{:S(2)}, u32[]{:S(2)}) collective-permute-start(f32[1848,128]{1,0:T(8,128)} %get-tuple-element.37), channel_id=1, source_target_pairs={{0,6},{1,3},{2,0},{3,5},{4,2},{5,7},{6,4},{7,1},{8,14},{9,11},{10,... | collective-permute-start | bytes 2838536 | tf_op jit(solution)/shard_map/ppermute | solution.py:46
  19.0 7.2 %collective-permute-start.2 = (f32[384,128]{1,0:T(8,128)S(1)}, f32[384,128]{1,0:T(8,128)S(1)}, u32[]{:S(2)}, u32[]{:S(2)}) collective-permute-start(f32[384,128]{1,0:T(8,128)S(1)} %shard_map.75.b0), channel_id=1, source_target_pairs={{0,32},{1,9},{2,34},{3,11},{4,36},{5,13},{6,38},{7,15},{8,40},{9,1... | collective-permute-start | bytes 589832 | tf_op jit(solution)/shard_map/ppermute | solution.py:46
  20.7 6.8 %collective-permute-start.3 = (f32[384,128]{1,0:T(8,128)S(1)}, f32[384,128]{1,0:T(8,128)S(1)}, u32[]{:S(2)}, u32[]{:S(2)}) collective-permute-start(f32[384,128]{1,0:T(8,128)S(1)} %shard_map.75.b0), channel_id=1, source_target_pairs={{0,96},{1,25},{2,98},{3,27},{4,100},{5,29},{6,102},{7,31},{8,104},... | collective-permute-start | bytes 589832 | tf_op jit(solution)/shard_map/ppermute | solution.py:46
  26.2 6.3 %collective-permute-start.4 = (f32[384,128]{1,0:T(8,128)S(1)}, f32[384,128]{1,0:T(8,128)S(1)}, u32[]{:S(2)}, u32[]{:S(2)}) collective-permute-start(f32[384,128]{1,0:T(8,128)S(1)} %shard_map.75.b0), channel_id=1, source_target_pairs={{0,64},{1,17},{2,66},{3,19},{4,68},{5,21},{6,70},{7,23},{8,72},{9,... | collective-permute-start | bytes 589832 | tf_op jit(solution)/shard_map/ppermute | solution.py:46
  27.5 7.8 %collective-permute-start.14 = (f32[108,1,216]{2,1,0:T(1,128)S(1)}, f32[108,1,216]{2,1,0:T(1,128)S(1)}, u32[]{:S(2)}, u32[]{:S(2)}) collective-permute-start(f32[108,1,216]{2,1,0:T(1,128)S(1)} %copy-done.7), channel_id=1, source_target_pairs={{0,8},{8,0},{16,24},{24,16},{1,9},{9,1},{17,25},{25,17},{2,10},{10... | collective-permute-start | bytes 279944 | tf_op jit(solution)/shard_map/ppermute | solution.py:410
  32.6 11.2 %collective-permute-start.10 = (f32[768,128]{1,0:T(8,128)S(1)}, f32[768,128]{1,0:T(8,128)S(1)}, u32[]{:S(2)}, u32[]{:S(2)}) collective-permute-start(f32[768,128]{1,0:T(8,128)S(1)} %get-tuple-element.31.witness.b0), channel_id=1, source_target_pairs={{0,24},{1,97},{2,26},{3,99},{4,28},{5,101},{6,30},{7,103},{8,0},{9... | collective-permute-start | bytes 1179656 | tf_op jit(solution)/shard_map/ppermute | solution.py:46
  34.8 8.9 %collective-permute-start.11 = (f32[768,128]{1,0:T(8,128)S(1)}, f32[768,128]{1,0:T(8,128)S(1)}, u32[]{:S(2)}, u32[]{:S(2)}) collective-permute-start(f32[768,128]{1,0:T(8,128)S(1)} %get-tuple-element.31.witness.b0), channel_id=1, source_target_pairs={{0,16},{1,65},{2,18},{3,67},{4,20},{5,69},{6,22},{7,71},{8,24},{9,... | collective-permute-start | bytes 1179656 | tf_op jit(solution)/shard_map/ppermute | solution.py:46
  35.3 12.1 %collective-permute-start.9 = (f32[768,128]{1,0:T(8,128)S(1)}, f32[768,128]{1,0:T(8,128)S(1)}, u32[]{:S(2)}, u32[]{:S(2)}) collective-permute-start(f32[768,128]{1,0:T(8,128)S(1)} %get-tuple-element.31.witness.b0), channel_id=1, source_target_pairs={{0,8},{1,33},{2,10},{3,35},{4,12},{5,37},{6,14},{7,39},{8,16},{9,4... | collective-permute-start | bytes 1179656 | tf_op jit(solution)/shard_map/ppermute | solution.py:46
  47.5 6.6 %collective-permute-start.15 = (f32[1848,128]{1,0:T(8,128)S(1)}, f32[1848,128]{1,0:T(8,128)S(1)}, u32[]{:S(2)}, u32[]{:S(2)}) collective-permute-start(f32[1848,128]{1,0:T(8,128)S(1)} %get-tuple-element.39.above), channel_id=1, source_target_pairs={{0,1},{1,0},{2,3},{3,2},{4,5},{5,4},{6,7},{7,6},{8,9},{9,8},{10,11... | collective-permute-start | bytes 2838536 | tf_op jit(solution)/shard_map/ppermute | solution.py:50
  51.0 3.5 %collective-permute-start.16 = (f32[1848,128]{1,0:T(8,128)S(1)}, f32[1848,128]{1,0:T(8,128)S(1)}, u32[]{:S(2)}, u32[]{:S(2)}) collective-permute-start(f32[1848,128]{1,0:T(8,128)S(1)} %get-tuple-element.38.below), channel_id=1, source_target_pairs={{0,1},{1,0},{2,3},{3,2},{4,5},{5,4},{6,7},{7,6},{8,9},{9,8},{10,11... | collective-permute-start | bytes 2838536 | tf_op jit(solution)/shard_map/ppermute | solution.py:50
  51.0 12.3 %collective-permute-start.6 = (f32[768,128]{1,0:T(8,128)S(1)}, f32[768,128]{1,0:T(8,128)S(1)}, u32[]{:S(2)}, u32[]{:S(2)}) collective-permute-start(f32[768,128]{1,0:T(8,128)S(1)} %get-tuple-element.30.b0), channel_id=1, source_target_pairs={{0,8},{1,33},{2,10},{3,35},{4,12},{5,37},{6,14},{7,39},{8,16},{9,4... | collective-permute-start | bytes 1179656 | tf_op jit(solution)/shard_map/ppermute | solution.py:46
  51.0 12.3 %collective-permute-start.7 = (f32[768,128]{1,0:T(8,128)S(1)}, f32[768,128]{1,0:T(8,128)S(1)}, u32[]{:S(2)}, u32[]{:S(2)}) collective-permute-start(f32[768,128]{1,0:T(8,128)S(1)} %get-tuple-element.30.b0), channel_id=1, source_target_pairs={{0,24},{1,97},{2,26},{3,99},{4,28},{5,101},{6,30},{7,103},{8,0},{9... | collective-permute-start | bytes 1179656 | tf_op jit(solution)/shard_map/ppermute | solution.py:46
  53.7 9.7 %collective-permute-start.8 = (f32[768,128]{1,0:T(8,128)S(1)}, f32[768,128]{1,0:T(8,128)S(1)}, u32[]{:S(2)}, u32[]{:S(2)}) collective-permute-start(f32[768,128]{1,0:T(8,128)S(1)} %get-tuple-element.30.b0), channel_id=1, source_target_pairs={{0,16},{1,65},{2,18},{3,67},{4,20},{5,69},{6,22},{7,71},{8,24},{9,... | collective-permute-start | bytes 1179656 | tf_op jit(solution)/shard_map/ppermute | solution.py:46
  57.3 6.1 %collective-permute-start.17 = (f32[144,256]{1,0:T(8,128)S(1)}, f32[144,256]{1,0:T(8,128)S(1)}, u32[]{:S(2)}, u32[]{:S(2)}) collective-permute-start(f32[144,256]{1,0:T(8,128)S(1)} %get-tuple-element.41), channel_id=1, source_target_pairs={{0,6},{1,3},{2,0},{3,5},{4,2},{5,7},{6,4},{7,1},{8,14},{9,11},{10,... | collective-permute-start | bytes 442376 | tf_op jit(solution)/shard_map/ppermute | solution.py:46
  57.4 6.0 %collective-permute-start.18 = (f32[144,256]{1,0:T(8,128)S(1)}, f32[144,256]{1,0:T(8,128)S(1)}, u32[]{:S(2)}, u32[]{:S(2)}) collective-permute-start(f32[144,256]{1,0:T(8,128)S(1)} %get-tuple-element.42), channel_id=1, source_target_pairs={{0,2},{1,7},{2,4},{3,1},{4,6},{5,3},{6,0},{7,5},{8,10},{9,15},{10,... | collective-permute-start | bytes 442376 | tf_op jit(solution)/shard_map/ppermute | solution.py:46
  63.4 10.8 %copy-start.3 = (f32[3,6,1,1296]{3,2,1,0:T(1,128)S(1)}, f32[3,6,1,1296]{3,2,1,0:T(1,128)}, u32[]{:S(2)}) copy-start(f32[3,6,1,1296]{3,2,1,0:T(1,128)} %amp_ref.3) | copy-start | bytes 279940
  63.4 10.8 %copy-start.5 = (s32[8]{0:T(128)S(1)}, s32[8]{0:T(128)}, u32[]{:S(2)}) copy-start(s32[8]{0:T(128)} %occ_ref.3) | copy-start | bytes 100
  65.6 16.2 %all-to-all-start = ((f32[32,8,128]{2,1,0:T(8,128)}), f32[32,8,128]{2,1,0:T(8,128)S(1)}, u32[]{:S(2)}, u32[]{:S(2)}) async-start(f32[32,8,128]{2,1,0:T(8,128)} %shard_map.82), calls=%async_computation | async-start | bytes 262144 | tf_op jit(solution)/shard_map/all_to_all | solution.py:507
  (6 other events, 34.7 us)

commit v10 on v8

--- a/solution.py
+++ b/solution.py
@@ -59,14 +59,9 @@
     return a, lane - 36 * a
 
 
-def window_copies(integrals, ref, first, sems, base):
-    copies = []
-    for t in range(SPAN):
-        start = pl.multiple_of((base + t) * LANES, LANES)
-        copies.append(
-            pltpu.make_async_copy(integrals.at[:, :, pl.ds(start, LANES)], ref.at[first + t, 0:81], sems.at[t])
-        )
-    return copies
+def window_copy(integrals, target, sem, chip):
+    start = pl.multiple_of((chip & 3) * 2560, LANES)
+    return pltpu.make_async_copy(integrals.at[:, :, pl.ds(start, DEPTH)], target.at[0:81], sem)
 
 
 def open_step(occ_ref, vir_ref, amp_ref, integrals, keep_out, send_out, first_out, second_out, home_out,
@@ -76,11 +71,11 @@
         pltpu.make_async_copy(source, target, sems.at[at])
         for at, (source, target) in enumerate(((occ_ref, occ), (vir_ref, vir), (amp_ref, amp)))
     ]
-    groups = [
-        window_copies(integrals, first_v, 0, cut_sems.at[0], ((y + 1 + 2 * core) & 3) * 20),
-        window_copies(integrals, second_v, 0, cut_sems.at[1], ((y + 3 - 2 * core) & 3) * 20),
-        window_copies(integrals, home, 0, cut_sems.at[2], y * 20),
-        window_copies(integrals, home, SPAN, cut_sems.at[3], ((y + 2) & 3) * 20),
+    cuts = [
+        window_copy(integrals, first_v, cut_sems.at[0], y + 1 + 2 * core),
+        window_copy(integrals, second_v, cut_sems.at[1], y + 3 - 2 * core),
+        window_copy(integrals, home.at[0], cut_sems.at[2], y),
+        window_copy(integrals, home.at[1], cut_sems.at[3], y + 2),
     ]
     outs = [
         pltpu.make_async_copy(source, target, out_sems.at[at])
@@ -88,18 +83,15 @@
             (
                 (first_v, first_out),
                 (second_v, second_out),
-                (home.at[0:SPAN], home_out.at[0:SPAN]),
-                (home.at[SPAN : 2 * SPAN], home_out.at[SPAN : 2 * SPAN]),
+                (home.at[0], home_out.at[0]),
+                (home.at[1], home_out.at[1]),
                 (keep, keep_out),
                 (send, send_out),
             )
         )
     ]
-    for copy in copies:
+    for copy in copies + cuts:
         copy.start()
-    for group in groups:
-        for copy in group:
-            copy.start()
     wide[...] = jnp.zeros_like(wide)
     for copy in copies:
         copy.wait()
@@ -136,9 +128,8 @@
 
     for copy in outs[4:]:
         copy.start()
-    for group, out in zip(groups, outs):
-        for copy in group:
-            copy.wait()
+    for copy, out in zip(cuts, outs):
+        copy.wait()
         out.start()
     for copy in outs:
         copy.wait()
@@ -215,10 +206,8 @@
     return high, (value - high.astype(F32)).astype(BF16)
 
 
-def tiles_side(ref, first):
-    return jnp.concatenate(
-        [ref[(first + t) * PSLOT : (first + t + 1) * PSLOT, :] for t in range(SPAN)], axis=1
-    )
+def rows_side(ref, first):
+    return jnp.concatenate([ref[pl.ds(first + t, PSLOT, stride=SPAN), :] for t in range(SPAN)], axis=1)
 
 
 def last_by_last(p, q):
@@ -227,11 +216,11 @@
 
 def split_home(home, home_other, witness, near_high, near_low, far_high, far_low):
     for side, ref in enumerate((home, home_other)):
-        high, low = split(tiles_side(ref, 0))
+        high, low = split(rows_side(ref, 0))
         rows = slice(side * PSLOT, (side + 1) * PSLOT)
         near_high[rows, :] = high
         near_low[rows, :] = low
-        high, low = split(tiles_side(ref, SPAN))
+        high, low = split(rows_side(ref, PROWS))
         pad = jnp.zeros((LANES - PSLOT, DEPTH), BF16)
         rows = slice(side * LANES, (side + 1) * LANES)
         far_high[rows, :] = jnp.concatenate([high, pad], axis=0)
@@ -241,7 +230,7 @@
 def multiply_near(b0, b1, b2, b3, near_high, near_low, below, below_other, above, above_other,
                   here_sum, below_sum, above_sum, extra, turned):
     high, low = left_side((b0, b1, b2, b3), extra)
-    sides = [tiles_side(ref, 0) for ref in (below, below_other, above, above_other)]
+    sides = [rows_side(ref, 0) for ref in (below, below_other, above, above_other)]
     v_high, v_low = split(jnp.concatenate(sides, axis=0))
     v_high = jnp.concatenate([near_high[...], v_high], axis=0)
     v_low = jnp.concatenate([near_low[...], v_low], axis=0)
@@ -372,12 +361,12 @@
     x, z, y, core = places()
     shape = jax.ShapeDtypeStruct
     integrals = vvvv.reshape(81, 1, 10368)
-    window = shape((SPAN, PSLOT, 1, LANES), F32)
+    window = shape((PSLOT, 1, DEPTH), F32)
     flat = lambda value: value.reshape(PROWS, LANES)
     keep, send, first_v, second_v, home = pl.pallas_call(
         open_step,
         out_shape=[shape((SHARD, LANES), F32)] * 2 + [window] * 2
-        + [shape((2 * SPAN, PSLOT, 1, LANES), F32)],
+        + [shape((2, PSLOT, 1, DEPTH), F32)],
         in_specs=[HBM] * 4,
         out_specs=[ANY] * 5,
         scratch_shapes=[
@@ -387,11 +376,11 @@
             pltpu.SMEM((8,), jnp.int32),
             pltpu.VMEM((SHARD, LANES), F32),
             pltpu.VMEM((SHARD, LANES), F32),
-            pltpu.VMEM((SPAN, PSLOT, 1, LANES), F32),
-            pltpu.VMEM((SPAN, PSLOT, 1, LANES), F32),
-            pltpu.VMEM((2 * SPAN, PSLOT, 1, LANES), F32),
+            pltpu.VMEM((PSLOT, 1, DEPTH), F32),
+            pltpu.VMEM((PSLOT, 1, DEPTH), F32),
+            pltpu.VMEM((2, PSLOT, 1, DEPTH), F32),
             pltpu.SemaphoreType.DMA((3,)),
-            pltpu.SemaphoreType.DMA((4, SPAN)),
+            pltpu.SemaphoreType.DMA((4,)),
             pltpu.SemaphoreType.DMA((6,)),
         ],
         compiler_params=HUGE,

time: 79.5 us -> 78 us (0.981)
  Pallas kernels: 16.3 us -> 14.8 us
    pallas_call x1, Pallas kernels: 5.38 us -> 3.87 us  [on_device(): pl.pallas_call(open_step, out_shape=[shape((SHARD, LANES), F32)] * 2 + [w...]
where the time goes in v10:
time: 78 us; the launch traced here: 77.7 us
  starting transfers between devices  35.5 us (46%)
  waiting for transfers between devices  26.5 us (34%)
  Pallas kernels  14.8 us (19%)
  local copies, waits for them, and re-layouts  0.85 us (1%)
    ppermute x14, waiting for transfers between devices, ring(): return lax.ppermute(value, AXES, pairs)  20.6 us
    ppermute x14, starting transfers between devices, ring(): return lax.ppermute(value, AXES, pairs)  20.5 us
    all_to_all x1, starting transfers between devices, on_device(): ladder = lax.all_to_all(packed, ('x', 'z', 'core'), 0, 0, tiled=True)  7.54 us
    ppermute x4, starting transfers between devices, swap_core(): return lax.ppermute(value, 'core', [(0, 1), (1, 0)])  7.38 us
    all_to_all x1, waiting for transfers between devices, on_device(): ladder = lax.all_to_all(packed, ('x', 'z', 'core'), 0, 0, tiled=True)  4.82 us
    pallas_call x1, Pallas kernels, on_device(): pl.pallas_call(open_step, out_shape=[shape((SHARD, LANES), F32)] * 2 + [w...  3.87 us
    pallas_call x1, Pallas kernels, on_device(): pl.pallas_call(local_step, out_shape=[shape((18, 1296), F32)] * 2, in_spe...  2.83 us
    pallas_call x1, Pallas kernels, on_device(): pl.pallas_call(multiply_near, out_shape=sums, in_specs=[VMEM] * 10, out_s...  2.74 us
  transfers between devices with their start and end apart: 20, of which 11 were waited for; matrix products, arithmetic and copies ran while one was open for 0% of the time, Pallas kernels for 10%

profile of v10, /device:TPU:1, one launch (start us, length us, event | category | flops | bytes accessed | tf_op | source)
XLA Modules:
  0.0 77.7 jit_solution(12677074052469111257)
XLA Ops:
  0.0 3.9 %shard_map.73 = (f32[104,128]{1,0:T(8,128)}, f32[104,128]{1,0:T(8,128)}, f32[88,1,2688]{2,1,0:T(1,128)}, f32[88,1,2688]{2,1,0:T(1,128)}, f32[2,88,1,2688]{3,2,1,0:T(1,128)}) custom-call(s32[8]{0:T(128)} %occ_ref.3, s32[8]{0:T(128)} %vir_ref.3, f32[3,6,1,1296]{3,2,1,0:T(1,128)} %amp_ref.3, f32[81,1,10368]{2,1,0:T(1,128)} %bitcast.5), custom_call_target="tpu_custom_call" | custom-call | tf_op jit(solution)/shard_map/pallas_call | solution.py:366
  3.9 1.5 %collective-permute-start = (f32[104,128]{1,0:T(8,128)}, f32[104,128]{1,0:T(8,128)S(1)}, u32[]{:S(2)}, u32[]{:S(2)}) collective-permute-start(f32[104,128]{1,0:T(8,128)} %get-tuple-element.26), channel_id=1, source_target_pairs={{0,1},{1,0},{2,3},{3,2},{4,5},{5,4},{6,7},{7,6},{8,9},{9,8},{10,11... | collective-permute-start | bytes 159752 | tf_op jit(solution)/shard_map/ppermute | solution.py:49
  7.7 3.0 %collective-permute-start.1 = (f32[192,128]{1,0:T(8,128)S(1)}, f32[192,128]{1,0:T(8,128)S(1)}, u32[]{:S(2)}, u32[]{:S(2)}) collective-permute-start(f32[192,128]{1,0:T(8,128)S(1)} %get-tuple-element.28.near), channel_id=1, source_target_pairs={{0,4},{1,5},{2,6},{3,7},{4,0},{5,1},{6,2},{7,3},{8,12},{9,13},{10,... | collective-permute-start | bytes 294920 | tf_op jit(solution)/shard_map/ppermute | solution.py:45
  11.5 2.0 %collective-permute-done.1.far.refs_1_ = f32[192,128]{1,0:T(8,128)S(1)} collective-permute-done((f32[192,128]{1,0:T(8,128)S(1)}, f32[192,128]{1,0:T(8,128)S(1)}, u32[]{:S(2)}, u32[]{:S(2)}) %collective-permute-start.1) | collective-permute-done | bytes 98336 | tf_op jit(solution)/shard_map/ppermute | solution.py:45
  13.6 1.3 %collective-permute-start.13 = (f32[1848,128]{1,0:T(8,128)S(1)}, f32[1848,128]{1,0:T(8,128)S(1)}, u32[]{:S(2)}, u32[]{:S(2)}) collective-permute-start(f32[1848,128]{1,0:T(8,128)S(1)} %shard_map.78), channel_id=1, source_target_pairs={{0,6},{1,3},{2,0},{3,5},{4,2},{5,7},{6,4},{7,1},{8,14},{9,11},{10,... | collective-permute-start | bytes 2838536 | tf_op jit(solution)/shard_map/ppermute | solution.py:45
  14.9 1.7 %collective-permute-start.3 = (f32[384,128]{1,0:T(8,128)S(1)}, f32[384,128]{1,0:T(8,128)S(1)}, u32[]{:S(2)}, u32[]{:S(2)}) collective-permute-start(f32[384,128]{1,0:T(8,128)S(1)} %shard_map.75.b0), channel_id=1, source_target_pairs={{0,32},{1,9},{2,34},{3,11},{4,36},{5,13},{6,38},{7,15},{8,40},{9,1... | collective-permute-start | bytes 589832 | tf_op jit(solution)/shard_map/ppermute | solution.py:45
  16.6 2.2 %collective-permute-start.4 = (f32[384,128]{1,0:T(8,128)S(1)}, f32[384,128]{1,0:T(8,128)S(1)}, u32[]{:S(2)}, u32[]{:S(2)}) collective-permute-start(f32[384,128]{1,0:T(8,128)S(1)} %shard_map.75.b0), channel_id=1, source_target_pairs={{0,96},{1,25},{2,98},{3,27},{4,100},{5,29},{6,102},{7,31},{8,104},... | collective-permute-start | bytes 589832 | tf_op jit(solution)/shard_map/ppermute | solution.py:45
  20.0 2.0 %collective-permute-done.3.b1 = f32[384,128]{1,0:T(8,128)S(1)} collective-permute-done((f32[384,128]{1,0:T(8,128)S(1)}, f32[384,128]{1,0:T(8,128)S(1)}, u32[]{:S(2)}, u32[]{:S(2)}) %collective-permute-start.3) | collective-permute-done | bytes 196640 | tf_op jit(solution)/shard_map/ppermute | solution.py:45
  22.1 1.4 %collective-permute-done.4.b2 = f32[384,128]{1,0:T(8,128)S(1)} collective-permute-done((f32[384,128]{1,0:T(8,128)S(1)}, f32[384,128]{1,0:T(8,128)S(1)}, u32[]{:S(2)}, u32[]{:S(2)}) %collective-permute-start.4) | collective-permute-done | bytes 196640 | tf_op jit(solution)/shard_map/ppermute | solution.py:45
  23.5 1.5 %collective-permute-done.5.b3 = f32[384,128]{1,0:T(8,128)S(1)} collective-permute-done((f32[384,128]{1,0:T(8,128)S(1)}, f32[384,128]{1,0:T(8,128)S(1)}, u32[]{:S(2)}, u32[]{:S(2)}) %collective-permute-start.5) | collective-permute-done | bytes 196640 | tf_op jit(solution)/shard_map/ppermute | solution.py:45
  25.1 2.8 %collective-permute-start.10 = (f32[768,128]{1,0:T(8,128)S(1)}, f32[768,128]{1,0:T(8,128)S(1)}, u32[]{:S(2)}, u32[]{:S(2)}) collective-permute-start(f32[768,128]{1,0:T(8,128)S(1)} %get-tuple-element.31.witness.b0), channel_id=1, source_target_pairs={{0,24},{1,97},{2,26},{3,99},{4,28},{5,101},{6,30},{7,103},{8,0},{9... | collective-permute-start | bytes 1179656 | tf_op jit(solution)/shard_map/ppermute | solution.py:45
  28.8 2.1 %shard_map.77 = (bf16[176,2688]{1,0:T(8,128)(2,1)S(1)}, bf16[176,2688]{1,0:T(8,128)(2,1)S(1)}, bf16[256,2688]{1,0:T(8,128)(2,1)S(1)}, bf16[256,2688]{1,0:T(8,128)(2,1)S(1)}) custom-call(f32[3696,128]{1,0:T(8,128)} %get-tuple-element.29.home, f32[3696,128]{1,0:T(8,128)S(1)} %collective-permute-done.2.home_other, f32[768,128]{1,0:T(8,128)S(1)} %get-tuple-element.31.witness.b0), custom_call_target="tpu_custom_call" | custom-call | flops 1 | bytes 1 | tf_op jit(solution)/shard_map/pallas_call | solution.py:419
  31.4 4.2 %collective-permute-done.13.refs_1_ = f32[1848,128]{1,0:T(8,128)S(1)} collective-permute-done((f32[1848,128]{1,0:T(8,128)S(1)}, f32[1848,128]{1,0:T(8,128)S(1)}, u32[]{:S(2)}, u32[]{:S(2)}) %collective-permute-start.13) | collective-permute-done | bytes 946208 | tf_op jit(solution)/shard_map/ppermute | solution.py:45
  35.5 1.4 %collective-permute-done.10.refs_3_.b2 = f32[768,128]{1,0:T(8,128)S(1)} collective-permute-done((f32[768,128]{1,0:T(8,128)S(1)}, f32[768,128]{1,0:T(8,128)S(1)}, u32[]{:S(2)}, u32[]{:S(2)}) %collective-permute-start.10) | collective-permute-done | bytes 393248 | tf_op jit(solution)/shard_map/ppermute | solution.py:45
  36.9 3.6 %collective-permute-done.9.refs_2_.b1 = f32[768,128]{1,0:T(8,128)S(1)} collective-permute-done((f32[768,128]{1,0:T(8,128)S(1)}, f32[768,128]{1,0:T(8,128)S(1)}, u32[]{:S(2)}, u32[]{:S(2)}) %collective-permute-start.9) | collective-permute-done | bytes 393248 | tf_op jit(solution)/shard_map/ppermute | solution.py:45
  40.6 5.4 %collective-permute-start.15 = (f32[1848,128]{1,0:T(8,128)S(1)}, f32[1848,128]{1,0:T(8,128)S(1)}, u32[]{:S(2)}, u32[]{:S(2)}) collective-permute-start(f32[1848,128]{1,0:T(8,128)S(1)} %get-tuple-element.39.above), channel_id=1, source_target_pairs={{0,1},{1,0},{2,3},{3,2},{4,5},{5,4},{6,7},{7,6},{8,9},{9,8},{10,11... | collective-permute-start | bytes 2838536 | tf_op jit(solution)/shard_map/ppermute | solution.py:49
  46.0 1.7 %collective-permute-start.6 = (f32[768,128]{1,0:T(8,128)S(1)}, f32[768,128]{1,0:T(8,128)S(1)}, u32[]{:S(2)}, u32[]{:S(2)}) collective-permute-start(f32[768,128]{1,0:T(8,128)S(1)} %get-tuple-element.30.b0), channel_id=1, source_target_pairs={{0,8},{1,33},{2,10},{3,35},{4,12},{5,37},{6,14},{7,39},{8,16},{9,4... | collective-permute-start | bytes 1179656 | tf_op jit(solution)/shard_map/ppermute | solution.py:45
  49.9 2.7 %shard_map.80 = (f32[144,256]{1,0:T(8,128)S(1)}, f32[144,256]{1,0:T(8,128)S(1)}, f32[144,256]{1,0:T(8,128)S(1)}) custom-call(f32[768,128]{1,0:T(8,128)S(1)} %get-tuple-element.31.witness.b0, f32[768,128]{1,0:T(8,128)S(1)} %collective-permute-done.9.refs_2_.b1, f32[768,128]{1,0:T(8,128)S(1)} %collective-permute-done.10.refs_3_.b2, ...), custom_call_target="tpu_custom_call" | custom-call | tf_op jit(solution)/shard_map/pallas_call | solution.py:455
  52.7 2.7 %collective-permute-start.18 = (f32[144,256]{1,0:T(8,128)S(1)}, f32[144,256]{1,0:T(8,128)S(1)}, u32[]{:S(2)}, u32[]{:S(2)}) collective-permute-start(f32[144,256]{1,0:T(8,128)S(1)} %get-tuple-element.42), channel_id=1, source_target_pairs={{0,2},{1,7},{2,4},{3,1},{4,6},{5,3},{6,0},{7,5},{8,10},{9,15},{10,... | collective-permute-start | bytes 442376 | tf_op jit(solution)/shard_map/ppermute | solution.py:45
  55.4 3.9 %collective-permute-done.8.b3 = f32[768,128]{1,0:T(8,128)S(1)} collective-permute-done((f32[768,128]{1,0:T(8,128)S(1)}, f32[768,128]{1,0:T(8,128)S(1)}, u32[]{:S(2)}, u32[]{:S(2)}) %collective-permute-start.8) | collective-permute-done | bytes 393248 | tf_op jit(solution)/shard_map/ppermute | solution.py:45
  59.3 2.2 %shard_map.81 = f32[32,8,128]{2,1,0:T(8,128)} custom-call(f32[768,128]{1,0:T(8,128)S(1)} %get-tuple-element.30.b0, f32[768,128]{1,0:T(8,128)S(1)} %collective-permute-done.6.b1, f32[768,128]{1,0:T(8,128)S(1)} %collective-permute-done.7.b2, f32[768,128]{1,0:T(8,128)S(1)} %collective-permute-done.8.b3, bf16[256,2688]{1,0:T(8,128)(2,1)S(1)} %get-tuple-element.32.v_high, ...), custom_call_target="tpu_custom_call" | custom-call | tf_op jit(solution)/shard_map/pallas_call | solution.py:465
  61.6 7.5 %all-to-all-start = ((f32[32,8,128]{2,1,0:T(8,128)}), f32[32,8,128]{2,1,0:T(8,128)S(1)}, u32[]{:S(2)}, u32[]{:S(2)}) async-start(f32[32,8,128]{2,1,0:T(8,128)} %shard_map.81), calls=%async_computation | async-start | bytes 262144 | tf_op jit(solution)/shard_map/all_to_all | solution.py:473
  69.2 2.8 %shard_map.82 = (f32[18,1296]{1,0:T(8,128)S(1)}, f32[18,1296]{1,0:T(8,128)S(1)}) custom-call(s32[8]{0:T(128)S(1)} %copy-done.3, s32[8]{0:T(128)S(1)} %copy-done.4, f32[8,6]{1,0:T(8,128)S(1)} %copy-done.6, f32[8,36]{1,0:T(8,128)S(1)} %copy-done.7, f32[3,6,1,1296]{3,2,1,0:T(1,128)S(1)} %copy-done.1, f32[108,1,216]{2,1,0:T(1,128)S(1)} %copy-done.5, ...), custom_call_target="tpu_custom_call" | custom-call | flops 100000000 | bytes 1000000 | tf_op jit(solution)/shard_map/pallas_call | solution.py:433
  72.0 4.8 %all-to-all-done.sums = f32[32,8,128]{2,1,0:T(8,128)S(1)} async-done(((f32[32,8,128]{2,1,0:T(8,128)}), f32[32,8,128]{2,1,0:T(8,128)S(1)}, u32[]{:S(2)}, u32[]{:S(2)}) %all-to-all-start) | async-done | bytes 131104 | tf_op jit(solution)/shard_map/all_to_all | solution.py:473
  (45 shorter events, 8.9 us)
Async XLA Ops:
  3.9 2.6 %collective-permute-start = (f32[104,128]{1,0:T(8,128)}, f32[104,128]{1,0:T(8,128)S(1)}, u32[]{:S(2)}, u32[]{:S(2)}) collective-permute-start(f32[104,128]{1,0:T(8,128)} %get-tuple-element.26), channel_id=1, source_target_pairs={{0,1},{1,0},{2,3},{3,2},{4,5},{5,4},{6,7},{7,6},{8,9},{9,8},{10,11... | collective-permute-start | bytes 159752 | tf_op jit(solution)/shard_map/ppermute | solution.py:49
  7.3 7.6 %collective-permute-start.2 = (f32[3696,128]{1,0:T(8,128)}, f32[3696,128]{1,0:T(8,128)S(1)}, u32[]{:S(2)}, u32[]{:S(2)}) collective-permute-start(f32[3696,128]{1,0:T(8,128)} %get-tuple-element.29.home), channel_id=1, source_target_pairs={{0,1},{1,0},{2,3},{3,2},{4,5},{5,4},{6,7},{7,6},{8,9},{9,8},{10,11... | collective-permute-start | bytes 5677064 | tf_op jit(solution)/shard_map/ppermute | solution.py:49
  7.7 5.8 %collective-permute-start.1 = (f32[192,128]{1,0:T(8,128)S(1)}, f32[192,128]{1,0:T(8,128)S(1)}, u32[]{:S(2)}, u32[]{:S(2)}) collective-permute-start(f32[192,128]{1,0:T(8,128)S(1)} %get-tuple-element.28.near), channel_id=1, source_target_pairs={{0,4},{1,5},{2,6},{3,7},{4,0},{5,1},{6,2},{7,3},{8,12},{9,13},{10,... | collective-permute-start | bytes 294920 | tf_op jit(solution)/shard_map/ppermute | solution.py:45
  10.7 20.6 %collective-permute-start.12 = (f32[1848,128]{1,0:T(8,128)S(1)}, f32[1848,128]{1,0:T(8,128)S(1)}, u32[]{:S(2)}, u32[]{:S(2)}) collective-permute-start(f32[1848,128]{1,0:T(8,128)S(1)} %bitcast.6), channel_id=1, source_target_pairs={{0,2},{1,7},{2,4},{3,1},{4,6},{5,3},{6,0},{7,5},{8,10},{9,15},{10,... | collective-permute-start | bytes 2838536 | tf_op jit(solution)/shard_map/ppermute | solution.py:45
  13.6 22.0 %collective-permute-start.13 = (f32[1848,128]{1,0:T(8,128)S(1)}, f32[1848,128]{1,0:T(8,128)S(1)}, u32[]{:S(2)}, u32[]{:S(2)}) collective-permute-start(f32[1848,128]{1,0:T(8,128)S(1)} %shard_map.78), channel_id=1, source_target_pairs={{0,6},{1,3},{2,0},{3,5},{4,2},{5,7},{6,4},{7,1},{8,14},{9,11},{10,... | collective-permute-start | bytes 2838536 | tf_op jit(solution)/shard_map/ppermute | solution.py:45
  14.9 7.2 %collective-permute-start.3 = (f32[384,128]{1,0:T(8,128)S(1)}, f32[384,128]{1,0:T(8,128)S(1)}, u32[]{:S(2)}, u32[]{:S(2)}) collective-permute-start(f32[384,128]{1,0:T(8,128)S(1)} %shard_map.75.b0), channel_id=1, source_target_pairs={{0,32},{1,9},{2,34},{3,11},{4,36},{5,13},{6,38},{7,15},{8,40},{9,1... | collective-permute-start | bytes 589832 | tf_op jit(solution)/shard_map/ppermute | solution.py:45
  16.6 6.9 %collective-permute-start.4 = (f32[384,128]{1,0:T(8,128)S(1)}, f32[384,128]{1,0:T(8,128)S(1)}, u32[]{:S(2)}, u32[]{:S(2)}) collective-permute-start(f32[384,128]{1,0:T(8,128)S(1)} %shard_map.75.b0), channel_id=1, source_target_pairs={{0,96},{1,25},{2,98},{3,27},{4,100},{5,29},{6,102},{7,31},{8,104},... | collective-permute-start | bytes 589832 | tf_op jit(solution)/shard_map/ppermute | solution.py:45
  18.8 6.3 %collective-permute-start.5 = (f32[384,128]{1,0:T(8,128)S(1)}, f32[384,128]{1,0:T(8,128)S(1)}, u32[]{:S(2)}, u32[]{:S(2)}) collective-permute-start(f32[384,128]{1,0:T(8,128)S(1)} %shard_map.75.b0), channel_id=1, source_target_pairs={{0,64},{1,17},{2,66},{3,19},{4,68},{5,21},{6,70},{7,23},{8,72},{9,... | collective-permute-start | bytes 589832 | tf_op jit(solution)/shard_map/ppermute | solution.py:45
  22.1 6.1 %collective-permute-start.14 = (f32[108,1,216]{2,1,0:T(1,128)S(1)}, f32[108,1,216]{2,1,0:T(1,128)S(1)}, u32[]{:S(2)}, u32[]{:S(2)}) collective-permute-start(f32[108,1,216]{2,1,0:T(1,128)S(1)} %copy-done.5), channel_id=1, source_target_pairs={{0,8},{8,0},{16,24},{24,16},{1,9},{9,1},{17,25},{25,17},{2,10},{10... | collective-permute-start | bytes 279944 | tf_op jit(solution)/shard_map/ppermute | solution.py:390
  25.1 11.8 %collective-permute-start.10 = (f32[768,128]{1,0:T(8,128)S(1)}, f32[768,128]{1,0:T(8,128)S(1)}, u32[]{:S(2)}, u32[]{:S(2)}) collective-permute-start(f32[768,128]{1,0:T(8,128)S(1)} %get-tuple-element.31.witness.b0), channel_id=1, source_target_pairs={{0,24},{1,97},{2,26},{3,99},{4,28},{5,101},{6,30},{7,103},{8,0},{9... | collective-permute-start | bytes 1179656 | tf_op jit(solution)/shard_map/ppermute | solution.py:45
  28.0 8.9 %collective-permute-start.11 = (f32[768,128]{1,0:T(8,128)S(1)}, f32[768,128]{1,0:T(8,128)S(1)}, u32[]{:S(2)}, u32[]{:S(2)}) collective-permute-start(f32[768,128]{1,0:T(8,128)S(1)} %get-tuple-element.31.witness.b0), channel_id=1, source_target_pairs={{0,16},{1,65},{2,18},{3,67},{4,20},{5,69},{6,22},{7,71},{8,24},{9,... | collective-permute-start | bytes 1179656 | tf_op jit(solution)/shard_map/ppermute | solution.py:45
  28.2 12.3 %collective-permute-start.9 = (f32[768,128]{1,0:T(8,128)S(1)}, f32[768,128]{1,0:T(8,128)S(1)}, u32[]{:S(2)}, u32[]{:S(2)}) collective-permute-start(f32[768,128]{1,0:T(8,128)S(1)} %get-tuple-element.31.witness.b0), channel_id=1, source_target_pairs={{0,8},{1,33},{2,10},{3,35},{4,12},{5,37},{6,14},{7,39},{8,16},{9,4... | collective-permute-start | bytes 1179656 | tf_op jit(solution)/shard_map/ppermute | solution.py:45
  40.6 9.4 %collective-permute-start.15 = (f32[1848,128]{1,0:T(8,128)S(1)}, f32[1848,128]{1,0:T(8,128)S(1)}, u32[]{:S(2)}, u32[]{:S(2)}) collective-permute-start(f32[1848,128]{1,0:T(8,128)S(1)} %get-tuple-element.39.above), channel_id=1, source_target_pairs={{0,1},{1,0},{2,3},{3,2},{4,5},{5,4},{6,7},{7,6},{8,9},{9,8},{10,11... | collective-permute-start | bytes 2838536 | tf_op jit(solution)/shard_map/ppermute | solution.py:49
  46.0 3.9 %collective-permute-start.16 = (f32[1848,128]{1,0:T(8,128)S(1)}, f32[1848,128]{1,0:T(8,128)S(1)}, u32[]{:S(2)}, u32[]{:S(2)}) collective-permute-start(f32[1848,128]{1,0:T(8,128)S(1)} %get-tuple-element.38.below), channel_id=1, source_target_pairs={{0,1},{1,0},{2,3},{3,2},{4,5},{5,4},{6,7},{7,6},{8,9},{9,8},{10,11... | collective-permute-start | bytes 2838536 | tf_op jit(solution)/shard_map/ppermute | solution.py:49
  46.0 9.4 %collective-permute-start.6 = (f32[768,128]{1,0:T(8,128)S(1)}, f32[768,128]{1,0:T(8,128)S(1)}, u32[]{:S(2)}, u32[]{:S(2)}) collective-permute-start(f32[768,128]{1,0:T(8,128)S(1)} %get-tuple-element.30.b0), channel_id=1, source_target_pairs={{0,8},{1,33},{2,10},{3,35},{4,12},{5,37},{6,14},{7,39},{8,16},{9,4... | collective-permute-start | bytes 1179656 | tf_op jit(solution)/shard_map/ppermute | solution.py:45
  47.7 7.7 %collective-permute-start.7 = (f32[768,128]{1,0:T(8,128)S(1)}, f32[768,128]{1,0:T(8,128)S(1)}, u32[]{:S(2)}, u32[]{:S(2)}) collective-permute-start(f32[768,128]{1,0:T(8,128)S(1)} %get-tuple-element.30.b0), channel_id=1, source_target_pairs={{0,24},{1,97},{2,26},{3,99},{4,28},{5,101},{6,30},{7,103},{8,0},{9... | collective-permute-start | bytes 1179656 | tf_op jit(solution)/shard_map/ppermute | solution.py:45
  48.7 10.6 %collective-permute-start.8 = (f32[768,128]{1,0:T(8,128)S(1)}, f32[768,128]{1,0:T(8,128)S(1)}, u32[]{:S(2)}, u32[]{:S(2)}) collective-permute-start(f32[768,128]{1,0:T(8,128)S(1)} %get-tuple-element.30.b0), channel_id=1, source_target_pairs={{0,16},{1,65},{2,18},{3,67},{4,20},{5,69},{6,22},{7,71},{8,24},{9,... | collective-permute-start | bytes 1179656 | tf_op jit(solution)/shard_map/ppermute | solution.py:45
  52.7 6.6 %collective-permute-start.17 = (f32[144,256]{1,0:T(8,128)S(1)}, f32[144,256]{1,0:T(8,128)S(1)}, u32[]{:S(2)}, u32[]{:S(2)}) collective-permute-start(f32[144,256]{1,0:T(8,128)S(1)} %get-tuple-element.41), channel_id=1, source_target_pairs={{0,6},{1,3},{2,0},{3,5},{4,2},{5,7},{6,4},{7,1},{8,14},{9,11},{10,... | collective-permute-start | bytes 442376 | tf_op jit(solution)/shard_map/ppermute | solution.py:45
  52.7 6.5 %collective-permute-start.18 = (f32[144,256]{1,0:T(8,128)S(1)}, f32[144,256]{1,0:T(8,128)S(1)}, u32[]{:S(2)}, u32[]{:S(2)}) collective-permute-start(f32[144,256]{1,0:T(8,128)S(1)} %get-tuple-element.42), channel_id=1, source_target_pairs={{0,2},{1,7},{2,4},{3,1},{4,6},{5,3},{6,0},{7,5},{8,10},{9,15},{10,... | collective-permute-start | bytes 442376 | tf_op jit(solution)/shard_map/ppermute | solution.py:45
  59.3 9.8 %copy-start.1 = (f32[3,6,1,1296]{3,2,1,0:T(1,128)S(1)}, f32[3,6,1,1296]{3,2,1,0:T(1,128)}, u32[]{:S(2)}) copy-start(f32[3,6,1,1296]{3,2,1,0:T(1,128)} %amp_ref.3) | copy-start | bytes 279940
  59.3 9.8 %copy-start.3 = (s32[8]{0:T(128)S(1)}, s32[8]{0:T(128)}, u32[]{:S(2)}) copy-start(s32[8]{0:T(128)} %occ_ref.3) | copy-start | bytes 100
  59.3 9.8 %copy-start.4 = (s32[8]{0:T(128)S(1)}, s32[8]{0:T(128)}, u32[]{:S(2)}) copy-start(s32[8]{0:T(128)} %vir_ref.3) | copy-start | bytes 100
  59.3 9.8 %copy-start.6 = (f32[8,6]{1,0:T(8,128)S(1)}, f32[8,6]{1,0:T(8,128)}, u32[]{:S(2)}) copy-start(f32[8,6]{1,0:T(8,128)} %eps_occ_ref.1) | copy-start | bytes 580
  61.6 15.3 %all-to-all-start = ((f32[32,8,128]{2,1,0:T(8,128)}), f32[32,8,128]{2,1,0:T(8,128)S(1)}, u32[]{:S(2)}, u32[]{:S(2)}) async-start(f32[32,8,128]{2,1,0:T(8,128)} %shard_map.81), calls=%async_computation | async-start | bytes 262144 | tf_op jit(solution)/shard_map/all_to_all | solution.py:473
  (5 other events, 32.3 us)

commit v11 on v10

--- a/solution.py
+++ b/solution.py
@@ -6,8 +6,8 @@
 from jax.sharding import Mesh, PartitionSpec as P
 
 AXES = ("x", "z", "y", "core")
-SHIFTS = ((1, 1), (-1, -1), (2, 2))
-STEPS = (0, 1, -1, 2)
+SHIFTS = ((2, 2), (1, 1), (-1, -1))
+STEPS = (0, 2, 1, -1)
 LANES = 128
 TILES = 11
 WINDOW = TILES * LANES

time: 78 us -> 75.4 us (0.967)
  waiting for transfers between devices: 26.5 us -> 21.1 us
  starting transfers between devices: 35.5 us -> 38.3 us
    ppermute x14, waiting for transfers between devices: 20.6 us -> 15.1 us  [ring(): return lax.ppermute(value, AXES, pairs)]
    ppermute x14, starting transfers between devices: 20.5 us -> 22.3 us  [ring(): return lax.ppermute(value, AXES, pairs)]
    ppermute x1, starting transfers between devices: 0.01 us -> 1.3 us  [on_device(): partner = lax.ppermute(ovov, 'z', [(0, 1), (1, 0), (2, 3), (3, 2)])]
where the time goes in v11:
time: 75.4 us; the launch traced here: 75.2 us
  starting transfers between devices  38.3 us (51%)
  waiting for transfers between devices  21.1 us (28%)
  Pallas kernels  14.8 us (20%)
  local copies, waits for them, and re-layouts  0.85 us (1%)
    ppermute x14, starting transfers between devices, ring(): return lax.ppermute(value, AXES, pairs)  22.3 us
    ppermute x14, waiting for transfers between devices, ring(): return lax.ppermute(value, AXES, pairs)  15.1 us
    ppermute x4, starting transfers between devices, swap_core(): return lax.ppermute(value, 'core', [(0, 1), (1, 0)])  7.81 us
    all_to_all x1, starting transfers between devices, on_device(): ladder = lax.all_to_all(packed, ('x', 'z', 'core'), 0, 0, tiled=True)  6.93 us
    all_to_all x1, waiting for transfers between devices, on_device(): ladder = lax.all_to_all(packed, ('x', 'z', 'core'), 0, 0, tiled=True)  4.82 us
    pallas_call x1, Pallas kernels, on_device(): pl.pallas_call(open_step, out_shape=[shape((SHARD, LANES), F32)] * 2 + [w...  3.87 us
    pallas_call x1, Pallas kernels, on_device(): pl.pallas_call(local_step, out_shape=[shape((18, 1296), F32)] * 2, in_spe...  2.83 us
    pallas_call x1, Pallas kernels, on_device(): pl.pallas_call(multiply_near, out_shape=sums, in_specs=[VMEM] * 10, out_s...  2.74 us
  transfers between devices with their start and end apart: 20, of which 11 were waited for; matrix products, arithmetic and copies ran while one was open for 0% of the time, Pallas kernels for 10%

profile of v11, /device:TPU:1, one launch (start us, length us, event | category | flops | bytes accessed | tf_op | source)
XLA Modules:
  0.0 75.2 jit_solution(13456385618437069021)
XLA Ops:
  0.0 3.9 %shard_map.73 = (f32[104,128]{1,0:T(8,128)}, f32[104,128]{1,0:T(8,128)}, f32[88,1,2688]{2,1,0:T(1,128)}, f32[88,1,2688]{2,1,0:T(1,128)}, f32[2,88,1,2688]{3,2,1,0:T(1,128)}) custom-call(s32[8]{0:T(128)} %occ_ref.3, s32[8]{0:T(128)} %vir_ref.3, f32[3,6,1,1296]{3,2,1,0:T(1,128)} %amp_ref.3, f32[81,1,10368]{2,1,0:T(1,128)} %bitcast.5), custom_call_target="tpu_custom_call" | custom-call | tf_op jit(solution)/shard_map/pallas_call | solution.py:366
  3.9 1.5 %collective-permute-start = (f32[104,128]{1,0:T(8,128)}, f32[104,128]{1,0:T(8,128)S(1)}, u32[]{:S(2)}, u32[]{:S(2)}) collective-permute-start(f32[104,128]{1,0:T(8,128)} %get-tuple-element.26), channel_id=1, source_target_pairs={{0,1},{1,0},{2,3},{3,2},{4,5},{5,4},{6,7},{7,6},{8,9},{9,8},{10,11... | collective-permute-start | bytes 159752 | tf_op jit(solution)/shard_map/ppermute | solution.py:49
  7.7 3.0 %collective-permute-start.1 = (f32[192,128]{1,0:T(8,128)S(1)}, f32[192,128]{1,0:T(8,128)S(1)}, u32[]{:S(2)}, u32[]{:S(2)}) collective-permute-start(f32[192,128]{1,0:T(8,128)S(1)} %get-tuple-element.28.near), channel_id=1, source_target_pairs={{0,4},{1,5},{2,6},{3,7},{4,0},{5,1},{6,2},{7,3},{8,12},{9,13},{10,... | collective-permute-start | bytes 294920 | tf_op jit(solution)/shard_map/ppermute | solution.py:45
  11.5 2.0 %collective-permute-done.1.far.refs_1_ = f32[192,128]{1,0:T(8,128)S(1)} collective-permute-done((f32[192,128]{1,0:T(8,128)S(1)}, f32[192,128]{1,0:T(8,128)S(1)}, u32[]{:S(2)}, u32[]{:S(2)}) %collective-permute-start.1) | collective-permute-done | bytes 98336 | tf_op jit(solution)/shard_map/ppermute | solution.py:45
  13.6 1.3 %collective-permute-start.13 = (f32[1848,128]{1,0:T(8,128)S(1)}, f32[1848,128]{1,0:T(8,128)S(1)}, u32[]{:S(2)}, u32[]{:S(2)}) collective-permute-start(f32[1848,128]{1,0:T(8,128)S(1)} %shard_map.78), channel_id=1, source_target_pairs={{0,6},{1,3},{2,0},{3,5},{4,2},{5,7},{6,4},{7,1},{8,14},{9,11},{10,... | collective-permute-start | bytes 2838536 | tf_op jit(solution)/shard_map/ppermute | solution.py:45
  14.9 3.7 %collective-permute-start.3 = (f32[384,128]{1,0:T(8,128)S(1)}, f32[384,128]{1,0:T(8,128)S(1)}, u32[]{:S(2)}, u32[]{:S(2)}) collective-permute-start(f32[384,128]{1,0:T(8,128)S(1)} %shard_map.75.b0), channel_id=1, source_target_pairs={{0,64},{1,17},{2,66},{3,19},{4,68},{5,21},{6,70},{7,23},{8,72},{9,... | collective-permute-start | bytes 589832 | tf_op jit(solution)/shard_map/ppermute | solution.py:45
  19.3 1.9 %collective-permute-start.5 = (f32[384,128]{1,0:T(8,128)S(1)}, f32[384,128]{1,0:T(8,128)S(1)}, u32[]{:S(2)}, u32[]{:S(2)}) collective-permute-start(f32[384,128]{1,0:T(8,128)S(1)} %shard_map.75.b0), channel_id=1, source_target_pairs={{0,96},{1,25},{2,98},{3,27},{4,100},{5,29},{6,102},{7,31},{8,104},... | collective-permute-start | bytes 589832 | tf_op jit(solution)/shard_map/ppermute | solution.py:45
  21.6 1.3 %collective-permute-start.14 = (f32[108,1,216]{2,1,0:T(1,128)S(1)}, f32[108,1,216]{2,1,0:T(1,128)S(1)}, u32[]{:S(2)}, u32[]{:S(2)}) collective-permute-start(f32[108,1,216]{2,1,0:T(1,128)S(1)} %copy-done.5), channel_id=1, source_target_pairs={{0,8},{8,0},{16,24},{24,16},{1,9},{9,1},{17,25},{25,17},{2,10},{10... | collective-permute-start | bytes 279944 | tf_op jit(solution)/shard_map/ppermute | solution.py:390
  22.9 1.7 %collective-permute-done.4.b2 = f32[384,128]{1,0:T(8,128)S(1)} collective-permute-done((f32[384,128]{1,0:T(8,128)S(1)}, f32[384,128]{1,0:T(8,128)S(1)}, u32[]{:S(2)}, u32[]{:S(2)}) %collective-permute-start.4) | collective-permute-done | bytes 196640 | tf_op jit(solution)/shard_map/ppermute | solution.py:45
  24.8 1.3 %collective-permute-start.10 = (f32[768,128]{1,0:T(8,128)S(1)}, f32[768,128]{1,0:T(8,128)S(1)}, u32[]{:S(2)}, u32[]{:S(2)}) collective-permute-start(f32[768,128]{1,0:T(8,128)S(1)} %get-tuple-element.31.witness.b0), channel_id=1, source_target_pairs={{0,8},{1,33},{2,10},{3,35},{4,12},{5,37},{6,14},{7,39},{8,16},{9,4... | collective-permute-start | bytes 1179656 | tf_op jit(solution)/shard_map/ppermute | solution.py:45
  26.1 1.5 %collective-permute-start.11 = (f32[768,128]{1,0:T(8,128)S(1)}, f32[768,128]{1,0:T(8,128)S(1)}, u32[]{:S(2)}, u32[]{:S(2)}) collective-permute-start(f32[768,128]{1,0:T(8,128)S(1)} %get-tuple-element.31.witness.b0), channel_id=1, source_target_pairs={{0,24},{1,97},{2,26},{3,99},{4,28},{5,101},{6,30},{7,103},{8,0},{9... | collective-permute-start | bytes 1179656 | tf_op jit(solution)/shard_map/ppermute | solution.py:45
  27.6 1.5 %collective-permute-start.9 = (f32[768,128]{1,0:T(8,128)S(1)}, f32[768,128]{1,0:T(8,128)S(1)}, u32[]{:S(2)}, u32[]{:S(2)}) collective-permute-start(f32[768,128]{1,0:T(8,128)S(1)} %get-tuple-element.31.witness.b0), channel_id=1, source_target_pairs={{0,16},{1,65},{2,18},{3,67},{4,20},{5,69},{6,22},{7,71},{8,24},{9,... | collective-permute-start | bytes 1179656 | tf_op jit(solution)/shard_map/ppermute | solution.py:45
  29.1 2.1 %shard_map.77 = (bf16[176,2688]{1,0:T(8,128)(2,1)S(1)}, bf16[176,2688]{1,0:T(8,128)(2,1)S(1)}, bf16[256,2688]{1,0:T(8,128)(2,1)S(1)}, bf16[256,2688]{1,0:T(8,128)(2,1)S(1)}) custom-call(f32[3696,128]{1,0:T(8,128)} %get-tuple-element.29.home, f32[3696,128]{1,0:T(8,128)S(1)} %collective-permute-done.2.home_other, f32[768,128]{1,0:T(8,128)S(1)} %get-tuple-element.31.witness.b0), custom_call_target="tpu_custom_call" | custom-call | flops 1 | bytes 1 | tf_op jit(solution)/shard_map/pallas_call | solution.py:419
  31.4 4.5 %collective-permute-done.13.refs_1_ = f32[1848,128]{1,0:T(8,128)S(1)} collective-permute-done((f32[1848,128]{1,0:T(8,128)S(1)}, f32[1848,128]{1,0:T(8,128)S(1)}, u32[]{:S(2)}, u32[]{:S(2)}) %collective-permute-start.13) | collective-permute-done | bytes 946208 | tf_op jit(solution)/shard_map/ppermute | solution.py:45
  35.8 2.1 %collective-permute-done.9.refs_2_.b1 = f32[768,128]{1,0:T(8,128)S(1)} collective-permute-done((f32[768,128]{1,0:T(8,128)S(1)}, f32[768,128]{1,0:T(8,128)S(1)}, u32[]{:S(2)}, u32[]{:S(2)}) %collective-permute-start.9) | collective-permute-done | bytes 393248 | tf_op jit(solution)/shard_map/ppermute | solution.py:45
  37.9 5.9 %collective-permute-start.15 = (f32[1848,128]{1,0:T(8,128)S(1)}, f32[1848,128]{1,0:T(8,128)S(1)}, u32[]{:S(2)}, u32[]{:S(2)}) collective-permute-start(f32[1848,128]{1,0:T(8,128)S(1)} %get-tuple-element.39.above), channel_id=1, source_target_pairs={{0,1},{1,0},{2,3},{3,2},{4,5},{5,4},{6,7},{7,6},{8,9},{9,8},{10,11... | collective-permute-start | bytes 2838536 | tf_op jit(solution)/shard_map/ppermute | solution.py:49
  45.0 2.7 %collective-permute-start.7 = (f32[768,128]{1,0:T(8,128)S(1)}, f32[768,128]{1,0:T(8,128)S(1)}, u32[]{:S(2)}, u32[]{:S(2)}) collective-permute-start(f32[768,128]{1,0:T(8,128)S(1)} %get-tuple-element.30.b0), channel_id=1, source_target_pairs={{0,8},{1,33},{2,10},{3,35},{4,12},{5,37},{6,14},{7,39},{8,16},{9,4... | collective-permute-start | bytes 1179656 | tf_op jit(solution)/shard_map/ppermute | solution.py:45
  47.7 2.7 %shard_map.80 = (f32[144,256]{1,0:T(8,128)S(1)}, f32[144,256]{1,0:T(8,128)S(1)}, f32[144,256]{1,0:T(8,128)S(1)}) custom-call(f32[768,128]{1,0:T(8,128)S(1)} %get-tuple-element.31.witness.b0, f32[768,128]{1,0:T(8,128)S(1)} %collective-permute-done.9.refs_2_.b1, f32[768,128]{1,0:T(8,128)S(1)} %collective-permute-done.10.refs_3_.b2, ...), custom_call_target="tpu_custom_call" | custom-call | tf_op jit(solution)/shard_map/pallas_call | solution.py:455
  50.5 2.7 %collective-permute-start.18 = (f32[144,256]{1,0:T(8,128)S(1)}, f32[144,256]{1,0:T(8,128)S(1)}, u32[]{:S(2)}, u32[]{:S(2)}) collective-permute-start(f32[144,256]{1,0:T(8,128)S(1)} %get-tuple-element.42), channel_id=1, source_target_pairs={{0,2},{1,7},{2,4},{3,1},{4,6},{5,3},{6,0},{7,5},{8,10},{9,15},{10,... | collective-permute-start | bytes 442376 | tf_op jit(solution)/shard_map/ppermute | solution.py:45
  53.2 3.3 %collective-permute-done.7.b2 = f32[768,128]{1,0:T(8,128)S(1)} collective-permute-done((f32[768,128]{1,0:T(8,128)S(1)}, f32[768,128]{1,0:T(8,128)S(1)}, u32[]{:S(2)}, u32[]{:S(2)}) %collective-permute-start.7) | collective-permute-done | bytes 393248 | tf_op jit(solution)/shard_map/ppermute | solution.py:45
  57.4 2.2 %shard_map.81 = f32[32,8,128]{2,1,0:T(8,128)} custom-call(f32[768,128]{1,0:T(8,128)S(1)} %get-tuple-element.30.b0, f32[768,128]{1,0:T(8,128)S(1)} %collective-permute-done.6.b1, f32[768,128]{1,0:T(8,128)S(1)} %collective-permute-done.7.b2, f32[768,128]{1,0:T(8,128)S(1)} %collective-permute-done.8.b3, bf16[256,2688]{1,0:T(8,128)(2,1)S(1)} %get-tuple-element.32.v_high, ...), custom_call_target="tpu_custom_call" | custom-call | tf_op jit(solution)/shard_map/pallas_call | solution.py:465
  59.6 6.9 %all-to-all-start = ((f32[32,8,128]{2,1,0:T(8,128)}), f32[32,8,128]{2,1,0:T(8,128)S(1)}, u32[]{:S(2)}, u32[]{:S(2)}) async-start(f32[32,8,128]{2,1,0:T(8,128)} %shard_map.81), calls=%async_computation | async-start | bytes 262144 | tf_op jit(solution)/shard_map/all_to_all | solution.py:473
  66.6 2.8 %shard_map.82 = (f32[18,1296]{1,0:T(8,128)S(1)}, f32[18,1296]{1,0:T(8,128)S(1)}) custom-call(s32[8]{0:T(128)S(1)} %copy-done.3, s32[8]{0:T(128)S(1)} %copy-done.4, f32[8,6]{1,0:T(8,128)S(1)} %copy-done.6, f32[8,36]{1,0:T(8,128)S(1)} %copy-done.7, f32[3,6,1,1296]{3,2,1,0:T(1,128)S(1)} %copy-done.1, f32[108,1,216]{2,1,0:T(1,128)S(1)} %copy-done.5, ...), custom_call_target="tpu_custom_call" | custom-call | flops 100000000 | bytes 1000000 | tf_op jit(solution)/shard_map/pallas_call | solution.py:433
  69.5 4.8 %all-to-all-done.sums = f32[32,8,128]{2,1,0:T(8,128)S(1)} async-done(((f32[32,8,128]{2,1,0:T(8,128)}), f32[32,8,128]{2,1,0:T(8,128)S(1)}, u32[]{:S(2)}, u32[]{:S(2)}) %all-to-all-start) | async-done | bytes 131104 | tf_op jit(solution)/shard_map/all_to_all | solution.py:473
  (45 shorter events, 7.7 us)
Async XLA Ops:
  3.9 9.7 %copy-start = (f32[88,1,2688]{2,1,0:T(1,128)S(1)}, f32[88,1,2688]{2,1,0:T(1,128)}, u32[]{:S(2)}) copy-start(f32[88,1,2688]{2,1,0:T(1,128)} %get-tuple-element.37) | copy-start | bytes 2838532
  3.9 2.6 %collective-permute-start = (f32[104,128]{1,0:T(8,128)}, f32[104,128]{1,0:T(8,128)S(1)}, u32[]{:S(2)}, u32[]{:S(2)}) collective-permute-start(f32[104,128]{1,0:T(8,128)} %get-tuple-element.26), channel_id=1, source_target_pairs={{0,1},{1,0},{2,3},{3,2},{4,5},{5,4},{6,7},{7,6},{8,9},{9,8},{10,11... | collective-permute-start | bytes 159752 | tf_op jit(solution)/shard_map/ppermute | solution.py:49
  7.3 7.6 %collective-permute-start.2 = (f32[3696,128]{1,0:T(8,128)}, f32[3696,128]{1,0:T(8,128)S(1)}, u32[]{:S(2)}, u32[]{:S(2)}) collective-permute-start(f32[3696,128]{1,0:T(8,128)} %get-tuple-element.29.home), channel_id=1, source_target_pairs={{0,1},{1,0},{2,3},{3,2},{4,5},{5,4},{6,7},{7,6},{8,9},{9,8},{10,11... | collective-permute-start | bytes 5677064 | tf_op jit(solution)/shard_map/ppermute | solution.py:49
  7.7 5.8 %collective-permute-start.1 = (f32[192,128]{1,0:T(8,128)S(1)}, f32[192,128]{1,0:T(8,128)S(1)}, u32[]{:S(2)}, u32[]{:S(2)}) collective-permute-start(f32[192,128]{1,0:T(8,128)S(1)} %get-tuple-element.28.near), channel_id=1, source_target_pairs={{0,4},{1,5},{2,6},{3,7},{4,0},{5,1},{6,2},{7,3},{8,12},{9,13},{10,... | collective-permute-start | bytes 294920 | tf_op jit(solution)/shard_map/ppermute | solution.py:45
  10.7 20.6 %collective-permute-start.12 = (f32[1848,128]{1,0:T(8,128)S(1)}, f32[1848,128]{1,0:T(8,128)S(1)}, u32[]{:S(2)}, u32[]{:S(2)}) collective-permute-start(f32[1848,128]{1,0:T(8,128)S(1)} %bitcast.6), channel_id=1, source_target_pairs={{0,2},{1,7},{2,4},{3,1},{4,6},{5,3},{6,0},{7,5},{8,10},{9,15},{10,... | collective-permute-start | bytes 2838536 | tf_op jit(solution)/shard_map/ppermute | solution.py:45
  13.6 22.3 %collective-permute-start.13 = (f32[1848,128]{1,0:T(8,128)S(1)}, f32[1848,128]{1,0:T(8,128)S(1)}, u32[]{:S(2)}, u32[]{:S(2)}) collective-permute-start(f32[1848,128]{1,0:T(8,128)S(1)} %shard_map.78), channel_id=1, source_target_pairs={{0,6},{1,3},{2,0},{3,5},{4,2},{5,7},{6,4},{7,1},{8,14},{9,11},{10,... | collective-permute-start | bytes 2838536 | tf_op jit(solution)/shard_map/ppermute | solution.py:45
  14.9 6.7 %collective-permute-start.3 = (f32[384,128]{1,0:T(8,128)S(1)}, f32[384,128]{1,0:T(8,128)S(1)}, u32[]{:S(2)}, u32[]{:S(2)}) collective-permute-start(f32[384,128]{1,0:T(8,128)S(1)} %shard_map.75.b0), channel_id=1, source_target_pairs={{0,64},{1,17},{2,66},{3,19},{4,68},{5,21},{6,70},{7,23},{8,72},{9,... | collective-permute-start | bytes 589832 | tf_op jit(solution)/shard_map/ppermute | solution.py:45
  18.6 6.0 %collective-permute-start.4 = (f32[384,128]{1,0:T(8,128)S(1)}, f32[384,128]{1,0:T(8,128)S(1)}, u32[]{:S(2)}, u32[]{:S(2)}) collective-permute-start(f32[384,128]{1,0:T(8,128)S(1)} %shard_map.75.b0), channel_id=1, source_target_pairs={{0,32},{1,9},{2,34},{3,11},{4,36},{5,13},{6,38},{7,15},{8,40},{9,1... | collective-permute-start | bytes 589832 | tf_op jit(solution)/shard_map/ppermute | solution.py:45
  19.3 5.5 %collective-permute-start.5 = (f32[384,128]{1,0:T(8,128)S(1)}, f32[384,128]{1,0:T(8,128)S(1)}, u32[]{:S(2)}, u32[]{:S(2)}) collective-permute-start(f32[384,128]{1,0:T(8,128)S(1)} %shard_map.75.b0), channel_id=1, source_target_pairs={{0,96},{1,25},{2,98},{3,27},{4,100},{5,29},{6,102},{7,31},{8,104},... | collective-permute-start | bytes 589832 | tf_op jit(solution)/shard_map/ppermute | solution.py:45
  21.6 5.9 %collective-permute-start.14 = (f32[108,1,216]{2,1,0:T(1,128)S(1)}, f32[108,1,216]{2,1,0:T(1,128)S(1)}, u32[]{:S(2)}, u32[]{:S(2)}) collective-permute-start(f32[108,1,216]{2,1,0:T(1,128)S(1)} %copy-done.5), channel_id=1, source_target_pairs={{0,8},{8,0},{16,24},{24,16},{1,9},{9,1},{17,25},{25,17},{2,10},{10... | collective-permute-start | bytes 279944 | tf_op jit(solution)/shard_map/ppermute | solution.py:390
  24.8 11.0 %collective-permute-start.10 = (f32[768,128]{1,0:T(8,128)S(1)}, f32[768,128]{1,0:T(8,128)S(1)}, u32[]{:S(2)}, u32[]{:S(2)}) collective-permute-start(f32[768,128]{1,0:T(8,128)S(1)} %get-tuple-element.31.witness.b0), channel_id=1, source_target_pairs={{0,8},{1,33},{2,10},{3,35},{4,12},{5,37},{6,14},{7,39},{8,16},{9,4... | collective-permute-start | bytes 1179656 | tf_op jit(solution)/shard_map/ppermute | solution.py:45
  26.1 9.7 %collective-permute-start.11 = (f32[768,128]{1,0:T(8,128)S(1)}, f32[768,128]{1,0:T(8,128)S(1)}, u32[]{:S(2)}, u32[]{:S(2)}) collective-permute-start(f32[768,128]{1,0:T(8,128)S(1)} %get-tuple-element.31.witness.b0), channel_id=1, source_target_pairs={{0,24},{1,97},{2,26},{3,99},{4,28},{5,101},{6,30},{7,103},{8,0},{9... | collective-permute-start | bytes 1179656 | tf_op jit(solution)/shard_map/ppermute | solution.py:45
  27.6 10.4 %collective-permute-start.9 = (f32[768,128]{1,0:T(8,128)S(1)}, f32[768,128]{1,0:T(8,128)S(1)}, u32[]{:S(2)}, u32[]{:S(2)}) collective-permute-start(f32[768,128]{1,0:T(8,128)S(1)} %get-tuple-element.31.witness.b0), channel_id=1, source_target_pairs={{0,16},{1,65},{2,18},{3,67},{4,20},{5,69},{6,22},{7,71},{8,24},{9,... | collective-permute-start | bytes 1179656 | tf_op jit(solution)/shard_map/ppermute | solution.py:45
  37.9 9.7 %collective-permute-start.15 = (f32[1848,128]{1,0:T(8,128)S(1)}, f32[1848,128]{1,0:T(8,128)S(1)}, u32[]{:S(2)}, u32[]{:S(2)}) collective-permute-start(f32[1848,128]{1,0:T(8,128)S(1)} %get-tuple-element.39.above), channel_id=1, source_target_pairs={{0,1},{1,0},{2,3},{3,2},{4,5},{5,4},{6,7},{7,6},{8,9},{9,8},{10,11... | collective-permute-start | bytes 2838536 | tf_op jit(solution)/shard_map/ppermute | solution.py:49
  43.8 3.8 %collective-permute-start.16 = (f32[1848,128]{1,0:T(8,128)S(1)}, f32[1848,128]{1,0:T(8,128)S(1)}, u32[]{:S(2)}, u32[]{:S(2)}) collective-permute-start(f32[1848,128]{1,0:T(8,128)S(1)} %get-tuple-element.38.below), channel_id=1, source_target_pairs={{0,1},{1,0},{2,3},{3,2},{4,5},{5,4},{6,7},{7,6},{8,9},{9,8},{10,11... | collective-permute-start | bytes 2838536 | tf_op jit(solution)/shard_map/ppermute | solution.py:49
  43.8 9.3 %collective-permute-start.6 = (f32[768,128]{1,0:T(8,128)S(1)}, f32[768,128]{1,0:T(8,128)S(1)}, u32[]{:S(2)}, u32[]{:S(2)}) collective-permute-start(f32[768,128]{1,0:T(8,128)S(1)} %get-tuple-element.30.b0), channel_id=1, source_target_pairs={{0,16},{1,65},{2,18},{3,67},{4,20},{5,69},{6,22},{7,71},{8,24},{9,... | collective-permute-start | bytes 1179656 | tf_op jit(solution)/shard_map/ppermute | solution.py:45
  45.0 11.5 %collective-permute-start.7 = (f32[768,128]{1,0:T(8,128)S(1)}, f32[768,128]{1,0:T(8,128)S(1)}, u32[]{:S(2)}, u32[]{:S(2)}) collective-permute-start(f32[768,128]{1,0:T(8,128)S(1)} %get-tuple-element.30.b0), channel_id=1, source_target_pairs={{0,8},{1,33},{2,10},{3,35},{4,12},{5,37},{6,14},{7,39},{8,16},{9,4... | collective-permute-start | bytes 1179656 | tf_op jit(solution)/shard_map/ppermute | solution.py:45
  47.6 9.7 %collective-permute-start.8 = (f32[768,128]{1,0:T(8,128)S(1)}, f32[768,128]{1,0:T(8,128)S(1)}, u32[]{:S(2)}, u32[]{:S(2)}) collective-permute-start(f32[768,128]{1,0:T(8,128)S(1)} %get-tuple-element.30.b0), channel_id=1, source_target_pairs={{0,24},{1,97},{2,26},{3,99},{4,28},{5,101},{6,30},{7,103},{8,0},{9... | collective-permute-start | bytes 1179656 | tf_op jit(solution)/shard_map/ppermute | solution.py:45
  50.4 6.9 %collective-permute-start.17 = (f32[144,256]{1,0:T(8,128)S(1)}, f32[144,256]{1,0:T(8,128)S(1)}, u32[]{:S(2)}, u32[]{:S(2)}) collective-permute-start(f32[144,256]{1,0:T(8,128)S(1)} %get-tuple-element.41), channel_id=1, source_target_pairs={{0,6},{1,3},{2,0},{3,5},{4,2},{5,7},{6,4},{7,1},{8,14},{9,11},{10,... | collective-permute-start | bytes 442376 | tf_op jit(solution)/shard_map/ppermute | solution.py:45
  50.5 6.9 %collective-permute-start.18 = (f32[144,256]{1,0:T(8,128)S(1)}, f32[144,256]{1,0:T(8,128)S(1)}, u32[]{:S(2)}, u32[]{:S(2)}) collective-permute-start(f32[144,256]{1,0:T(8,128)S(1)} %get-tuple-element.42), channel_id=1, source_target_pairs={{0,2},{1,7},{2,4},{3,1},{4,6},{5,3},{6,0},{7,5},{8,10},{9,15},{10,... | collective-permute-start | bytes 442376 | tf_op jit(solution)/shard_map/ppermute | solution.py:45
  57.4 9.2 %copy-start.3 = (s32[8]{0:T(128)S(1)}, s32[8]{0:T(128)}, u32[]{:S(2)}) copy-start(s32[8]{0:T(128)} %occ_ref.3) | copy-start | bytes 100
  57.4 9.2 %copy-start.4 = (s32[8]{0:T(128)S(1)}, s32[8]{0:T(128)}, u32[]{:S(2)}) copy-start(s32[8]{0:T(128)} %vir_ref.3) | copy-start | bytes 100
  57.4 9.2 %copy-start.6 = (f32[8,6]{1,0:T(8,128)S(1)}, f32[8,6]{1,0:T(8,128)}, u32[]{:S(2)}) copy-start(f32[8,6]{1,0:T(8,128)} %eps_occ_ref.1) | copy-start | bytes 580
  59.6 14.6 %all-to-all-start = ((f32[32,8,128]{2,1,0:T(8,128)}), f32[32,8,128]{2,1,0:T(8,128)S(1)}, u32[]{:S(2)}, u32[]{:S(2)}) async-start(f32[32,8,128]{2,1,0:T(8,128)} %shard_map.81), calls=%async_computation | async-start | bytes 262144 | tf_op jit(solution)/shard_map/all_to_all | solution.py:473
  (5 other events, 30.8 us)

commit v12 on v11

--- a/solution.py
+++ b/solution.py
@@ -227,7 +227,7 @@
         far_low[rows, :] = jnp.concatenate([low, pad], axis=0)
 
 
-def multiply_near(b0, b1, b2, b3, near_high, near_low, below, below_other, above, above_other,
+def multiply_near(b0, b2, b1, b3, near_high, near_low, below, below_other, above, above_other,
                   here_sum, below_sum, above_sum, extra, turned):
     high, low = left_side((b0, b1, b2, b3), extra)
     sides = [rows_side(ref, 0) for ref in (below, below_other, above, above_other)]
@@ -424,10 +424,11 @@
         compiler_params=LARGE,
         cost_estimate=pl.CostEstimate(flops=1, bytes_accessed=1, transcendentals=0),
     )(home, home_other, near)
-    near_blocks = [near] + [ring(near, "zx", step) for step in SHIFTS]
+    next_one, opposite, last_one = [ring(near, "zx", SHIFTS[at]) for at in (1, 0, 2)]
+    near_blocks = [near, next_one, opposite, last_one]
     far_blocks = [far] + [ring(far, "zx", step) for step in SHIFTS]
 
-    moved_a, moved_b = hold([moved_a, moved_b], *near_blocks[1:], near_high, partner)
+    moved_a, moved_b = hold([moved_a, moved_b], next_one, opposite, last_one, near_high, partner)
     swapped_a, swapped_b = swap_core(moved_a), swap_core(moved_b)
 
     scale, cycle = pl.pallas_call(

time: 75.4 us -> 79.6 us (1.056)
  starting transfers between devices: 38.3 us -> 43 us
    ppermute x4, starting transfers between devices: 7.81 us -> 11.6 us  [swap_core(): return lax.ppermute(value, 'core', [(0, 1), (1, 0)])]
where the time goes in v12:
time: 79.6 us; the launch traced here: 79.3 us
  starting transfers between devices  43 us (54%)
  waiting for transfers between devices  20.5 us (26%)
  Pallas kernels  14.8 us (19%)
  local copies, waits for them, and re-layouts  0.85 us (1%)
    ppermute x14, starting transfers between devices, ring(): return lax.ppermute(value, AXES, pairs)  22.6 us
    ppermute x14, waiting for transfers between devices, ring(): return lax.ppermute(value, AXES, pairs)  14.6 us
    ppermute x4, starting transfers between devices, swap_core(): return lax.ppermute(value, 'core', [(0, 1), (1, 0)])  11.6 us
    all_to_all x1, starting transfers between devices, on_device(): ladder = lax.all_to_all(packed, ('x', 'z', 'core'), 0, 0, tiled=True)  7.56 us
    all_to_all x1, waiting for transfers between devices, on_device(): ladder = lax.all_to_all(packed, ('x', 'z', 'core'), 0, 0, tiled=True)  4.82 us
    pallas_call x1, Pallas kernels, on_device(): pl.pallas_call(open_step, out_shape=[shape((SHARD, LANES), F32)] * 2 + [w...  3.87 us
    pallas_call x1, Pallas kernels, on_device(): pl.pallas_call(local_step, out_shape=[shape((18, 1296), F32)] * 2, in_spe...  2.83 us
    pallas_call x1, Pallas kernels, on_device(): pl.pallas_call(multiply_near, out_shape=sums, in_specs=[VMEM] * 10, out_s...  2.74 us
  transfers between devices with their start and end apart: 20, of which 11 were waited for; matrix products, arithmetic and copies ran while one was open for 0% of the time, Pallas kernels for 10%

profile of v12, /device:TPU:1, one launch (start us, length us, event | category | flops | bytes accessed | tf_op | source)
XLA Modules:
  0.0 79.3 jit_solution(12801366081750739722)
XLA Ops:
  0.0 3.9 %shard_map.73 = (f32[104,128]{1,0:T(8,128)}, f32[104,128]{1,0:T(8,128)}, f32[88,1,2688]{2,1,0:T(1,128)}, f32[88,1,2688]{2,1,0:T(1,128)}, f32[2,88,1,2688]{3,2,1,0:T(1,128)}) custom-call(s32[8]{0:T(128)} %occ_ref.3, s32[8]{0:T(128)} %vir_ref.3, f32[3,6,1,1296]{3,2,1,0:T(1,128)} %amp_ref.3, f32[81,1,10368]{2,1,0:T(1,128)} %bitcast.5), custom_call_target="tpu_custom_call" | custom-call | tf_op jit(solution)/shard_map/pallas_call | solution.py:366
  3.9 1.5 %collective-permute-start = (f32[104,128]{1,0:T(8,128)}, f32[104,128]{1,0:T(8,128)S(1)}, u32[]{:S(2)}, u32[]{:S(2)}) collective-permute-start(f32[104,128]{1,0:T(8,128)} %get-tuple-element.26), channel_id=1, source_target_pairs={{0,1},{1,0},{2,3},{3,2},{4,5},{5,4},{6,7},{7,6},{8,9},{9,8},{10,11... | collective-permute-start | bytes 159752 | tf_op jit(solution)/shard_map/ppermute | solution.py:49
  5.4 1.1 %collective-permute-done.got = f32[104,128]{1,0:T(8,128)S(1)} collective-permute-done((f32[104,128]{1,0:T(8,128)}, f32[104,128]{1,0:T(8,128)S(1)}, u32[]{:S(2)}, u32[]{:S(2)}) %collective-permute-start) | collective-permute-done | bytes 53280 | tf_op jit(solution)/shard_map/ppermute | solution.py:49
  7.7 3.0 %collective-permute-start.1 = (f32[192,128]{1,0:T(8,128)S(1)}, f32[192,128]{1,0:T(8,128)S(1)}, u32[]{:S(2)}, u32[]{:S(2)}) collective-permute-start(f32[192,128]{1,0:T(8,128)S(1)} %get-tuple-element.28.near), channel_id=1, source_target_pairs={{0,4},{1,5},{2,6},{3,7},{4,0},{5,1},{6,2},{7,3},{8,12},{9,13},{10,... | collective-permute-start | bytes 294920 | tf_op jit(solution)/shard_map/ppermute | solution.py:45
  11.5 2.0 %collective-permute-done.1.far.refs_1_ = f32[192,128]{1,0:T(8,128)S(1)} collective-permute-done((f32[192,128]{1,0:T(8,128)S(1)}, f32[192,128]{1,0:T(8,128)S(1)}, u32[]{:S(2)}, u32[]{:S(2)}) %collective-permute-start.1) | collective-permute-done | bytes 98336 | tf_op jit(solution)/shard_map/ppermute | solution.py:45
  13.6 1.3 %collective-permute-start.13 = (f32[1848,128]{1,0:T(8,128)S(1)}, f32[1848,128]{1,0:T(8,128)S(1)}, u32[]{:S(2)}, u32[]{:S(2)}) collective-permute-start(f32[1848,128]{1,0:T(8,128)S(1)} %shard_map.78), channel_id=1, source_target_pairs={{0,6},{1,3},{2,0},{3,5},{4,2},{5,7},{6,4},{7,1},{8,14},{9,11},{10,... | collective-permute-start | bytes 2838536 | tf_op jit(solution)/shard_map/ppermute | solution.py:45
  14.9 3.7 %collective-permute-start.3 = (f32[384,128]{1,0:T(8,128)S(1)}, f32[384,128]{1,0:T(8,128)S(1)}, u32[]{:S(2)}, u32[]{:S(2)}) collective-permute-start(f32[384,128]{1,0:T(8,128)S(1)} %shard_map.75.b0), channel_id=1, source_target_pairs={{0,64},{1,17},{2,66},{3,19},{4,68},{5,21},{6,70},{7,23},{8,72},{9,... | collective-permute-start | bytes 589832 | tf_op jit(solution)/shard_map/ppermute | solution.py:45
  19.3 1.9 %collective-permute-start.5 = (f32[384,128]{1,0:T(8,128)S(1)}, f32[384,128]{1,0:T(8,128)S(1)}, u32[]{:S(2)}, u32[]{:S(2)}) collective-permute-start(f32[384,128]{1,0:T(8,128)S(1)} %shard_map.75.b0), channel_id=1, source_target_pairs={{0,96},{1,25},{2,98},{3,27},{4,100},{5,29},{6,102},{7,31},{8,104},... | collective-permute-start | bytes 589832 | tf_op jit(solution)/shard_map/ppermute | solution.py:45
  21.6 1.3 %collective-permute-start.14 = (f32[108,1,216]{2,1,0:T(1,128)S(1)}, f32[108,1,216]{2,1,0:T(1,128)S(1)}, u32[]{:S(2)}, u32[]{:S(2)}) collective-permute-start(f32[108,1,216]{2,1,0:T(1,128)S(1)} %copy-done.5), channel_id=1, source_target_pairs={{0,8},{8,0},{16,24},{24,16},{1,9},{9,1},{17,25},{25,17},{2,10},{10... | collective-permute-start | bytes 279944 | tf_op jit(solution)/shard_map/ppermute | solution.py:390
  22.9 1.7 %collective-permute-done.4.b2 = f32[384,128]{1,0:T(8,128)S(1)} collective-permute-done((f32[384,128]{1,0:T(8,128)S(1)}, f32[384,128]{1,0:T(8,128)S(1)}, u32[]{:S(2)}, u32[]{:S(2)}) %collective-permute-start.4) | collective-permute-done | bytes 196640 | tf_op jit(solution)/shard_map/ppermute | solution.py:45
  24.8 2.8 %collective-permute-start.10 = (f32[768,128]{1,0:T(8,128)S(1)}, f32[768,128]{1,0:T(8,128)S(1)}, u32[]{:S(2)}, u32[]{:S(2)}) collective-permute-start(f32[768,128]{1,0:T(8,128)S(1)} %get-tuple-element.31.witness.b0), channel_id=1, source_target_pairs={{0,16},{1,65},{2,18},{3,67},{4,20},{5,69},{6,22},{7,71},{8,24},{9,... | collective-permute-start | bytes 1179656 | tf_op jit(solution)/shard_map/ppermute | solution.py:45
  29.1 2.1 %shard_map.77 = (bf16[176,2688]{1,0:T(8,128)(2,1)S(1)}, bf16[176,2688]{1,0:T(8,128)(2,1)S(1)}, bf16[256,2688]{1,0:T(8,128)(2,1)S(1)}, bf16[256,2688]{1,0:T(8,128)(2,1)S(1)}) custom-call(f32[3696,128]{1,0:T(8,128)} %get-tuple-element.29.home, f32[3696,128]{1,0:T(8,128)S(1)} %collective-permute-done.2.home_other, f32[768,128]{1,0:T(8,128)S(1)} %get-tuple-element.31.witness.b0), custom_call_target="tpu_custom_call" | custom-call | flops 1 | bytes 1 | tf_op jit(solution)/shard_map/pallas_call | solution.py:419
  31.4 4.2 %collective-permute-done.13.refs_1_ = f32[1848,128]{1,0:T(8,128)S(1)} collective-permute-done((f32[1848,128]{1,0:T(8,128)S(1)}, f32[1848,128]{1,0:T(8,128)S(1)}, u32[]{:S(2)}, u32[]{:S(2)}) %collective-permute-start.13) | collective-permute-done | bytes 946208 | tf_op jit(solution)/shard_map/ppermute | solution.py:45
  35.5 1.8 %collective-permute-done.11.refs_4_.b3 = f32[768,128]{1,0:T(8,128)S(1)} collective-permute-done((f32[768,128]{1,0:T(8,128)S(1)}, f32[768,128]{1,0:T(8,128)S(1)}, u32[]{:S(2)}, u32[]{:S(2)}) %collective-permute-start.11) | collective-permute-done | bytes 393248 | tf_op jit(solution)/shard_map/ppermute | solution.py:45
  37.4 9.6 %collective-permute-start.15 = (f32[1848,128]{1,0:T(8,128)S(1)}, f32[1848,128]{1,0:T(8,128)S(1)}, u32[]{:S(2)}, u32[]{:S(2)}) collective-permute-start(f32[1848,128]{1,0:T(8,128)S(1)} %get-tuple-element.39.above), channel_id=1, source_target_pairs={{0,1},{1,0},{2,3},{3,2},{4,5},{5,4},{6,7},{7,6},{8,9},{9,8},{10,11... | collective-permute-start | bytes 2838536 | tf_op jit(solution)/shard_map/ppermute | solution.py:49
  47.0 4.1 %collective-permute-start.7 = (f32[768,128]{1,0:T(8,128)S(1)}, f32[768,128]{1,0:T(8,128)S(1)}, u32[]{:S(2)}, u32[]{:S(2)}) collective-permute-start(f32[768,128]{1,0:T(8,128)S(1)} %get-tuple-element.30.b0), channel_id=1, source_target_pairs={{0,8},{1,33},{2,10},{3,35},{4,12},{5,37},{6,14},{7,39},{8,16},{9,4... | collective-permute-start | bytes 1179656 | tf_op jit(solution)/shard_map/ppermute | solution.py:45
  51.2 2.7 %shard_map.80 = (f32[144,256]{1,0:T(8,128)S(1)}, f32[144,256]{1,0:T(8,128)S(1)}, f32[144,256]{1,0:T(8,128)S(1)}) custom-call(f32[768,128]{1,0:T(8,128)S(1)} %get-tuple-element.31.witness.b0, f32[768,128]{1,0:T(8,128)S(1)} %collective-permute-done.9.refs_2_.b2, f32[768,128]{1,0:T(8,128)S(1)} %collective-permute-done.10.refs_3_.b1, ...), custom_call_target="tpu_custom_call" | custom-call | tf_op jit(solution)/shard_map/pallas_call | solution.py:456
  54.0 2.7 %collective-permute-start.18 = (f32[144,256]{1,0:T(8,128)S(1)}, f32[144,256]{1,0:T(8,128)S(1)}, u32[]{:S(2)}, u32[]{:S(2)}) collective-permute-start(f32[144,256]{1,0:T(8,128)S(1)} %get-tuple-element.42), channel_id=1, source_target_pairs={{0,2},{1,7},{2,4},{3,1},{4,6},{5,3},{6,0},{7,5},{8,10},{9,15},{10,... | collective-permute-start | bytes 442376 | tf_op jit(solution)/shard_map/ppermute | solution.py:45
  56.7 3.0 %collective-permute-done.7.b2 = f32[768,128]{1,0:T(8,128)S(1)} collective-permute-done((f32[768,128]{1,0:T(8,128)S(1)}, f32[768,128]{1,0:T(8,128)S(1)}, u32[]{:S(2)}, u32[]{:S(2)}) %collective-permute-start.7) | collective-permute-done | bytes 393248 | tf_op jit(solution)/shard_map/ppermute | solution.py:45
  59.7 1.2 %collective-permute-done.8.b3 = f32[768,128]{1,0:T(8,128)S(1)} collective-permute-done((f32[768,128]{1,0:T(8,128)S(1)}, f32[768,128]{1,0:T(8,128)S(1)}, u32[]{:S(2)}, u32[]{:S(2)}) %collective-permute-start.8) | collective-permute-done | bytes 393248 | tf_op jit(solution)/shard_map/ppermute | solution.py:45
  60.9 2.2 %shard_map.81 = f32[32,8,128]{2,1,0:T(8,128)} custom-call(f32[768,128]{1,0:T(8,128)S(1)} %get-tuple-element.30.b0, f32[768,128]{1,0:T(8,128)S(1)} %collective-permute-done.6.b1, f32[768,128]{1,0:T(8,128)S(1)} %collective-permute-done.7.b2, f32[768,128]{1,0:T(8,128)S(1)} %collective-permute-done.8.b3, bf16[256,2688]{1,0:T(8,128)(2,1)S(1)} %get-tuple-element.32.v_high, ...), custom_call_target="tpu_custom_call" | custom-call | tf_op jit(solution)/shard_map/pallas_call | solution.py:466
  63.2 7.6 %all-to-all-start = ((f32[32,8,128]{2,1,0:T(8,128)}), f32[32,8,128]{2,1,0:T(8,128)S(1)}, u32[]{:S(2)}, u32[]{:S(2)}) async-start(f32[32,8,128]{2,1,0:T(8,128)} %shard_map.81), calls=%async_computation | async-start | bytes 262144 | tf_op jit(solution)/shard_map/all_to_all | solution.py:474
  70.8 2.8 %shard_map.82 = (f32[18,1296]{1,0:T(8,128)S(1)}, f32[18,1296]{1,0:T(8,128)S(1)}) custom-call(s32[8]{0:T(128)S(1)} %copy-done.3, s32[8]{0:T(128)S(1)} %copy-done.4, f32[8,6]{1,0:T(8,128)S(1)} %copy-done.6, f32[8,36]{1,0:T(8,128)S(1)} %copy-done.7, f32[3,6,1,1296]{3,2,1,0:T(1,128)S(1)} %copy-done.1, f32[108,1,216]{2,1,0:T(1,128)S(1)} %copy-done.5, ...), custom_call_target="tpu_custom_call" | custom-call | flops 100000000 | bytes 1000000 | tf_op jit(solution)/shard_map/pallas_call | solution.py:434
  73.6 4.8 %all-to-all-done.sums = f32[32,8,128]{2,1,0:T(8,128)S(1)} async-done(((f32[32,8,128]{2,1,0:T(8,128)}), f32[32,8,128]{2,1,0:T(8,128)S(1)}, u32[]{:S(2)}, u32[]{:S(2)}) %all-to-all-start) | async-done | bytes 131104 | tf_op jit(solution)/shard_map/all_to_all | solution.py:474
  (45 shorter events, 6.0 us)
Async XLA Ops:
  3.9 2.6 %collective-permute-start = (f32[104,128]{1,0:T(8,128)}, f32[104,128]{1,0:T(8,128)S(1)}, u32[]{:S(2)}, u32[]{:S(2)}) collective-permute-start(f32[104,128]{1,0:T(8,128)} %get-tuple-element.26), channel_id=1, source_target_pairs={{0,1},{1,0},{2,3},{3,2},{4,5},{5,4},{6,7},{7,6},{8,9},{9,8},{10,11... | collective-permute-start | bytes 159752 | tf_op jit(solution)/shard_map/ppermute | solution.py:49
  7.3 7.6 %collective-permute-start.2 = (f32[3696,128]{1,0:T(8,128)}, f32[3696,128]{1,0:T(8,128)S(1)}, u32[]{:S(2)}, u32[]{:S(2)}) collective-permute-start(f32[3696,128]{1,0:T(8,128)} %get-tuple-element.29.home), channel_id=1, source_target_pairs={{0,1},{1,0},{2,3},{3,2},{4,5},{5,4},{6,7},{7,6},{8,9},{9,8},{10,11... | collective-permute-start | bytes 5677064 | tf_op jit(solution)/shard_map/ppermute | solution.py:49
  7.7 5.8 %collective-permute-start.1 = (f32[192,128]{1,0:T(8,128)S(1)}, f32[192,128]{1,0:T(8,128)S(1)}, u32[]{:S(2)}, u32[]{:S(2)}) collective-permute-start(f32[192,128]{1,0:T(8,128)S(1)} %get-tuple-element.28.near), channel_id=1, source_target_pairs={{0,4},{1,5},{2,6},{3,7},{4,0},{5,1},{6,2},{7,3},{8,12},{9,13},{10,... | collective-permute-start | bytes 294920 | tf_op jit(solution)/shard_map/ppermute | solution.py:45
  10.7 20.6 %collective-permute-start.12 = (f32[1848,128]{1,0:T(8,128)S(1)}, f32[1848,128]{1,0:T(8,128)S(1)}, u32[]{:S(2)}, u32[]{:S(2)}) collective-permute-start(f32[1848,128]{1,0:T(8,128)S(1)} %bitcast.6), channel_id=1, source_target_pairs={{0,2},{1,7},{2,4},{3,1},{4,6},{5,3},{6,0},{7,5},{8,10},{9,15},{10,... | collective-permute-start | bytes 2838536 | tf_op jit(solution)/shard_map/ppermute | solution.py:45
  13.6 22.0 %collective-permute-start.13 = (f32[1848,128]{1,0:T(8,128)S(1)}, f32[1848,128]{1,0:T(8,128)S(1)}, u32[]{:S(2)}, u32[]{:S(2)}) collective-permute-start(f32[1848,128]{1,0:T(8,128)S(1)} %shard_map.78), channel_id=1, source_target_pairs={{0,6},{1,3},{2,0},{3,5},{4,2},{5,7},{6,4},{7,1},{8,14},{9,11},{10,... | collective-permute-start | bytes 2838536 | tf_op jit(solution)/shard_map/ppermute | solution.py:45
  14.9 6.7 %collective-permute-start.3 = (f32[384,128]{1,0:T(8,128)S(1)}, f32[384,128]{1,0:T(8,128)S(1)}, u32[]{:S(2)}, u32[]{:S(2)}) collective-permute-start(f32[384,128]{1,0:T(8,128)S(1)} %shard_map.75.b0), channel_id=1, source_target_pairs={{0,64},{1,17},{2,66},{3,19},{4,68},{5,21},{6,70},{7,23},{8,72},{9,... | collective-permute-start | bytes 589832 | tf_op jit(solution)/shard_map/ppermute | solution.py:45
  18.6 6.0 %collective-permute-start.4 = (f32[384,128]{1,0:T(8,128)S(1)}, f32[384,128]{1,0:T(8,128)S(1)}, u32[]{:S(2)}, u32[]{:S(2)}) collective-permute-start(f32[384,128]{1,0:T(8,128)S(1)} %shard_map.75.b0), channel_id=1, source_target_pairs={{0,32},{1,9},{2,34},{3,11},{4,36},{5,13},{6,38},{7,15},{8,40},{9,1... | collective-permute-start | bytes 589832 | tf_op jit(solution)/shard_map/ppermute | solution.py:45
  19.3 5.5 %collective-permute-start.5 = (f32[384,128]{1,0:T(8,128)S(1)}, f32[384,128]{1,0:T(8,128)S(1)}, u32[]{:S(2)}, u32[]{:S(2)}) collective-permute-start(f32[384,128]{1,0:T(8,128)S(1)} %shard_map.75.b0), channel_id=1, source_target_pairs={{0,96},{1,25},{2,98},{3,27},{4,100},{5,29},{6,102},{7,31},{8,104},... | collective-permute-start | bytes 589832 | tf_op jit(solution)/shard_map/ppermute | solution.py:45
  21.6 6.9 %collective-permute-start.14 = (f32[108,1,216]{2,1,0:T(1,128)S(1)}, f32[108,1,216]{2,1,0:T(1,128)S(1)}, u32[]{:S(2)}, u32[]{:S(2)}) collective-permute-start(f32[108,1,216]{2,1,0:T(1,128)S(1)} %copy-done.5), channel_id=1, source_target_pairs={{0,8},{8,0},{16,24},{24,16},{1,9},{9,1},{17,25},{25,17},{2,10},{10... | collective-permute-start | bytes 279944 | tf_op jit(solution)/shard_map/ppermute | solution.py:390
  24.8 10.7 %collective-permute-start.10 = (f32[768,128]{1,0:T(8,128)S(1)}, f32[768,128]{1,0:T(8,128)S(1)}, u32[]{:S(2)}, u32[]{:S(2)}) collective-permute-start(f32[768,128]{1,0:T(8,128)S(1)} %get-tuple-element.31.witness.b0), channel_id=1, source_target_pairs={{0,16},{1,65},{2,18},{3,67},{4,20},{5,69},{6,22},{7,71},{8,24},{9,... | collective-permute-start | bytes 1179656 | tf_op jit(solution)/shard_map/ppermute | solution.py:45
  27.7 9.7 %collective-permute-start.11 = (f32[768,128]{1,0:T(8,128)S(1)}, f32[768,128]{1,0:T(8,128)S(1)}, u32[]{:S(2)}, u32[]{:S(2)}) collective-permute-start(f32[768,128]{1,0:T(8,128)S(1)} %get-tuple-element.31.witness.b0), channel_id=1, source_target_pairs={{0,24},{1,97},{2,26},{3,99},{4,28},{5,101},{6,30},{7,103},{8,0},{9... | collective-permute-start | bytes 1179656 | tf_op jit(solution)/shard_map/ppermute | solution.py:45
  28.5 8.9 %collective-permute-start.9 = (f32[768,128]{1,0:T(8,128)S(1)}, f32[768,128]{1,0:T(8,128)S(1)}, u32[]{:S(2)}, u32[]{:S(2)}) collective-permute-start(f32[768,128]{1,0:T(8,128)S(1)} %get-tuple-element.31.witness.b0), channel_id=1, source_target_pairs={{0,8},{1,33},{2,10},{3,35},{4,12},{5,37},{6,14},{7,39},{8,16},{9,4... | collective-permute-start | bytes 1179656 | tf_op jit(solution)/shard_map/ppermute | solution.py:45
  37.4 13.8 %collective-permute-start.15 = (f32[1848,128]{1,0:T(8,128)S(1)}, f32[1848,128]{1,0:T(8,128)S(1)}, u32[]{:S(2)}, u32[]{:S(2)}) collective-permute-start(f32[1848,128]{1,0:T(8,128)S(1)} %get-tuple-element.39.above), channel_id=1, source_target_pairs={{0,1},{1,0},{2,3},{3,2},{4,5},{5,4},{6,7},{7,6},{8,9},{9,8},{10,11... | collective-permute-start | bytes 2838536 | tf_op jit(solution)/shard_map/ppermute | solution.py:49
  47.0 4.2 %collective-permute-start.16 = (f32[1848,128]{1,0:T(8,128)S(1)}, f32[1848,128]{1,0:T(8,128)S(1)}, u32[]{:S(2)}, u32[]{:S(2)}) collective-permute-start(f32[1848,128]{1,0:T(8,128)S(1)} %get-tuple-element.38.below), channel_id=1, source_target_pairs={{0,1},{1,0},{2,3},{3,2},{4,5},{5,4},{6,7},{7,6},{8,9},{9,8},{10,11... | collective-permute-start | bytes 2838536 | tf_op jit(solution)/shard_map/ppermute | solution.py:49
  47.0 9.6 %collective-permute-start.6 = (f32[768,128]{1,0:T(8,128)S(1)}, f32[768,128]{1,0:T(8,128)S(1)}, u32[]{:S(2)}, u32[]{:S(2)}) collective-permute-start(f32[768,128]{1,0:T(8,128)S(1)} %get-tuple-element.30.b0), channel_id=1, source_target_pairs={{0,16},{1,65},{2,18},{3,67},{4,20},{5,69},{6,22},{7,71},{8,24},{9,... | collective-permute-start | bytes 1179656 | tf_op jit(solution)/shard_map/ppermute | solution.py:45
  47.0 12.6 %collective-permute-start.7 = (f32[768,128]{1,0:T(8,128)S(1)}, f32[768,128]{1,0:T(8,128)S(1)}, u32[]{:S(2)}, u32[]{:S(2)}) collective-permute-start(f32[768,128]{1,0:T(8,128)S(1)} %get-tuple-element.30.b0), channel_id=1, source_target_pairs={{0,8},{1,33},{2,10},{3,35},{4,12},{5,37},{6,14},{7,39},{8,16},{9,4... | collective-permute-start | bytes 1179656 | tf_op jit(solution)/shard_map/ppermute | solution.py:45
  51.2 9.7 %collective-permute-start.8 = (f32[768,128]{1,0:T(8,128)S(1)}, f32[768,128]{1,0:T(8,128)S(1)}, u32[]{:S(2)}, u32[]{:S(2)}) collective-permute-start(f32[768,128]{1,0:T(8,128)S(1)} %get-tuple-element.30.b0), channel_id=1, source_target_pairs={{0,24},{1,97},{2,26},{3,99},{4,28},{5,101},{6,30},{7,103},{8,0},{9... | collective-permute-start | bytes 1179656 | tf_op jit(solution)/shard_map/ppermute | solution.py:45
  53.9 7.0 %collective-permute-start.17 = (f32[144,256]{1,0:T(8,128)S(1)}, f32[144,256]{1,0:T(8,128)S(1)}, u32[]{:S(2)}, u32[]{:S(2)}) collective-permute-start(f32[144,256]{1,0:T(8,128)S(1)} %get-tuple-element.41), channel_id=1, source_target_pairs={{0,6},{1,3},{2,0},{3,5},{4,2},{5,7},{6,4},{7,1},{8,14},{9,11},{10,... | collective-permute-start | bytes 442376 | tf_op jit(solution)/shard_map/ppermute | solution.py:45
  54.0 6.9 %collective-permute-start.18 = (f32[144,256]{1,0:T(8,128)S(1)}, f32[144,256]{1,0:T(8,128)S(1)}, u32[]{:S(2)}, u32[]{:S(2)}) collective-permute-start(f32[144,256]{1,0:T(8,128)S(1)} %get-tuple-element.42), channel_id=1, source_target_pairs={{0,2},{1,7},{2,4},{3,1},{4,6},{5,3},{6,0},{7,5},{8,10},{9,15},{10,... | collective-permute-start | bytes 442376 | tf_op jit(solution)/shard_map/ppermute | solution.py:45
  60.9 9.9 %copy-start.1 = (f32[3,6,1,1296]{3,2,1,0:T(1,128)S(1)}, f32[3,6,1,1296]{3,2,1,0:T(1,128)}, u32[]{:S(2)}) copy-start(f32[3,6,1,1296]{3,2,1,0:T(1,128)} %amp_ref.3) | copy-start | bytes 279940
  60.9 9.9 %copy-start.3 = (s32[8]{0:T(128)S(1)}, s32[8]{0:T(128)}, u32[]{:S(2)}) copy-start(s32[8]{0:T(128)} %occ_ref.3) | copy-start | bytes 100
  60.9 9.9 %copy-start.4 = (s32[8]{0:T(128)S(1)}, s32[8]{0:T(128)}, u32[]{:S(2)}) copy-start(s32[8]{0:T(128)} %vir_ref.3) | copy-start | bytes 100
  60.9 9.9 %copy-start.6 = (f32[8,6]{1,0:T(8,128)S(1)}, f32[8,6]{1,0:T(8,128)}, u32[]{:S(2)}) copy-start(f32[8,6]{1,0:T(8,128)} %eps_occ_ref.1) | copy-start | bytes 580
  63.2 15.3 %all-to-all-start = ((f32[32,8,128]{2,1,0:T(8,128)}), f32[32,8,128]{2,1,0:T(8,128)S(1)}, u32[]{:S(2)}, u32[]{:S(2)}) async-start(f32[32,8,128]{2,1,0:T(8,128)} %shard_map.81), calls=%async_computation | async-start | bytes 262144 | tf_op jit(solution)/shard_map/all_to_all | solution.py:474
  (5 other events, 31.9 us)

commit v13 on v11

--- a/solution.py
+++ b/solution.py
@@ -6,8 +6,8 @@
 from jax.sharding import Mesh, PartitionSpec as P
 
 AXES = ("x", "z", "y", "core")
-SHIFTS = ((2, 2), (1, 1), (-1, -1))
-STEPS = (0, 2, 1, -1)
+FIRST_STEPS = (0, 1, -1, 2)
+LAST_STEPS = (0, 2, 1, -1)
 LANES = 128
 TILES = 11
 WINDOW = TILES * LANES
@@ -227,20 +227,31 @@
         far_low[rows, :] = jnp.concatenate([low, pad], axis=0)
 
 
-def multiply_near(b0, b1, b2, b3, near_high, near_low, below, below_other, above, above_other,
-                  here_sum, below_sum, above_sum, extra, turned):
-    high, low = left_side((b0, b1, b2, b3), extra)
-    sides = [rows_side(ref, 0) for ref in (below, below_other, above, above_other)]
-    v_high, v_low = split(jnp.concatenate(sides, axis=0))
-    v_high = jnp.concatenate([near_high[...], v_high], axis=0)
-    v_low = jnp.concatenate([near_low[...], v_low], axis=0)
-    total = last_by_last(v_high, high) + (last_by_last(v_low, high) + last_by_last(v_high, low))
+def turn_sums(total, refs, turned):
     turned[...] = jnp.zeros_like(turned)
-    for at, ref in enumerate((here_sum, below_sum, above_sum)):
+    for at, ref in enumerate(refs):
         for side in range(2):
             rows = slice((2 * at + side) * PSLOT, (2 * at + side + 1) * PSLOT)
             turned[0:PSLOT, 0:144] = total[rows, :]
             ref[:, side * LANES : (side + 1) * LANES] = turned[...].T[0:144, :]
+
+
+def multiply_moved(b0, b1, b2, b3, below, below_other, above, above_other,
+                   below_sum, above_sum, high_out, low_out, extra, turned):
+    high, low = left_side((b0, b1, b2, b3), extra)
+    high_out[...] = high
+    low_out[...] = low
+    sides = [rows_side(ref, 0) for ref in (below, below_other, above, above_other)]
+    v_high, v_low = split(jnp.concatenate(sides, axis=0))
+    total = last_by_last(v_high, high) + (last_by_last(v_low, high) + last_by_last(v_high, low))
+    turn_sums(total, (below_sum, above_sum), turned)
+
+
+def multiply_home(high, low, v_high, v_low, below_sum, here_sum, turned):
+    total = last_by_last(v_high[...], high[...]) + (
+        last_by_last(v_low[...], high[...]) + last_by_last(v_high[...], low[...])
+    )
+    turn_sums(total, (here_sum,), turned)
 
 
 def multiply_far(b0, b1, b2, b3, v_high, v_low, here_sum, back_a, back_b, out, extra):
@@ -261,8 +272,8 @@
         for d in range(4):
             for e in range(4):
                 s = 4 * d + e
-                x_step = jnp.where(core == 0, STEPS[e], STEPS[d])
-                z_step = jnp.where(core == 0, STEPS[d], STEPS[e])
+                x_step = jnp.where(core == 0, FIRST_STEPS[e], LAST_STEPS[d])
+                z_step = jnp.where(core == 0, LAST_STEPS[d], FIRST_STEPS[e])
                 there = ((x - x_step) & 3) * 4 + ((z - z_step) & 3)
                 main = total[8 * s : 8 * s + 8, columns]
                 tail = jnp.where(row == 0, last_a[s : s + 1, :], last_b[s : s + 1, :])
@@ -415,7 +426,7 @@
         in_specs=[VMEM] * 4,
         out_specs=[VMEM] * 2,
         compiler_params=SMALL,
-    )(quad, *[ring(quad, "xz", step) for step in SHIFTS])
+    )(quad, *[ring(quad, "xz", (step, step)) for step in FIRST_STEPS[1:]])
     near_high, near_low, far_high, far_low = pl.pallas_call(
         split_home,
         out_shape=[shape((2 * PSLOT, DEPTH), BF16)] * 2 + [shape((2 * LANES, DEPTH), BF16)] * 2,
@@ -424,8 +435,8 @@
         compiler_params=LARGE,
         cost_estimate=pl.CostEstimate(flops=1, bytes_accessed=1, transcendentals=0),
     )(home, home_other, near)
-    near_blocks = [near] + [ring(near, "zx", step) for step in SHIFTS]
-    far_blocks = [far] + [ring(far, "zx", step) for step in SHIFTS]
+    near_blocks = [near] + [ring(near, "zx", (step, step)) for step in LAST_STEPS[1:]]
+    far_blocks = [far] + [ring(far, "zx", (step, step)) for step in LAST_STEPS[1:]]
 
     moved_a, moved_b = hold([moved_a, moved_b], *near_blocks[1:], near_high, partner)
     swapped_a, swapped_b = swap_core(moved_a), swap_core(moved_b)
@@ -451,17 +462,26 @@
         cost_estimate=pl.CostEstimate(flops=100000000, bytes_accessed=1000000, transcendentals=0),
     )(occ_count, vir_count, eps_occ, eps_vir, amplitudes, ovov, partner)
 
-    sums = [shape((144, 2 * LANES), F32)] * 3
-    here_sum, below_sum, above_sum = pl.pallas_call(
-        multiply_near,
-        out_shape=sums,
-        in_specs=[VMEM] * 10,
-        out_specs=[VMEM] * 3,
+    sums = shape((144, 2 * LANES), F32)
+    left = shape((144, DEPTH), BF16)
+    below_sum, above_sum, high, low = pl.pallas_call(
+        multiply_moved,
+        out_shape=[sums, sums, left, left],
+        in_specs=[VMEM] * 8,
+        out_specs=[VMEM] * 4,
         scratch_shapes=[pltpu.VMEM((16, DEPTH), F32), pltpu.VMEM((LANES, 2 * LANES), F32)],
         compiler_params=LARGE,
-    )(*near_blocks, near_high, near_low, moved_a, swapped_b, moved_b, swapped_a)
+    )(*near_blocks, moved_a, swapped_b, moved_b, swapped_a)
     back_a = ring(below_sum, "yy", (-1, 1))
     back_b = ring(above_sum, "yy", (1, -1))
+    here_sum = pl.pallas_call(
+        multiply_home,
+        out_shape=sums,
+        in_specs=[VMEM] * 4 + [ANY],
+        out_specs=VMEM,
+        scratch_shapes=[pltpu.VMEM((LANES, 2 * LANES), F32)],
+        compiler_params=LARGE,
+    )(high, low, near_high, near_low, below_sum)
     packed = pl.pallas_call(
         multiply_far,
         out_shape=shape((32, 8, LANES), F32),

time: 75.4 us -> 75.1 us (level)
  starting transfers between devices: 38.3 us -> 35.6 us
  waiting for transfers between devices: 21.1 us -> 23.2 us
    ppermute x14, waiting for transfers between devices: 15.1 us -> 17.2 us  [ring(): return lax.ppermute(value, AXES, pairs)]
    all_to_all x1, starting transfers between devices: 6.93 us -> 5.57 us  [on_device(): ladder = lax.all_to_all(packed, ('x', 'z', 'core'), 0, 0, tiled=True)]
    ppermute x1, starting transfers between devices: 1.3 us -> 0.01 us  [on_device(): partner = lax.ppermute(ovov, 'z', [(0, 1), (1, 0), (2, 3), (3, 2)])]
    pallas_call x1 -> x2, Pallas kernels: 2.74 us -> 3.03 us  [the longest x1 1.97 us: on_device(): pl.pallas_call(multiply_moved, out_shape=[sums, sums, left, left], in_spe...]
  transfers between devices with their start and end apart: 20 -> 20, of which waited for: 11 -> 11; matrix products, arithmetic and copies ran while one was open for 0% -> 0% of each run, Pallas kernels for 10% -> 11%
where the time goes in v13:
time: 75.1 us; the launch traced here: 74.9 us
  starting transfers between devices  35.6 us (47%)
  waiting for transfers between devices  23.2 us (31%)
  Pallas kernels  15.1 us (20%)
  local copies, waits for them, and re-layouts  0.84 us (1%)
    ppermute x14, starting transfers between devices, ring(): return lax.ppermute(value, AXES, pairs)  22.3 us
    ppermute x14, waiting for transfers between devices, ring(): return lax.ppermute(value, AXES, pairs)  17.2 us
    ppermute x4, starting transfers between devices, swap_core(): return lax.ppermute(value, 'core', [(0, 1), (1, 0)])  7.72 us
    all_to_all x1, starting transfers between devices, on_device(): ladder = lax.all_to_all(packed, ('x', 'z', 'core'), 0, 0, tiled=True)  5.57 us
    all_to_all x1, waiting for transfers between devices, on_device(): ladder = lax.all_to_all(packed, ('x', 'z', 'core'), 0, 0, tiled=True)  4.82 us
    pallas_call x1, Pallas kernels, on_device(): pl.pallas_call(open_step, out_shape=[shape((SHARD, LANES), F32)] * 2 + [w...  3.87 us
    pallas_call x1, Pallas kernels, on_device(): pl.pallas_call(local_step, out_shape=[shape((18, 1296), F32)] * 2, in_spe...  2.83 us
    pallas_call x1, Pallas kernels, on_device(): pl.pallas_call(multiply_far, out_shape=shape((32, 8, LANES), F32), in_spe...  2.24 us
  transfers between devices with their start and end apart: 20, of which 11 were waited for; matrix products, arithmetic and copies ran while one was open for 0% of the time, Pallas kernels for 11%

profile of v13, /device:TPU:1, one launch (start us, length us, event | category | flops | bytes accessed | tf_op | source)
XLA Modules:
  0.0 74.9 jit_solution(2164895425288936299)
XLA Ops:
  0.0 3.9 %shard_map.73 = (f32[104,128]{1,0:T(8,128)}, f32[104,128]{1,0:T(8,128)}, f32[88,1,2688]{2,1,0:T(1,128)}, f32[88,1,2688]{2,1,0:T(1,128)}, f32[2,88,1,2688]{3,2,1,0:T(1,128)}) custom-call(s32[8]{0:T(128)} %occ_ref.3, s32[8]{0:T(128)} %vir_ref.3, f32[3,6,1,1296]{3,2,1,0:T(1,128)} %amp_ref.3, f32[81,1,10368]{2,1,0:T(1,128)} %bitcast.5), custom_call_target="tpu_custom_call" | custom-call | tf_op jit(solution)/shard_map/pallas_call | solution.py:377
  3.9 1.5 %collective-permute-start = (f32[104,128]{1,0:T(8,128)}, f32[104,128]{1,0:T(8,128)S(1)}, u32[]{:S(2)}, u32[]{:S(2)}) collective-permute-start(f32[104,128]{1,0:T(8,128)} %get-tuple-element.27), channel_id=1, source_target_pairs={{0,1},{1,0},{2,3},{3,2},{4,5},{5,4},{6,7},{7,6},{8,9},{9,8},{10,11... | collective-permute-start | bytes 159752 | tf_op jit(solution)/shard_map/ppermute | solution.py:49
  7.7 3.0 %collective-permute-start.1 = (f32[192,128]{1,0:T(8,128)S(1)}, f32[192,128]{1,0:T(8,128)S(1)}, u32[]{:S(2)}, u32[]{:S(2)}) collective-permute-start(f32[192,128]{1,0:T(8,128)S(1)} %get-tuple-element.29.near), channel_id=1, source_target_pairs={{0,4},{1,5},{2,6},{3,7},{4,0},{5,1},{6,2},{7,3},{8,12},{9,13},{10,... | collective-permute-start | bytes 294920 | tf_op jit(solution)/shard_map/ppermute | solution.py:45
  11.5 2.0 %collective-permute-done.1.far.refs_1_ = f32[192,128]{1,0:T(8,128)S(1)} collective-permute-done((f32[192,128]{1,0:T(8,128)S(1)}, f32[192,128]{1,0:T(8,128)S(1)}, u32[]{:S(2)}, u32[]{:S(2)}) %collective-permute-start.1) | collective-permute-done | bytes 98336 | tf_op jit(solution)/shard_map/ppermute | solution.py:45
  14.9 1.7 %collective-permute-start.3 = (f32[384,128]{1,0:T(8,128)S(1)}, f32[384,128]{1,0:T(8,128)S(1)}, u32[]{:S(2)}, u32[]{:S(2)}) collective-permute-start(f32[384,128]{1,0:T(8,128)S(1)} %shard_map.75.b0), channel_id=1, source_target_pairs={{0,32},{1,9},{2,34},{3,11},{4,36},{5,13},{6,38},{7,15},{8,40},{9,1... | collective-permute-start | bytes 589832 | tf_op jit(solution)/shard_map/ppermute | solution.py:45
  16.6 2.2 %collective-permute-start.4 = (f32[384,128]{1,0:T(8,128)S(1)}, f32[384,128]{1,0:T(8,128)S(1)}, u32[]{:S(2)}, u32[]{:S(2)}) collective-permute-start(f32[384,128]{1,0:T(8,128)S(1)} %shard_map.75.b0), channel_id=1, source_target_pairs={{0,96},{1,25},{2,98},{3,27},{4,100},{5,29},{6,102},{7,31},{8,104},... | collective-permute-start | bytes 589832 | tf_op jit(solution)/shard_map/ppermute | solution.py:45
  20.0 2.0 %collective-permute-done.3.b1 = f32[384,128]{1,0:T(8,128)S(1)} collective-permute-done((f32[384,128]{1,0:T(8,128)S(1)}, f32[384,128]{1,0:T(8,128)S(1)}, u32[]{:S(2)}, u32[]{:S(2)}) %collective-permute-start.3) | collective-permute-done | bytes 196640 | tf_op jit(solution)/shard_map/ppermute | solution.py:45
  22.1 1.4 %collective-permute-done.4.b2 = f32[384,128]{1,0:T(8,128)S(1)} collective-permute-done((f32[384,128]{1,0:T(8,128)S(1)}, f32[384,128]{1,0:T(8,128)S(1)}, u32[]{:S(2)}, u32[]{:S(2)}) %collective-permute-start.4) | collective-permute-done | bytes 196640 | tf_op jit(solution)/shard_map/ppermute | solution.py:45
  23.5 1.5 %collective-permute-done.5.b3 = f32[384,128]{1,0:T(8,128)S(1)} collective-permute-done((f32[384,128]{1,0:T(8,128)S(1)}, f32[384,128]{1,0:T(8,128)S(1)}, u32[]{:S(2)}, u32[]{:S(2)}) %collective-permute-start.5) | collective-permute-done | bytes 196640 | tf_op jit(solution)/shard_map/ppermute | solution.py:45
  26.4 1.6 %collective-permute-start.11 = (f32[768,128]{1,0:T(8,128)S(1)}, f32[768,128]{1,0:T(8,128)S(1)}, u32[]{:S(2)}, u32[]{:S(2)}) collective-permute-start(f32[768,128]{1,0:T(8,128)S(1)} %get-tuple-element.32.witness.b0), channel_id=1, source_target_pairs={{0,24},{1,97},{2,26},{3,99},{4,28},{5,101},{6,30},{7,103},{8,0},{9... | collective-permute-start | bytes 1179656 | tf_op jit(solution)/shard_map/ppermute | solution.py:45
  29.4 2.1 %shard_map.77 = (bf16[176,2688]{1,0:T(8,128)(2,1)S(1)}, bf16[176,2688]{1,0:T(8,128)(2,1)S(1)}, bf16[256,2688]{1,0:T(8,128)(2,1)S(1)}, bf16[256,2688]{1,0:T(8,128)(2,1)S(1)}) custom-call(f32[3696,128]{1,0:T(8,128)} %get-tuple-element.30.home, f32[3696,128]{1,0:T(8,128)S(1)} %collective-permute-done.2.home_other, f32[768,128]{1,0:T(8,128)S(1)} %get-tuple-element.32.witness.b0), custom_call_target="tpu_custom_call" | custom-call | flops 1 | bytes 1 | tf_op jit(solution)/shard_map/pallas_call | solution.py:430
  31.6 4.3 %collective-permute-done.13.refs_1_ = f32[1848,128]{1,0:T(8,128)S(1)} collective-permute-done((f32[1848,128]{1,0:T(8,128)S(1)}, f32[1848,128]{1,0:T(8,128)S(1)}, u32[]{:S(2)}, u32[]{:S(2)}) %collective-permute-start.13) | collective-permute-done | bytes 946208 | tf_op jit(solution)/shard_map/ppermute | solution.py:45
  37.0 1.5 %collective-permute-done.9.refs_2_.b1 = f32[768,128]{1,0:T(8,128)S(1)} collective-permute-done((f32[768,128]{1,0:T(8,128)S(1)}, f32[768,128]{1,0:T(8,128)S(1)}, u32[]{:S(2)}, u32[]{:S(2)}) %collective-permute-start.9) | collective-permute-done | bytes 393248 | tf_op jit(solution)/shard_map/ppermute | solution.py:45
  38.5 5.8 %collective-permute-start.15 = (f32[1848,128]{1,0:T(8,128)S(1)}, f32[1848,128]{1,0:T(8,128)S(1)}, u32[]{:S(2)}, u32[]{:S(2)}) collective-permute-start(f32[1848,128]{1,0:T(8,128)S(1)} %get-tuple-element.39.above), channel_id=1, source_target_pairs={{0,1},{1,0},{2,3},{3,2},{4,5},{5,4},{6,7},{7,6},{8,9},{9,8},{10,11... | collective-permute-start | bytes 2838536 | tf_op jit(solution)/shard_map/ppermute | solution.py:49
  44.3 2.4 %collective-permute-start.6 = (f32[768,128]{1,0:T(8,128)S(1)}, f32[768,128]{1,0:T(8,128)S(1)}, u32[]{:S(2)}, u32[]{:S(2)}) collective-permute-start(f32[768,128]{1,0:T(8,128)S(1)} %get-tuple-element.31.b0), channel_id=1, source_target_pairs={{0,16},{1,65},{2,18},{3,67},{4,20},{5,69},{6,22},{7,71},{8,24},{9,... | collective-permute-start | bytes 1179656 | tf_op jit(solution)/shard_map/ppermute | solution.py:45
  46.8 2.7 %collective-permute-start.8 = (f32[768,128]{1,0:T(8,128)S(1)}, f32[768,128]{1,0:T(8,128)S(1)}, u32[]{:S(2)}, u32[]{:S(2)}) collective-permute-start(f32[768,128]{1,0:T(8,128)S(1)} %get-tuple-element.31.b0), channel_id=1, source_target_pairs={{0,24},{1,97},{2,26},{3,99},{4,28},{5,101},{6,30},{7,103},{8,0},{9... | collective-permute-start | bytes 1179656 | tf_op jit(solution)/shard_map/ppermute | solution.py:45
  49.4 2.0 %shard_map.80 = (f32[144,256]{1,0:T(8,128)S(1)}, f32[144,256]{1,0:T(8,128)S(1)}, bf16[144,2688]{1,0:T(8,128)(2,1)S(1)}, bf16[144,2688]{1,0:T(8,128)(2,1)S(1)}) custom-call(f32[768,128]{1,0:T(8,128)S(1)} %get-tuple-element.32.witness.b0, f32[768,128]{1,0:T(8,128)S(1)} %collective-permute-done.9.refs_2_.b1, f32[768,128]{1,0:T(8,128)S(1)} %collective-permute-done.10.refs_3_.b2, ...), custom_call_target="tpu_custom_call" | custom-call | tf_op jit(solution)/shard_map/pallas_call | solution.py:467
  51.5 2.7 %collective-permute-start.18 = (f32[144,256]{1,0:T(8,128)S(1)}, f32[144,256]{1,0:T(8,128)S(1)}, u32[]{:S(2)}, u32[]{:S(2)}) collective-permute-start(f32[144,256]{1,0:T(8,128)S(1)} %get-tuple-element.44), channel_id=1, source_target_pairs={{0,2},{1,7},{2,4},{3,1},{4,6},{5,3},{6,0},{7,5},{8,10},{9,15},{10,... | collective-permute-start | bytes 442376 | tf_op jit(solution)/shard_map/ppermute | solution.py:45
  55.2 1.7 %collective-permute-done.7.b2 = f32[768,128]{1,0:T(8,128)S(1)} collective-permute-done((f32[768,128]{1,0:T(8,128)S(1)}, f32[768,128]{1,0:T(8,128)S(1)}, u32[]{:S(2)}, u32[]{:S(2)}) %collective-permute-start.7) | collective-permute-done | bytes 393248 | tf_op jit(solution)/shard_map/ppermute | solution.py:45
  57.0 1.5 %collective-permute-done.17.back_a = f32[144,256]{1,0:T(8,128)S(1)} collective-permute-done((f32[144,256]{1,0:T(8,128)S(1)}, f32[144,256]{1,0:T(8,128)S(1)}, u32[]{:S(2)}, u32[]{:S(2)}) %collective-permute-start.17) | collective-permute-done | bytes 147488 | tf_op jit(solution)/shard_map/ppermute | solution.py:45
  58.5 2.2 %shard_map.82 = f32[32,8,128]{2,1,0:T(8,128)} custom-call(f32[768,128]{1,0:T(8,128)S(1)} %get-tuple-element.31.b0, f32[768,128]{1,0:T(8,128)S(1)} %collective-permute-done.6.b1, f32[768,128]{1,0:T(8,128)S(1)} %collective-permute-done.7.b2, f32[768,128]{1,0:T(8,128)S(1)} %collective-permute-done.8.b3, bf16[256,2688]{1,0:T(8,128)(2,1)S(1)} %get-tuple-element.33.v_high, ...), custom_call_target="tpu_custom_call" | custom-call | tf_op jit(solution)/shard_map/pallas_call | solution.py:485
  60.7 5.6 %all-to-all-start = ((f32[32,8,128]{2,1,0:T(8,128)}), f32[32,8,128]{2,1,0:T(8,128)S(1)}, u32[]{:S(2)}, u32[]{:S(2)}) async-start(f32[32,8,128]{2,1,0:T(8,128)} %shard_map.82), calls=%async_computation | async-start | bytes 262144 | tf_op jit(solution)/shard_map/all_to_all | solution.py:493
  66.3 2.8 %shard_map.83 = (f32[18,1296]{1,0:T(8,128)S(1)}, f32[18,1296]{1,0:T(8,128)S(1)}) custom-call(s32[8]{0:T(128)S(1)} %copy-done.3, s32[8]{0:T(128)S(1)} %copy-done.4, f32[8,6]{1,0:T(8,128)S(1)} %copy-done.6, f32[8,36]{1,0:T(8,128)S(1)} %copy-done.7, f32[3,6,1,1296]{3,2,1,0:T(1,128)S(1)} %copy-done.1, f32[108,1,216]{2,1,0:T(1,128)S(1)} %copy-done.5, ...), custom_call_target="tpu_custom_call" | custom-call | flops 100000000 | bytes 1000000 | tf_op jit(solution)/shard_map/pallas_call | solution.py:444
  69.2 4.8 %all-to-all-done.sums = f32[32,8,128]{2,1,0:T(8,128)S(1)} async-done(((f32[32,8,128]{2,1,0:T(8,128)}), f32[32,8,128]{2,1,0:T(8,128)S(1)}, u32[]{:S(2)}, u32[]{:S(2)}) %all-to-all-start) | async-done | bytes 131104 | tf_op jit(solution)/shard_map/all_to_all | solution.py:493
  (46 shorter events, 11.6 us)
Async XLA Ops:
  3.9 9.7 %copy-start = (f32[88,1,2688]{2,1,0:T(1,128)S(1)}, f32[88,1,2688]{2,1,0:T(1,128)}, u32[]{:S(2)}) copy-start(f32[88,1,2688]{2,1,0:T(1,128)} %get-tuple-element.36) | copy-start | bytes 2838532
  3.9 2.6 %collective-permute-start = (f32[104,128]{1,0:T(8,128)}, f32[104,128]{1,0:T(8,128)S(1)}, u32[]{:S(2)}, u32[]{:S(2)}) collective-permute-start(f32[104,128]{1,0:T(8,128)} %get-tuple-element.27), channel_id=1, source_target_pairs={{0,1},{1,0},{2,3},{3,2},{4,5},{5,4},{6,7},{7,6},{8,9},{9,8},{10,11... | collective-permute-start | bytes 159752 | tf_op jit(solution)/shard_map/ppermute | solution.py:49
  7.3 7.6 %collective-permute-start.2 = (f32[3696,128]{1,0:T(8,128)}, f32[3696,128]{1,0:T(8,128)S(1)}, u32[]{:S(2)}, u32[]{:S(2)}) collective-permute-start(f32[3696,128]{1,0:T(8,128)} %get-tuple-element.30.home), channel_id=1, source_target_pairs={{0,1},{1,0},{2,3},{3,2},{4,5},{5,4},{6,7},{7,6},{8,9},{9,8},{10,11... | collective-permute-start | bytes 5677064 | tf_op jit(solution)/shard_map/ppermute | solution.py:49
  7.7 5.8 %collective-permute-start.1 = (f32[192,128]{1,0:T(8,128)S(1)}, f32[192,128]{1,0:T(8,128)S(1)}, u32[]{:S(2)}, u32[]{:S(2)}) collective-permute-start(f32[192,128]{1,0:T(8,128)S(1)} %get-tuple-element.29.near), channel_id=1, source_target_pairs={{0,4},{1,5},{2,6},{3,7},{4,0},{5,1},{6,2},{7,3},{8,12},{9,13},{10,... | collective-permute-start | bytes 294920 | tf_op jit(solution)/shard_map/ppermute | solution.py:45
  10.7 20.8 %collective-permute-start.12 = (f32[1848,128]{1,0:T(8,128)S(1)}, f32[1848,128]{1,0:T(8,128)S(1)}, u32[]{:S(2)}, u32[]{:S(2)}) collective-permute-start(f32[1848,128]{1,0:T(8,128)S(1)} %bitcast.6), channel_id=1, source_target_pairs={{0,2},{1,7},{2,4},{3,1},{4,6},{5,3},{6,0},{7,5},{8,10},{9,15},{10,... | collective-permute-start | bytes 2838536 | tf_op jit(solution)/shard_map/ppermute | solution.py:45
  13.6 8.5 %copy-start.5 = (f32[108,1,216]{2,1,0:T(1,128)S(1)}, f32[108,1,216]{2,1,0:T(1,128)}, u32[]{:S(2)}) copy-start(f32[108,1,216]{2,1,0:T(1,128)} %ovov.1) | copy-start | bytes 279940
  13.6 22.3 %collective-permute-start.13 = (f32[1848,128]{1,0:T(8,128)S(1)}, f32[1848,128]{1,0:T(8,128)S(1)}, u32[]{:S(2)}, u32[]{:S(2)}) collective-permute-start(f32[1848,128]{1,0:T(8,128)S(1)} %shard_map.78), channel_id=1, source_target_pairs={{0,6},{1,3},{2,0},{3,5},{4,2},{5,7},{6,4},{7,1},{8,14},{9,11},{10,... | collective-permute-start | bytes 2838536 | tf_op jit(solution)/shard_map/ppermute | solution.py:45
  14.9 7.2 %collective-permute-start.3 = (f32[384,128]{1,0:T(8,128)S(1)}, f32[384,128]{1,0:T(8,128)S(1)}, u32[]{:S(2)}, u32[]{:S(2)}) collective-permute-start(f32[384,128]{1,0:T(8,128)S(1)} %shard_map.75.b0), channel_id=1, source_target_pairs={{0,32},{1,9},{2,34},{3,11},{4,36},{5,13},{6,38},{7,15},{8,40},{9,1... | collective-permute-start | bytes 589832 | tf_op jit(solution)/shard_map/ppermute | solution.py:45
  16.6 6.9 %collective-permute-start.4 = (f32[384,128]{1,0:T(8,128)S(1)}, f32[384,128]{1,0:T(8,128)S(1)}, u32[]{:S(2)}, u32[]{:S(2)}) collective-permute-start(f32[384,128]{1,0:T(8,128)S(1)} %shard_map.75.b0), channel_id=1, source_target_pairs={{0,96},{1,25},{2,98},{3,27},{4,100},{5,29},{6,102},{7,31},{8,104},... | collective-permute-start | bytes 589832 | tf_op jit(solution)/shard_map/ppermute | solution.py:45
  18.8 6.3 %collective-permute-start.5 = (f32[384,128]{1,0:T(8,128)S(1)}, f32[384,128]{1,0:T(8,128)S(1)}, u32[]{:S(2)}, u32[]{:S(2)}) collective-permute-start(f32[384,128]{1,0:T(8,128)S(1)} %shard_map.75.b0), channel_id=1, source_target_pairs={{0,64},{1,17},{2,66},{3,19},{4,68},{5,21},{6,70},{7,23},{8,72},{9,... | collective-permute-start | bytes 589832 | tf_op jit(solution)/shard_map/ppermute | solution.py:45
  22.1 6.0 %collective-permute-start.14 = (f32[108,1,216]{2,1,0:T(1,128)S(1)}, f32[108,1,216]{2,1,0:T(1,128)S(1)}, u32[]{:S(2)}, u32[]{:S(2)}) collective-permute-start(f32[108,1,216]{2,1,0:T(1,128)S(1)} %copy-done.5), channel_id=1, source_target_pairs={{0,8},{8,0},{16,24},{24,16},{1,9},{9,1},{17,25},{25,17},{2,10},{10... | collective-permute-start | bytes 279944 | tf_op jit(solution)/shard_map/ppermute | solution.py:401
  25.1 10.7 %collective-permute-start.10 = (f32[768,128]{1,0:T(8,128)S(1)}, f32[768,128]{1,0:T(8,128)S(1)}, u32[]{:S(2)}, u32[]{:S(2)}) collective-permute-start(f32[768,128]{1,0:T(8,128)S(1)} %get-tuple-element.32.witness.b0), channel_id=1, source_target_pairs={{0,8},{1,33},{2,10},{3,35},{4,12},{5,37},{6,14},{7,39},{8,16},{9,4... | collective-permute-start | bytes 1179656 | tf_op jit(solution)/shard_map/ppermute | solution.py:45
  26.4 10.6 %collective-permute-start.11 = (f32[768,128]{1,0:T(8,128)S(1)}, f32[768,128]{1,0:T(8,128)S(1)}, u32[]{:S(2)}, u32[]{:S(2)}) collective-permute-start(f32[768,128]{1,0:T(8,128)S(1)} %get-tuple-element.32.witness.b0), channel_id=1, source_target_pairs={{0,24},{1,97},{2,26},{3,99},{4,28},{5,101},{6,30},{7,103},{8,0},{9... | collective-permute-start | bytes 1179656 | tf_op jit(solution)/shard_map/ppermute | solution.py:45
  28.1 10.5 %collective-permute-start.9 = (f32[768,128]{1,0:T(8,128)S(1)}, f32[768,128]{1,0:T(8,128)S(1)}, u32[]{:S(2)}, u32[]{:S(2)}) collective-permute-start(f32[768,128]{1,0:T(8,128)S(1)} %get-tuple-element.32.witness.b0), channel_id=1, source_target_pairs={{0,16},{1,65},{2,18},{3,67},{4,20},{5,69},{6,22},{7,71},{8,24},{9,... | collective-permute-start | bytes 1179656 | tf_op jit(solution)/shard_map/ppermute | solution.py:45
  38.5 10.9 %collective-permute-start.15 = (f32[1848,128]{1,0:T(8,128)S(1)}, f32[1848,128]{1,0:T(8,128)S(1)}, u32[]{:S(2)}, u32[]{:S(2)}) collective-permute-start(f32[1848,128]{1,0:T(8,128)S(1)} %get-tuple-element.39.above), channel_id=1, source_target_pairs={{0,1},{1,0},{2,3},{3,2},{4,5},{5,4},{6,7},{7,6},{8,9},{9,8},{10,11... | collective-permute-start | bytes 2838536 | tf_op jit(solution)/shard_map/ppermute | solution.py:49
  44.3 5.1 %collective-permute-start.16 = (f32[1848,128]{1,0:T(8,128)S(1)}, f32[1848,128]{1,0:T(8,128)S(1)}, u32[]{:S(2)}, u32[]{:S(2)}) collective-permute-start(f32[1848,128]{1,0:T(8,128)S(1)} %get-tuple-element.38.below), channel_id=1, source_target_pairs={{0,1},{1,0},{2,3},{3,2},{4,5},{5,4},{6,7},{7,6},{8,9},{9,8},{10,11... | collective-permute-start | bytes 2838536 | tf_op jit(solution)/shard_map/ppermute | solution.py:49
  44.3 10.9 %collective-permute-start.6 = (f32[768,128]{1,0:T(8,128)S(1)}, f32[768,128]{1,0:T(8,128)S(1)}, u32[]{:S(2)}, u32[]{:S(2)}) collective-permute-start(f32[768,128]{1,0:T(8,128)S(1)} %get-tuple-element.31.b0), channel_id=1, source_target_pairs={{0,16},{1,65},{2,18},{3,67},{4,20},{5,69},{6,22},{7,71},{8,24},{9,... | collective-permute-start | bytes 1179656 | tf_op jit(solution)/shard_map/ppermute | solution.py:45
  46.8 10.2 %collective-permute-start.7 = (f32[768,128]{1,0:T(8,128)S(1)}, f32[768,128]{1,0:T(8,128)S(1)}, u32[]{:S(2)}, u32[]{:S(2)}) collective-permute-start(f32[768,128]{1,0:T(8,128)S(1)} %get-tuple-element.31.b0), channel_id=1, source_target_pairs={{0,8},{1,33},{2,10},{3,35},{4,12},{5,37},{6,14},{7,39},{8,16},{9,4... | collective-permute-start | bytes 1179656 | tf_op jit(solution)/shard_map/ppermute | solution.py:45
  46.8 10.2 %collective-permute-start.8 = (f32[768,128]{1,0:T(8,128)S(1)}, f32[768,128]{1,0:T(8,128)S(1)}, u32[]{:S(2)}, u32[]{:S(2)}) collective-permute-start(f32[768,128]{1,0:T(8,128)S(1)} %get-tuple-element.31.b0), channel_id=1, source_target_pairs={{0,24},{1,97},{2,26},{3,99},{4,28},{5,101},{6,30},{7,103},{8,0},{9... | collective-permute-start | bytes 1179656 | tf_op jit(solution)/shard_map/ppermute | solution.py:45
  51.4 7.0 %collective-permute-start.17 = (f32[144,256]{1,0:T(8,128)S(1)}, f32[144,256]{1,0:T(8,128)S(1)}, u32[]{:S(2)}, u32[]{:S(2)}) collective-permute-start(f32[144,256]{1,0:T(8,128)S(1)} %get-tuple-element.43.below_sum), channel_id=1, source_target_pairs={{0,6},{1,3},{2,0},{3,5},{4,2},{5,7},{6,4},{7,1},{8,14},{9,11},{10,... | collective-permute-start | bytes 442376 | tf_op jit(solution)/shard_map/ppermute | solution.py:45
  51.5 6.9 %collective-permute-start.18 = (f32[144,256]{1,0:T(8,128)S(1)}, f32[144,256]{1,0:T(8,128)S(1)}, u32[]{:S(2)}, u32[]{:S(2)}) collective-permute-start(f32[144,256]{1,0:T(8,128)S(1)} %get-tuple-element.44), channel_id=1, source_target_pairs={{0,2},{1,7},{2,4},{3,1},{4,6},{5,3},{6,0},{7,5},{8,10},{9,15},{10,... | collective-permute-start | bytes 442376 | tf_op jit(solution)/shard_map/ppermute | solution.py:45
  58.4 7.9 %copy-start.6 = (f32[8,6]{1,0:T(8,128)S(1)}, f32[8,6]{1,0:T(8,128)}, u32[]{:S(2)}) copy-start(f32[8,6]{1,0:T(8,128)} %eps_occ_ref.1) | copy-start | bytes 580
  58.5 7.9 %copy-start.7 = (f32[8,36]{1,0:T(8,128)S(1)}, f32[8,36]{1,0:T(8,128)}, u32[]{:S(2)}) copy-start(f32[8,36]{1,0:T(8,128)} %eps_vir_ref.1) | copy-start | bytes 3460
  60.7 13.3 %all-to-all-start = ((f32[32,8,128]{2,1,0:T(8,128)}), f32[32,8,128]{2,1,0:T(8,128)S(1)}, u32[]{:S(2)}, u32[]{:S(2)}) async-start(f32[32,8,128]{2,1,0:T(8,128)} %shard_map.82), calls=%async_computation | async-start | bytes 262144 | tf_op jit(solution)/shard_map/all_to_all | solution.py:493
  (5 other events, 27.8 us)

commit v14 on v13

--- a/solution.py
+++ b/solution.py
@@ -172,6 +172,10 @@
 
 def nothing(*refs):
     pass
+
+
+def relay(value, witness, out):
+    out[...] = value[...]
 
 
 def hold(values, *witnesses):
@@ -398,7 +402,6 @@
     )(occ_count, vir_count, amplitudes, integrals)
     got = swap_core(send)
     moved_a = ring(flat(first_v), "yy", (1, -1))
-    partner = lax.ppermute(ovov, "z", [(0, 1), (1, 0), (2, 3), (3, 2)])
     home = home.reshape(2 * PROWS, LANES)
     pair, home = pl.pallas_call(
         merge_pair,
@@ -435,6 +438,15 @@
         compiler_params=LARGE,
         cost_estimate=pl.CostEstimate(flops=1, bytes_accessed=1, transcendentals=0),
     )(home, home_other, near)
+    panel = pl.pallas_call(
+        relay,
+        out_shape=shape(ovov.shape, F32),
+        in_specs=[VMEM, ANY],
+        out_specs=VMEM,
+        compiler_params=SMALL,
+        cost_estimate=pl.CostEstimate(flops=1, bytes_accessed=1, transcendentals=0),
+    )(ovov, near_high)
+    partner = lax.ppermute(panel, "z", [(0, 1), (1, 0), (2, 3), (3, 2)])
     near_blocks = [near] + [ring(near, "zx", (step, step)) for step in LAST_STEPS[1:]]
     far_blocks = [far] + [ring(far, "zx", (step, step)) for step in LAST_STEPS[1:]]
 
@@ -460,7 +472,7 @@
         ],
         compiler_params=SMALL,
         cost_estimate=pl.CostEstimate(flops=100000000, bytes_accessed=1000000, transcendentals=0),
-    )(occ_count, vir_count, eps_occ, eps_vir, amplitudes, ovov, partner)
+    )(occ_count, vir_count, eps_occ, eps_vir, amplitudes, panel, partner)
 
     sums = shape((144, 2 * LANES), F32)
     left = shape((144, DEPTH), BF16)

time: 75.1 us -> 76.6 us (1.020)
  starting transfers between devices: 35.6 us -> 39.6 us
  waiting for transfers between devices: 23.2 us -> 20.6 us
    ppermute x14, waiting for transfers between devices: 17.2 us -> 13.7 us  [ring(): return lax.ppermute(value, AXES, pairs)]
    ppermute x1, starting transfers between devices: 0.01 us -> 1.37 us  [on_device(): partner = lax.ppermute(panel, 'z', [(0, 1), (1, 0), (2, 3), (3, 2)])]
    all_to_all x1, starting transfers between devices: 5.57 us -> 6.76 us  [on_device(): ladder = lax.all_to_all(packed, ('x', 'z', 'core'), 0, 0, tiled=True)]
    ppermute x4, starting transfers between devices: 7.72 us -> 8.9 us  [swap_core(): return lax.ppermute(value, 'core', [(0, 1), (1, 0)])]
    ppermute x1, waiting for transfers between devices: 0.01 us -> 0.95 us  [on_device(): partner = lax.ppermute(panel, 'z', [(0, 1), (1, 0), (2, 3), (3, 2)])]
  transfers between devices with their start and end apart: 20 -> 20, of which waited for: 11 -> 13; matrix products, arithmetic and copies ran while one was open for 0% -> 0% of each run, Pallas kernels for 11% -> 11%
where the time goes in v14:
time: 76.6 us; the launch traced here: 76.3 us
  starting transfers between devices  39.6 us (52%)
  waiting for transfers between devices  20.6 us (27%)
  Pallas kernels  15.1 us (20%)
  local copies, waits for them, and re-layouts  0.84 us (1%)
    ppermute x14, starting transfers between devices, ring(): return lax.ppermute(value, AXES, pairs)  22.5 us
    ppermute x14, waiting for transfers between devices, ring(): return lax.ppermute(value, AXES, pairs)  13.7 us
    ppermute x4, starting transfers between devices, swap_core(): return lax.ppermute(value, 'core', [(0, 1), (1, 0)])  8.9 us
    all_to_all x1, starting transfers between devices, on_device(): ladder = lax.all_to_all(packed, ('x', 'z', 'core'), 0, 0, tiled=True)  6.76 us
    all_to_all x1, waiting for transfers between devices, on_device(): ladder = lax.all_to_all(packed, ('x', 'z', 'core'), 0, 0, tiled=True)  4.82 us
    pallas_call x1, Pallas kernels, on_device(): pl.pallas_call(open_step, out_shape=[shape((SHARD, LANES), F32)] * 2 + [w...  3.87 us
    pallas_call x1, Pallas kernels, on_device(): pl.pallas_call(local_step, out_shape=[shape((18, 1296), F32)] * 2, in_spe...  2.83 us
    pallas_call x1, Pallas kernels, on_device(): pl.pallas_call(multiply_far, out_shape=shape((32, 8, LANES), F32), in_spe...  2.25 us
  transfers between devices with their start and end apart: 20, of which 13 were waited for; matrix products, arithmetic and copies ran while one was open for 0% of the time, Pallas kernels for 11%

profile of v14, /device:TPU:1, one launch (start us, length us, event | category | flops | bytes accessed | tf_op | source)
XLA Modules:
  0.0 76.3 jit_solution(7297455792967683233)
XLA Ops:
  0.0 3.9 %shard_map.73 = (f32[104,128]{1,0:T(8,128)}, f32[104,128]{1,0:T(8,128)}, f32[88,1,2688]{2,1,0:T(1,128)}, f32[88,1,2688]{2,1,0:T(1,128)}, f32[2,88,1,2688]{3,2,1,0:T(1,128)}) custom-call(s32[8]{0:T(128)} %occ_ref.3, s32[8]{0:T(128)} %vir_ref.3, f32[3,6,1,1296]{3,2,1,0:T(1,128)} %amp_ref.3, f32[81,1,10368]{2,1,0:T(1,128)} %bitcast.5), custom_call_target="tpu_custom_call" | custom-call | tf_op jit(solution)/shard_map/pallas_call | solution.py:381
  3.9 1.5 %collective-permute-start = (f32[104,128]{1,0:T(8,128)}, f32[104,128]{1,0:T(8,128)S(1)}, u32[]{:S(2)}, u32[]{:S(2)}) collective-permute-start(f32[104,128]{1,0:T(8,128)} %get-tuple-element.27), channel_id=1, source_target_pairs={{0,1},{1,0},{2,3},{3,2},{4,5},{5,4},{6,7},{7,6},{8,9},{9,8},{10,11... | collective-permute-start | bytes 159752 | tf_op jit(solution)/shard_map/ppermute | solution.py:49
  7.7 3.0 %collective-permute-start.1 = (f32[192,128]{1,0:T(8,128)S(1)}, f32[192,128]{1,0:T(8,128)S(1)}, u32[]{:S(2)}, u32[]{:S(2)}) collective-permute-start(f32[192,128]{1,0:T(8,128)S(1)} %get-tuple-element.29.near), channel_id=1, source_target_pairs={{0,4},{1,5},{2,6},{3,7},{4,0},{5,1},{6,2},{7,3},{8,12},{9,13},{10,... | collective-permute-start | bytes 294920 | tf_op jit(solution)/shard_map/ppermute | solution.py:45
  11.5 2.0 %collective-permute-done.1.far.refs_1_ = f32[192,128]{1,0:T(8,128)S(1)} collective-permute-done((f32[192,128]{1,0:T(8,128)S(1)}, f32[192,128]{1,0:T(8,128)S(1)}, u32[]{:S(2)}, u32[]{:S(2)}) %collective-permute-start.1) | collective-permute-done | bytes 98336 | tf_op jit(solution)/shard_map/ppermute | solution.py:45
  14.9 1.7 %collective-permute-start.3 = (f32[384,128]{1,0:T(8,128)S(1)}, f32[384,128]{1,0:T(8,128)S(1)}, u32[]{:S(2)}, u32[]{:S(2)}) collective-permute-start(f32[384,128]{1,0:T(8,128)S(1)} %shard_map.75.b0), channel_id=1, source_target_pairs={{0,32},{1,9},{2,34},{3,11},{4,36},{5,13},{6,38},{7,15},{8,40},{9,1... | collective-permute-start | bytes 589832 | tf_op jit(solution)/shard_map/ppermute | solution.py:45
  16.6 2.2 %collective-permute-start.4 = (f32[384,128]{1,0:T(8,128)S(1)}, f32[384,128]{1,0:T(8,128)S(1)}, u32[]{:S(2)}, u32[]{:S(2)}) collective-permute-start(f32[384,128]{1,0:T(8,128)S(1)} %shard_map.75.b0), channel_id=1, source_target_pairs={{0,96},{1,25},{2,98},{3,27},{4,100},{5,29},{6,102},{7,31},{8,104},... | collective-permute-start | bytes 589832 | tf_op jit(solution)/shard_map/ppermute | solution.py:45
  20.0 2.0 %collective-permute-done.3.b1 = f32[384,128]{1,0:T(8,128)S(1)} collective-permute-done((f32[384,128]{1,0:T(8,128)S(1)}, f32[384,128]{1,0:T(8,128)S(1)}, u32[]{:S(2)}, u32[]{:S(2)}) %collective-permute-start.3) | collective-permute-done | bytes 196640 | tf_op jit(solution)/shard_map/ppermute | solution.py:45
  22.1 1.4 %collective-permute-done.4.b2 = f32[384,128]{1,0:T(8,128)S(1)} collective-permute-done((f32[384,128]{1,0:T(8,128)S(1)}, f32[384,128]{1,0:T(8,128)S(1)}, u32[]{:S(2)}, u32[]{:S(2)}) %collective-permute-start.4) | collective-permute-done | bytes 196640 | tf_op jit(solution)/shard_map/ppermute | solution.py:45
  23.5 1.5 %collective-permute-done.5.b3 = f32[384,128]{1,0:T(8,128)S(1)} collective-permute-done((f32[384,128]{1,0:T(8,128)S(1)}, f32[384,128]{1,0:T(8,128)S(1)}, u32[]{:S(2)}, u32[]{:S(2)}) %collective-permute-start.5) | collective-permute-done | bytes 196640 | tf_op jit(solution)/shard_map/ppermute | solution.py:45
  26.4 1.6 %collective-permute-start.11 = (f32[768,128]{1,0:T(8,128)S(1)}, f32[768,128]{1,0:T(8,128)S(1)}, u32[]{:S(2)}, u32[]{:S(2)}) collective-permute-start(f32[768,128]{1,0:T(8,128)S(1)} %get-tuple-element.32.witness.b0), channel_id=1, source_target_pairs={{0,24},{1,97},{2,26},{3,99},{4,28},{5,101},{6,30},{7,103},{8,0},{9... | collective-permute-start | bytes 1179656 | tf_op jit(solution)/shard_map/ppermute | solution.py:45
  29.4 2.1 %shard_map.77 = (bf16[176,2688]{1,0:T(8,128)(2,1)S(1)}, bf16[176,2688]{1,0:T(8,128)(2,1)S(1)}, bf16[256,2688]{1,0:T(8,128)(2,1)S(1)}, bf16[256,2688]{1,0:T(8,128)(2,1)S(1)}) custom-call(f32[3696,128]{1,0:T(8,128)} %get-tuple-element.30.home, f32[3696,128]{1,0:T(8,128)S(1)} %collective-permute-done.2.home_other, f32[768,128]{1,0:T(8,128)S(1)} %get-tuple-element.32.witness.b0), custom_call_target="tpu_custom_call" | custom-call | flops 1 | bytes 1 | tf_op jit(solution)/shard_map/pallas_call | solution.py:433
  31.6 1.4 %collective-permute-start.14 = (f32[108,1,216]{2,1,0:T(1,128)S(1)}, f32[108,1,216]{2,1,0:T(1,128)S(1)}, u32[]{:S(2)}, u32[]{:S(2)}) collective-permute-start(f32[108,1,216]{2,1,0:T(1,128)S(1)} %shard_map.79.ovov), channel_id=1, source_target_pairs={{0,8},{8,0},{16,24},{24,16},{1,9},{9,1},{17,25},{25,17},{2,10},{10... | collective-permute-start | bytes 279944 | tf_op jit(solution)/shard_map/ppermute | solution.py:449
  33.0 2.8 %collective-permute-done.13.refs_1_ = f32[1848,128]{1,0:T(8,128)S(1)} collective-permute-done((f32[1848,128]{1,0:T(8,128)S(1)}, f32[1848,128]{1,0:T(8,128)S(1)}, u32[]{:S(2)}, u32[]{:S(2)}) %collective-permute-start.13) | collective-permute-done | bytes 946208 | tf_op jit(solution)/shard_map/ppermute | solution.py:45
  37.0 1.5 %collective-permute-done.9.refs_2_.b1 = f32[768,128]{1,0:T(8,128)S(1)} collective-permute-done((f32[768,128]{1,0:T(8,128)S(1)}, f32[768,128]{1,0:T(8,128)S(1)}, u32[]{:S(2)}, u32[]{:S(2)}) %collective-permute-start.9) | collective-permute-done | bytes 393248 | tf_op jit(solution)/shard_map/ppermute | solution.py:45
  38.5 7.0 %collective-permute-start.15 = (f32[1848,128]{1,0:T(8,128)S(1)}, f32[1848,128]{1,0:T(8,128)S(1)}, u32[]{:S(2)}, u32[]{:S(2)}) collective-permute-start(f32[1848,128]{1,0:T(8,128)S(1)} %get-tuple-element.39.above), channel_id=1, source_target_pairs={{0,1},{1,0},{2,3},{3,2},{4,5},{5,4},{6,7},{7,6},{8,9},{9,8},{10,11... | collective-permute-start | bytes 2838536 | tf_op jit(solution)/shard_map/ppermute | solution.py:49
  45.5 2.6 %collective-permute-start.6 = (f32[768,128]{1,0:T(8,128)S(1)}, f32[768,128]{1,0:T(8,128)S(1)}, u32[]{:S(2)}, u32[]{:S(2)}) collective-permute-start(f32[768,128]{1,0:T(8,128)S(1)} %get-tuple-element.31.b0), channel_id=1, source_target_pairs={{0,16},{1,65},{2,18},{3,67},{4,20},{5,69},{6,22},{7,71},{8,24},{9,... | collective-permute-start | bytes 1179656 | tf_op jit(solution)/shard_map/ppermute | solution.py:45
  48.2 2.7 %collective-permute-start.8 = (f32[768,128]{1,0:T(8,128)S(1)}, f32[768,128]{1,0:T(8,128)S(1)}, u32[]{:S(2)}, u32[]{:S(2)}) collective-permute-start(f32[768,128]{1,0:T(8,128)S(1)} %get-tuple-element.31.b0), channel_id=1, source_target_pairs={{0,24},{1,97},{2,26},{3,99},{4,28},{5,101},{6,30},{7,103},{8,0},{9... | collective-permute-start | bytes 1179656 | tf_op jit(solution)/shard_map/ppermute | solution.py:45
  50.8 2.0 %shard_map.81 = (f32[144,256]{1,0:T(8,128)S(1)}, f32[144,256]{1,0:T(8,128)S(1)}, bf16[144,2688]{1,0:T(8,128)(2,1)S(1)}, bf16[144,2688]{1,0:T(8,128)(2,1)S(1)}) custom-call(f32[768,128]{1,0:T(8,128)S(1)} %get-tuple-element.32.witness.b0, f32[768,128]{1,0:T(8,128)S(1)} %collective-permute-done.9.refs_2_.b1, f32[768,128]{1,0:T(8,128)S(1)} %collective-permute-done.10.refs_3_.b2, ...), custom_call_target="tpu_custom_call" | custom-call | tf_op jit(solution)/shard_map/pallas_call | solution.py:479
  52.9 2.7 %collective-permute-start.18 = (f32[144,256]{1,0:T(8,128)S(1)}, f32[144,256]{1,0:T(8,128)S(1)}, u32[]{:S(2)}, u32[]{:S(2)}) collective-permute-start(f32[144,256]{1,0:T(8,128)S(1)} %get-tuple-element.44), channel_id=1, source_target_pairs={{0,2},{1,7},{2,4},{3,1},{4,6},{5,3},{6,0},{7,5},{8,10},{9,15},{10,... | collective-permute-start | bytes 442376 | tf_op jit(solution)/shard_map/ppermute | solution.py:45
  56.7 1.5 %collective-permute-done.7.b2 = f32[768,128]{1,0:T(8,128)S(1)} collective-permute-done((f32[768,128]{1,0:T(8,128)S(1)}, f32[768,128]{1,0:T(8,128)S(1)}, u32[]{:S(2)}, u32[]{:S(2)}) %collective-permute-start.7) | collective-permute-done | bytes 393248 | tf_op jit(solution)/shard_map/ppermute | solution.py:45
  58.7 2.3 %shard_map.83 = f32[32,8,128]{2,1,0:T(8,128)} custom-call(f32[768,128]{1,0:T(8,128)S(1)} %get-tuple-element.31.b0, f32[768,128]{1,0:T(8,128)S(1)} %collective-permute-done.6.b1, f32[768,128]{1,0:T(8,128)S(1)} %collective-permute-done.7.b2, f32[768,128]{1,0:T(8,128)S(1)} %collective-permute-done.8.b3, bf16[256,2688]{1,0:T(8,128)(2,1)S(1)} %get-tuple-element.33.v_high, ...), custom_call_target="tpu_custom_call" | custom-call | tf_op jit(solution)/shard_map/pallas_call | solution.py:497
  60.9 6.8 %all-to-all-start = ((f32[32,8,128]{2,1,0:T(8,128)}), f32[32,8,128]{2,1,0:T(8,128)S(1)}, u32[]{:S(2)}, u32[]{:S(2)}) async-start(f32[32,8,128]{2,1,0:T(8,128)} %shard_map.83), calls=%async_computation | async-start | bytes 262144 | tf_op jit(solution)/shard_map/all_to_all | solution.py:505
  67.8 2.8 %shard_map.84 = (f32[18,1296]{1,0:T(8,128)S(1)}, f32[18,1296]{1,0:T(8,128)S(1)}) custom-call(s32[8]{0:T(128)S(1)} %copy-done.4, s32[8]{0:T(128)S(1)} %copy-done.5, f32[8,6]{1,0:T(8,128)S(1)} %copy-done.6, f32[8,36]{1,0:T(8,128)S(1)} %copy-done.7, f32[3,6,1,1296]{3,2,1,0:T(1,128)S(1)} %copy-done.2, f32[108,1,216]{2,1,0:T(1,128)S(1)} %shard_map.79.ovov, ...), custom_call_target="tpu_custom_call" | custom-call | flops 100000000 | bytes 1000000 | tf_op jit(solution)/shard_map/pallas_call | solution.py:456
  70.6 4.8 %all-to-all-done.sums = f32[32,8,128]{2,1,0:T(8,128)S(1)} async-done(((f32[32,8,128]{2,1,0:T(8,128)}), f32[32,8,128]{2,1,0:T(8,128)S(1)}, u32[]{:S(2)}, u32[]{:S(2)}) %all-to-all-start) | async-done | bytes 131104 | tf_op jit(solution)/shard_map/all_to_all | solution.py:505
  (47 shorter events, 12.2 us)
Async XLA Ops:
  3.9 9.7 %copy-start = (f32[88,1,2688]{2,1,0:T(1,128)S(1)}, f32[88,1,2688]{2,1,0:T(1,128)}, u32[]{:S(2)}) copy-start(f32[88,1,2688]{2,1,0:T(1,128)} %get-tuple-element.36) | copy-start | bytes 2838532
  3.9 2.6 %collective-permute-start = (f32[104,128]{1,0:T(8,128)}, f32[104,128]{1,0:T(8,128)S(1)}, u32[]{:S(2)}, u32[]{:S(2)}) collective-permute-start(f32[104,128]{1,0:T(8,128)} %get-tuple-element.27), channel_id=1, source_target_pairs={{0,1},{1,0},{2,3},{3,2},{4,5},{5,4},{6,7},{7,6},{8,9},{9,8},{10,11... | collective-permute-start | bytes 159752 | tf_op jit(solution)/shard_map/ppermute | solution.py:49
  7.3 7.6 %collective-permute-start.2 = (f32[3696,128]{1,0:T(8,128)}, f32[3696,128]{1,0:T(8,128)S(1)}, u32[]{:S(2)}, u32[]{:S(2)}) collective-permute-start(f32[3696,128]{1,0:T(8,128)} %get-tuple-element.30.home), channel_id=1, source_target_pairs={{0,1},{1,0},{2,3},{3,2},{4,5},{5,4},{6,7},{7,6},{8,9},{9,8},{10,11... | collective-permute-start | bytes 5677064 | tf_op jit(solution)/shard_map/ppermute | solution.py:49
  7.7 5.8 %collective-permute-start.1 = (f32[192,128]{1,0:T(8,128)S(1)}, f32[192,128]{1,0:T(8,128)S(1)}, u32[]{:S(2)}, u32[]{:S(2)}) collective-permute-start(f32[192,128]{1,0:T(8,128)S(1)} %get-tuple-element.29.near), channel_id=1, source_target_pairs={{0,4},{1,5},{2,6},{3,7},{4,0},{5,1},{6,2},{7,3},{8,12},{9,13},{10,... | collective-permute-start | bytes 294920 | tf_op jit(solution)/shard_map/ppermute | solution.py:45
  10.7 20.9 %collective-permute-start.12 = (f32[1848,128]{1,0:T(8,128)S(1)}, f32[1848,128]{1,0:T(8,128)S(1)}, u32[]{:S(2)}, u32[]{:S(2)}) collective-permute-start(f32[1848,128]{1,0:T(8,128)S(1)} %bitcast.6), channel_id=1, source_target_pairs={{0,2},{1,7},{2,4},{3,1},{4,6},{5,3},{6,0},{7,5},{8,10},{9,15},{10,... | collective-permute-start | bytes 2838536 | tf_op jit(solution)/shard_map/ppermute | solution.py:45
  13.6 22.3 %collective-permute-start.13 = (f32[1848,128]{1,0:T(8,128)S(1)}, f32[1848,128]{1,0:T(8,128)S(1)}, u32[]{:S(2)}, u32[]{:S(2)}) collective-permute-start(f32[1848,128]{1,0:T(8,128)S(1)} %shard_map.78), channel_id=1, source_target_pairs={{0,6},{1,3},{2,0},{3,5},{4,2},{5,7},{6,4},{7,1},{8,14},{9,11},{10,... | collective-permute-start | bytes 2838536 | tf_op jit(solution)/shard_map/ppermute | solution.py:45
  14.9 7.2 %collective-permute-start.3 = (f32[384,128]{1,0:T(8,128)S(1)}, f32[384,128]{1,0:T(8,128)S(1)}, u32[]{:S(2)}, u32[]{:S(2)}) collective-permute-start(f32[384,128]{1,0:T(8,128)S(1)} %shard_map.75.b0), channel_id=1, source_target_pairs={{0,32},{1,9},{2,34},{3,11},{4,36},{5,13},{6,38},{7,15},{8,40},{9,1... | collective-permute-start | bytes 589832 | tf_op jit(solution)/shard_map/ppermute | solution.py:45
  16.6 6.9 %collective-permute-start.4 = (f32[384,128]{1,0:T(8,128)S(1)}, f32[384,128]{1,0:T(8,128)S(1)}, u32[]{:S(2)}, u32[]{:S(2)}) collective-permute-start(f32[384,128]{1,0:T(8,128)S(1)} %shard_map.75.b0), channel_id=1, source_target_pairs={{0,96},{1,25},{2,98},{3,27},{4,100},{5,29},{6,102},{7,31},{8,104},... | collective-permute-start | bytes 589832 | tf_op jit(solution)/shard_map/ppermute | solution.py:45
  18.8 6.3 %collective-permute-start.5 = (f32[384,128]{1,0:T(8,128)S(1)}, f32[384,128]{1,0:T(8,128)S(1)}, u32[]{:S(2)}, u32[]{:S(2)}) collective-permute-start(f32[384,128]{1,0:T(8,128)S(1)} %shard_map.75.b0), channel_id=1, source_target_pairs={{0,64},{1,17},{2,66},{3,19},{4,68},{5,21},{6,70},{7,23},{8,72},{9,... | collective-permute-start | bytes 589832 | tf_op jit(solution)/shard_map/ppermute | solution.py:45
  25.1 11.6 %collective-permute-start.10 = (f32[768,128]{1,0:T(8,128)S(1)}, f32[768,128]{1,0:T(8,128)S(1)}, u32[]{:S(2)}, u32[]{:S(2)}) collective-permute-start(f32[768,128]{1,0:T(8,128)S(1)} %get-tuple-element.32.witness.b0), channel_id=1, source_target_pairs={{0,8},{1,33},{2,10},{3,35},{4,12},{5,37},{6,14},{7,39},{8,16},{9,4... | collective-permute-start | bytes 1179656 | tf_op jit(solution)/shard_map/ppermute | solution.py:45
  26.4 10.6 %collective-permute-start.11 = (f32[768,128]{1,0:T(8,128)S(1)}, f32[768,128]{1,0:T(8,128)S(1)}, u32[]{:S(2)}, u32[]{:S(2)}) collective-permute-start(f32[768,128]{1,0:T(8,128)S(1)} %get-tuple-element.32.witness.b0), channel_id=1, source_target_pairs={{0,24},{1,97},{2,26},{3,99},{4,28},{5,101},{6,30},{7,103},{8,0},{9... | collective-permute-start | bytes 1179656 | tf_op jit(solution)/shard_map/ppermute | solution.py:45
  28.1 10.5 %collective-permute-start.9 = (f32[768,128]{1,0:T(8,128)S(1)}, f32[768,128]{1,0:T(8,128)S(1)}, u32[]{:S(2)}, u32[]{:S(2)}) collective-permute-start(f32[768,128]{1,0:T(8,128)S(1)} %get-tuple-element.32.witness.b0), channel_id=1, source_target_pairs={{0,16},{1,65},{2,18},{3,67},{4,20},{5,69},{6,22},{7,71},{8,24},{9,... | collective-permute-start | bytes 1179656 | tf_op jit(solution)/shard_map/ppermute | solution.py:45
  31.6 5.2 %collective-permute-start.14 = (f32[108,1,216]{2,1,0:T(1,128)S(1)}, f32[108,1,216]{2,1,0:T(1,128)S(1)}, u32[]{:S(2)}, u32[]{:S(2)}) collective-permute-start(f32[108,1,216]{2,1,0:T(1,128)S(1)} %shard_map.79.ovov), channel_id=1, source_target_pairs={{0,8},{8,0},{16,24},{24,16},{1,9},{9,1},{17,25},{25,17},{2,10},{10... | collective-permute-start | bytes 279944 | tf_op jit(solution)/shard_map/ppermute | solution.py:449
  38.5 12.3 %collective-permute-start.15 = (f32[1848,128]{1,0:T(8,128)S(1)}, f32[1848,128]{1,0:T(8,128)S(1)}, u32[]{:S(2)}, u32[]{:S(2)}) collective-permute-start(f32[1848,128]{1,0:T(8,128)S(1)} %get-tuple-element.39.above), channel_id=1, source_target_pairs={{0,1},{1,0},{2,3},{3,2},{4,5},{5,4},{6,7},{7,6},{8,9},{9,8},{10,11... | collective-permute-start | bytes 2838536 | tf_op jit(solution)/shard_map/ppermute | solution.py:49
  45.5 5.3 %collective-permute-start.16 = (f32[1848,128]{1,0:T(8,128)S(1)}, f32[1848,128]{1,0:T(8,128)S(1)}, u32[]{:S(2)}, u32[]{:S(2)}) collective-permute-start(f32[1848,128]{1,0:T(8,128)S(1)} %get-tuple-element.38.below), channel_id=1, source_target_pairs={{0,1},{1,0},{2,3},{3,2},{4,5},{5,4},{6,7},{7,6},{8,9},{9,8},{10,11... | collective-permute-start | bytes 2838536 | tf_op jit(solution)/shard_map/ppermute | solution.py:49
  45.5 11.1 %collective-permute-start.6 = (f32[768,128]{1,0:T(8,128)S(1)}, f32[768,128]{1,0:T(8,128)S(1)}, u32[]{:S(2)}, u32[]{:S(2)}) collective-permute-start(f32[768,128]{1,0:T(8,128)S(1)} %get-tuple-element.31.b0), channel_id=1, source_target_pairs={{0,16},{1,65},{2,18},{3,67},{4,20},{5,69},{6,22},{7,71},{8,24},{9,... | collective-permute-start | bytes 1179656 | tf_op jit(solution)/shard_map/ppermute | solution.py:45
  48.2 10.0 %collective-permute-start.7 = (f32[768,128]{1,0:T(8,128)S(1)}, f32[768,128]{1,0:T(8,128)S(1)}, u32[]{:S(2)}, u32[]{:S(2)}) collective-permute-start(f32[768,128]{1,0:T(8,128)S(1)} %get-tuple-element.31.b0), channel_id=1, source_target_pairs={{0,8},{1,33},{2,10},{3,35},{4,12},{5,37},{6,14},{7,39},{8,16},{9,4... | collective-permute-start | bytes 1179656 | tf_op jit(solution)/shard_map/ppermute | solution.py:45
  48.2 10.0 %collective-permute-start.8 = (f32[768,128]{1,0:T(8,128)S(1)}, f32[768,128]{1,0:T(8,128)S(1)}, u32[]{:S(2)}, u32[]{:S(2)}) collective-permute-start(f32[768,128]{1,0:T(8,128)S(1)} %get-tuple-element.31.b0), channel_id=1, source_target_pairs={{0,24},{1,97},{2,26},{3,99},{4,28},{5,101},{6,30},{7,103},{8,0},{9... | collective-permute-start | bytes 1179656 | tf_op jit(solution)/shard_map/ppermute | solution.py:45
  52.8 5.6 %collective-permute-start.17 = (f32[144,256]{1,0:T(8,128)S(1)}, f32[144,256]{1,0:T(8,128)S(1)}, u32[]{:S(2)}, u32[]{:S(2)}) collective-permute-start(f32[144,256]{1,0:T(8,128)S(1)} %get-tuple-element.43.below_sum), channel_id=1, source_target_pairs={{0,6},{1,3},{2,0},{3,5},{4,2},{5,7},{6,4},{7,1},{8,14},{9,11},{10,... | collective-permute-start | bytes 442376 | tf_op jit(solution)/shard_map/ppermute | solution.py:45
  52.9 5.8 %collective-permute-start.18 = (f32[144,256]{1,0:T(8,128)S(1)}, f32[144,256]{1,0:T(8,128)S(1)}, u32[]{:S(2)}, u32[]{:S(2)}) collective-permute-start(f32[144,256]{1,0:T(8,128)S(1)} %get-tuple-element.44), channel_id=1, source_target_pairs={{0,2},{1,7},{2,4},{3,1},{4,6},{5,3},{6,0},{7,5},{8,10},{9,15},{10,... | collective-permute-start | bytes 442376 | tf_op jit(solution)/shard_map/ppermute | solution.py:45
  58.7 9.1 %copy-start.5 = (s32[8]{0:T(128)S(1)}, s32[8]{0:T(128)}, u32[]{:S(2)}) copy-start(s32[8]{0:T(128)} %vir_ref.3) | copy-start | bytes 100
  58.7 9.1 %copy-start.6 = (f32[8,6]{1,0:T(8,128)S(1)}, f32[8,6]{1,0:T(8,128)}, u32[]{:S(2)}) copy-start(f32[8,6]{1,0:T(8,128)} %eps_occ_ref.1) | copy-start | bytes 580
  58.7 9.1 %copy-start.7 = (f32[8,36]{1,0:T(8,128)S(1)}, f32[8,36]{1,0:T(8,128)}, u32[]{:S(2)}) copy-start(f32[8,36]{1,0:T(8,128)} %eps_vir_ref.1) | copy-start | bytes 3460
  60.9 14.5 %all-to-all-start = ((f32[32,8,128]{2,1,0:T(8,128)}), f32[32,8,128]{2,1,0:T(8,128)S(1)}, u32[]{:S(2)}, u32[]{:S(2)}) async-start(f32[32,8,128]{2,1,0:T(8,128)} %shard_map.83), calls=%async_computation | async-start | bytes 262144 | tf_op jit(solution)/shard_map/all_to_all | solution.py:505
  (5 other events, 28.8 us)

commit v15 on v13

--- a/solution.py
+++ b/solution.py
@@ -236,6 +236,27 @@
             ref[:, side * LANES : (side + 1) * LANES] = turned[...].T[0:144, :]
 
 
+def pack_sides(first, second):
+    lane = lax.broadcasted_iota(jnp.int32, (144, LANES), 1)
+    turned = pltpu.roll(second, 81, 1)
+    main = jnp.where(lane < 81, first, turned)
+    low = lane[0:48]
+    rest = jnp.where(
+        low < 34,
+        turned[0:48],
+        jnp.where(low < 68, pltpu.roll(turned[48:96], 34, 1), pltpu.roll(turned[96:144], 68, 1)),
+    )
+    return jnp.concatenate([main, rest], axis=0)
+
+
+def unpack_sides(packed):
+    lane = lax.broadcasted_iota(jnp.int32, (144, LANES), 1)
+    main, rest = packed[0:144], packed[144:192]
+    tail = jnp.concatenate([pltpu.roll(rest, at, 1) for at in (47, 13, 107)], axis=0)
+    second = jnp.where(lane < 47, pltpu.roll(main, 47, 1), tail)
+    return jnp.concatenate([main, second], axis=1)
+
+
 def multiply_moved(b0, b1, b2, b3, below, below_other, above, above_other,
                    below_sum, above_sum, high_out, low_out, extra, turned):
     high, low = left_side((b0, b1, b2, b3), extra)
@@ -244,7 +265,13 @@
     sides = [rows_side(ref, 0) for ref in (below, below_other, above, above_other)]
     v_high, v_low = split(jnp.concatenate(sides, axis=0))
     total = last_by_last(v_high, high) + (last_by_last(v_low, high) + last_by_last(v_high, low))
-    turn_sums(total, (below_sum, above_sum), turned)
+    turned[...] = jnp.zeros_like(turned)
+    for at, ref in enumerate((below_sum, above_sum)):
+        sides = []
+        for side in range(2):
+            turned[0:PSLOT, 0:144] = total[(2 * at + side) * PSLOT : (2 * at + side + 1) * PSLOT, :]
+            sides.append(turned[...].T[0:144, :])
+        ref[...] = pack_sides(*sides)
 
 
 def multiply_home(high, low, v_high, v_low, below_sum, here_sum, turned):
@@ -257,7 +284,7 @@
 def multiply_far(b0, b1, b2, b3, v_high, v_low, here_sum, back_a, back_b, out, extra):
     x, z, y, core = places()
     high, low = left_side((b0, b1, b2, b3), extra)
-    partial = here_sum[...] + back_a[...] + back_b[...]
+    partial = here_sum[...] + unpack_sides(back_a[...] + back_b[...])
     row = lax.broadcasted_iota(jnp.int32, (8, LANES), 0)
     lane = lax.broadcasted_iota(jnp.int32, (8, LANES), 1)
     total = partial + (
@@ -466,7 +493,7 @@
     left = shape((144, DEPTH), BF16)
     below_sum, above_sum, high, low = pl.pallas_call(
         multiply_moved,
-        out_shape=[sums, sums, left, left],
+        out_shape=[shape((192, LANES), F32)] * 2 + [left] * 2,
         in_specs=[VMEM] * 8,
         out_specs=[VMEM] * 4,
         scratch_shapes=[pltpu.VMEM((16, DEPTH), F32), pltpu.VMEM((LANES, 2 * LANES), F32)],

time: 75.1 us -> 75.2 us (level)
  waiting for transfers between devices: 23.2 us -> 22.1 us
  starting transfers between devices: 35.6 us -> 36.5 us
    ppermute x14, waiting for transfers between devices: 17.2 us -> 16.2 us  [ring(): return lax.ppermute(value, AXES, pairs)]
    all_to_all x1, starting transfers between devices: 5.57 us -> 6.44 us  [on_device(): ladder = lax.all_to_all(packed, ('x', 'z', 'core'), 0, 0, tiled=True)]
where the time goes in v15:
time: 75.2 us; the launch traced here: 74.9 us
  starting transfers between devices  36.5 us (49%)
  waiting for transfers between devices  22.1 us (29%)
  Pallas kernels  15.3 us (20%)
  local copies, waits for them, and re-layouts  0.84 us (1%)
    ppermute x14, starting transfers between devices, ring(): return lax.ppermute(value, AXES, pairs)  22.3 us
    ppermute x14, waiting for transfers between devices, ring(): return lax.ppermute(value, AXES, pairs)  16.2 us
    ppermute x4, starting transfers between devices, swap_core(): return lax.ppermute(value, 'core', [(0, 1), (1, 0)])  7.72 us
    all_to_all x1, starting transfers between devices, on_device(): ladder = lax.all_to_all(packed, ('x', 'z', 'core'), 0, 0, tiled=True)  6.44 us
    all_to_all x1, waiting for transfers between devices, on_device(): ladder = lax.all_to_all(packed, ('x', 'z', 'core'), 0, 0, tiled=True)  4.82 us
    pallas_call x1, Pallas kernels, on_device(): pl.pallas_call(open_step, out_shape=[shape((SHARD, LANES), F32)] * 2 + [w...  3.87 us
    pallas_call x1, Pallas kernels, on_device(): pl.pallas_call(local_step, out_shape=[shape((18, 1296), F32)] * 2, in_spe...  2.83 us
    pallas_call x1, Pallas kernels, on_device(): pl.pallas_call(multiply_far, out_shape=shape((32, 8, LANES), F32), in_spe...  2.26 us
  transfers between devices with their start and end apart: 20, of which 11 were waited for; matrix products, arithmetic and copies ran while one was open for 0% of the time, Pallas kernels for 11%

profile of v15, /device:TPU:1, one launch (start us, length us, event | category | flops | bytes accessed | tf_op | source)
XLA Modules:
  0.0 74.9 jit_solution(9763418375327655142)
XLA Ops:
  0.0 3.9 %shard_map.73 = (f32[104,128]{1,0:T(8,128)}, f32[104,128]{1,0:T(8,128)}, f32[88,1,2688]{2,1,0:T(1,128)}, f32[88,1,2688]{2,1,0:T(1,128)}, f32[2,88,1,2688]{3,2,1,0:T(1,128)}) custom-call(s32[8]{0:T(128)} %occ_ref.3, s32[8]{0:T(128)} %vir_ref.3, f32[3,6,1,1296]{3,2,1,0:T(1,128)} %amp_ref.3, f32[81,1,10368]{2,1,0:T(1,128)} %bitcast.5), custom_call_target="tpu_custom_call" | custom-call | tf_op jit(solution)/shard_map/pallas_call | solution.py:404
  3.9 1.5 %collective-permute-start = (f32[104,128]{1,0:T(8,128)}, f32[104,128]{1,0:T(8,128)S(1)}, u32[]{:S(2)}, u32[]{:S(2)}) collective-permute-start(f32[104,128]{1,0:T(8,128)} %get-tuple-element.27), channel_id=1, source_target_pairs={{0,1},{1,0},{2,3},{3,2},{4,5},{5,4},{6,7},{7,6},{8,9},{9,8},{10,11... | collective-permute-start | bytes 159752 | tf_op jit(solution)/shard_map/ppermute | solution.py:49
  7.7 3.0 %collective-permute-start.1 = (f32[192,128]{1,0:T(8,128)S(1)}, f32[192,128]{1,0:T(8,128)S(1)}, u32[]{:S(2)}, u32[]{:S(2)}) collective-permute-start(f32[192,128]{1,0:T(8,128)S(1)} %get-tuple-element.29.near), channel_id=1, source_target_pairs={{0,4},{1,5},{2,6},{3,7},{4,0},{5,1},{6,2},{7,3},{8,12},{9,13},{10,... | collective-permute-start | bytes 294920 | tf_op jit(solution)/shard_map/ppermute | solution.py:45
  11.5 2.0 %collective-permute-done.1.far.refs_1_ = f32[192,128]{1,0:T(8,128)S(1)} collective-permute-done((f32[192,128]{1,0:T(8,128)S(1)}, f32[192,128]{1,0:T(8,128)S(1)}, u32[]{:S(2)}, u32[]{:S(2)}) %collective-permute-start.1) | collective-permute-done | bytes 98336 | tf_op jit(solution)/shard_map/ppermute | solution.py:45
  14.9 1.7 %collective-permute-start.3 = (f32[384,128]{1,0:T(8,128)S(1)}, f32[384,128]{1,0:T(8,128)S(1)}, u32[]{:S(2)}, u32[]{:S(2)}) collective-permute-start(f32[384,128]{1,0:T(8,128)S(1)} %shard_map.75.b0), channel_id=1, source_target_pairs={{0,32},{1,9},{2,34},{3,11},{4,36},{5,13},{6,38},{7,15},{8,40},{9,1... | collective-permute-start | bytes 589832 | tf_op jit(solution)/shard_map/ppermute | solution.py:45
  16.6 2.2 %collective-permute-start.4 = (f32[384,128]{1,0:T(8,128)S(1)}, f32[384,128]{1,0:T(8,128)S(1)}, u32[]{:S(2)}, u32[]{:S(2)}) collective-permute-start(f32[384,128]{1,0:T(8,128)S(1)} %shard_map.75.b0), channel_id=1, source_target_pairs={{0,96},{1,25},{2,98},{3,27},{4,100},{5,29},{6,102},{7,31},{8,104},... | collective-permute-start | bytes 589832 | tf_op jit(solution)/shard_map/ppermute | solution.py:45
  20.0 2.0 %collective-permute-done.3.b1 = f32[384,128]{1,0:T(8,128)S(1)} collective-permute-done((f32[384,128]{1,0:T(8,128)S(1)}, f32[384,128]{1,0:T(8,128)S(1)}, u32[]{:S(2)}, u32[]{:S(2)}) %collective-permute-start.3) | collective-permute-done | bytes 196640 | tf_op jit(solution)/shard_map/ppermute | solution.py:45
  22.1 1.4 %collective-permute-done.4.b2 = f32[384,128]{1,0:T(8,128)S(1)} collective-permute-done((f32[384,128]{1,0:T(8,128)S(1)}, f32[384,128]{1,0:T(8,128)S(1)}, u32[]{:S(2)}, u32[]{:S(2)}) %collective-permute-start.4) | collective-permute-done | bytes 196640 | tf_op jit(solution)/shard_map/ppermute | solution.py:45
  23.5 1.5 %collective-permute-done.5.b3 = f32[384,128]{1,0:T(8,128)S(1)} collective-permute-done((f32[384,128]{1,0:T(8,128)S(1)}, f32[384,128]{1,0:T(8,128)S(1)}, u32[]{:S(2)}, u32[]{:S(2)}) %collective-permute-start.5) | collective-permute-done | bytes 196640 | tf_op jit(solution)/shard_map/ppermute | solution.py:45
  26.4 1.6 %collective-permute-start.11 = (f32[768,128]{1,0:T(8,128)S(1)}, f32[768,128]{1,0:T(8,128)S(1)}, u32[]{:S(2)}, u32[]{:S(2)}) collective-permute-start(f32[768,128]{1,0:T(8,128)S(1)} %get-tuple-element.32.witness.b0), channel_id=1, source_target_pairs={{0,24},{1,97},{2,26},{3,99},{4,28},{5,101},{6,30},{7,103},{8,0},{9... | collective-permute-start | bytes 1179656 | tf_op jit(solution)/shard_map/ppermute | solution.py:45
  28.1 1.4 %collective-permute-start.9 = (f32[768,128]{1,0:T(8,128)S(1)}, f32[768,128]{1,0:T(8,128)S(1)}, u32[]{:S(2)}, u32[]{:S(2)}) collective-permute-start(f32[768,128]{1,0:T(8,128)S(1)} %get-tuple-element.32.witness.b0), channel_id=1, source_target_pairs={{0,16},{1,65},{2,18},{3,67},{4,20},{5,69},{6,22},{7,71},{8,24},{9,... | collective-permute-start | bytes 1179656 | tf_op jit(solution)/shard_map/ppermute | solution.py:45
  29.4 2.1 %shard_map.77 = (bf16[176,2688]{1,0:T(8,128)(2,1)S(1)}, bf16[176,2688]{1,0:T(8,128)(2,1)S(1)}, bf16[256,2688]{1,0:T(8,128)(2,1)S(1)}, bf16[256,2688]{1,0:T(8,128)(2,1)S(1)}) custom-call(f32[3696,128]{1,0:T(8,128)} %get-tuple-element.30.home, f32[3696,128]{1,0:T(8,128)S(1)} %collective-permute-done.2.home_other, f32[768,128]{1,0:T(8,128)S(1)} %get-tuple-element.32.witness.b0), custom_call_target="tpu_custom_call" | custom-call | flops 1 | bytes 1 | tf_op jit(solution)/shard_map/pallas_call | solution.py:457
  31.6 4.3 %collective-permute-done.13.refs_1_ = f32[1848,128]{1,0:T(8,128)S(1)} collective-permute-done((f32[1848,128]{1,0:T(8,128)S(1)}, f32[1848,128]{1,0:T(8,128)S(1)}, u32[]{:S(2)}, u32[]{:S(2)}) %collective-permute-start.13) | collective-permute-done | bytes 946208 | tf_op jit(solution)/shard_map/ppermute | solution.py:45
  37.0 1.5 %collective-permute-done.9.refs_2_.b1 = f32[768,128]{1,0:T(8,128)S(1)} collective-permute-done((f32[768,128]{1,0:T(8,128)S(1)}, f32[768,128]{1,0:T(8,128)S(1)}, u32[]{:S(2)}, u32[]{:S(2)}) %collective-permute-start.9) | collective-permute-done | bytes 393248 | tf_op jit(solution)/shard_map/ppermute | solution.py:45
  38.5 5.8 %collective-permute-start.15 = (f32[1848,128]{1,0:T(8,128)S(1)}, f32[1848,128]{1,0:T(8,128)S(1)}, u32[]{:S(2)}, u32[]{:S(2)}) collective-permute-start(f32[1848,128]{1,0:T(8,128)S(1)} %get-tuple-element.39.above), channel_id=1, source_target_pairs={{0,1},{1,0},{2,3},{3,2},{4,5},{5,4},{6,7},{7,6},{8,9},{9,8},{10,11... | collective-permute-start | bytes 2838536 | tf_op jit(solution)/shard_map/ppermute | solution.py:49
  44.3 2.4 %collective-permute-start.6 = (f32[768,128]{1,0:T(8,128)S(1)}, f32[768,128]{1,0:T(8,128)S(1)}, u32[]{:S(2)}, u32[]{:S(2)}) collective-permute-start(f32[768,128]{1,0:T(8,128)S(1)} %get-tuple-element.31.b0), channel_id=1, source_target_pairs={{0,16},{1,65},{2,18},{3,67},{4,20},{5,69},{6,22},{7,71},{8,24},{9,... | collective-permute-start | bytes 1179656 | tf_op jit(solution)/shard_map/ppermute | solution.py:45
  46.8 2.7 %collective-permute-start.8 = (f32[768,128]{1,0:T(8,128)S(1)}, f32[768,128]{1,0:T(8,128)S(1)}, u32[]{:S(2)}, u32[]{:S(2)}) collective-permute-start(f32[768,128]{1,0:T(8,128)S(1)} %get-tuple-element.31.b0), channel_id=1, source_target_pairs={{0,24},{1,97},{2,26},{3,99},{4,28},{5,101},{6,30},{7,103},{8,0},{9... | collective-permute-start | bytes 1179656 | tf_op jit(solution)/shard_map/ppermute | solution.py:45
  49.4 2.2 %shard_map.80 = (f32[192,128]{1,0:T(8,128)S(1)}, f32[192,128]{1,0:T(8,128)S(1)}, bf16[144,2688]{1,0:T(8,128)(2,1)S(1)}, bf16[144,2688]{1,0:T(8,128)(2,1)S(1)}) custom-call(f32[768,128]{1,0:T(8,128)S(1)} %get-tuple-element.32.witness.b0, f32[768,128]{1,0:T(8,128)S(1)} %collective-permute-done.9.refs_2_.b1, f32[768,128]{1,0:T(8,128)S(1)} %collective-permute-done.10.refs_3_.b2, ...), custom_call_target="tpu_custom_call" | custom-call | tf_op jit(solution)/shard_map/pallas_call | solution.py:494
  51.7 2.7 %collective-permute-start.18 = (f32[192,128]{1,0:T(8,128)S(1)}, f32[192,128]{1,0:T(8,128)S(1)}, u32[]{:S(2)}, u32[]{:S(2)}) collective-permute-start(f32[192,128]{1,0:T(8,128)S(1)} %get-tuple-element.44), channel_id=1, source_target_pairs={{0,2},{1,7},{2,4},{3,1},{4,6},{5,3},{6,0},{7,5},{8,10},{9,15},{10,... | collective-permute-start | bytes 294920 | tf_op jit(solution)/shard_map/ppermute | solution.py:45
  55.4 1.5 %collective-permute-done.7.b2 = f32[768,128]{1,0:T(8,128)S(1)} collective-permute-done((f32[768,128]{1,0:T(8,128)S(1)}, f32[768,128]{1,0:T(8,128)S(1)}, u32[]{:S(2)}, u32[]{:S(2)}) %collective-permute-start.7) | collective-permute-done | bytes 393248 | tf_op jit(solution)/shard_map/ppermute | solution.py:45
  57.6 2.3 %shard_map.82 = f32[32,8,128]{2,1,0:T(8,128)} custom-call(f32[768,128]{1,0:T(8,128)S(1)} %get-tuple-element.31.b0, f32[768,128]{1,0:T(8,128)S(1)} %collective-permute-done.6.b1, f32[768,128]{1,0:T(8,128)S(1)} %collective-permute-done.7.b2, f32[768,128]{1,0:T(8,128)S(1)} %collective-permute-done.8.b3, bf16[256,2688]{1,0:T(8,128)(2,1)S(1)} %get-tuple-element.33.v_high, ...), custom_call_target="tpu_custom_call" | custom-call | tf_op jit(solution)/shard_map/pallas_call | solution.py:512
  59.9 6.4 %all-to-all-start = ((f32[32,8,128]{2,1,0:T(8,128)}), f32[32,8,128]{2,1,0:T(8,128)S(1)}, u32[]{:S(2)}, u32[]{:S(2)}) async-start(f32[32,8,128]{2,1,0:T(8,128)} %shard_map.82), calls=%async_computation | async-start | bytes 262144 | tf_op jit(solution)/shard_map/all_to_all | solution.py:520
  66.4 2.8 %shard_map.83 = (f32[18,1296]{1,0:T(8,128)S(1)}, f32[18,1296]{1,0:T(8,128)S(1)}) custom-call(s32[8]{0:T(128)S(1)} %copy-done.3, s32[8]{0:T(128)S(1)} %copy-done.4, f32[8,6]{1,0:T(8,128)S(1)} %copy-done.6, f32[8,36]{1,0:T(8,128)S(1)} %copy-done.7, f32[3,6,1,1296]{3,2,1,0:T(1,128)S(1)} %copy-done.1, f32[108,1,216]{2,1,0:T(1,128)S(1)} %copy-done.5, ...), custom_call_target="tpu_custom_call" | custom-call | flops 100000000 | bytes 1000000 | tf_op jit(solution)/shard_map/pallas_call | solution.py:471
  69.2 4.8 %all-to-all-done.sums = f32[32,8,128]{2,1,0:T(8,128)S(1)} async-done(((f32[32,8,128]{2,1,0:T(8,128)}), f32[32,8,128]{2,1,0:T(8,128)S(1)}, u32[]{:S(2)}, u32[]{:S(2)}) %all-to-all-start) | async-done | bytes 131104 | tf_op jit(solution)/shard_map/all_to_all | solution.py:520
  (46 shorter events, 10.8 us)
Async XLA Ops:
  3.9 9.7 %copy-start = (f32[88,1,2688]{2,1,0:T(1,128)S(1)}, f32[88,1,2688]{2,1,0:T(1,128)}, u32[]{:S(2)}) copy-start(f32[88,1,2688]{2,1,0:T(1,128)} %get-tuple-element.36) | copy-start | bytes 2838532
  3.9 2.6 %collective-permute-start = (f32[104,128]{1,0:T(8,128)}, f32[104,128]{1,0:T(8,128)S(1)}, u32[]{:S(2)}, u32[]{:S(2)}) collective-permute-start(f32[104,128]{1,0:T(8,128)} %get-tuple-element.27), channel_id=1, source_target_pairs={{0,1},{1,0},{2,3},{3,2},{4,5},{5,4},{6,7},{7,6},{8,9},{9,8},{10,11... | collective-permute-start | bytes 159752 | tf_op jit(solution)/shard_map/ppermute | solution.py:49
  7.3 7.6 %collective-permute-start.2 = (f32[3696,128]{1,0:T(8,128)}, f32[3696,128]{1,0:T(8,128)S(1)}, u32[]{:S(2)}, u32[]{:S(2)}) collective-permute-start(f32[3696,128]{1,0:T(8,128)} %get-tuple-element.30.home), channel_id=1, source_target_pairs={{0,1},{1,0},{2,3},{3,2},{4,5},{5,4},{6,7},{7,6},{8,9},{9,8},{10,11... | collective-permute-start | bytes 5677064 | tf_op jit(solution)/shard_map/ppermute | solution.py:49
  7.7 5.8 %collective-permute-start.1 = (f32[192,128]{1,0:T(8,128)S(1)}, f32[192,128]{1,0:T(8,128)S(1)}, u32[]{:S(2)}, u32[]{:S(2)}) collective-permute-start(f32[192,128]{1,0:T(8,128)S(1)} %get-tuple-element.29.near), channel_id=1, source_target_pairs={{0,4},{1,5},{2,6},{3,7},{4,0},{5,1},{6,2},{7,3},{8,12},{9,13},{10,... | collective-permute-start | bytes 294920 | tf_op jit(solution)/shard_map/ppermute | solution.py:45
  10.7 20.8 %collective-permute-start.12 = (f32[1848,128]{1,0:T(8,128)S(1)}, f32[1848,128]{1,0:T(8,128)S(1)}, u32[]{:S(2)}, u32[]{:S(2)}) collective-permute-start(f32[1848,128]{1,0:T(8,128)S(1)} %bitcast.6), channel_id=1, source_target_pairs={{0,2},{1,7},{2,4},{3,1},{4,6},{5,3},{6,0},{7,5},{8,10},{9,15},{10,... | collective-permute-start | bytes 2838536 | tf_op jit(solution)/shard_map/ppermute | solution.py:45
  13.6 22.3 %collective-permute-start.13 = (f32[1848,128]{1,0:T(8,128)S(1)}, f32[1848,128]{1,0:T(8,128)S(1)}, u32[]{:S(2)}, u32[]{:S(2)}) collective-permute-start(f32[1848,128]{1,0:T(8,128)S(1)} %shard_map.78), channel_id=1, source_target_pairs={{0,6},{1,3},{2,0},{3,5},{4,2},{5,7},{6,4},{7,1},{8,14},{9,11},{10,... | collective-permute-start | bytes 2838536 | tf_op jit(solution)/shard_map/ppermute | solution.py:45
  14.9 7.2 %collective-permute-start.3 = (f32[384,128]{1,0:T(8,128)S(1)}, f32[384,128]{1,0:T(8,128)S(1)}, u32[]{:S(2)}, u32[]{:S(2)}) collective-permute-start(f32[384,128]{1,0:T(8,128)S(1)} %shard_map.75.b0), channel_id=1, source_target_pairs={{0,32},{1,9},{2,34},{3,11},{4,36},{5,13},{6,38},{7,15},{8,40},{9,1... | collective-permute-start | bytes 589832 | tf_op jit(solution)/shard_map/ppermute | solution.py:45
  16.6 6.9 %collective-permute-start.4 = (f32[384,128]{1,0:T(8,128)S(1)}, f32[384,128]{1,0:T(8,128)S(1)}, u32[]{:S(2)}, u32[]{:S(2)}) collective-permute-start(f32[384,128]{1,0:T(8,128)S(1)} %shard_map.75.b0), channel_id=1, source_target_pairs={{0,96},{1,25},{2,98},{3,27},{4,100},{5,29},{6,102},{7,31},{8,104},... | collective-permute-start | bytes 589832 | tf_op jit(solution)/shard_map/ppermute | solution.py:45
  18.8 6.3 %collective-permute-start.5 = (f32[384,128]{1,0:T(8,128)S(1)}, f32[384,128]{1,0:T(8,128)S(1)}, u32[]{:S(2)}, u32[]{:S(2)}) collective-permute-start(f32[384,128]{1,0:T(8,128)S(1)} %shard_map.75.b0), channel_id=1, source_target_pairs={{0,64},{1,17},{2,66},{3,19},{4,68},{5,21},{6,70},{7,23},{8,72},{9,... | collective-permute-start | bytes 589832 | tf_op jit(solution)/shard_map/ppermute | solution.py:45
  22.1 6.0 %collective-permute-start.14 = (f32[108,1,216]{2,1,0:T(1,128)S(1)}, f32[108,1,216]{2,1,0:T(1,128)S(1)}, u32[]{:S(2)}, u32[]{:S(2)}) collective-permute-start(f32[108,1,216]{2,1,0:T(1,128)S(1)} %copy-done.5), channel_id=1, source_target_pairs={{0,8},{8,0},{16,24},{24,16},{1,9},{9,1},{17,25},{25,17},{2,10},{10... | collective-permute-start | bytes 279944 | tf_op jit(solution)/shard_map/ppermute | solution.py:428
  25.1 10.7 %collective-permute-start.10 = (f32[768,128]{1,0:T(8,128)S(1)}, f32[768,128]{1,0:T(8,128)S(1)}, u32[]{:S(2)}, u32[]{:S(2)}) collective-permute-start(f32[768,128]{1,0:T(8,128)S(1)} %get-tuple-element.32.witness.b0), channel_id=1, source_target_pairs={{0,8},{1,33},{2,10},{3,35},{4,12},{5,37},{6,14},{7,39},{8,16},{9,4... | collective-permute-start | bytes 1179656 | tf_op jit(solution)/shard_map/ppermute | solution.py:45
  26.4 10.6 %collective-permute-start.11 = (f32[768,128]{1,0:T(8,128)S(1)}, f32[768,128]{1,0:T(8,128)S(1)}, u32[]{:S(2)}, u32[]{:S(2)}) collective-permute-start(f32[768,128]{1,0:T(8,128)S(1)} %get-tuple-element.32.witness.b0), channel_id=1, source_target_pairs={{0,24},{1,97},{2,26},{3,99},{4,28},{5,101},{6,30},{7,103},{8,0},{9... | collective-permute-start | bytes 1179656 | tf_op jit(solution)/shard_map/ppermute | solution.py:45
  28.1 10.5 %collective-permute-start.9 = (f32[768,128]{1,0:T(8,128)S(1)}, f32[768,128]{1,0:T(8,128)S(1)}, u32[]{:S(2)}, u32[]{:S(2)}) collective-permute-start(f32[768,128]{1,0:T(8,128)S(1)} %get-tuple-element.32.witness.b0), channel_id=1, source_target_pairs={{0,16},{1,65},{2,18},{3,67},{4,20},{5,69},{6,22},{7,71},{8,24},{9,... | collective-permute-start | bytes 1179656 | tf_op jit(solution)/shard_map/ppermute | solution.py:45
  38.5 10.9 %collective-permute-start.15 = (f32[1848,128]{1,0:T(8,128)S(1)}, f32[1848,128]{1,0:T(8,128)S(1)}, u32[]{:S(2)}, u32[]{:S(2)}) collective-permute-start(f32[1848,128]{1,0:T(8,128)S(1)} %get-tuple-element.39.above), channel_id=1, source_target_pairs={{0,1},{1,0},{2,3},{3,2},{4,5},{5,4},{6,7},{7,6},{8,9},{9,8},{10,11... | collective-permute-start | bytes 2838536 | tf_op jit(solution)/shard_map/ppermute | solution.py:49
  44.3 5.1 %collective-permute-start.16 = (f32[1848,128]{1,0:T(8,128)S(1)}, f32[1848,128]{1,0:T(8,128)S(1)}, u32[]{:S(2)}, u32[]{:S(2)}) collective-permute-start(f32[1848,128]{1,0:T(8,128)S(1)} %get-tuple-element.38.below), channel_id=1, source_target_pairs={{0,1},{1,0},{2,3},{3,2},{4,5},{5,4},{6,7},{7,6},{8,9},{9,8},{10,11... | collective-permute-start | bytes 2838536 | tf_op jit(solution)/shard_map/ppermute | solution.py:49
  44.3 11.1 %collective-permute-start.6 = (f32[768,128]{1,0:T(8,128)S(1)}, f32[768,128]{1,0:T(8,128)S(1)}, u32[]{:S(2)}, u32[]{:S(2)}) collective-permute-start(f32[768,128]{1,0:T(8,128)S(1)} %get-tuple-element.31.b0), channel_id=1, source_target_pairs={{0,16},{1,65},{2,18},{3,67},{4,20},{5,69},{6,22},{7,71},{8,24},{9,... | collective-permute-start | bytes 1179656 | tf_op jit(solution)/shard_map/ppermute | solution.py:45
  46.8 10.2 %collective-permute-start.7 = (f32[768,128]{1,0:T(8,128)S(1)}, f32[768,128]{1,0:T(8,128)S(1)}, u32[]{:S(2)}, u32[]{:S(2)}) collective-permute-start(f32[768,128]{1,0:T(8,128)S(1)} %get-tuple-element.31.b0), channel_id=1, source_target_pairs={{0,8},{1,33},{2,10},{3,35},{4,12},{5,37},{6,14},{7,39},{8,16},{9,4... | collective-permute-start | bytes 1179656 | tf_op jit(solution)/shard_map/ppermute | solution.py:45
  46.8 10.2 %collective-permute-start.8 = (f32[768,128]{1,0:T(8,128)S(1)}, f32[768,128]{1,0:T(8,128)S(1)}, u32[]{:S(2)}, u32[]{:S(2)}) collective-permute-start(f32[768,128]{1,0:T(8,128)S(1)} %get-tuple-element.31.b0), channel_id=1, source_target_pairs={{0,24},{1,97},{2,26},{3,99},{4,28},{5,101},{6,30},{7,103},{8,0},{9... | collective-permute-start | bytes 1179656 | tf_op jit(solution)/shard_map/ppermute | solution.py:45
  51.6 6.0 %collective-permute-start.17 = (f32[192,128]{1,0:T(8,128)S(1)}, f32[192,128]{1,0:T(8,128)S(1)}, u32[]{:S(2)}, u32[]{:S(2)}) collective-permute-start(f32[192,128]{1,0:T(8,128)S(1)} %get-tuple-element.43.below_sum), channel_id=1, source_target_pairs={{0,6},{1,3},{2,0},{3,5},{4,2},{5,7},{6,4},{7,1},{8,14},{9,11},{10,... | collective-permute-start | bytes 294920 | tf_op jit(solution)/shard_map/ppermute | solution.py:45
  51.7 5.9 %collective-permute-start.18 = (f32[192,128]{1,0:T(8,128)S(1)}, f32[192,128]{1,0:T(8,128)S(1)}, u32[]{:S(2)}, u32[]{:S(2)}) collective-permute-start(f32[192,128]{1,0:T(8,128)S(1)} %get-tuple-element.44), channel_id=1, source_target_pairs={{0,2},{1,7},{2,4},{3,1},{4,6},{5,3},{6,0},{7,5},{8,10},{9,15},{10,... | collective-permute-start | bytes 294920 | tf_op jit(solution)/shard_map/ppermute | solution.py:45
  57.6 8.8 %copy-start.4 = (s32[8]{0:T(128)S(1)}, s32[8]{0:T(128)}, u32[]{:S(2)}) copy-start(s32[8]{0:T(128)} %vir_ref.3) | copy-start | bytes 100
  57.6 8.8 %copy-start.6 = (f32[8,6]{1,0:T(8,128)S(1)}, f32[8,6]{1,0:T(8,128)}, u32[]{:S(2)}) copy-start(f32[8,6]{1,0:T(8,128)} %eps_occ_ref.1) | copy-start | bytes 580
  57.6 8.8 %copy-start.7 = (f32[8,36]{1,0:T(8,128)S(1)}, f32[8,36]{1,0:T(8,128)}, u32[]{:S(2)}) copy-start(f32[8,36]{1,0:T(8,128)} %eps_vir_ref.1) | copy-start | bytes 3460
  59.9 14.1 %all-to-all-start = ((f32[32,8,128]{2,1,0:T(8,128)}), f32[32,8,128]{2,1,0:T(8,128)S(1)}, u32[]{:S(2)}, u32[]{:S(2)}) async-start(f32[32,8,128]{2,1,0:T(8,128)} %shard_map.82), calls=%async_computation | async-start | bytes 262144 | tf_op jit(solution)/shard_map/all_to_all | solution.py:520
  (5 other events, 30.3 us)

commit v16 on v15

--- a/solution.py
+++ b/solution.py
@@ -72,8 +72,8 @@
         for at, (source, target) in enumerate(((occ_ref, occ), (vir_ref, vir), (amp_ref, amp)))
     ]
     cuts = [
-        window_copy(integrals, first_v, cut_sems.at[0], y + 1 + 2 * core),
-        window_copy(integrals, second_v, cut_sems.at[1], y + 3 - 2 * core),
+        window_copy(integrals, first_v, cut_sems.at[0], y + 3 - 2 * core),
+        window_copy(integrals, second_v, cut_sems.at[1], y + 1 + 2 * core),
         window_copy(integrals, home.at[0], cut_sems.at[2], y),
         window_copy(integrals, home.at[1], cut_sems.at[3], y + 2),
     ]
@@ -424,7 +424,7 @@
         compiler_params=HUGE,
     )(occ_count, vir_count, amplitudes, integrals)
     got = swap_core(send)
-    moved_a = ring(flat(first_v), "yy", (1, -1))
+    moved_a = ring(flat(first_v), "yy", (-1, 1))
     partner = lax.ppermute(ovov, "z", [(0, 1), (1, 0), (2, 3), (3, 2)])
     home = home.reshape(2 * PROWS, LANES)
     pair, home = pl.pallas_call(
@@ -445,7 +445,7 @@
         compiler_params=SMALL,
     )(pair, far_pair, home_other)
     (second_v,) = hold([flat(second_v)], far_pair)
-    moved_b = ring(second_v, "yy", (-1, 1))
+    moved_b = ring(second_v, "yy", (1, -1))
 
     near, far = pl.pallas_call(
         gather_four,
@@ -499,8 +499,8 @@
         scratch_shapes=[pltpu.VMEM((16, DEPTH), F32), pltpu.VMEM((LANES, 2 * LANES), F32)],
         compiler_params=LARGE,
     )(*near_blocks, moved_a, swapped_b, moved_b, swapped_a)
-    back_a = ring(below_sum, "yy", (-1, 1))
-    back_b = ring(above_sum, "yy", (1, -1))
+    back_a = ring(below_sum, "yy", (1, -1))
+    back_b = ring(above_sum, "yy", (-1, 1))
     here_sum = pl.pallas_call(
         multiply_home,
         out_shape=sums,

time: 75.2 us -> 73 us (0.971)
  starting transfers between devices: 36.5 us -> 33 us
  waiting for transfers between devices: 22.1 us -> 23.2 us
    ppermute x4, starting transfers between devices: 7.72 us -> 4.25 us  [swap_core(): return lax.ppermute(value, 'core', [(0, 1), (1, 0)])]
    ppermute x14, waiting for transfers between devices: 16.2 us -> 17.3 us  [ring(): return lax.ppermute(value, AXES, pairs)]
  transfers between devices with their start and end apart: 20 -> 20, of which waited for: 11 -> 10; matrix products, arithmetic and copies ran while one was open for 0% -> 0% of each run, Pallas kernels for 11% -> 11%
where the time goes in v16:
time: 73 us; the launch traced here: 72.5 us
  starting transfers between devices  33 us (45%)
  waiting for transfers between devices  23.2 us (32%)
  Pallas kernels  15.3 us (21%)
  local copies, waits for them, and re-layouts  0.84 us (1%)
    ppermute x14, starting transfers between devices, ring(): return lax.ppermute(value, AXES, pairs)  22.8 us
    ppermute x14, waiting for transfers between devices, ring(): return lax.ppermute(value, AXES, pairs)  17.3 us
    all_to_all x1, starting transfers between devices, on_device(): ladder = lax.all_to_all(packed, ('x', 'z', 'core'), 0, 0, tiled=True)  5.99 us
    all_to_all x1, waiting for transfers between devices, on_device(): ladder = lax.all_to_all(packed, ('x', 'z', 'core'), 0, 0, tiled=True)  4.82 us
    ppermute x4, starting transfers between devices, swap_core(): return lax.ppermute(value, 'core', [(0, 1), (1, 0)])  4.25 us
    pallas_call x1, Pallas kernels, on_device(): pl.pallas_call(open_step, out_shape=[shape((SHARD, LANES), F32)] * 2 + [w...  3.87 us
    pallas_call x1, Pallas kernels, on_device(): pl.pallas_call(local_step, out_shape=[shape((18, 1296), F32)] * 2, in_spe...  2.83 us
    pallas_call x1, Pallas kernels, on_device(): pl.pallas_call(multiply_far, out_shape=shape((32, 8, LANES), F32), in_spe...  2.27 us
  transfers between devices with their start and end apart: 20, of which 10 were waited for; matrix products, arithmetic and copies ran while one was open for 0% of the time, Pallas kernels for 11%

profile of v16, /device:TPU:1, one launch (start us, length us, event | category | flops | bytes accessed | tf_op | source)
XLA Modules:
  0.0 72.5 jit_solution(4105083685717274883)
XLA Ops:
  0.0 3.9 %shard_map.73 = (f32[104,128]{1,0:T(8,128)}, f32[104,128]{1,0:T(8,128)}, f32[88,1,2688]{2,1,0:T(1,128)}, f32[88,1,2688]{2,1,0:T(1,128)}, f32[2,88,1,2688]{3,2,1,0:T(1,128)}) custom-call(s32[8]{0:T(128)} %occ_ref.3, s32[8]{0:T(128)} %vir_ref.3, f32[3,6,1,1296]{3,2,1,0:T(1,128)} %amp_ref.3, f32[81,1,10368]{2,1,0:T(1,128)} %bitcast.5), custom_call_target="tpu_custom_call" | custom-call | tf_op jit(solution)/shard_map/pallas_call | solution.py:404
  3.9 1.5 %collective-permute-start = (f32[104,128]{1,0:T(8,128)}, f32[104,128]{1,0:T(8,128)S(1)}, u32[]{:S(2)}, u32[]{:S(2)}) collective-permute-start(f32[104,128]{1,0:T(8,128)} %get-tuple-element.27), channel_id=1, source_target_pairs={{0,1},{1,0},{2,3},{3,2},{4,5},{5,4},{6,7},{7,6},{8,9},{9,8},{10,11... | collective-permute-start | bytes 159752 | tf_op jit(solution)/shard_map/ppermute | solution.py:49
  7.7 3.0 %collective-permute-start.1 = (f32[192,128]{1,0:T(8,128)S(1)}, f32[192,128]{1,0:T(8,128)S(1)}, u32[]{:S(2)}, u32[]{:S(2)}) collective-permute-start(f32[192,128]{1,0:T(8,128)S(1)} %get-tuple-element.29.near), channel_id=1, source_target_pairs={{0,4},{1,5},{2,6},{3,7},{4,0},{5,1},{6,2},{7,3},{8,12},{9,13},{10,... | collective-permute-start | bytes 294920 | tf_op jit(solution)/shard_map/ppermute | solution.py:45
  11.1 2.4 %collective-permute-done.1.far.refs_1_ = f32[192,128]{1,0:T(8,128)S(1)} collective-permute-done((f32[192,128]{1,0:T(8,128)S(1)}, f32[192,128]{1,0:T(8,128)S(1)}, u32[]{:S(2)}, u32[]{:S(2)}) %collective-permute-start.1) | collective-permute-done | bytes 98336 | tf_op jit(solution)/shard_map/ppermute | solution.py:45
  13.6 2.7 %collective-permute-start.13 = (f32[1848,128]{1,0:T(8,128)S(1)}, f32[1848,128]{1,0:T(8,128)S(1)}, u32[]{:S(2)}, u32[]{:S(2)}) collective-permute-start(f32[1848,128]{1,0:T(8,128)S(1)} %shard_map.78), channel_id=1, source_target_pairs={{0,2},{1,7},{2,4},{3,1},{4,6},{5,3},{6,0},{7,5},{8,10},{9,15},{10,... | collective-permute-start | bytes 2838536 | tf_op jit(solution)/shard_map/ppermute | solution.py:45
  16.3 1.7 %collective-permute-start.3 = (f32[384,128]{1,0:T(8,128)S(1)}, f32[384,128]{1,0:T(8,128)S(1)}, u32[]{:S(2)}, u32[]{:S(2)}) collective-permute-start(f32[384,128]{1,0:T(8,128)S(1)} %shard_map.75.b0), channel_id=1, source_target_pairs={{0,32},{1,9},{2,34},{3,11},{4,36},{5,13},{6,38},{7,15},{8,40},{9,1... | collective-permute-start | bytes 589832 | tf_op jit(solution)/shard_map/ppermute | solution.py:45
  18.1 2.2 %collective-permute-start.4 = (f32[384,128]{1,0:T(8,128)S(1)}, f32[384,128]{1,0:T(8,128)S(1)}, u32[]{:S(2)}, u32[]{:S(2)}) collective-permute-start(f32[384,128]{1,0:T(8,128)S(1)} %shard_map.75.b0), channel_id=1, source_target_pairs={{0,96},{1,25},{2,98},{3,27},{4,100},{5,29},{6,102},{7,31},{8,104},... | collective-permute-start | bytes 589832 | tf_op jit(solution)/shard_map/ppermute | solution.py:45
  21.5 2.0 %collective-permute-done.3.b1 = f32[384,128]{1,0:T(8,128)S(1)} collective-permute-done((f32[384,128]{1,0:T(8,128)S(1)}, f32[384,128]{1,0:T(8,128)S(1)}, u32[]{:S(2)}, u32[]{:S(2)}) %collective-permute-start.3) | collective-permute-done | bytes 196640 | tf_op jit(solution)/shard_map/ppermute | solution.py:45
  25.0 1.5 %collective-permute-done.5.b3 = f32[384,128]{1,0:T(8,128)S(1)} collective-permute-done((f32[384,128]{1,0:T(8,128)S(1)}, f32[384,128]{1,0:T(8,128)S(1)}, u32[]{:S(2)}, u32[]{:S(2)}) %collective-permute-start.5) | collective-permute-done | bytes 196640 | tf_op jit(solution)/shard_map/ppermute | solution.py:45
  29.3 1.5 %collective-permute-start.9 = (f32[768,128]{1,0:T(8,128)S(1)}, f32[768,128]{1,0:T(8,128)S(1)}, u32[]{:S(2)}, u32[]{:S(2)}) collective-permute-start(f32[768,128]{1,0:T(8,128)S(1)} %get-tuple-element.32.witness.b0), channel_id=1, source_target_pairs={{0,16},{1,65},{2,18},{3,67},{4,20},{5,69},{6,22},{7,71},{8,24},{9,... | collective-permute-start | bytes 1179656 | tf_op jit(solution)/shard_map/ppermute | solution.py:45
  30.9 2.1 %shard_map.77 = (bf16[176,2688]{1,0:T(8,128)(2,1)S(1)}, bf16[176,2688]{1,0:T(8,128)(2,1)S(1)}, bf16[256,2688]{1,0:T(8,128)(2,1)S(1)}, bf16[256,2688]{1,0:T(8,128)(2,1)S(1)}) custom-call(f32[3696,128]{1,0:T(8,128)} %get-tuple-element.30.home, f32[3696,128]{1,0:T(8,128)S(1)} %collective-permute-done.2.home_other, f32[768,128]{1,0:T(8,128)S(1)} %get-tuple-element.32.witness.b0), custom_call_target="tpu_custom_call" | custom-call | flops 1 | bytes 1 | tf_op jit(solution)/shard_map/pallas_call | solution.py:457
  33.0 1.8 %collective-permute-done.13.refs_1_ = f32[1848,128]{1,0:T(8,128)S(1)} collective-permute-done((f32[1848,128]{1,0:T(8,128)S(1)}, f32[1848,128]{1,0:T(8,128)S(1)}, u32[]{:S(2)}, u32[]{:S(2)}) %collective-permute-start.13) | collective-permute-done | bytes 946208 | tf_op jit(solution)/shard_map/ppermute | solution.py:45
  34.8 5.2 %collective-permute-done.9.refs_2_.b1 = f32[768,128]{1,0:T(8,128)S(1)} collective-permute-done((f32[768,128]{1,0:T(8,128)S(1)}, f32[768,128]{1,0:T(8,128)S(1)}, u32[]{:S(2)}, u32[]{:S(2)}) %collective-permute-start.9) | collective-permute-done | bytes 393248 | tf_op jit(solution)/shard_map/ppermute | solution.py:45
  40.0 2.3 %collective-permute-start.15 = (f32[1848,128]{1,0:T(8,128)S(1)}, f32[1848,128]{1,0:T(8,128)S(1)}, u32[]{:S(2)}, u32[]{:S(2)}) collective-permute-start(f32[1848,128]{1,0:T(8,128)S(1)} %get-tuple-element.39.above), channel_id=1, source_target_pairs={{0,1},{1,0},{2,3},{3,2},{4,5},{5,4},{6,7},{7,6},{8,9},{9,8},{10,11... | collective-permute-start | bytes 2838536 | tf_op jit(solution)/shard_map/ppermute | solution.py:49
  42.3 1.5 %collective-permute-start.6 = (f32[768,128]{1,0:T(8,128)S(1)}, f32[768,128]{1,0:T(8,128)S(1)}, u32[]{:S(2)}, u32[]{:S(2)}) collective-permute-start(f32[768,128]{1,0:T(8,128)S(1)} %get-tuple-element.31.b0), channel_id=1, source_target_pairs={{0,16},{1,65},{2,18},{3,67},{4,20},{5,69},{6,22},{7,71},{8,24},{9,... | collective-permute-start | bytes 1179656 | tf_op jit(solution)/shard_map/ppermute | solution.py:45
  44.4 2.1 %collective-permute-start.8 = (f32[768,128]{1,0:T(8,128)S(1)}, f32[768,128]{1,0:T(8,128)S(1)}, u32[]{:S(2)}, u32[]{:S(2)}) collective-permute-start(f32[768,128]{1,0:T(8,128)S(1)} %get-tuple-element.31.b0), channel_id=1, source_target_pairs={{0,24},{1,97},{2,26},{3,99},{4,28},{5,101},{6,30},{7,103},{8,0},{9... | collective-permute-start | bytes 1179656 | tf_op jit(solution)/shard_map/ppermute | solution.py:45
  46.5 2.2 %shard_map.80 = (f32[192,128]{1,0:T(8,128)S(1)}, f32[192,128]{1,0:T(8,128)S(1)}, bf16[144,2688]{1,0:T(8,128)(2,1)S(1)}, bf16[144,2688]{1,0:T(8,128)(2,1)S(1)}) custom-call(f32[768,128]{1,0:T(8,128)S(1)} %get-tuple-element.32.witness.b0, f32[768,128]{1,0:T(8,128)S(1)} %collective-permute-done.9.refs_2_.b1, f32[768,128]{1,0:T(8,128)S(1)} %collective-permute-done.10.refs_3_.b2, ...), custom_call_target="tpu_custom_call" | custom-call | tf_op jit(solution)/shard_map/pallas_call | solution.py:494
  48.7 1.5 %collective-permute-start.17 = (f32[192,128]{1,0:T(8,128)S(1)}, f32[192,128]{1,0:T(8,128)S(1)}, u32[]{:S(2)}, u32[]{:S(2)}) collective-permute-start(f32[192,128]{1,0:T(8,128)S(1)} %get-tuple-element.43.below_sum), channel_id=1, source_target_pairs={{0,2},{1,7},{2,4},{3,1},{4,6},{5,3},{6,0},{7,5},{8,10},{9,15},{10,... | collective-permute-start | bytes 294920 | tf_op jit(solution)/shard_map/ppermute | solution.py:45
  50.2 1.5 %collective-permute-start.18 = (f32[192,128]{1,0:T(8,128)S(1)}, f32[192,128]{1,0:T(8,128)S(1)}, u32[]{:S(2)}, u32[]{:S(2)}) collective-permute-start(f32[192,128]{1,0:T(8,128)S(1)} %get-tuple-element.44), channel_id=1, source_target_pairs={{0,6},{1,3},{2,0},{3,5},{4,2},{5,7},{6,4},{7,1},{8,14},{9,11},{10,... | collective-permute-start | bytes 294920 | tf_op jit(solution)/shard_map/ppermute | solution.py:45
  52.8 2.1 %collective-permute-done.7.b2 = f32[768,128]{1,0:T(8,128)S(1)} collective-permute-done((f32[768,128]{1,0:T(8,128)S(1)}, f32[768,128]{1,0:T(8,128)S(1)}, u32[]{:S(2)}, u32[]{:S(2)}) %collective-permute-start.7) | collective-permute-done | bytes 393248 | tf_op jit(solution)/shard_map/ppermute | solution.py:45
  55.7 2.3 %shard_map.82 = f32[32,8,128]{2,1,0:T(8,128)} custom-call(f32[768,128]{1,0:T(8,128)S(1)} %get-tuple-element.31.b0, f32[768,128]{1,0:T(8,128)S(1)} %collective-permute-done.6.b1, f32[768,128]{1,0:T(8,128)S(1)} %collective-permute-done.7.b2, f32[768,128]{1,0:T(8,128)S(1)} %collective-permute-done.8.b3, bf16[256,2688]{1,0:T(8,128)(2,1)S(1)} %get-tuple-element.33.v_high, ...), custom_call_target="tpu_custom_call" | custom-call | tf_op jit(solution)/shard_map/pallas_call | solution.py:512
  57.9 6.0 %all-to-all-start = ((f32[32,8,128]{2,1,0:T(8,128)}), f32[32,8,128]{2,1,0:T(8,128)S(1)}, u32[]{:S(2)}, u32[]{:S(2)}) async-start(f32[32,8,128]{2,1,0:T(8,128)} %shard_map.82), calls=%async_computation | async-start | bytes 262144 | tf_op jit(solution)/shard_map/all_to_all | solution.py:520
  64.0 2.8 %shard_map.83 = (f32[18,1296]{1,0:T(8,128)S(1)}, f32[18,1296]{1,0:T(8,128)S(1)}) custom-call(s32[8]{0:T(128)S(1)} %copy-done.3, s32[8]{0:T(128)S(1)} %copy-done.4, f32[8,6]{1,0:T(8,128)S(1)} %copy-done.6, f32[8,36]{1,0:T(8,128)S(1)} %copy-done.7, f32[3,6,1,1296]{3,2,1,0:T(1,128)S(1)} %copy-done.1, f32[108,1,216]{2,1,0:T(1,128)S(1)} %copy-done.5, ...), custom_call_target="tpu_custom_call" | custom-call | flops 100000000 | bytes 1000000 | tf_op jit(solution)/shard_map/pallas_call | solution.py:471
  66.8 4.8 %all-to-all-done.sums = f32[32,8,128]{2,1,0:T(8,128)S(1)} async-done(((f32[32,8,128]{2,1,0:T(8,128)}), f32[32,8,128]{2,1,0:T(8,128)S(1)}, u32[]{:S(2)}, u32[]{:S(2)}) %all-to-all-start) | async-done | bytes 131104 | tf_op jit(solution)/shard_map/all_to_all | solution.py:520
  (46 shorter events, 11.5 us)
Async XLA Ops:
  3.9 9.7 %copy-start = (f32[88,1,2688]{2,1,0:T(1,128)S(1)}, f32[88,1,2688]{2,1,0:T(1,128)}, u32[]{:S(2)}) copy-start(f32[88,1,2688]{2,1,0:T(1,128)} %get-tuple-element.36) | copy-start | bytes 2838532
  3.9 2.6 %collective-permute-start = (f32[104,128]{1,0:T(8,128)}, f32[104,128]{1,0:T(8,128)S(1)}, u32[]{:S(2)}, u32[]{:S(2)}) collective-permute-start(f32[104,128]{1,0:T(8,128)} %get-tuple-element.27), channel_id=1, source_target_pairs={{0,1},{1,0},{2,3},{3,2},{4,5},{5,4},{6,7},{7,6},{8,9},{9,8},{10,11... | collective-permute-start | bytes 159752 | tf_op jit(solution)/shard_map/ppermute | solution.py:49
  7.3 9.0 %collective-permute-start.2 = (f32[3696,128]{1,0:T(8,128)}, f32[3696,128]{1,0:T(8,128)S(1)}, u32[]{:S(2)}, u32[]{:S(2)}) collective-permute-start(f32[3696,128]{1,0:T(8,128)} %get-tuple-element.30.home), channel_id=1, source_target_pairs={{0,1},{1,0},{2,3},{3,2},{4,5},{5,4},{6,7},{7,6},{8,9},{9,8},{10,11... | collective-permute-start | bytes 5677064 | tf_op jit(solution)/shard_map/ppermute | solution.py:49
  7.7 5.8 %collective-permute-start.1 = (f32[192,128]{1,0:T(8,128)S(1)}, f32[192,128]{1,0:T(8,128)S(1)}, u32[]{:S(2)}, u32[]{:S(2)}) collective-permute-start(f32[192,128]{1,0:T(8,128)S(1)} %get-tuple-element.29.near), channel_id=1, source_target_pairs={{0,4},{1,5},{2,6},{3,7},{4,0},{5,1},{6,2},{7,3},{8,12},{9,13},{10,... | collective-permute-start | bytes 294920 | tf_op jit(solution)/shard_map/ppermute | solution.py:45
  10.7 22.2 %collective-permute-start.12 = (f32[1848,128]{1,0:T(8,128)S(1)}, f32[1848,128]{1,0:T(8,128)S(1)}, u32[]{:S(2)}, u32[]{:S(2)}) collective-permute-start(f32[1848,128]{1,0:T(8,128)S(1)} %bitcast.6), channel_id=1, source_target_pairs={{0,6},{1,3},{2,0},{3,5},{4,2},{5,7},{6,4},{7,1},{8,14},{9,11},{10,... | collective-permute-start | bytes 2838536 | tf_op jit(solution)/shard_map/ppermute | solution.py:45
  13.6 10.0 %copy-start.5 = (f32[108,1,216]{2,1,0:T(1,128)S(1)}, f32[108,1,216]{2,1,0:T(1,128)}, u32[]{:S(2)}) copy-start(f32[108,1,216]{2,1,0:T(1,128)} %ovov.1) | copy-start | bytes 279940
  13.6 21.2 %collective-permute-start.13 = (f32[1848,128]{1,0:T(8,128)S(1)}, f32[1848,128]{1,0:T(8,128)S(1)}, u32[]{:S(2)}, u32[]{:S(2)}) collective-permute-start(f32[1848,128]{1,0:T(8,128)S(1)} %shard_map.78), channel_id=1, source_target_pairs={{0,2},{1,7},{2,4},{3,1},{4,6},{5,3},{6,0},{7,5},{8,10},{9,15},{10,... | collective-permute-start | bytes 2838536 | tf_op jit(solution)/shard_map/ppermute | solution.py:45
  16.3 7.2 %collective-permute-start.3 = (f32[384,128]{1,0:T(8,128)S(1)}, f32[384,128]{1,0:T(8,128)S(1)}, u32[]{:S(2)}, u32[]{:S(2)}) collective-permute-start(f32[384,128]{1,0:T(8,128)S(1)} %shard_map.75.b0), channel_id=1, source_target_pairs={{0,32},{1,9},{2,34},{3,11},{4,36},{5,13},{6,38},{7,15},{8,40},{9,1... | collective-permute-start | bytes 589832 | tf_op jit(solution)/shard_map/ppermute | solution.py:45
  18.1 6.9 %collective-permute-start.4 = (f32[384,128]{1,0:T(8,128)S(1)}, f32[384,128]{1,0:T(8,128)S(1)}, u32[]{:S(2)}, u32[]{:S(2)}) collective-permute-start(f32[384,128]{1,0:T(8,128)S(1)} %shard_map.75.b0), channel_id=1, source_target_pairs={{0,96},{1,25},{2,98},{3,27},{4,100},{5,29},{6,102},{7,31},{8,104},... | collective-permute-start | bytes 589832 | tf_op jit(solution)/shard_map/ppermute | solution.py:45
  20.3 6.3 %collective-permute-start.5 = (f32[384,128]{1,0:T(8,128)S(1)}, f32[384,128]{1,0:T(8,128)S(1)}, u32[]{:S(2)}, u32[]{:S(2)}) collective-permute-start(f32[384,128]{1,0:T(8,128)S(1)} %shard_map.75.b0), channel_id=1, source_target_pairs={{0,64},{1,17},{2,66},{3,19},{4,68},{5,21},{6,70},{7,23},{8,72},{9,... | collective-permute-start | bytes 589832 | tf_op jit(solution)/shard_map/ppermute | solution.py:45
  23.5 5.8 %collective-permute-start.14 = (f32[108,1,216]{2,1,0:T(1,128)S(1)}, f32[108,1,216]{2,1,0:T(1,128)S(1)}, u32[]{:S(2)}, u32[]{:S(2)}) collective-permute-start(f32[108,1,216]{2,1,0:T(1,128)S(1)} %copy-done.5), channel_id=1, source_target_pairs={{0,8},{8,0},{16,24},{24,16},{1,9},{9,1},{17,25},{25,17},{2,10},{10... | collective-permute-start | bytes 279944 | tf_op jit(solution)/shard_map/ppermute | solution.py:428
  26.6 8.2 %collective-permute-start.10 = (f32[768,128]{1,0:T(8,128)S(1)}, f32[768,128]{1,0:T(8,128)S(1)}, u32[]{:S(2)}, u32[]{:S(2)}) collective-permute-start(f32[768,128]{1,0:T(8,128)S(1)} %get-tuple-element.32.witness.b0), channel_id=1, source_target_pairs={{0,8},{1,33},{2,10},{3,35},{4,12},{5,37},{6,14},{7,39},{8,16},{9,4... | collective-permute-start | bytes 1179656 | tf_op jit(solution)/shard_map/ppermute | solution.py:45
  27.9 6.9 %collective-permute-start.11 = (f32[768,128]{1,0:T(8,128)S(1)}, f32[768,128]{1,0:T(8,128)S(1)}, u32[]{:S(2)}, u32[]{:S(2)}) collective-permute-start(f32[768,128]{1,0:T(8,128)S(1)} %get-tuple-element.32.witness.b0), channel_id=1, source_target_pairs={{0,24},{1,97},{2,26},{3,99},{4,28},{5,101},{6,30},{7,103},{8,0},{9... | collective-permute-start | bytes 1179656 | tf_op jit(solution)/shard_map/ppermute | solution.py:45
  29.3 10.7 %collective-permute-start.9 = (f32[768,128]{1,0:T(8,128)S(1)}, f32[768,128]{1,0:T(8,128)S(1)}, u32[]{:S(2)}, u32[]{:S(2)}) collective-permute-start(f32[768,128]{1,0:T(8,128)S(1)} %get-tuple-element.32.witness.b0), channel_id=1, source_target_pairs={{0,16},{1,65},{2,18},{3,67},{4,20},{5,69},{6,22},{7,71},{8,24},{9,... | collective-permute-start | bytes 1179656 | tf_op jit(solution)/shard_map/ppermute | solution.py:45
  40.0 6.5 %collective-permute-start.15 = (f32[1848,128]{1,0:T(8,128)S(1)}, f32[1848,128]{1,0:T(8,128)S(1)}, u32[]{:S(2)}, u32[]{:S(2)}) collective-permute-start(f32[1848,128]{1,0:T(8,128)S(1)} %get-tuple-element.39.above), channel_id=1, source_target_pairs={{0,1},{1,0},{2,3},{3,2},{4,5},{5,4},{6,7},{7,6},{8,9},{9,8},{10,11... | collective-permute-start | bytes 2838536 | tf_op jit(solution)/shard_map/ppermute | solution.py:49
  42.3 4.2 %collective-permute-start.16 = (f32[1848,128]{1,0:T(8,128)S(1)}, f32[1848,128]{1,0:T(8,128)S(1)}, u32[]{:S(2)}, u32[]{:S(2)}) collective-permute-start(f32[1848,128]{1,0:T(8,128)S(1)} %get-tuple-element.38.below), channel_id=1, source_target_pairs={{0,1},{1,0},{2,3},{3,2},{4,5},{5,4},{6,7},{7,6},{8,9},{9,8},{10,11... | collective-permute-start | bytes 2838536 | tf_op jit(solution)/shard_map/ppermute | solution.py:49
  42.3 10.5 %collective-permute-start.6 = (f32[768,128]{1,0:T(8,128)S(1)}, f32[768,128]{1,0:T(8,128)S(1)}, u32[]{:S(2)}, u32[]{:S(2)}) collective-permute-start(f32[768,128]{1,0:T(8,128)S(1)} %get-tuple-element.31.b0), channel_id=1, source_target_pairs={{0,16},{1,65},{2,18},{3,67},{4,20},{5,69},{6,22},{7,71},{8,24},{9,... | collective-permute-start | bytes 1179656 | tf_op jit(solution)/shard_map/ppermute | solution.py:45
  43.8 11.1 %collective-permute-start.7 = (f32[768,128]{1,0:T(8,128)S(1)}, f32[768,128]{1,0:T(8,128)S(1)}, u32[]{:S(2)}, u32[]{:S(2)}) collective-permute-start(f32[768,128]{1,0:T(8,128)S(1)} %get-tuple-element.31.b0), channel_id=1, source_target_pairs={{0,8},{1,33},{2,10},{3,35},{4,12},{5,37},{6,14},{7,39},{8,16},{9,4... | collective-permute-start | bytes 1179656 | tf_op jit(solution)/shard_map/ppermute | solution.py:45
  44.4 10.5 %collective-permute-start.8 = (f32[768,128]{1,0:T(8,128)S(1)}, f32[768,128]{1,0:T(8,128)S(1)}, u32[]{:S(2)}, u32[]{:S(2)}) collective-permute-start(f32[768,128]{1,0:T(8,128)S(1)} %get-tuple-element.31.b0), channel_id=1, source_target_pairs={{0,24},{1,97},{2,26},{3,99},{4,28},{5,101},{6,30},{7,103},{8,0},{9... | collective-permute-start | bytes 1179656 | tf_op jit(solution)/shard_map/ppermute | solution.py:45
  48.7 6.3 %collective-permute-start.17 = (f32[192,128]{1,0:T(8,128)S(1)}, f32[192,128]{1,0:T(8,128)S(1)}, u32[]{:S(2)}, u32[]{:S(2)}) collective-permute-start(f32[192,128]{1,0:T(8,128)S(1)} %get-tuple-element.43.below_sum), channel_id=1, source_target_pairs={{0,2},{1,7},{2,4},{3,1},{4,6},{5,3},{6,0},{7,5},{8,10},{9,15},{10,... | collective-permute-start | bytes 294920 | tf_op jit(solution)/shard_map/ppermute | solution.py:45
  50.2 5.4 %collective-permute-start.18 = (f32[192,128]{1,0:T(8,128)S(1)}, f32[192,128]{1,0:T(8,128)S(1)}, u32[]{:S(2)}, u32[]{:S(2)}) collective-permute-start(f32[192,128]{1,0:T(8,128)S(1)} %get-tuple-element.44), channel_id=1, source_target_pairs={{0,6},{1,3},{2,0},{3,5},{4,2},{5,7},{6,4},{7,1},{8,14},{9,11},{10,... | collective-permute-start | bytes 294920 | tf_op jit(solution)/shard_map/ppermute | solution.py:45
  55.6 8.3 %copy-start.6 = (f32[8,6]{1,0:T(8,128)S(1)}, f32[8,6]{1,0:T(8,128)}, u32[]{:S(2)}) copy-start(f32[8,6]{1,0:T(8,128)} %eps_occ_ref.1) | copy-start | bytes 580
  55.7 8.3 %copy-start.7 = (f32[8,36]{1,0:T(8,128)S(1)}, f32[8,36]{1,0:T(8,128)}, u32[]{:S(2)}) copy-start(f32[8,36]{1,0:T(8,128)} %eps_vir_ref.1) | copy-start | bytes 3460
  57.9 13.7 %all-to-all-start = ((f32[32,8,128]{2,1,0:T(8,128)}), f32[32,8,128]{2,1,0:T(8,128)S(1)}, u32[]{:S(2)}, u32[]{:S(2)}) async-start(f32[32,8,128]{2,1,0:T(8,128)} %shard_map.82), calls=%async_computation | async-start | bytes 262144 | tf_op jit(solution)/shard_map/all_to_all | solution.py:520
  (5 other events, 29.2 us)
